TPU v7x, 256 devices: a whole 4x4x8 slice. The times are simulated.
256 devices in a mesh: dp: 32 (over y, z), col: 8 (over x, core).
Axes of the slice: x: 4, y: 4, z: 8, core: 2. Of those that a mesh axis runs over, the one named last changes fastest.
Arguments:
- grads: bfloat16 [65536, 4096], P('dp', 'col'), may hold values from -6 to 6
- signs: int32 [65536], P('dp'), may hold values from -1 to 1, as said below
- picks: int32 [128], replicated, may hold values from 0 to 511, as said below
Outputs:
- gram: float32 [4096, 4096], P('dp', 'col')
Inputs may be any that keep to these rules, and one draw needn't show every extreme that they name: `signs`: each entry is +1 or -1. `picks`: the 128 indices are distinct; both 0 and 511 are always among them.
All inputs are finite; a program needn't handle non-finite values.
Results may differ from a plain program's by a relative error of at most 0.0026.
Values may be sent and summed in bfloat16 or wider, within the bound.
No kernel may reach another device: no remote copies, remote signals or barrier semaphores. Data moves between devices by JAX's collectives and lax.ppermute only.
A program may use at most 128 MiB of HBM per device.

v0:
```python
import math

import jax
import jax.numpy as jnp
from jax import lax
from jax.sharding import PartitionSpec as P

BLOCK = 128


def parity_sign(left, right):
    both = jnp.bitwise_and(left, right)
    count = jnp.zeros_like(both)
    for shift_bit in range(16):
        count = count + jnp.bitwise_and(jnp.right_shift(both, shift_bit), 1)
    return 1 - 2 * jnp.bitwise_and(count, 1)


def hadamard_table(order):
    index = jnp.arange(order, dtype=jnp.int32)
    return parity_sign(index[:, None], index[None, :])


def sketch_gram(sketch, sketch_total):
    whole = lax.all_gather(sketch, "col", axis=1, tiled=True)
    gram = lax.psum_scatter(
        lax.dot_general(
            whole, sketch, (((0,), (0,)), ((), ())), preferred_element_type=jnp.float32
        ),
        "dp",
        scatter_dimension=0,
        tiled=True,
    )
    return gram / jnp.float32(sketch_total)


def on_device(grads, signs, picks):
    rows_dev, width = grads.shape
    groups = lax.axis_size("dp")
    rank = lax.axis_index("dp")
    flipped = grads * signs.astype(jnp.bfloat16)[:, None]
    table = hadamard_table(rows_dev).astype(jnp.bfloat16)
    local = jnp.dot(table, flipped, preferred_element_type=jnp.float32).astype(jnp.bfloat16)
    scale = 1.0 / math.sqrt(rows_dev * groups)
    per_dev = rows_dev // BLOCK
    share = picks.shape[0] // groups
    blocks = local.reshape(per_dev, BLOCK, width)
    outgoing = blocks[jnp.remainder(picks, per_dev)].reshape(picks.shape[0] * BLOCK, width)
    incoming = lax.all_to_all(outgoing, "dp", split_axis=0, concat_axis=0, tiled=True)
    incoming = incoming.reshape(groups, share, BLOCK, width)
    mine = lax.dynamic_slice_in_dim(picks, rank * share, share)
    sources = jnp.arange(groups, dtype=jnp.int32)
    signs_mix = parity_sign(sources[:, None], (mine // per_dev)[None, :]).astype(jnp.bfloat16)
    mixed = jnp.einsum("sm,smtc->mtc", signs_mix, incoming, preferred_element_type=jnp.float32)
    sketch = (mixed * scale).astype(jnp.bfloat16).reshape(share * BLOCK, width)
    return sketch_gram(sketch, picks.shape[0] * BLOCK)


def solution(mesh):
    placed = (P("dp", "col"), P("dp"), P())
    return jax.shard_map(
        on_device, mesh=mesh, in_specs=placed, out_specs=P("dp", "col"), check_vma=False
    )
```

profile of v0, /device:TPU:64, one launch (start us, length us, event | category | flops | bytes accessed | tf_op | source)
XLA Modules:
  0.0 762.0 jit_solution(15454747802610738292)
XLA Ops:
  6.5 0.7 convert_element_type.17
  7.2 0.7 compare_select_fusion
  7.9 30.9 %fusion.19 = bf16[2048,512]{1,0:T(8,128)(2,1)S(1)} fusion(bf16[2048,512]{1,0:T(8,128)(2,1)} %param.3, bf16[2048]{0:T(1024)(128)(2,1)S(1)} %convert_element_type.17), kind=kOutput, calls=%fused_computation.21 | convolution fusion | flops 4515168256 | bytes 4198400 | tf_op jit(solution)/shard_map/dot_general | solution.py:43
  38.8 8.3 %gather_fusion = bf16[128,128,512]{2,1,0:T(8,128)(2,1)} fusion(bf16[16,128,512]{2,1,0:T(8,128)(2,1)S(1)} %bitcast.12, s32[1024]{0:T(1024)S(1)} %pad_clamp_fusion), kind=kCustom, calls=%fused_computation | custom fusion | bytes 33554944 | tf_op jit(solution)/shard_map/gather | solution.py:48
  47.1 0.0 copy-start
  47.1 11.1 %all-to-all-start = ((bf16[32,512,512]{2,1,0:T(8,128)(2,1)}), bf16[32,512,512]{2,1,0:T(8,128)(2,1)}, u32[]{:S(2)}, u32[]{:S(2)}) async-start(bf16[32,512,512]{2,1,0:T(8,128)(2,1)} %bitcast.13), calls=%async_computation | async-start | bytes 33554432 | tf_op jit(solution)/shard_map/all_to_all | solution.py:49
  58.2 0.0 all-gather.2.cloned.1.call-start
  58.3 0.0 copy-done
  58.3 0.1 and_select_fusion.1
  58.3 0.1 fusion.24
  58.4 392.0 %all-to-all-done = bf16[32,512,512]{2,1,0:T(8,128)(2,1)} async-done(((bf16[32,512,512]{2,1,0:T(8,128)(2,1)}), bf16[32,512,512]{2,1,0:T(8,128)(2,1)}, u32[]{:S(2)}, u32[]{:S(2)}) %all-to-all-start) | async-done | bytes 16777248 | tf_op jit(solution)/shard_map/all_to_all | solution.py:49
  450.4 15.2 %fusion = f32[4,1,128,512]{3,1,2,0:T(1,128)S(1)} fusion(bf16[32,4,128,512]{3,2,1,0:T(8,128)(2,1)} %bitcast.3, bf16[32,4,1,1]{0,1,2,3:T(4,128)(2,1)S(1)} %fusion.24), kind=kOutput, calls=%fused_computation.1 | convolution fusion | flops 16777216 | bytes 17826048 | tf_op jit(solution)/shard_map/sm,smtc->mtc/dot_general | solution.py:54
  465.6 0.9 fusion.21
  466.5 0.0 all-gather.2.cloned.1.call-update
  466.5 0.0 reduce-scatter.2.cloned.1.call-start
  466.6 50.2 %all-gather.2.cloned.1.call-done = bf16[512,4096]{1,0:T(8,128)(2,1)} async-done(((bf16[512,512]{1,0:T(8,128)(2,1)}), bf16[512,4096]{1,0:T(8,128)(2,1)}) %all-gather.2.cloned.1.call-update) | async-done | bytes 4194320 | tf_op jit(solution)/shard_map/all_gather | solution.py:25
  516.7 7.9 %fusion.42 = f32[4096,512]{1,0:T(8,128)} fusion(bf16[512,4096]{1,0:T(8,128)(2,1)} %all-gather.2.cloned.1.call-done, bf16[512,512]{1,0:T(8,128)(2,1)} %bitcast.15), kind=kOutput, calls=%fused_computation.56 | convolution fusion | flops 2147483648 | bytes 13107200 | tf_op jit(solution)/shard_map/dot_general | solution.py:27
  524.7 0.0 reduce-scatter.2.cloned.1.call-update
  524.7 228.8 %reduce-scatter.2.cloned.1.call-done = f32[128,512]{1,0:T(8,128)} async-done(((f32[4096,512]{1,0:T(8,128)}), f32[128,512]{1,0:T(8,128)}) %reduce-scatter.2.cloned.1.call-update) | async-done | bytes 262160 | tf_op jit(solution)/shard_map/reduce_scatter | solution.py:26
  753.5 1.7 broadcast_multiply_fusion
  (1 shorter events, 0.0 us)
Async XLA Ops:
  47.1 11.2 %copy-start = (s32[128]{0:T(128)S(1)}, s32[128]{0:T(128)}, u32[]{:S(2)}) copy-start(s32[128]{0:T(128)} %param.5) | copy-start | bytes 1540
  47.1 403.3 %all-to-all-start = ((bf16[32,512,512]{2,1,0:T(8,128)(2,1)}), bf16[32,512,512]{2,1,0:T(8,128)(2,1)}, u32[]{:S(2)}, u32[]{:S(2)}) async-start(bf16[32,512,512]{2,1,0:T(8,128)(2,1)} %bitcast.13), calls=%async_computation | async-start | bytes 33554432 | tf_op jit(solution)/shard_map/all_to_all | solution.py:49
  58.2 458.5 %all-gather.2.cloned.1.call-start = ((), (), s32[]{:S(2)}) async-start(), calls=%async_computation.2 | async-start | bytes 4718592 | tf_op jit(solution)/shard_map/all_gather | solution.py:25
  466.5 287.0 %reduce-scatter.2.cloned.1.call-start = ((), (), s32[]{:S(2)}) async-start(), calls=%async_computation.3 | async-start | bytes 8650752 | tf_op jit(solution)/shard_map/reduce_scatter | solution.py:26
Sparse Core Ops, SparseCore 0:
  466.6 50.0 all-gather.1
  524.8 228.6 reduce-scatter.1
where the time goes:
time: 763 us; the launch traced here: 762 us
  waiting for transfers between devices  671 us (88%)
  matrix products  54 us (7%)
  between operations  13.4 us (2%)
  starting transfers between devices  11.2 us (1%)
  local copies, waits for them, and re-layouts  8.29 us (1%)
    all_to_all x1, waiting for transfers between devices, on_device(): lax.all_to_all(outgoing, 'dp', split_axis=0, concat_axis=0, tiled=True)  392 us
    reduce_scatter x1, waiting for transfers between devices, sketch_gram(): lax.psum_scatter(lax.dot_general(whole, sketch, (((0,), (0,)), ((), ())),...  229 us
    all_gather x1, waiting for transfers between devices, sketch_gram(): whole = lax.all_gather(sketch, 'col', axis=1, tiled=True)  50.2 us
    dot_general x1, matrix products, on_device(): jnp.dot(table, flipped, preferred_element_type=jnp.float32)  30.9 us
  transfers between devices with their start and end apart: 3, of which 3 were waited for; matrix products, arithmetic and copies ran while one was open for 0% of the time, Pallas kernels for 0%

commit v1 on v0

v1 whole, which is shorter than its diff:
```python
import jax
import jax.numpy as jnp
from jax import lax
from jax.experimental import pallas as pl
from jax.experimental.pallas import tpu as pltpu
from jax.sharding import PartitionSpec as P

NY, NZ, NX, NCORE = 4, 8, 4, 2
BLOCK = 128
LANES = 128
PER_DEV = 16
N_BLOCKS = 512
CHUNK = BLOCK // NZ
MIB = 1 << 20


def pack_kernel(at, grads_ref, signs_ref, out_ref):
    z = pl.program_id(0)
    for b in range(PER_DEV):
        sign = jnp.broadcast_to(signs_ref[:, b : b + 1], (CHUNK, LANES)).astype(jnp.bfloat16)
        for y in range(NY):
            quarter = lax.rem(z - y + at[0] + NY, NY)
            lanes = pl.ds(pl.multiple_of(quarter * LANES, LANES), LANES)
            out_ref[y, 0, b] = grads_ref[b, :, lanes] * sign


def pack(grads, signs, x):
    blocks = grads.reshape(PER_DEV, BLOCK, NY * LANES)
    columns = signs.reshape(PER_DEV, BLOCK).T.astype(jnp.float32)
    return pl.pallas_call(
        pack_kernel,
        grid_spec=pltpu.PrefetchScalarGridSpec(
            num_scalar_prefetch=1,
            grid=(NZ,),
            in_specs=[
                pl.BlockSpec((PER_DEV, CHUNK, NY * LANES), lambda z, at: (0, z, 0)),
                pl.BlockSpec((CHUNK, PER_DEV), lambda z, at: (z, 0)),
            ],
            out_specs=pl.BlockSpec(
                (NY, 1, PER_DEV, CHUNK, LANES), lambda z, at: (0, z, 0, 0, 0)
            ),
        ),
        out_shape=jax.ShapeDtypeStruct((NY, NZ, PER_DEV, CHUNK, LANES), jnp.bfloat16),
        name="pack",
    )(x.reshape(1), blocks, columns)


def hadamard(parts):
    span = 1
    while span < len(parts):
        done = list(parts)
        for i in range(len(parts)):
            if not i & span:
                done[i] = parts[i] + parts[i + span]
                done[i + span] = parts[i] - parts[i + span]
        parts = done
        span *= 2
    return parts


def mix_kernel(picks_ref, raw_ref, out_ref, work):
    half = N_BLOCKS // 2

    @pl.loop(0, N_BLOCKS // 16)
    def _(d):
        base = d * 16
        parts = [raw_ref[base + b].astype(jnp.float32) for b in range(16)]
        for b, part in enumerate(hadamard(parts)):
            work[base + b] = part

    @pl.loop(0, 32)
    def _(i):
        base = lax.div(i, 16) * half + lax.rem(i, 16)
        parts = [work[base + 16 * e] for e in range(16)]
        for e, part in enumerate(hadamard(parts)):
            work[base + 16 * e] = part

    @pl.loop(0, out_ref.shape[0], unroll=4)
    def _(k):
        pick = picks_ref[k]
        low = lax.rem(pick, half)
        side = (1 - 2 * lax.div(pick, half)).astype(jnp.float32)
        out_ref[k] = (work[low] + side * work[low + half]).astype(out_ref.dtype)


def mix(raw, picks):
    samples = picks.shape[0]
    return pl.pallas_call(
        mix_kernel,
        grid_spec=pltpu.PrefetchScalarGridSpec(
            num_scalar_prefetch=1,
            grid=(1,),
            in_specs=[pl.BlockSpec((N_BLOCKS, CHUNK, LANES), lambda i, p: (0, 0, 0))],
            out_specs=pl.BlockSpec((samples, CHUNK, LANES), lambda i, p: (0, 0, 0)),
            scratch_shapes=[pltpu.VMEM((N_BLOCKS, CHUNK, LANES), jnp.float32)],
        ),
        out_shape=jax.ShapeDtypeStruct((samples, CHUNK, LANES), jnp.bfloat16),
        compiler_params=pltpu.CompilerParams(vmem_limit_bytes=24 * MIB),
        name="mix",
    )(picks, raw)


def gram_kernel(at, *refs):
    cols = refs[:4]
    rows = (refs[4:8], refs[8:12])
    out_ref, flat, right, left, flat_sems, right_sems = refs[12:]
    depth = cols[0].shape[0]
    x, core, turn = at[0], at[1], at[2]
    flat_copies = [
        pltpu.make_async_copy(cols[j], flat.at[j], flat_sems.at[j]) for j in range(NY)
    ]
    right_copies = [
        [
            pltpu.make_async_copy(
                rows[c][j], right.at[j, :, pl.ds(c * LANES, LANES)], right_sems.at[j, c]
            )
            for c in range(NCORE)
        ]
        for j in range(NX)
    ]
    for copy in flat_copies:
        copy.start()
    for pair in right_copies:
        for copy in pair:
            copy.start()
    for j in range(NY):
        flat_copies[j].wait()
        quarter = lax.rem(turn + j, NY)
        where = pl.ds(pl.multiple_of(quarter * LANES, LANES), LANES)
        left[where, :] = flat[j].T
    for j in range(NX):
        for copy in right_copies[j]:
            copy.wait()
        panel = lax.rem(x + NX - j, NX) * NCORE
        for m in range(2):
            part = pl.ds(m * 2 * LANES, 2 * LANES)
            block = jnp.dot(left[part, :], right[j], preferred_element_type=jnp.float32)
            block = block.astype(out_ref.dtype)
            out_ref[panel + core, part, :] = block[:, :LANES]
            out_ref[panel + 1 - core, part, :] = block[:, LANES:]


def gram_part(at, cols, own, other):
    depth = cols[0].shape[0]
    whole = pl.BlockSpec(memory_space=pl.ANY)
    return pl.pallas_call(
        gram_kernel,
        grid_spec=pltpu.PrefetchScalarGridSpec(
            num_scalar_prefetch=1,
            grid=(1,),
            in_specs=[whole] * 12,
            out_specs=pl.BlockSpec((NX * NCORE, NY * LANES, LANES), lambda i, at: (0, 0, 0)),
            scratch_shapes=[
                pltpu.VMEM((NY, depth, LANES), jnp.bfloat16),
                pltpu.VMEM((NX, depth, NCORE * LANES), jnp.bfloat16),
                pltpu.VMEM((NY * LANES, depth), jnp.bfloat16),
                pltpu.SemaphoreType.DMA((NY,)),
                pltpu.SemaphoreType.DMA((NX, NCORE)),
            ],
        ),
        out_shape=jax.ShapeDtypeStruct((NX * NCORE, NY * LANES, LANES), jnp.bfloat16),
        compiler_params=pltpu.CompilerParams(vmem_limit_bytes=32 * MIB),
        name="gram_part",
    )(at, *cols, *own, *other)


def finish_kernel(scale, parts_ref, out_ref):
    total = parts_ref[0].astype(jnp.float32)
    for k in range(1, parts_ref.shape[0]):
        total = total + parts_ref[k].astype(jnp.float32)
    out_ref[...] = (total * scale).T


def finish(parts, scale):
    count, width, rows = parts.shape
    return pl.pallas_call(
        lambda parts_ref, out_ref: finish_kernel(scale, parts_ref, out_ref),
        grid=(width // LANES,),
        in_specs=[pl.BlockSpec((count, LANES, rows), lambda i: (0, i, 0))],
        out_specs=pl.BlockSpec((rows, LANES), lambda i: (0, i)),
        out_shape=jax.ShapeDtypeStruct((rows, width), jnp.float32),
        name="finish",
    )(parts)


def on_device(grads, signs, picks):
    dp, col = lax.axis_index("dp"), lax.axis_index("col")
    y, z = dp // NZ, dp % NZ
    x, core = col // NCORE, col % NCORE

    outgoing = pack(grads, signs, x).reshape(NY * NZ, PER_DEV, CHUNK, LANES)
    raw = lax.all_to_all(outgoing, "dp", split_axis=0, concat_axis=0, tiled=True)
    sketch = mix(raw.reshape(N_BLOCKS, CHUNK, LANES), picks).reshape(-1, LANES)

    def along_x(value, step):
        return lax.ppermute(value, "col", [(i, (i + NCORE * step) % (NX * NCORE)) for i in range(NX * NCORE)])

    def along_y(value, step):
        return lax.ppermute(value, "dp", [(i, (i + NZ * step) % (NY * NZ)) for i in range(NY * NZ)])

    def swap(value):
        return lax.ppermute(value, "col", [(i, i ^ 1) for i in range(NX * NCORE)])

    own = [sketch] + [along_x(sketch, j) for j in range(1, NX)]
    cols = [sketch] + [along_y(sketch, j) for j in range(1, NY)]
    other = [swap(piece) for piece in own]
    at = jnp.stack([x, core, (z - y + x + NY) % NY]).astype(jnp.int32)
    partial = gram_part(at, cols, own, other)

    groups = [
        [gy * NZ + (s + gy) % NY + NY * half for gy in range(NY) for half in range(NZ // NY)]
        for s in range(NY)
    ]
    parts = lax.all_to_all(
        partial, "dp", split_axis=0, concat_axis=0, axis_index_groups=groups, tiled=True
    )
    total_rows = grads.shape[0] * NY * NZ
    scale = BLOCK / (total_rows * picks.shape[0] * BLOCK)
    return finish(parts, scale)


def solution(mesh):
    placed = (P("dp", "col"), P("dp"), P())
    return jax.shard_map(
        on_device, mesh=mesh, in_specs=placed, out_specs=P("dp", "col"), check_vma=False
    )
```

time: 763 us -> 155 us (0.20)
  waiting for transfers between devices: 671 us -> 32.2 us
  blocking collectives: 0 us -> 93.2 us
  matrix products: 54 us -> 0 us
  Pallas kernels: 0 us -> 17.7 us
  between operations: 13.4 us -> 0.04 us
    all_to_all x1 -> x0, waiting for transfers between devices: 392 us -> none  [on_device(): lax.all_to_all(outgoing, 'dp', split_axis=0, concat_axis=0, tiled=True)]
    reduce_scatter x1 -> x0, waiting for transfers between devices: 229 us -> none  [sketch_gram(): lax.psum_scatter(lax.dot_general(whole, sketch, (((0,), (0,)), ((), ())),...]
    all_to_all x0 -> x2, blocking collectives: none -> 93.2 us  [the longest x1 60.3 us: on_device(): lax.all_to_all(outgoing, 'dp', split_axis=0, concat_axis=0, tiled=True)]
    dot_general x3 -> x0, matrix products: 54 us -> none  [the longest x1 30.9 us: on_device(): jnp.dot(table, flipped, preferred_element_type=jnp.float32)]
    all_gather x1 -> x0, waiting for transfers between devices: 50.2 us -> none  [sketch_gram(): whole = lax.all_gather(sketch, 'col', axis=1, tiled=True)]
    ppermute x0 -> x10, waiting for transfers between devices: none -> 32.2 us  [the longest x3 21.8 us: along_x(): lax.ppermute(value, 'col', [(i, (i + NCORE * step) % (NX * NCORE)) for i...]
    pallas_call x0 -> x4, Pallas kernels: none -> 17.7 us  [the longest x1 6.03 us: pack(): pl.pallas_call(pack_kernel, grid_spec=pltpu.PrefetchScalarGridSpec(num_sc...]
    all_to_all x1 -> x0, starting transfers between devices: 11.1 us -> none  [on_device(): lax.all_to_all(outgoing, 'dp', split_axis=0, concat_axis=0, tiled=True)]
  transfers between devices with their start and end apart: 3 -> 10, of which waited for: 3 -> 3; matrix products, arithmetic and copies ran while one was open for 0% -> 0% of each run, Pallas kernels for 0% -> 0%
where the time goes in v1:
time: 155 us; the launch traced here: 153 us
  blocking collectives  93.2 us (60%)
  waiting for transfers between devices  32.2 us (21%)
  Pallas kernels  17.7 us (11%)
  starting transfers between devices  8.33 us (5%)
    all_to_all x1, blocking collectives, on_device(): lax.all_to_all(outgoing, 'dp', split_axis=0, concat_axis=0, tiled=True)  60.3 us
    all_to_all x1, blocking collectives, on_device(): lax.all_to_all(partial, 'dp', split_axis=0, concat_axis=0, axis_index_gro...  32.8 us
    ppermute x3, waiting for transfers between devices, along_x(): lax.ppermute(value, 'col', [(i, (i + NCORE * step) % (NX * NCORE)) for i...  21.8 us
    ppermute x3, waiting for transfers between devices, along_y(): lax.ppermute(value, 'dp', [(i, (i + NZ * step) % (NY * NZ)) for i in rang...  10.4 us
    pallas_call x1, Pallas kernels, pack(): pl.pallas_call(pack_kernel, grid_spec=pltpu.PrefetchScalarGridSpec(num_sc...  6.03 us
    pallas_call x1, Pallas kernels, gram_part(): pl.pallas_call(gram_kernel, grid_spec=pltpu.PrefetchScalarGridSpec(num_sc...  5.2 us
    ppermute x3, starting transfers between devices, along_x(): lax.ppermute(value, 'col', [(i, (i + NCORE * step) % (NX * NCORE)) for i...  4.52 us
    pallas_call x1, Pallas kernels, finish(): pl.pallas_call(lambda parts_ref, out_ref: finish_kernel(scale, parts_ref,...  3.4 us
  transfers between devices with their start and end apart: 10, of which 3 were waited for; matrix products, arithmetic and copies ran while one was open for 0% of the time, Pallas kernels for 0%

profile of v1, /device:TPU:64, one launch (start us, length us, event | category | flops | bytes accessed | tf_op | source)
XLA Modules:
  0.0 153.0 jit_solution(372839660558556427)
XLA Ops:
  0.0 0.7 convert_bitcast_fusion
  0.7 0.7 copy.4
  1.4 6.0 %pack.1 = bf16[4,8,16,16,128]{4,3,2,1,0:T(8,128)(2,1)} custom-call(s32[1]{0:T(128)} %bitcast.at, bf16[16,128,512]{2,1,0:T(8,128)(2,1)} %bitcast.21, f32[128,16]{1,0:T(8,128)} %bitcast.22), custom_call_target="tpu_custom_call" | custom-call | tf_op jit(solution)/shard_map/pack/pallas_call | solution.py:30
  7.5 60.3 %all_to_all.10 = bf16[32,16,16,128]{3,2,1,0:T(8,128)(2,1)S(1)} all-to-all(bf16[32,16,16,128]{3,2,1,0:T(8,128)(2,1)} %bitcast.20), channel_id=1, replica_groups=mesh['dp'=32,'col'=8] {'dp'}, dimensions={0} | all-to-all | bytes 4194304 | tf_op jit(solution)/shard_map/all_to_all | solution.py:192
  67.8 3.1 %mix.1 = bf16[128,16,128]{2,1,0:T(8,128)(2,1)S(1)} custom-call(s32[128]{0:T(128)S(1)} %copy-done, bf16[512,16,128]{2,1,0:T(8,128)(2,1)S(1)} %bitcast.10), custom_call_target="tpu_custom_call" | custom-call | tf_op jit(solution)/shard_map/mix/pallas_call | solution.py:88
  70.9 0.1 collective-permute-start.6
  71.0 2.8 %collective-permute-start.5 = (bf16[2048,128]{1,0:T(8,128)(2,1)S(1)}, bf16[2048,128]{1,0:T(8,128)(2,1)S(1)}, u32[]{:S(2)}, u32[]{:S(2)}) collective-permute-start(bf16[2048,128]{1,0:T(8,128)(2,1)S(1)} %bitcast.12), channel_id=1, source_target_pairs={{0,6},{1,7},{2,0},{3,1},{4,2},{5,3},{6,4},{7,5},{8,14},{9,15},{10,... | collective-permute-start | bytes 1572872 | tf_op jit(solution)/shard_map/ppermute | solution.py:196
  73.8 0.8 collective-permute-start.4
  74.6 0.9 collective-permute-start.3
  75.5 2.1 %collective-permute-start.2 = (bf16[2048,128]{1,0:T(8,128)(2,1)S(1)}, bf16[2048,128]{1,0:T(8,128)(2,1)S(1)}, u32[]{:S(2)}, u32[]{:S(2)}) collective-permute-start(bf16[2048,128]{1,0:T(8,128)(2,1)S(1)} %bitcast.15), channel_id=1, source_target_pairs={{0,192},{8,200},{16,208},{24,216},{32,224},{40,232},{48,240},{56,2... | collective-permute-start | bytes 1572872 | tf_op jit(solution)/shard_map/ppermute | solution.py:199
  77.6 0.0 collective-permute-done.6.refs_8_
  77.6 0.5 collective-permute-start.1
  78.2 18.7 %collective-permute-done.5.refs_7_ = bf16[2048,128]{1,0:T(8,128)(2,1)S(1)} collective-permute-done((bf16[2048,128]{1,0:T(8,128)(2,1)S(1)}, bf16[2048,128]{1,0:T(8,128)(2,1)S(1)}, u32[]{:S(2)}, u32[]{:S(2)}) %collective-permute-start.5) | collective-permute-done | bytes 524320 | tf_op jit(solution)/shard_map/ppermute | solution.py:196
  96.9 0.6 collective-permute-start
  97.5 0.0 collective-permute-done.4.refs_6_
  97.5 0.0 collective-permute-start.9
  97.5 3.1 %collective-permute-done.3.refs_5_ = bf16[2048,128]{1,0:T(8,128)(2,1)S(1)} collective-permute-done((bf16[2048,128]{1,0:T(8,128)(2,1)S(1)}, bf16[2048,128]{1,0:T(8,128)(2,1)S(1)}, u32[]{:S(2)}, u32[]{:S(2)}) %collective-permute-start.3) | collective-permute-done | bytes 524320 | tf_op jit(solution)/shard_map/ppermute | solution.py:196
  100.6 0.0 collective-permute-start.8
  100.6 0.5 collective-permute-start.7
  101.1 0.1 pad_add_fusion.at
  101.2 10.3 %collective-permute-done.refs_1_ = bf16[2048,128]{1,0:T(8,128)(2,1)} collective-permute-done((bf16[2048,128]{1,0:T(8,128)(2,1)S(1)}, bf16[2048,128]{1,0:T(8,128)(2,1)}, u32[]{:S(2)}, u32[]{:S(2)}) %collective-permute-start) | collective-permute-done | bytes 524320 | tf_op jit(solution)/shard_map/ppermute | solution.py:199
  111.5 5.2 %gram_part.1 = bf16[8,512,128]{2,1,0:T(8,128)(2,1)S(1)} custom-call(s32[3]{0:T(128)S(1)} %pad_add_fusion.at, bf16[2048,128]{1,0:T(8,128)(2,1)S(1)} %bitcast.18, bf16[2048,128]{1,0:T(8,128)(2,1)} %collective-permute-done.refs_1_, bf16[2048,128]{1,0:T(8,128)(2,1)} %collective-permute-done.1.refs_2_, bf16[2048,128]{1,0:T(8,128)(2,1)S(1)} %collective-permute-done.2.refs_3_, ...), custom_call_target="tpu_custom_call" | custom-call | tf_op jit(solution)/shard_map/gram_part/pallas_call | solution.py:146
  116.7 32.8 %all_to_all.11.parts_ref = bf16[8,512,128]{2,1,0:T(8,128)(2,1)} all-to-all(bf16[8,512,128]{2,1,0:T(8,128)(2,1)S(1)} %gram_part.1), channel_id=1, replica_groups={{0,32,72,104,144,176,216,248},{8,40,80,112,152,184,192,224},{16,48,88,1..., dimensions={0} | all-to-all | bytes 2097152 | tf_op jit(solution)/shard_map/all_to_all | solution.py:214
  149.6 3.4 %finish.1 = f32[128,512]{1,0:T(8,128)} custom-call(bf16[8,512,128]{2,1,0:T(8,128)(2,1)} %all_to_all.11.parts_ref), custom_call_target="tpu_custom_call" | custom-call | tf_op jit(solution)/shard_map/finish/pallas_call | solution.py:176
  (7 shorter events, 0.0 us)
Async XLA Ops:
  7.5 60.3 %copy-start = (s32[128]{0:T(128)S(1)}, s32[128]{0:T(128)}, u32[]{:S(2)}) copy-start(s32[128]{0:T(128)} %picks_ref.1) | copy-start | bytes 1540
  70.9 6.7 %collective-permute-start.6 = (bf16[2048,128]{1,0:T(8,128)(2,1)S(1)}, bf16[2048,128]{1,0:T(8,128)(2,1)S(1)}, u32[]{:S(2)}, u32[]{:S(2)}) collective-permute-start(bf16[2048,128]{1,0:T(8,128)(2,1)S(1)} %bitcast.11), channel_id=1, source_target_pairs={{0,1},{1,0},{2,3},{3,2},{4,5},{5,4},{6,7},{7,6},{8,9},{9,8},{10,11... | collective-permute-start | bytes 1572872 | tf_op jit(solution)/shard_map/ppermute | solution.py:202
  71.0 25.9 %collective-permute-start.5 = (bf16[2048,128]{1,0:T(8,128)(2,1)S(1)}, bf16[2048,128]{1,0:T(8,128)(2,1)S(1)}, u32[]{:S(2)}, u32[]{:S(2)}) collective-permute-start(bf16[2048,128]{1,0:T(8,128)(2,1)S(1)} %bitcast.12), channel_id=1, source_target_pairs={{0,6},{1,7},{2,0},{3,1},{4,2},{5,3},{6,4},{7,5},{8,14},{9,15},{10,... | collective-permute-start | bytes 1572872 | tf_op jit(solution)/shard_map/ppermute | solution.py:196
  73.8 23.6 %collective-permute-start.4 = (bf16[2048,128]{1,0:T(8,128)(2,1)S(1)}, bf16[2048,128]{1,0:T(8,128)(2,1)S(1)}, u32[]{:S(2)}, u32[]{:S(2)}) collective-permute-start(bf16[2048,128]{1,0:T(8,128)(2,1)S(1)} %bitcast.13), channel_id=1, source_target_pairs={{0,4},{1,5},{2,6},{3,7},{4,0},{5,1},{6,2},{7,3},{8,12},{9,13},{10,... | collective-permute-start | bytes 1572872 | tf_op jit(solution)/shard_map/ppermute | solution.py:196
  74.6 25.9 %collective-permute-start.3 = (bf16[2048,128]{1,0:T(8,128)(2,1)S(1)}, bf16[2048,128]{1,0:T(8,128)(2,1)S(1)}, u32[]{:S(2)}, u32[]{:S(2)}) collective-permute-start(bf16[2048,128]{1,0:T(8,128)(2,1)S(1)} %bitcast.14), channel_id=1, source_target_pairs={{0,2},{1,3},{2,4},{3,5},{4,6},{5,7},{6,0},{7,1},{8,10},{9,11},{10,... | collective-permute-start | bytes 1572872 | tf_op jit(solution)/shard_map/ppermute | solution.py:196
  75.5 25.1 %collective-permute-start.2 = (bf16[2048,128]{1,0:T(8,128)(2,1)S(1)}, bf16[2048,128]{1,0:T(8,128)(2,1)S(1)}, u32[]{:S(2)}, u32[]{:S(2)}) collective-permute-start(bf16[2048,128]{1,0:T(8,128)(2,1)S(1)} %bitcast.15), channel_id=1, source_target_pairs={{0,192},{8,200},{16,208},{24,216},{32,224},{40,232},{48,240},{56,2... | collective-permute-start | bytes 1572872 | tf_op jit(solution)/shard_map/ppermute | solution.py:199
  77.6 23.5 %collective-permute-start.1 = (bf16[2048,128]{1,0:T(8,128)(2,1)S(1)}, bf16[2048,128]{1,0:T(8,128)(2,1)}, u32[]{:S(2)}, u32[]{:S(2)}) collective-permute-start(bf16[2048,128]{1,0:T(8,128)(2,1)S(1)} %bitcast.16), channel_id=1, source_target_pairs={{0,128},{8,136},{16,144},{24,152},{32,160},{40,168},{48,176},{56,1... | collective-permute-start | bytes 1572872 | tf_op jit(solution)/shard_map/ppermute | solution.py:199
  96.9 14.6 %collective-permute-start = (bf16[2048,128]{1,0:T(8,128)(2,1)S(1)}, bf16[2048,128]{1,0:T(8,128)(2,1)}, u32[]{:S(2)}, u32[]{:S(2)}) collective-permute-start(bf16[2048,128]{1,0:T(8,128)(2,1)S(1)} %bitcast.17), channel_id=1, source_target_pairs={{0,64},{8,72},{16,80},{24,88},{32,96},{40,104},{48,112},{56,120},{... | collective-permute-start | bytes 1572872 | tf_op jit(solution)/shard_map/ppermute | solution.py:199
  97.5 14.0 %collective-permute-start.9 = (bf16[2048,128]{1,0:T(8,128)(2,1)S(1)}, bf16[2048,128]{1,0:T(8,128)(2,1)}, u32[]{:S(2)}, u32[]{:S(2)}) collective-permute-start(bf16[2048,128]{1,0:T(8,128)(2,1)S(1)} %collective-permute-done.5.refs_7_), channel_id=1, source_target_pairs={{0,1},{1,0},{2,3},{3,2},{4,5},{5,4},{6,7},{7,6},{8,9},{9,8},{10,11... | collective-permute-start | bytes 1572872 | tf_op jit(solution)/shard_map/ppermute | solution.py:202
  100.6 10.9 %collective-permute-start.8 = (bf16[2048,128]{1,0:T(8,128)(2,1)S(1)}, bf16[2048,128]{1,0:T(8,128)(2,1)}, u32[]{:S(2)}, u32[]{:S(2)}) collective-permute-start(bf16[2048,128]{1,0:T(8,128)(2,1)S(1)} %collective-permute-done.4.refs_6_), channel_id=1, source_target_pairs={{0,1},{1,0},{2,3},{3,2},{4,5},{5,4},{6,7},{7,6},{8,9},{9,8},{10,11... | collective-permute-start | bytes 1572872 | tf_op jit(solution)/shard_map/ppermute | solution.py:202
  100.6 10.9 %collective-permute-start.7 = (bf16[2048,128]{1,0:T(8,128)(2,1)S(1)}, bf16[2048,128]{1,0:T(8,128)(2,1)}, u32[]{:S(2)}, u32[]{:S(2)}) collective-permute-start(bf16[2048,128]{1,0:T(8,128)(2,1)S(1)} %collective-permute-done.3.refs_5_), channel_id=1, source_target_pairs={{0,1},{1,0},{2,3},{3,2},{4,5},{5,4},{6,7},{7,6},{8,9},{9,8},{10,11... | collective-permute-start | bytes 1572872 | tf_op jit(solution)/shard_map/ppermute | solution.py:202

commit v2 on v1

v2 whole, which is shorter than its diff:
```python
import jax
import jax.numpy as jnp
from jax import lax
from jax.experimental import pallas as pl
from jax.experimental.pallas import tpu as pltpu
from jax.sharding import PartitionSpec as P

NY, NZ, NX, NCORE = 4, 8, 4, 2
BLOCK = 128
LANES = 128
PER_DEV = 16
N_BLOCKS = 512
CHUNK = BLOCK // NZ
MIB = 1 << 20


SCALARS = pl.BlockSpec(memory_space=pltpu.SMEM)
LOCAL = pl.BlockSpec(memory_space=pltpu.VMEM)


def pack_kernel(at, grads_ref, signs_ref, out_ref):
    columns = signs_ref[...].astype(jnp.float32).T
    for z in range(NZ):
        for y in range(NY):
            quarter = lax.rem(z - y + at[0] + NY, NY)
            lanes = pl.ds(pl.multiple_of(quarter * LANES, LANES), LANES)
            for b in range(PER_DEV):
                sign = columns[z * CHUNK : (z + 1) * CHUNK, b : b + 1]
                sign = jnp.broadcast_to(sign, (CHUNK, LANES)).astype(jnp.bfloat16)
                rows = pl.ds(z * CHUNK, CHUNK)
                out_ref[y, z, b] = grads_ref[b, rows, lanes] * sign


def pack(grads, signs, at):
    blocks = grads.reshape(PER_DEV, BLOCK, NY * LANES)
    return pl.pallas_call(
        pack_kernel,
        in_specs=[SCALARS, LOCAL, LOCAL],
        out_specs=LOCAL,
        out_shape=jax.ShapeDtypeStruct((NY, NZ, PER_DEV, CHUNK, LANES), jnp.bfloat16),
        compiler_params=pltpu.CompilerParams(vmem_limit_bytes=16 * MIB),
        name="pack",
    )(at, blocks, signs.reshape(PER_DEV, BLOCK))


def hadamard(parts):
    span = 1
    while span < len(parts):
        done = list(parts)
        for i in range(len(parts)):
            if not i & span:
                done[i] = parts[i] + parts[i + span]
                done[i + span] = parts[i] - parts[i + span]
        parts = done
        span *= 2
    return parts


def mix_kernel(picks_ref, raw_ref, out_ref, work):
    half = N_BLOCKS // 2

    @pl.loop(0, N_BLOCKS // 16)
    def _(d):
        base = d * 16
        parts = [raw_ref[base + b].astype(jnp.float32) for b in range(16)]
        for b, part in enumerate(hadamard(parts)):
            work[base + b] = part

    @pl.loop(0, 32)
    def _(i):
        base = lax.div(i, 16) * half + lax.rem(i, 16)
        parts = [work[base + 16 * e] for e in range(16)]
        for e, part in enumerate(hadamard(parts)):
            work[base + 16 * e] = part

    @pl.loop(0, out_ref.shape[0], unroll=4)
    def _(k):
        pick = picks_ref[k]
        low = lax.rem(pick, half)
        side = (1 - 2 * lax.div(pick, half)).astype(jnp.float32)
        out_ref[k] = (work[low] + side * work[low + half]).astype(out_ref.dtype)


def mix(raw, picks):
    samples = picks.shape[0]
    return pl.pallas_call(
        mix_kernel,
        in_specs=[SCALARS, LOCAL],
        out_specs=LOCAL,
        scratch_shapes=[pltpu.VMEM((N_BLOCKS, CHUNK, LANES), jnp.float32)],
        out_shape=jax.ShapeDtypeStruct((samples, CHUNK, LANES), jnp.bfloat16),
        compiler_params=pltpu.CompilerParams(vmem_limit_bytes=16 * MIB),
        name="mix",
    )(picks, raw)


PIECES = 5


def gram_kernel(at, *refs):
    cols, rows = refs[:PIECES], (refs[PIECES : 2 * PIECES], refs[2 * PIECES : 3 * PIECES])
    out_ref, left = refs[3 * PIECES :]
    half = cols[2].shape[0]
    x, core, turn = at[0], at[1], at[2]
    spots = [(0, 0, 2 * half), (1, 0, 2 * half), (2, 0, half), (2, half, half), (3, 0, 2 * half)]
    for p, (j, start, size) in enumerate(spots):
        quarter = lax.rem(turn + j, NY)
        where = pl.ds(pl.multiple_of(quarter * LANES, LANES), LANES)
        left[where, pl.ds(start, size)] = cols[p][...].T
    for pieces, j in (((0,), 0), ((1,), 1), ((4,), 3), ((2, 3), 2)):
        panel = lax.rem(x + NX - j, NX) * NCORE
        for m in range(2):
            part = pl.ds(m * 2 * LANES, 2 * LANES)
            block = None
            for p in pieces:
                pair = jnp.concatenate([rows[0][p][...], rows[1][p][...]], axis=1)
                depth = pl.ds(spots[p][1], spots[p][2])
                term = jnp.dot(left[part, depth], pair, preferred_element_type=jnp.float32)
                block = term if block is None else block + term
            block = block.astype(out_ref.dtype)
            out_ref[panel + core, part, :] = block[:, :LANES]
            out_ref[panel + 1 - core, part, :] = block[:, LANES:]


def gram_part(at, cols, own, other):
    return pl.pallas_call(
        gram_kernel,
        in_specs=[SCALARS] + [LOCAL] * (3 * PIECES),
        out_specs=LOCAL,
        scratch_shapes=[pltpu.VMEM((NY * LANES, cols[0].shape[0]), jnp.bfloat16)],
        out_shape=jax.ShapeDtypeStruct((NX * NCORE, NY * LANES, LANES), jnp.bfloat16),
        compiler_params=pltpu.CompilerParams(vmem_limit_bytes=24 * MIB),
        name="gram_part",
    )(at, *cols, *own, *other)


def finish_kernel(scale, parts_ref, out_ref):
    for i in range(out_ref.shape[1] // LANES):
        part = pl.ds(i * LANES, LANES)
        total = parts_ref[0, part].astype(jnp.float32)
        for k in range(1, parts_ref.shape[0]):
            total = total + parts_ref[k, part].astype(jnp.float32)
        out_ref[:, part] = (total * scale).T


def finish(parts, scale):
    count, width, rows = parts.shape
    return pl.pallas_call(
        lambda parts_ref, out_ref: finish_kernel(scale, parts_ref, out_ref),
        out_shape=jax.ShapeDtypeStruct((rows, width), jnp.float32),
        compiler_params=pltpu.CompilerParams(vmem_limit_bytes=16 * MIB),
        name="finish",
    )(parts)


def on_device(grads, signs, picks):
    dp, col = lax.axis_index("dp"), lax.axis_index("col")
    y, z = lax.div(dp, NZ), lax.rem(dp, NZ)
    x, core = lax.div(col, NCORE), lax.rem(col, NCORE)
    at = jnp.stack([x, core, lax.rem(z - y + x + NY, NY)])

    outgoing = pack(grads, signs, at).reshape(NY * NZ, PER_DEV, CHUNK, LANES)
    raw = lax.all_to_all(outgoing, "dp", split_axis=0, concat_axis=0, tiled=True)
    sketch = mix(raw.reshape(N_BLOCKS, CHUNK, LANES), picks).reshape(-1, LANES)

    def along_x(value, step):
        return lax.ppermute(value, "col", [(i, (i + NCORE * step) % (NX * NCORE)) for i in range(NX * NCORE)])

    def along_y(value, step):
        return lax.ppermute(value, "dp", [(i, (i + NZ * step) % (NY * NZ)) for i in range(NY * NZ)])

    def swap(value):
        return lax.ppermute(value, "col", [(i, i ^ 1) for i in range(NX * NCORE)])

    depth = sketch.shape[0] // 2
    x_up, x_down = along_x(sketch, 1), along_x(sketch, -1)
    y_up, y_down = along_y(sketch, 1), along_y(sketch, -1)
    x_far = (along_x(x_up[:depth], 1), along_x(x_down[depth:], -1))
    y_far = (along_y(y_up[:depth], 1), along_y(y_down[depth:], -1))
    own = [sketch, x_up, *x_far, x_down]
    cols = [sketch, y_up, *y_far, y_down]
    other = [swap(piece) for piece in own]
    partial = gram_part(at, cols, own, other)

    groups = [
        [gy * NZ + (s + gy) % NY + NY * half for gy in range(NY) for half in range(NZ // NY)]
        for s in range(NY)
    ]
    parts = lax.all_to_all(
        partial, "dp", split_axis=0, concat_axis=0, axis_index_groups=groups, tiled=True
    )
    total_rows = grads.shape[0] * NY * NZ
    scale = BLOCK / (total_rows * picks.shape[0] * BLOCK)
    return finish(parts, scale)


def solution(mesh):
    placed = (P("dp", "col"), P("dp"), P())
    return jax.shard_map(
        on_device, mesh=mesh, in_specs=placed, out_specs=P("dp", "col"), check_vma=False
    )
```

time: 155 us -> 136 us (0.88)
  waiting for transfers between devices: 32.2 us -> 18.2 us
  Pallas kernels: 17.7 us -> 8.46 us
  starting transfers between devices: 8.33 us -> 11.6 us
  local copies, waits for them, and re-layouts: 0.74 us -> 2.37 us
    ppermute x3 -> x4, waiting for transfers between devices: 21.8 us -> 8.68 us  [along_x(): lax.ppermute(value, 'col', [(i, (i + NCORE * step) % (NX * NCORE)) for i...]
    pallas_call x3, Pallas kernels: 14.3 us -> 7.55 us  [the longest x1 3.45 us: gram_part(): pl.pallas_call(gram_kernel, in_specs=[SCALARS] + [LOCAL] * (3 * PIECES),...]
    pallas_call x1, Pallas kernels: 3.4 us -> 0.91 us  [finish(): pl.pallas_call(lambda parts_ref, out_ref: finish_kernel(scale, parts_ref,...]
    unnamed x2 -> x6, local copies, waits for them, and re-layouts: 0.01 us -> 2.29 us
    ppermute x3 -> x4, starting transfers between devices: 4.52 us -> 6.69 us  [along_x(): lax.ppermute(value, 'col', [(i, (i + NCORE * step) % (NX * NCORE)) for i...]
    ppermute x3 -> x4, starting transfers between devices: 3.21 us -> 4.22 us  [along_y(): lax.ppermute(value, 'dp', [(i, (i + NZ * step) % (NY * NZ)) for i in rang...]
    ppermute x3 -> x4, waiting for transfers between devices: 10.4 us -> 9.35 us  [along_y(): lax.ppermute(value, 'dp', [(i, (i + NZ * step) % (NY * NZ)) for i in rang...]
  transfers between devices with their start and end apart: 10 -> 13, of which waited for: 3 -> 6; matrix products, arithmetic and copies ran while one was open for 0% -> 0% of each run, Pallas kernels for 0% -> 0%
where the time goes in v2:
time: 136 us; the launch traced here: 135 us
  blocking collectives  94.3 us (69%)
  waiting for transfers between devices  18.2 us (13%)
  starting transfers between devices  11.6 us (9%)
  Pallas kernels  8.46 us (6%)
  local copies, waits for them, and re-layouts  2.37 us (2%)
    all_to_all x1, blocking collectives, on_device(): lax.all_to_all(outgoing, 'dp', split_axis=0, concat_axis=0, tiled=True)  60 us
    all_to_all x1, blocking collectives, on_device(): lax.all_to_all(partial, 'dp', split_axis=0, concat_axis=0, axis_index_gro...  34.3 us
    ppermute x4, waiting for transfers between devices, along_y(): lax.ppermute(value, 'dp', [(i, (i + NZ * step) % (NY * NZ)) for i in rang...  9.35 us
    ppermute x4, waiting for transfers between devices, along_x(): lax.ppermute(value, 'col', [(i, (i + NCORE * step) % (NX * NCORE)) for i...  8.68 us
    ppermute x4, starting transfers between devices, along_x(): lax.ppermute(value, 'col', [(i, (i + NCORE * step) % (NX * NCORE)) for i...  6.69 us
    ppermute x4, starting transfers between devices, along_y(): lax.ppermute(value, 'dp', [(i, (i + NZ * step) % (NY * NZ)) for i in rang...  4.22 us
    pallas_call x1, Pallas kernels, gram_part(): pl.pallas_call(gram_kernel, in_specs=[SCALARS] + [LOCAL] * (3 * PIECES),...  3.45 us
    pallas_call x1, Pallas kernels, mix(): pl.pallas_call(mix_kernel, in_specs=[SCALARS, LOCAL], out_specs=LOCAL, sc...  3.1 us
  transfers between devices with their start and end apart: 13, of which 6 were waited for; matrix products, arithmetic and copies ran while one was open for 0% of the time, Pallas kernels for 0%

profile of v2, /device:TPU:64, one launch (start us, length us, event | category | flops | bytes accessed | tf_op | source)
XLA Modules:
  0.0 135.1 jit_solution(5887455717808881180)
XLA Ops:
  0.0 0.1 pad_add_fusion.at
  0.1 1.6 %copy-done = bf16[2048,512]{1,0:T(8,128)(2,1)S(1)} copy-done((bf16[2048,512]{1,0:T(8,128)(2,1)S(1)}, bf16[2048,512]{1,0:T(8,128)(2,1)}, u32[]{:S(2)}) %copy-start) | copy-done | bytes 2097176
  1.7 0.7 copy-done.1
  2.4 1.0 pack.1
  3.4 0.0 copy-start.2
  3.4 60.0 %all_to_all.10 = bf16[32,16,16,128]{3,2,1,0:T(8,128)(2,1)S(1)} all-to-all(bf16[32,16,16,128]{3,2,1,0:T(8,128)(2,1)S(1)} %bitcast.9), channel_id=1, replica_groups=mesh['dp'=32,'col'=8] {'dp'}, dimensions={0} | all-to-all | bytes 4194304 | tf_op jit(solution)/shard_map/all_to_all | solution.py:163
  63.4 3.1 %mix.1 = bf16[128,16,128]{2,1,0:T(8,128)(2,1)S(1)} custom-call(s32[128]{0:T(128)S(1)} %copy-done.2, bf16[512,16,128]{2,1,0:T(8,128)(2,1)S(1)} %bitcast.8), custom_call_target="tpu_custom_call" | custom-call | tf_op jit(solution)/shard_map/mix/pallas_call | solution.py:86
  66.5 2.8 %collective-permute-start.6 = (bf16[2048,128]{1,0:T(8,128)(2,1)S(1)}, bf16[2048,128]{1,0:T(8,128)(2,1)S(1)}, u32[]{:S(2)}, u32[]{:S(2)}) collective-permute-start(bf16[2048,128]{1,0:T(8,128)(2,1)S(1)} %bitcast.10), channel_id=1, source_target_pairs={{0,6},{1,7},{2,0},{3,1},{4,2},{5,3},{6,4},{7,5},{8,14},{9,15},{10,... | collective-permute-start | bytes 1572872 | tf_op jit(solution)/shard_map/ppermute | solution.py:167
  69.3 2.1 %collective-permute-start.2 = (bf16[2048,128]{1,0:T(8,128)(2,1)S(1)}, bf16[2048,128]{1,0:T(8,128)(2,1)S(1)}, u32[]{:S(2)}, u32[]{:S(2)}) collective-permute-start(bf16[2048,128]{1,0:T(8,128)(2,1)S(1)} %bitcast.12), channel_id=1, source_target_pairs={{0,192},{8,200},{16,208},{24,216},{32,224},{40,232},{48,240},{56,2... | collective-permute-start | bytes 1572872 | tf_op jit(solution)/shard_map/ppermute | solution.py:170
  71.5 7.4 %collective-permute-done.6.refs_9_ = bf16[2048,128]{1,0:T(8,128)(2,1)S(1)} collective-permute-done((bf16[2048,128]{1,0:T(8,128)(2,1)S(1)}, bf16[2048,128]{1,0:T(8,128)(2,1)S(1)}, u32[]{:S(2)}, u32[]{:S(2)}) %collective-permute-start.6) | collective-permute-done | bytes 524320 | tf_op jit(solution)/shard_map/ppermute | solution.py:167
  78.9 3.8 %collective-permute-start.7 = (bf16[1024,128]{1,0:T(8,128)(2,1)S(1)}, bf16[1024,128]{1,0:T(8,128)(2,1)S(1)}, u32[]{:S(2)}, u32[]{:S(2)}) collective-permute-start(bf16[1024,128]{1,0:T(8,128)(2,1)S(1)} %slice.19), channel_id=1, source_target_pairs={{0,6},{1,7},{2,0},{3,1},{4,2},{5,3},{6,4},{7,5},{8,14},{9,15},{10,... | collective-permute-start | bytes 786440 | tf_op jit(solution)/shard_map/ppermute | solution.py:167
  82.7 0.1 collective-permute-start.5
  82.8 0.1 collective-permute-start.12
  82.9 0.6 collective-permute-start.9
  83.5 3.5 %collective-permute-done.refs_1_ = bf16[2048,128]{1,0:T(8,128)(2,1)S(1)} collective-permute-done((bf16[2048,128]{1,0:T(8,128)(2,1)S(1)}, bf16[2048,128]{1,0:T(8,128)(2,1)S(1)}, u32[]{:S(2)}, u32[]{:S(2)}) %collective-permute-start) | collective-permute-done | bytes 524320 | tf_op jit(solution)/shard_map/ppermute | solution.py:170
  87.0 2.1 %collective-permute-start.1 = (bf16[1024,128]{1,0:T(8,128)(2,1)S(1)}, bf16[1024,128]{1,0:T(8,128)(2,1)S(1)}, u32[]{:S(2)}, u32[]{:S(2)}) collective-permute-start(bf16[1024,128]{1,0:T(8,128)(2,1)S(1)} %slice.16), channel_id=1, source_target_pairs={{0,64},{8,72},{16,80},{24,88},{32,96},{40,104},{48,112},{56,120},{... | collective-permute-start | bytes 786440 | tf_op jit(solution)/shard_map/ppermute | solution.py:170
  89.1 1.2 collective-permute-done.5.refs_7_
  90.4 4.6 %collective-permute-done.3.refs_3_ = bf16[1024,128]{1,0:T(8,128)(2,1)S(1)} collective-permute-done((bf16[1024,128]{1,0:T(8,128)(2,1)S(1)}, bf16[1024,128]{1,0:T(8,128)(2,1)S(1)}, u32[]{:S(2)}, u32[]{:S(2)}) %collective-permute-start.3) | collective-permute-done | bytes 262176 | tf_op jit(solution)/shard_map/ppermute | solution.py:170
  94.9 0.0 collective-permute-start.10
  94.9 1.3 collective-permute-done.1.refs_2_
  96.3 0.2 collective-permute-done.10.refs_12_
  96.5 3.5 %gram_part.1 = bf16[8,512,128]{2,1,0:T(8,128)(2,1)S(1)} custom-call(s32[3]{0:T(128)S(1)} %pad_add_fusion.at, bf16[2048,128]{1,0:T(8,128)(2,1)S(1)} %bitcast.15, bf16[2048,128]{1,0:T(8,128)(2,1)S(1)} %collective-permute-done.refs_1_, bf16[1024,128]{1,0:T(8,128)(2,1)S(1)} %collective-permute-done.1.refs_2_, ...), custom_call_target="tpu_custom_call" | custom-call | tf_op jit(solution)/shard_map/gram_part/pallas_call | solution.py:126
  99.9 34.3 %all_to_all.11.parts_ref = bf16[8,512,128]{2,1,0:T(8,128)(2,1)S(1)} all-to-all(bf16[8,512,128]{2,1,0:T(8,128)(2,1)S(1)} %gram_part.1), channel_id=1, replica_groups={{0,32,72,104,144,176,216,248},{8,40,80,112,152,184,192,224},{16,48,88,1..., dimensions={0} | all-to-all | bytes 2097152 | tf_op jit(solution)/shard_map/all_to_all | solution.py:189
  134.2 0.9 finish.1
  (19 shorter events, 0.1 us)
Async XLA Ops:
  0.1 1.6 %copy-start = (bf16[2048,512]{1,0:T(8,128)(2,1)S(1)}, bf16[2048,512]{1,0:T(8,128)(2,1)}, u32[]{:S(2)}) copy-start(bf16[2048,512]{1,0:T(8,128)(2,1)} %param.3) | copy-start | bytes 6291460
  1.7 0.7 copy-start.1
  3.4 60.0 %copy-start.2 = (s32[128]{0:T(128)S(1)}, s32[128]{0:T(128)}, u32[]{:S(2)}) copy-start(s32[128]{0:T(128)} %picks_ref.1) | copy-start | bytes 1540
  66.5 12.4 %collective-permute-start.6 = (bf16[2048,128]{1,0:T(8,128)(2,1)S(1)}, bf16[2048,128]{1,0:T(8,128)(2,1)S(1)}, u32[]{:S(2)}, u32[]{:S(2)}) collective-permute-start(bf16[2048,128]{1,0:T(8,128)(2,1)S(1)} %bitcast.10), channel_id=1, source_target_pairs={{0,6},{1,7},{2,0},{3,1},{4,2},{5,3},{6,4},{7,5},{8,14},{9,15},{10,... | collective-permute-start | bytes 1572872 | tf_op jit(solution)/shard_map/ppermute | solution.py:167
  69.3 13.4 %collective-permute-start.4 = (bf16[2048,128]{1,0:T(8,128)(2,1)S(1)}, bf16[2048,128]{1,0:T(8,128)(2,1)S(1)}, u32[]{:S(2)}, u32[]{:S(2)}) collective-permute-start(bf16[2048,128]{1,0:T(8,128)(2,1)S(1)} %bitcast.11), channel_id=1, source_target_pairs={{0,2},{1,3},{2,4},{3,5},{4,6},{5,7},{6,0},{7,1},{8,10},{9,11},{10,... | collective-permute-start | bytes 1572872 | tf_op jit(solution)/shard_map/ppermute | solution.py:167
  69.3 13.5 %collective-permute-start.2 = (bf16[2048,128]{1,0:T(8,128)(2,1)S(1)}, bf16[2048,128]{1,0:T(8,128)(2,1)S(1)}, u32[]{:S(2)}, u32[]{:S(2)}) collective-permute-start(bf16[2048,128]{1,0:T(8,128)(2,1)S(1)} %bitcast.12), channel_id=1, source_target_pairs={{0,192},{8,200},{16,208},{24,216},{32,224},{40,232},{48,240},{56,2... | collective-permute-start | bytes 1572872 | tf_op jit(solution)/shard_map/ppermute | solution.py:170
  71.4 11.5 %collective-permute-start.8 = (bf16[2048,128]{1,0:T(8,128)(2,1)S(1)}, bf16[2048,128]{1,0:T(8,128)(2,1)S(1)}, u32[]{:S(2)}, u32[]{:S(2)}) collective-permute-start(bf16[2048,128]{1,0:T(8,128)(2,1)S(1)} %bitcast.13), channel_id=1, source_target_pairs={{0,1},{1,0},{2,3},{3,2},{4,5},{5,4},{6,7},{7,6},{8,9},{9,8},{10,11... | collective-permute-start | bytes 1572872 | tf_op jit(solution)/shard_map/ppermute | solution.py:173
  71.4 15.5 %collective-permute-start = (bf16[2048,128]{1,0:T(8,128)(2,1)S(1)}, bf16[2048,128]{1,0:T(8,128)(2,1)S(1)}, u32[]{:S(2)}, u32[]{:S(2)}) collective-permute-start(bf16[2048,128]{1,0:T(8,128)(2,1)S(1)} %bitcast.14), channel_id=1, source_target_pairs={{0,64},{8,72},{16,80},{24,88},{32,96},{40,104},{48,112},{56,120},{... | collective-permute-start | bytes 1572872 | tf_op jit(solution)/shard_map/ppermute | solution.py:170
  78.9 8.1 %collective-permute-start.7 = (bf16[1024,128]{1,0:T(8,128)(2,1)S(1)}, bf16[1024,128]{1,0:T(8,128)(2,1)S(1)}, u32[]{:S(2)}, u32[]{:S(2)}) collective-permute-start(bf16[1024,128]{1,0:T(8,128)(2,1)S(1)} %slice.19), channel_id=1, source_target_pairs={{0,6},{1,7},{2,0},{3,1},{4,2},{5,3},{6,4},{7,5},{8,14},{9,15},{10,... | collective-permute-start | bytes 786440 | tf_op jit(solution)/shard_map/ppermute | solution.py:167
  82.7 7.7 %collective-permute-start.5 = (bf16[1024,128]{1,0:T(8,128)(2,1)S(1)}, bf16[1024,128]{1,0:T(8,128)(2,1)S(1)}, u32[]{:S(2)}, u32[]{:S(2)}) collective-permute-start(bf16[1024,128]{1,0:T(8,128)(2,1)S(1)} %slice.18), channel_id=1, source_target_pairs={{0,2},{1,3},{2,4},{3,5},{4,6},{5,7},{6,0},{7,1},{8,10},{9,11},{10,... | collective-permute-start | bytes 786440 | tf_op jit(solution)/shard_map/ppermute | solution.py:167
  82.8 13.4 %collective-permute-start.12 = (bf16[2048,128]{1,0:T(8,128)(2,1)S(1)}, bf16[2048,128]{1,0:T(8,128)(2,1)S(1)}, u32[]{:S(2)}, u32[]{:S(2)}) collective-permute-start(bf16[2048,128]{1,0:T(8,128)(2,1)S(1)} %collective-permute-done.6.refs_9_), channel_id=1, source_target_pairs={{0,1},{1,0},{2,3},{3,2},{4,5},{5,4},{6,7},{7,6},{8,9},{9,8},{10,11... | collective-permute-start | bytes 1572872 | tf_op jit(solution)/shard_map/ppermute | solution.py:173
  82.9 13.3 %collective-permute-start.9 = (bf16[2048,128]{1,0:T(8,128)(2,1)S(1)}, bf16[2048,128]{1,0:T(8,128)(2,1)S(1)}, u32[]{:S(2)}, u32[]{:S(2)}) collective-permute-start(bf16[2048,128]{1,0:T(8,128)(2,1)S(1)} %collective-permute-done.4.refs_6_), channel_id=1, source_target_pairs={{0,1},{1,0},{2,3},{3,2},{4,5},{5,4},{6,7},{7,6},{8,9},{9,8},{10,11... | collective-permute-start | bytes 1572872 | tf_op jit(solution)/shard_map/ppermute | solution.py:173
  87.0 7.9 %collective-permute-start.3 = (bf16[1024,128]{1,0:T(8,128)(2,1)S(1)}, bf16[1024,128]{1,0:T(8,128)(2,1)S(1)}, u32[]{:S(2)}, u32[]{:S(2)}) collective-permute-start(bf16[1024,128]{1,0:T(8,128)(2,1)S(1)} %slice.17), channel_id=1, source_target_pairs={{0,192},{8,200},{16,208},{24,216},{32,224},{40,232},{48,240},{56,2... | collective-permute-start | bytes 786440 | tf_op jit(solution)/shard_map/ppermute | solution.py:170
  87.0 9.2 %collective-permute-start.1 = (bf16[1024,128]{1,0:T(8,128)(2,1)S(1)}, bf16[1024,128]{1,0:T(8,128)(2,1)S(1)}, u32[]{:S(2)}, u32[]{:S(2)}) collective-permute-start(bf16[1024,128]{1,0:T(8,128)(2,1)S(1)} %slice.16), channel_id=1, source_target_pairs={{0,64},{8,72},{16,80},{24,88},{32,96},{40,104},{48,112},{56,120},{... | collective-permute-start | bytes 786440 | tf_op jit(solution)/shard_map/ppermute | solution.py:170
  90.4 5.9 %collective-permute-start.11 = (bf16[1024,128]{1,0:T(8,128)(2,1)S(1)}, bf16[1024,128]{1,0:T(8,128)(2,1)S(1)}, u32[]{:S(2)}, u32[]{:S(2)}) collective-permute-start(bf16[1024,128]{1,0:T(8,128)(2,1)S(1)} %collective-permute-done.7.refs_8_), channel_id=1, source_target_pairs={{0,1},{1,0},{2,3},{3,2},{4,5},{5,4},{6,7},{7,6},{8,9},{9,8},{10,11... | collective-permute-start | bytes 786440 | tf_op jit(solution)/shard_map/ppermute | solution.py:173
  94.9 1.5 %collective-permute-start.10 = (bf16[1024,128]{1,0:T(8,128)(2,1)S(1)}, bf16[1024,128]{1,0:T(8,128)(2,1)S(1)}, u32[]{:S(2)}, u32[]{:S(2)}) collective-permute-start(bf16[1024,128]{1,0:T(8,128)(2,1)S(1)} %collective-permute-done.5.refs_7_), channel_id=1, source_target_pairs={{0,1},{1,0},{2,3},{3,2},{4,5},{5,4},{6,7},{7,6},{8,9},{9,8},{10,11... | collective-permute-start | bytes 786440 | tf_op jit(solution)/shard_map/ppermute | solution.py:173

commit v3 on v2

v3 whole, which is shorter than its diff:
```python
import functools

import jax
import jax.numpy as jnp
from jax import lax
from jax.experimental import pallas as pl
from jax.experimental.pallas import tpu as pltpu
from jax.sharding import PartitionSpec as P

NY, NZ, NX, NCORE = 4, 8, 4, 2
BLOCK = 128
LANES = 128
PER_DEV = 16
N_BLOCKS = 512
CHUNK = BLOCK // NZ
MIB = 1 << 20
PACK_STEPS = 4


SCALARS = pl.BlockSpec(memory_space=pltpu.SMEM)
LOCAL = pl.BlockSpec(memory_space=pltpu.VMEM)


def pack_kernel(at, grads_ref, signs_ref, out_ref, taken, packed, signs, in_sems, out_sems):
    step = PER_DEV // PACK_STEPS
    parts = [pl.ds(i * step, step) for i in range(PACK_STEPS)]
    reads = [
        pltpu.make_async_copy(grads_ref.at[part], taken.at[part], in_sems.at[i])
        for i, part in enumerate(parts)
    ]
    writes = [
        pltpu.make_async_copy(packed.at[:, :, part], out_ref.at[:, :, part], out_sems.at[i])
        for i, part in enumerate(parts)
    ]
    sign_read = pltpu.make_async_copy(signs_ref, signs, in_sems.at[PACK_STEPS])
    sign_read.start()
    for read in reads:
        read.start()
    sign_read.wait()
    columns = signs[...].astype(jnp.float32).T
    for b in range(PER_DEV):
        if b % step == 0:
            reads[b // step].wait()
        for z in range(NZ):
            sign = columns[z * CHUNK : (z + 1) * CHUNK, b : b + 1]
            sign = jnp.broadcast_to(sign, (CHUNK, LANES)).astype(jnp.bfloat16)
            for y in range(NY):
                quarter = lax.rem(z - y + at[0] + NY, NY)
                lanes = pl.ds(pl.multiple_of(quarter * LANES, LANES), LANES)
                packed[y, z, b] = taken[b, pl.ds(z * CHUNK, CHUNK), lanes] * sign
        if b % step == step - 1:
            writes[b // step].start()
    for write in writes:
        write.wait()


def pack(grads, signs, at):
    blocks = grads.reshape(PER_DEV, BLOCK, NY * LANES)
    packed = jax.ShapeDtypeStruct((NY, NZ, PER_DEV, CHUNK, LANES), jnp.bfloat16)
    whole = pl.BlockSpec(memory_space=pl.ANY)
    return pl.pallas_call(
        pack_kernel,
        in_specs=[SCALARS, whole, whole],
        out_specs=whole,
        out_shape=packed,
        scratch_shapes=[
            pltpu.VMEM(blocks.shape, jnp.bfloat16),
            pltpu.VMEM(packed.shape, jnp.bfloat16),
            pltpu.VMEM((PER_DEV, BLOCK), jnp.int32),
            pltpu.SemaphoreType.DMA((PACK_STEPS + 1,)),
            pltpu.SemaphoreType.DMA((PACK_STEPS,)),
        ],
        compiler_params=pltpu.CompilerParams(vmem_limit_bytes=62 * MIB),
        name="pack",
    )(at, blocks, signs.reshape(PER_DEV, BLOCK))


def hadamard(parts):
    span = 1
    while span < len(parts):
        done = list(parts)
        for i in range(len(parts)):
            if not i & span:
                done[i] = parts[i] + parts[i + span]
                done[i + span] = parts[i] - parts[i + span]
        parts = done
        span *= 2
    return parts


def mix_kernel(at, picks_ref, raw_ref, kept_ref, given_ref, work):
    half = N_BLOCKS // 2

    @pl.loop(0, N_BLOCKS // 16)
    def _(d):
        base = d * 16
        parts = [raw_ref[base + b].astype(jnp.float32) for b in range(16)]
        for b, part in enumerate(hadamard(parts)):
            work[base + b] = part

    @pl.loop(0, 32)
    def _(i):
        base = lax.div(i, 16) * half + lax.rem(i, 16)
        parts = [work[base + 16 * e] for e in range(16)]
        for e, part in enumerate(hadamard(parts)):
            work[base + 16 * e] = part

    def sample(k):
        pick = picks_ref[k]
        low = lax.rem(pick, half)
        side = (1 - 2 * lax.div(pick, half)).astype(jnp.float32)
        return (work[low] + side * work[low + half]).astype(kept_ref.dtype)

    count = kept_ref.shape[0]

    @pl.loop(0, count, unroll=4)
    def _(k):
        kept_ref[k] = sample(at[1] * count + k)
        given_ref[k] = sample((1 - at[1]) * count + k)


def mix(at, raw, picks):
    part = jax.ShapeDtypeStruct((picks.shape[0] // NCORE, CHUNK, LANES), jnp.bfloat16)
    return pl.pallas_call(
        mix_kernel,
        in_specs=[SCALARS, SCALARS, LOCAL],
        out_specs=[LOCAL, LOCAL],
        scratch_shapes=[pltpu.VMEM((N_BLOCKS, CHUNK, LANES), jnp.float32)],
        out_shape=[part, part],
        compiler_params=pltpu.CompilerParams(vmem_limit_bytes=16 * MIB),
        name="mix",
    )(at, picks, raw)


def gram_kernel(which, at, *refs):
    cols, rows, (out_ref, left) = refs[:5], refs[5:10], refs[10:]
    x, core, turn = at[0], at[1], at[2]
    for j in range(NY):
        piece = (cols[0], cols[1], cols[2 + which], cols[4])[j]
        quarter = lax.rem(turn + j, NY)
        where = pl.ds(pl.multiple_of(quarter * LANES, LANES), LANES)
        left[where, :] = (piece[...] if j == 2 else piece[which]).T
    for j in range(NX):
        if j == 2:
            pair = [rows[2][...], rows[3][...]]
        else:
            piece = (rows[0], rows[1], None, rows[4])[j]
            pair = [piece[0], piece[1]]
        pair = jnp.concatenate(pair, axis=1)
        panel = lax.rem(x + NX - j, NX) * NCORE
        for m in range(2):
            part = pl.ds(m * 2 * LANES, 2 * LANES)
            block = jnp.dot(left[part, :], pair, preferred_element_type=jnp.float32)
            block = block.astype(out_ref.dtype)
            out_ref[panel + core, part, :] = block[:, :LANES]
            out_ref[panel + 1 - core, part, :] = block[:, LANES:]


def gram_part(which, at, cols, rows, dtype):
    depth = cols[0].shape[1]
    flops = 2 * depth * NY * LANES * NX * NCORE * LANES
    return pl.pallas_call(
        functools.partial(gram_kernel, which),
        in_specs=[SCALARS] + [LOCAL] * 10,
        out_specs=LOCAL,
        scratch_shapes=[pltpu.VMEM((NY * LANES, depth), jnp.bfloat16)],
        out_shape=jax.ShapeDtypeStruct((NX * NCORE, NY * LANES, LANES), dtype),
        compiler_params=pltpu.CompilerParams(vmem_limit_bytes=16 * MIB),
        cost_estimate=pl.CostEstimate(flops=flops, bytes_accessed=8 * MIB, transcendentals=0),
        name="gram_other" if which else "gram_own",
    )(at, *cols, *rows)


def finish_kernel(scale, parts_ref, out_ref):
    for i in range(out_ref.shape[1] // LANES):
        part = pl.ds(i * LANES, LANES)
        total = parts_ref[0, part].astype(jnp.float32)
        for k in range(1, parts_ref.shape[0]):
            total = total + parts_ref[k, part].astype(jnp.float32)
        out_ref[:, part] = (total * scale).T


def finish(parts, scale):
    count, width, rows = parts.shape
    return pl.pallas_call(
        lambda parts_ref, out_ref: finish_kernel(scale, parts_ref, out_ref),
        out_shape=jax.ShapeDtypeStruct((rows, width), jnp.float32),
        compiler_params=pltpu.CompilerParams(vmem_limit_bytes=16 * MIB),
        name="finish",
    )(parts)


def on_device(grads, signs, picks):
    dp, col = lax.axis_index("dp"), lax.axis_index("col")
    y, z = lax.div(dp, NZ), lax.rem(dp, NZ)
    x, core = lax.div(col, NCORE), lax.rem(col, NCORE)
    at = jnp.stack([x, core, lax.rem(z - y + x + NY, NY)])

    outgoing = pack(grads, signs, at).reshape(NY * NZ, PER_DEV, CHUNK, LANES)
    raw = lax.all_to_all(outgoing, "dp", split_axis=0, concat_axis=0, tiled=True)
    kept, given = mix(at, raw.reshape(N_BLOCKS, CHUNK, LANES), picks)

    def along_x(value, step):
        return lax.ppermute(value, "col", [(i, (i + NCORE * step) % (NX * NCORE)) for i in range(NX * NCORE)])

    def along_y(value, step):
        return lax.ppermute(value, "dp", [(i, (i + NZ * step) % (NY * NZ)) for i in range(NY * NZ)])

    def swap(value):
        return lax.ppermute(value, "col", [(i, i ^ 1) for i in range(NX * NCORE)])

    sketch = jnp.stack([kept, swap(given)]).reshape(NCORE, -1, LANES)
    x_up, x_down = along_x(sketch, 1), along_x(sketch, -1)
    y_up, y_down = along_y(sketch, 1), along_y(sketch, -1)
    rows = [sketch, x_up, along_x(x_up[0], 1), along_x(x_down[1], -1), x_down]
    cols = [sketch, y_up, along_y(y_up[0], 1), along_y(y_down[1], -1), y_down]
    away = swap(gram_part(1, at, cols, rows, jnp.bfloat16))
    partial = gram_part(0, at, cols, rows, jnp.float32)
    partial = (partial + away.astype(jnp.float32)).astype(jnp.bfloat16)

    groups = [
        [gy * NZ + (s + gy) % NY + NY * half for gy in range(NY) for half in range(NZ // NY)]
        for s in range(NY)
    ]
    parts = lax.all_to_all(
        partial, "dp", split_axis=0, concat_axis=0, axis_index_groups=groups, tiled=True
    )
    total_rows = grads.shape[0] * NY * NZ
    scale = BLOCK / (total_rows * picks.shape[0] * BLOCK)
    return finish(parts, scale)


def solution(mesh):
    placed = (P("dp", "col"), P("dp"), P())
    return jax.shard_map(
        on_device, mesh=mesh, in_specs=placed, out_specs=P("dp", "col"), check_vma=False
    )
```

time: 136 us -> 138 us (1.015)
  Pallas kernels: 8.46 us -> 11.5 us
  local copies, waits for them, and re-layouts: 2.37 us -> 0.08 us
  waiting for transfers between devices: 18.2 us -> 19.6 us
    ppermute x4, waiting for transfers between devices: 9.35 us -> 2.07 us  [along_y(): lax.ppermute(value, 'dp', [(i, (i + NZ * step) % (NY * NZ)) for i in rang...]
    ppermute x4, waiting for transfers between devices: 8.68 us -> 15.5 us  [along_x(): lax.ppermute(value, 'col', [(i, (i + NCORE * step) % (NX * NCORE)) for i...]
    pallas_call x3 -> x4, Pallas kernels: 7.55 us -> 10.6 us  [the longest x2 4.22 us: gram_part(): pl.pallas_call(functools.partial(gram_kernel, which), in_specs=[SCALARS]...]
    unnamed x6 -> x4, local copies, waits for them, and re-layouts: 2.29 us -> 0.01 us
    ppermute x5 -> x2, waiting for transfers between devices: 0.21 us -> 2.02 us  [swap(): return lax.ppermute(value, 'col', [(i, i ^ 1) for i in range(NX * NCORE)])]
  transfers between devices with their start and end apart: 13 -> 10, of which waited for: 6 -> 6; matrix products, arithmetic and copies ran while one was open for 0% -> 0% of each run, Pallas kernels for 0% -> 2%
where the time goes in v3:
time: 138 us; the launch traced here: 137 us
  blocking collectives  93.5 us (68%)
  waiting for transfers between devices  19.6 us (14%)
  Pallas kernels  11.5 us (8%)
  starting transfers between devices  11.3 us (8%)
    all_to_all x1, blocking collectives, on_device(): lax.all_to_all(outgoing, 'dp', split_axis=0, concat_axis=0, tiled=True)  60.2 us
    all_to_all x1, blocking collectives, on_device(): lax.all_to_all(partial, 'dp', split_axis=0, concat_axis=0, axis_index_gro...  33.3 us
    ppermute x4, waiting for transfers between devices, along_x(): lax.ppermute(value, 'col', [(i, (i + NCORE * step) % (NX * NCORE)) for i...  15.5 us
    ppermute x4, starting transfers between devices, along_x(): lax.ppermute(value, 'col', [(i, (i + NCORE * step) % (NX * NCORE)) for i...  6.69 us
    ppermute x4, starting transfers between devices, along_y(): lax.ppermute(value, 'dp', [(i, (i + NZ * step) % (NY * NZ)) for i in rang...  4.39 us
    pallas_call x2, Pallas kernels, gram_part(): pl.pallas_call(functools.partial(gram_kernel, which), in_specs=[SCALARS]...  4.22 us
    pallas_call x1, Pallas kernels, pack(): pl.pallas_call(pack_kernel, in_specs=[SCALARS, whole, whole], out_specs=w...  3.36 us
    pallas_call x1, Pallas kernels, mix(): pl.pallas_call(mix_kernel, in_specs=[SCALARS, SCALARS, LOCAL], out_specs=...  3.05 us
  transfers between devices with their start and end apart: 10, of which 6 were waited for; matrix products, arithmetic and copies ran while one was open for 0% of the time, Pallas kernels for 2%

profile of v3, /device:TPU:64, one launch (start us, length us, event | category | flops | bytes accessed | tf_op | source)
XLA Modules:
  0.0 136.9 jit_solution(5732486700948935675)
XLA Ops:
  0.0 0.6 pad_add_fusion.at
  0.6 3.4 %pack.1 = bf16[4,8,16,16,128]{4,3,2,1,0:T(8,128)(2,1)} custom-call(s32[3]{0:T(128)} %pad_add_fusion.at, bf16[16,128,512]{2,1,0:T(8,128)(2,1)} %bitcast.20, s32[16,128]{1,0:T(8,128)} %bitcast.22), custom_call_target="tpu_custom_call" | custom-call | tf_op jit(solution)/shard_map/pack/pallas_call | solution.py:61
  4.0 60.2 %all_to_all.10 = bf16[32,16,16,128]{3,2,1,0:T(8,128)(2,1)S(1)} all-to-all(bf16[32,16,16,128]{3,2,1,0:T(8,128)(2,1)} %bitcast.19), channel_id=1, replica_groups=mesh['dp'=32,'col'=8] {'dp'}, dimensions={0} | all-to-all | bytes 4194304 | tf_op jit(solution)/shard_map/all_to_all | solution.py:200
  64.2 3.0 %mix.1 = (bf16[64,16,128]{2,1,0:T(8,128)(2,1)S(1)}, bf16[64,16,128]{2,1,0:T(8,128)(2,1)S(1)}) custom-call(s32[3]{0:T(128)S(1)} %copy-done, s32[128]{0:T(128)S(1)} %copy-done.1, bf16[512,16,128]{2,1,0:T(8,128)(2,1)S(1)} %bitcast.17), custom_call_target="tpu_custom_call" | custom-call | tf_op jit(solution)/shard_map/mix/pallas_call | solution.py:124
  67.2 0.1 collective-permute-start
  67.3 1.5 %collective-permute-done = bf16[64,16,128]{2,1,0:T(8,128)(2,1)S(1)} collective-permute-done((bf16[64,16,128]{2,1,0:T(8,128)(2,1)S(1)}, bf16[64,16,128]{2,1,0:T(8,128)(2,1)S(1)}, u32[]{:S(2)}, u32[]{:S(2)}) %collective-permute-start) | collective-permute-done | bytes 262176 | tf_op jit(solution)/shard_map/ppermute | solution.py:210
  68.8 0.1 pad_maximum_fusion.refs_0_.refs_5_
  68.9 2.8 %collective-permute-start.7 = (bf16[2,1024,128]{2,1,0:T(8,128)(2,1)S(1)}, bf16[2,1024,128]{2,1,0:T(8,128)(2,1)S(1)}, u32[]{:S(2)}, u32[]{:S(2)}) collective-permute-start(bf16[2,1024,128]{2,1,0:T(8,128)(2,1)S(1)} %pad_maximum_fusion.refs_0_.refs_5_), channel_id=1, source_target_pairs={{0,6},{1,7},{2,0},{3,1},{4,2},{5,3},{6,4},{7,5},{8,14},{9,15},{10,... | collective-permute-start | bytes 1572872 | tf_op jit(solution)/shard_map/ppermute | solution.py:204
  71.7 2.1 %collective-permute-start.3 = (bf16[2,1024,128]{2,1,0:T(8,128)(2,1)S(1)}, bf16[2,1024,128]{2,1,0:T(8,128)(2,1)S(1)}, u32[]{:S(2)}, u32[]{:S(2)}) collective-permute-start(bf16[2,1024,128]{2,1,0:T(8,128)(2,1)S(1)} %pad_maximum_fusion.refs_0_.refs_5_), channel_id=1, source_target_pairs={{0,192},{8,200},{16,208},{24,216},{32,224},{40,232},{48,240},{56,2... | collective-permute-start | bytes 1572872 | tf_op jit(solution)/shard_map/ppermute | solution.py:207
  73.8 9.4 %collective-permute-done.7.refs_9_ = bf16[2,1024,128]{2,1,0:T(8,128)(2,1)S(1)} collective-permute-done((bf16[2,1024,128]{2,1,0:T(8,128)(2,1)S(1)}, bf16[2,1024,128]{2,1,0:T(8,128)(2,1)S(1)}, u32[]{:S(2)}, u32[]{:S(2)}) %collective-permute-start.7) | collective-permute-done | bytes 524320 | tf_op jit(solution)/shard_map/ppermute | solution.py:204
  83.2 3.8 %collective-permute-start.8 = (bf16[1024,128]{1,0:T(8,128)(2,1)S(1)}, bf16[1024,128]{1,0:T(8,128)(2,1)S(1)}, u32[]{:S(2)}, u32[]{:S(2)}) collective-permute-start(bf16[1024,128]{1,0:T(8,128)(2,1)S(1)} %slice_bitcast_fusion), channel_id=1, source_target_pairs={{0,6},{1,7},{2,0},{3,1},{4,2},{5,3},{6,4},{7,5},{8,14},{9,15},{10,... | collective-permute-start | bytes 786440 | tf_op jit(solution)/shard_map/ppermute | solution.py:204
  87.0 0.1 collective-permute-start.6
  87.2 2.2 %collective-permute-start.4 = (bf16[1024,128]{1,0:T(8,128)(2,1)S(1)}, bf16[1024,128]{1,0:T(8,128)(2,1)S(1)}, u32[]{:S(2)}, u32[]{:S(2)}) collective-permute-start(bf16[1024,128]{1,0:T(8,128)(2,1)S(1)} %slice_bitcast_fusion.2), channel_id=1, source_target_pairs={{0,192},{8,200},{16,208},{24,216},{32,224},{40,232},{48,240},{56,2... | collective-permute-start | bytes 786440 | tf_op jit(solution)/shard_map/ppermute | solution.py:207
  89.4 0.1 collective-permute-start.2
  89.5 2.6 %collective-permute-done.8.refs_8_ = bf16[1024,128]{1,0:T(8,128)(2,1)S(1)} collective-permute-done((bf16[1024,128]{1,0:T(8,128)(2,1)S(1)}, bf16[1024,128]{1,0:T(8,128)(2,1)S(1)}, u32[]{:S(2)}, u32[]{:S(2)}) %collective-permute-start.8) | collective-permute-done | bytes 262176 | tf_op jit(solution)/shard_map/ppermute | solution.py:204
  92.0 3.5 %collective-permute-done.6.refs_7_ = bf16[1024,128]{1,0:T(8,128)(2,1)S(1)} collective-permute-done((bf16[1024,128]{1,0:T(8,128)(2,1)S(1)}, bf16[1024,128]{1,0:T(8,128)(2,1)S(1)}, u32[]{:S(2)}, u32[]{:S(2)}) %collective-permute-start.6) | collective-permute-done | bytes 262176 | tf_op jit(solution)/shard_map/ppermute | solution.py:204
  95.6 2.1 %collective-permute-done.2.refs_2_ = bf16[1024,128]{1,0:T(8,128)(2,1)S(1)} collective-permute-done((bf16[1024,128]{1,0:T(8,128)(2,1)S(1)}, bf16[1024,128]{1,0:T(8,128)(2,1)S(1)}, u32[]{:S(2)}, u32[]{:S(2)}) %collective-permute-start.2) | collective-permute-done | bytes 262176 | tf_op jit(solution)/shard_map/ppermute | solution.py:207
  97.6 2.1 %gram_other.1 = bf16[8,512,128]{2,1,0:T(8,128)(2,1)S(1)} custom-call(s32[3]{0:T(128)S(1)} %copy-done, bf16[2,1024,128]{2,1,0:T(8,128)(2,1)S(1)} %pad_maximum_fusion.refs_0_.refs_5_, bf16[2,1024,128]{2,1,0:T(8,128)(2,1)S(1)} %collective-permute-done.1.refs_1_, bf16[1024,128]{1,0:T(8,128)(2,1)S(1)} %collective-permute-done.2.refs_2_, ...), custom_call_target="tpu_custom_call" | custom-call | flops 1073741824 | bytes 8388608 | tf_op jit(solution)/shard_map/gram_other/pallas_call | solution.py:162
  99.7 0.1 collective-permute-start.9
  99.8 2.1 %gram_own.1 = f32[8,512,128]{2,1,0:T(8,128)S(1)} custom-call(s32[3]{0:T(128)S(1)} %copy-done, bf16[2,1024,128]{2,1,0:T(8,128)(2,1)S(1)} %pad_maximum_fusion.refs_0_.refs_5_, bf16[2,1024,128]{2,1,0:T(8,128)(2,1)S(1)} %collective-permute-done.1.refs_1_, bf16[1024,128]{1,0:T(8,128)(2,1)S(1)} %collective-permute-done.2.refs_2_, ...), custom_call_target="tpu_custom_call" | custom-call | flops 1073741824 | bytes 8388608 | tf_op jit(solution)/shard_map/gram_own/pallas_call | solution.py:162
  102.0 0.5 collective-permute-done.9
  102.5 0.2 add_convert_fusion
  102.7 33.3 %all_to_all.11.parts_ref = bf16[8,512,128]{2,1,0:T(8,128)(2,1)S(1)} all-to-all(bf16[8,512,128]{2,1,0:T(8,128)(2,1)S(1)} %add_convert_fusion), channel_id=1, replica_groups={{0,32,72,104,144,176,216,248},{8,40,80,112,152,184,192,224},{16,48,88,1..., dimensions={0} | all-to-all | bytes 2097152 | tf_op jit(solution)/shard_map/all_to_all | solution.py:225
  136.0 0.9 finish.1
  (14 shorter events, 0.1 us)
Async XLA Ops:
  3.9 60.2 %copy-start = (s32[3]{0:T(128)S(1)}, s32[3]{0:T(128)}, u32[]{:S(2)}) copy-start(s32[3]{0:T(128)} %pad_add_fusion.at) | copy-start | bytes 40
  3.9 60.2 %copy-start.1 = (s32[128]{0:T(128)S(1)}, s32[128]{0:T(128)}, u32[]{:S(2)}) copy-start(s32[128]{0:T(128)} %picks_ref.1) | copy-start | bytes 1540
  67.2 1.6 %collective-permute-start = (bf16[64,16,128]{2,1,0:T(8,128)(2,1)S(1)}, bf16[64,16,128]{2,1,0:T(8,128)(2,1)S(1)}, u32[]{:S(2)}, u32[]{:S(2)}) collective-permute-start(bf16[64,16,128]{2,1,0:T(8,128)(2,1)S(1)} %get-tuple-element.8), channel_id=1, source_target_pairs={{0,1},{1,0},{2,3},{3,2},{4,5},{5,4},{6,7},{7,6},{8,9},{9,8},{10,11... | collective-permute-start | bytes 786440 | tf_op jit(solution)/shard_map/ppermute | solution.py:210
  68.9 14.3 %collective-permute-start.7 = (bf16[2,1024,128]{2,1,0:T(8,128)(2,1)S(1)}, bf16[2,1024,128]{2,1,0:T(8,128)(2,1)S(1)}, u32[]{:S(2)}, u32[]{:S(2)}) collective-permute-start(bf16[2,1024,128]{2,1,0:T(8,128)(2,1)S(1)} %pad_maximum_fusion.refs_0_.refs_5_), channel_id=1, source_target_pairs={{0,6},{1,7},{2,0},{3,1},{4,2},{5,3},{6,4},{7,5},{8,14},{9,15},{10,... | collective-permute-start | bytes 1572872 | tf_op jit(solution)/shard_map/ppermute | solution.py:204
  71.7 15.3 %collective-permute-start.5 = (bf16[2,1024,128]{2,1,0:T(8,128)(2,1)S(1)}, bf16[2,1024,128]{2,1,0:T(8,128)(2,1)S(1)}, u32[]{:S(2)}, u32[]{:S(2)}) collective-permute-start(bf16[2,1024,128]{2,1,0:T(8,128)(2,1)S(1)} %pad_maximum_fusion.refs_0_.refs_5_), channel_id=1, source_target_pairs={{0,2},{1,3},{2,4},{3,5},{4,6},{5,7},{6,0},{7,1},{8,10},{9,11},{10,... | collective-permute-start | bytes 1572872 | tf_op jit(solution)/shard_map/ppermute | solution.py:204
  71.7 15.4 %collective-permute-start.3 = (bf16[2,1024,128]{2,1,0:T(8,128)(2,1)S(1)}, bf16[2,1024,128]{2,1,0:T(8,128)(2,1)S(1)}, u32[]{:S(2)}, u32[]{:S(2)}) collective-permute-start(bf16[2,1024,128]{2,1,0:T(8,128)(2,1)S(1)} %pad_maximum_fusion.refs_0_.refs_5_), channel_id=1, source_target_pairs={{0,192},{8,200},{16,208},{24,216},{32,224},{40,232},{48,240},{56,2... | collective-permute-start | bytes 1572872 | tf_op jit(solution)/shard_map/ppermute | solution.py:207
  73.8 15.5 %collective-permute-start.1 = (bf16[2,1024,128]{2,1,0:T(8,128)(2,1)S(1)}, bf16[2,1024,128]{2,1,0:T(8,128)(2,1)S(1)}, u32[]{:S(2)}, u32[]{:S(2)}) collective-permute-start(bf16[2,1024,128]{2,1,0:T(8,128)(2,1)S(1)} %pad_maximum_fusion.refs_0_.refs_5_), channel_id=1, source_target_pairs={{0,64},{8,72},{16,80},{24,88},{32,96},{40,104},{48,112},{56,120},{... | collective-permute-start | bytes 1572872 | tf_op jit(solution)/shard_map/ppermute | solution.py:207
  83.2 8.8 %collective-permute-start.8 = (bf16[1024,128]{1,0:T(8,128)(2,1)S(1)}, bf16[1024,128]{1,0:T(8,128)(2,1)S(1)}, u32[]{:S(2)}, u32[]{:S(2)}) collective-permute-start(bf16[1024,128]{1,0:T(8,128)(2,1)S(1)} %slice_bitcast_fusion), channel_id=1, source_target_pairs={{0,6},{1,7},{2,0},{3,1},{4,2},{5,3},{6,4},{7,5},{8,14},{9,15},{10,... | collective-permute-start | bytes 786440 | tf_op jit(solution)/shard_map/ppermute | solution.py:204
  87.0 8.5 %collective-permute-start.6 = (bf16[1024,128]{1,0:T(8,128)(2,1)S(1)}, bf16[1024,128]{1,0:T(8,128)(2,1)S(1)}, u32[]{:S(2)}, u32[]{:S(2)}) collective-permute-start(bf16[1024,128]{1,0:T(8,128)(2,1)S(1)} %slice_bitcast_fusion.1), channel_id=1, source_target_pairs={{0,2},{1,3},{2,4},{3,5},{4,6},{5,7},{6,0},{7,1},{8,10},{9,11},{10,... | collective-permute-start | bytes 786440 | tf_op jit(solution)/shard_map/ppermute | solution.py:204
  87.2 8.4 %collective-permute-start.4 = (bf16[1024,128]{1,0:T(8,128)(2,1)S(1)}, bf16[1024,128]{1,0:T(8,128)(2,1)S(1)}, u32[]{:S(2)}, u32[]{:S(2)}) collective-permute-start(bf16[1024,128]{1,0:T(8,128)(2,1)S(1)} %slice_bitcast_fusion.2), channel_id=1, source_target_pairs={{0,192},{8,200},{16,208},{24,216},{32,224},{40,232},{48,240},{56,2... | collective-permute-start | bytes 786440 | tf_op jit(solution)/shard_map/ppermute | solution.py:207
  89.4 8.2 %collective-permute-start.2 = (bf16[1024,128]{1,0:T(8,128)(2,1)S(1)}, bf16[1024,128]{1,0:T(8,128)(2,1)S(1)}, u32[]{:S(2)}, u32[]{:S(2)}) collective-permute-start(bf16[1024,128]{1,0:T(8,128)(2,1)S(1)} %slice_bitcast_fusion.3), channel_id=1, source_target_pairs={{0,64},{8,72},{16,80},{24,88},{32,96},{40,104},{48,112},{56,120},{... | collective-permute-start | bytes 786440 | tf_op jit(solution)/shard_map/ppermute | solution.py:207
  99.7 2.7 %collective-permute-start.9 = (bf16[8,512,128]{2,1,0:T(8,128)(2,1)S(1)}, bf16[8,512,128]{2,1,0:T(8,128)(2,1)S(1)}, u32[]{:S(2)}, u32[]{:S(2)}) collective-permute-start(bf16[8,512,128]{2,1,0:T(8,128)(2,1)S(1)} %gram_other.1), channel_id=1, source_target_pairs={{0,1},{1,0},{2,3},{3,2},{4,5},{5,4},{6,7},{7,6},{8,9},{9,8},{10,11... | collective-permute-start | bytes 3145736 | tf_op jit(solution)/shard_map/ppermute | solution.py:210

commit v4 on v2

--- a/solution.py
+++ b/solution.py
@@ -1,3 +1,5 @@
+import functools
+
 import jax
 import jax.numpy as jnp
 from jax import lax
@@ -56,82 +58,119 @@
     return parts
 
 
-def mix_kernel(picks_ref, raw_ref, out_ref, work):
+def mix_kernel(at, picks_ref, raw_ref, kept_ref, given_ref, work):
     half = N_BLOCKS // 2
 
-    @pl.loop(0, N_BLOCKS // 16)
+    @pl.loop(0, N_BLOCKS // 16, unroll=2)
     def _(d):
         base = d * 16
         parts = [raw_ref[base + b].astype(jnp.float32) for b in range(16)]
         for b, part in enumerate(hadamard(parts)):
             work[base + b] = part
 
-    @pl.loop(0, 32)
+    @pl.loop(0, 32, unroll=2)
     def _(i):
         base = lax.div(i, 16) * half + lax.rem(i, 16)
         parts = [work[base + 16 * e] for e in range(16)]
         for e, part in enumerate(hadamard(parts)):
             work[base + 16 * e] = part
 
-    @pl.loop(0, out_ref.shape[0], unroll=4)
-    def _(k):
+    def sample(k):
         pick = picks_ref[k]
         low = lax.rem(pick, half)
         side = (1 - 2 * lax.div(pick, half)).astype(jnp.float32)
-        out_ref[k] = (work[low] + side * work[low + half]).astype(out_ref.dtype)
-
-
-def mix(raw, picks):
-    samples = picks.shape[0]
+        return (work[low] + side * work[low + half]).astype(kept_ref.dtype)
+
+    count = kept_ref.shape[0]
+
+    @pl.loop(0, count, unroll=4)
+    def _(k):
+        kept_ref[k] = sample(at[1] * count + k)
+        given_ref[k] = sample((1 - at[1]) * count + k)
+
+
+def mix(at, raw, picks):
+    part = jax.ShapeDtypeStruct((picks.shape[0] // NCORE, CHUNK, LANES), jnp.bfloat16)
     return pl.pallas_call(
         mix_kernel,
-        in_specs=[SCALARS, LOCAL],
+        in_specs=[SCALARS, SCALARS, LOCAL],
+        out_specs=[LOCAL, LOCAL],
+        scratch_shapes=[pltpu.VMEM((N_BLOCKS, CHUNK, LANES), jnp.float32)],
+        out_shape=[part, part],
+        compiler_params=pltpu.CompilerParams(vmem_limit_bytes=16 * MIB),
+        name="mix",
+    )(at, picks, raw)
+
+
+NEAR = (0, 1, 3)
+
+
+def near_kernel(*refs):
+    cols, rows, (left, other_ref, own_ref) = refs[:3], (refs[0], refs[3], refs[4]), refs[5:]
+    for which, out_ref in ((1, other_ref), (0, own_ref)):
+        for j in range(len(NEAR)):
+            left[which, pl.ds(j * LANES, LANES), :] = cols[j][which].T
+        for j in range(len(NEAR)):
+            pair = jnp.concatenate([rows[j][0], rows[j][1]], axis=1)
+            block = jnp.dot(left[which], pair, preferred_element_type=jnp.float32)
+            out_ref[j] = block.astype(out_ref.dtype)
+
+
+def gram_near(sketch, x_up, x_down, y_up, y_down):
+    depth, near = sketch.shape[1], len(NEAR)
+    shape = (near, near * LANES, NCORE * LANES)
+    flops = 2 * depth * NCORE * near * near * LANES * NCORE * LANES
+    return pl.pallas_call(
+        near_kernel,
+        in_specs=[LOCAL] * 5,
+        out_specs=[LOCAL] * 3,
+        out_shape=[
+            jax.ShapeDtypeStruct((NCORE, near * LANES, depth), jnp.bfloat16),
+            jax.ShapeDtypeStruct(shape, jnp.bfloat16),
+            jax.ShapeDtypeStruct(shape, jnp.float32),
+        ],
+        compiler_params=pltpu.CompilerParams(vmem_limit_bytes=16 * MIB),
+        cost_estimate=pl.CostEstimate(flops=flops, bytes_accessed=8 * MIB, transcendentals=0),
+        name="gram_near",
+    )(sketch, y_up, y_down, x_up, x_down)
+
+
+def far_kernel(which, at, near_ref, left, far_cols_0, far_cols_1, own, up, down, far_own, far_other, out_ref):
+    x, core, turn = at[0], at[1], at[2]
+    rows = (own, up, down)
+
+    def put(step_x, step_y, block):
+        panel = lax.rem(x + NX - step_x, NX) * NCORE
+        quarter = pl.multiple_of(lax.rem(turn + step_y, NY) * LANES, LANES)
+        block = block.astype(out_ref.dtype)
+        out_ref[panel + core, pl.ds(quarter, LANES), :] = block[:, :LANES]
+        out_ref[panel + 1 - core, pl.ds(quarter, LANES), :] = block[:, LANES:]
+
+    last = (far_cols_1 if which else far_cols_0)[...].T
+    pair = jnp.concatenate([far_own[...], far_other[...]], axis=1)
+    block = jnp.dot(left[which], pair, preferred_element_type=jnp.float32)
+    for j, step in enumerate(NEAR):
+        put(2, step, block[j * LANES : (j + 1) * LANES])
+    put(2, 2, jnp.dot(last, pair, preferred_element_type=jnp.float32))
+    for i, step_x in enumerate(NEAR):
+        pair = jnp.concatenate([rows[i][0], rows[i][1]], axis=1)
+        put(step_x, 2, jnp.dot(last, pair, preferred_element_type=jnp.float32))
+        for j, step_y in enumerate(NEAR):
+            put(step_x, step_y, near_ref[i, pl.ds(j * LANES, LANES), :])
+
+
+def gram_far(which, at, near, left, far_cols, rows):
+    depth = far_cols[0].shape[0]
+    flops = 2 * depth * 7 * LANES * NCORE * LANES
+    return pl.pallas_call(
+        functools.partial(far_kernel, which),
+        in_specs=[SCALARS] + [LOCAL] * 9,
         out_specs=LOCAL,
-        scratch_shapes=[pltpu.VMEM((N_BLOCKS, CHUNK, LANES), jnp.float32)],
-        out_shape=jax.ShapeDtypeStruct((samples, CHUNK, LANES), jnp.bfloat16),
-        compiler_params=pltpu.CompilerParams(vmem_limit_bytes=16 * MIB),
-        name="mix",
-    )(picks, raw)
-
-
-PIECES = 5
-
-
-def gram_kernel(at, *refs):
-    cols, rows = refs[:PIECES], (refs[PIECES : 2 * PIECES], refs[2 * PIECES : 3 * PIECES])
-    out_ref, left = refs[3 * PIECES :]
-    half = cols[2].shape[0]
-    x, core, turn = at[0], at[1], at[2]
-    spots = [(0, 0, 2 * half), (1, 0, 2 * half), (2, 0, half), (2, half, half), (3, 0, 2 * half)]
-    for p, (j, start, size) in enumerate(spots):
-        quarter = lax.rem(turn + j, NY)
-        where = pl.ds(pl.multiple_of(quarter * LANES, LANES), LANES)
-        left[where, pl.ds(start, size)] = cols[p][...].T
-    for pieces, j in (((0,), 0), ((1,), 1), ((4,), 3), ((2, 3), 2)):
-        panel = lax.rem(x + NX - j, NX) * NCORE
-        for m in range(2):
-            part = pl.ds(m * 2 * LANES, 2 * LANES)
-            block = None
-            for p in pieces:
-                pair = jnp.concatenate([rows[0][p][...], rows[1][p][...]], axis=1)
-                depth = pl.ds(spots[p][1], spots[p][2])
-                term = jnp.dot(left[part, depth], pair, preferred_element_type=jnp.float32)
-                block = term if block is None else block + term
-            block = block.astype(out_ref.dtype)
-            out_ref[panel + core, part, :] = block[:, :LANES]
-            out_ref[panel + 1 - core, part, :] = block[:, LANES:]
-
-
-def gram_part(at, cols, own, other):
-    return pl.pallas_call(
-        gram_kernel,
-        in_specs=[SCALARS] + [LOCAL] * (3 * PIECES),
-        out_specs=LOCAL,
-        scratch_shapes=[pltpu.VMEM((NY * LANES, cols[0].shape[0]), jnp.bfloat16)],
-        out_shape=jax.ShapeDtypeStruct((NX * NCORE, NY * LANES, LANES), jnp.bfloat16),
-        compiler_params=pltpu.CompilerParams(vmem_limit_bytes=24 * MIB),
-        name="gram_part",
-    )(at, *cols, *own, *other)
+        out_shape=jax.ShapeDtypeStruct((NX * NCORE, NY * LANES, LANES), near.dtype),
+        compiler_params=pltpu.CompilerParams(vmem_limit_bytes=16 * MIB),
+        cost_estimate=pl.CostEstimate(flops=flops, bytes_accessed=6 * MIB, transcendentals=0),
+        name="gram_other" if which else "gram_own",
+    )(at, near, left, *far_cols, *rows)
 
 
 def finish_kernel(scale, parts_ref, out_ref):
@@ -161,7 +200,7 @@
 
     outgoing = pack(grads, signs, at).reshape(NY * NZ, PER_DEV, CHUNK, LANES)
     raw = lax.all_to_all(outgoing, "dp", split_axis=0, concat_axis=0, tiled=True)
-    sketch = mix(raw.reshape(N_BLOCKS, CHUNK, LANES), picks).reshape(-1, LANES)
+    kept, given = mix(at, raw.reshape(N_BLOCKS, CHUNK, LANES), picks)
 
     def along_x(value, step):
         return lax.ppermute(value, "col", [(i, (i + NCORE * step) % (NX * NCORE)) for i in range(NX * NCORE)])
@@ -172,15 +211,16 @@
     def swap(value):
         return lax.ppermute(value, "col", [(i, i ^ 1) for i in range(NX * NCORE)])
 
-    depth = sketch.shape[0] // 2
+    sketch = jnp.stack([kept, swap(given)]).reshape(NCORE, -1, LANES)
     x_up, x_down = along_x(sketch, 1), along_x(sketch, -1)
     y_up, y_down = along_y(sketch, 1), along_y(sketch, -1)
-    x_far = (along_x(x_up[:depth], 1), along_x(x_down[depth:], -1))
-    y_far = (along_y(y_up[:depth], 1), along_y(y_down[depth:], -1))
-    own = [sketch, x_up, *x_far, x_down]
-    cols = [sketch, y_up, *y_far, y_down]
-    other = [swap(piece) for piece in own]
-    partial = gram_part(at, cols, own, other)
+    x_far = (along_x(x_up[0], 1), along_x(x_down[1], -1))
+    y_far = (along_y(y_up[0], 1), along_y(y_down[1], -1))
+    left, near_other, near_own = gram_near(sketch, x_up, x_down, y_up, y_down)
+    rows = (sketch, x_up, x_down, *x_far)
+    away = swap(gram_far(1, at, near_other, left, y_far, rows))
+    partial = gram_far(0, at, near_own, left, y_far, rows)
+    partial = (partial + away.astype(jnp.float32)).astype(jnp.bfloat16)
 
     groups = [
         [gy * NZ + (s + gy) % NY + NY * half for gy in range(NY) for half in range(NZ // NY)]

time: 136 us -> 136 us (level)
    ppermute x4, waiting for transfers between devices: 9.35 us -> 2.07 us  [along_y(): lax.ppermute(value, 'dp', [(i, (i + NZ * step) % (NY * NZ)) for i in rang...]
    ppermute x4, waiting for transfers between devices: 8.68 us -> 14 us  [along_x(): lax.ppermute(value, 'col', [(i, (i + NCORE * step) % (NX * NCORE)) for i...]
    ppermute x5 -> x2, waiting for transfers between devices: 0.21 us -> 2.83 us  [swap(): return lax.ppermute(value, 'col', [(i, i ^ 1) for i in range(NX * NCORE)])]
    pallas_call x2 -> x4, Pallas kernels: 6.56 us -> 6.95 us  [the longest x1 2.89 us: mix(): pl.pallas_call(mix_kernel, in_specs=[SCALARS, SCALARS, LOCAL], out_specs=...]
  transfers between devices with their start and end apart: 13 -> 10, of which waited for: 6 -> 6; matrix products, arithmetic and copies ran while one was open for 0% -> 0% of each run, Pallas kernels for 0% -> 2%
where the time goes in v4:
time: 136 us; the launch traced here: 135 us
  blocking collectives  93.3 us (69%)
  waiting for transfers between devices  18.9 us (14%)
  starting transfers between devices  11.3 us (8%)
  Pallas kernels  8.85 us (7%)
  local copies, waits for them, and re-layouts  2.37 us (2%)
    all_to_all x1, blocking collectives, on_device(): lax.all_to_all(outgoing, 'dp', split_axis=0, concat_axis=0, tiled=True)  60 us
    all_to_all x1, blocking collectives, on_device(): lax.all_to_all(partial, 'dp', split_axis=0, concat_axis=0, axis_index_gro...  33.3 us
    ppermute x4, waiting for transfers between devices, along_x(): lax.ppermute(value, 'col', [(i, (i + NCORE * step) % (NX * NCORE)) for i...  14 us
    ppermute x4, starting transfers between devices, along_x(): lax.ppermute(value, 'col', [(i, (i + NCORE * step) % (NX * NCORE)) for i...  6.69 us
    ppermute x4, starting transfers between devices, along_y(): lax.ppermute(value, 'dp', [(i, (i + NZ * step) % (NY * NZ)) for i in rang...  4.39 us
    pallas_call x1, Pallas kernels, mix(): pl.pallas_call(mix_kernel, in_specs=[SCALARS, SCALARS, LOCAL], out_specs=...  2.89 us
    ppermute x2, waiting for transfers between devices, swap(): return lax.ppermute(value, 'col', [(i, i ^ 1) for i in range(NX * NCORE)])  2.83 us
  transfers between devices with their start and end apart: 10, of which 6 were waited for; matrix products, arithmetic and copies ran while one was open for 0% of the time, Pallas kernels for 2%

profile of v4, /device:TPU:64, one launch (start us, length us, event | category | flops | bytes accessed | tf_op | source)
XLA Modules:
  0.0 135.1 jit_solution(17268607164478229313)
XLA Ops:
  0.1 1.6 %copy-done = bf16[2048,512]{1,0:T(8,128)(2,1)S(1)} copy-done((bf16[2048,512]{1,0:T(8,128)(2,1)S(1)}, bf16[2048,512]{1,0:T(8,128)(2,1)}, u32[]{:S(2)}) %copy-start) | copy-done | bytes 2097176
  1.7 0.7 copy-done.1
  2.4 1.0 pack.1
  3.4 60.0 %all_to_all.10 = bf16[32,16,16,128]{3,2,1,0:T(8,128)(2,1)S(1)} all-to-all(bf16[32,16,16,128]{3,2,1,0:T(8,128)(2,1)S(1)} %bitcast.18), channel_id=1, replica_groups=mesh['dp'=32,'col'=8] {'dp'}, dimensions={0} | all-to-all | bytes 4194304 | tf_op jit(solution)/shard_map/all_to_all | solution.py:202
  63.4 2.9 %mix.1 = (bf16[64,16,128]{2,1,0:T(8,128)(2,1)S(1)}, bf16[64,16,128]{2,1,0:T(8,128)(2,1)S(1)}) custom-call(s32[3]{0:T(128)S(1)} %pad_add_fusion.at, s32[128]{0:T(128)S(1)} %copy-done.2, bf16[512,16,128]{2,1,0:T(8,128)(2,1)S(1)} %bitcast.17), custom_call_target="tpu_custom_call" | custom-call | tf_op jit(solution)/shard_map/mix/pallas_call | solution.py:94
  66.3 0.1 collective-permute-start
  66.4 1.5 %collective-permute-done = bf16[64,16,128]{2,1,0:T(8,128)(2,1)S(1)} collective-permute-done((bf16[64,16,128]{2,1,0:T(8,128)(2,1)S(1)}, bf16[64,16,128]{2,1,0:T(8,128)(2,1)S(1)}, u32[]{:S(2)}, u32[]{:S(2)}) %collective-permute-start) | collective-permute-done | bytes 262176 | tf_op jit(solution)/shard_map/ppermute | solution.py:212
  68.0 2.8 %collective-permute-start.4 = (bf16[2,1024,128]{2,1,0:T(8,128)(2,1)S(1)}, bf16[2,1024,128]{2,1,0:T(8,128)(2,1)S(1)}, u32[]{:S(2)}, u32[]{:S(2)}) collective-permute-start(bf16[2,1024,128]{2,1,0:T(8,128)(2,1)S(1)} %pad_maximum_fusion.refs_0_.own), channel_id=1, source_target_pairs={{0,6},{1,7},{2,0},{3,1},{4,2},{5,3},{6,4},{7,5},{8,14},{9,15},{10,... | collective-permute-start | bytes 1572872 | tf_op jit(solution)/shard_map/ppermute | solution.py:206
  70.8 2.1 %collective-permute-start.2 = (bf16[2,1024,128]{2,1,0:T(8,128)(2,1)S(1)}, bf16[2,1024,128]{2,1,0:T(8,128)(2,1)S(1)}, u32[]{:S(2)}, u32[]{:S(2)}) collective-permute-start(bf16[2,1024,128]{2,1,0:T(8,128)(2,1)S(1)} %pad_maximum_fusion.refs_0_.own), channel_id=1, source_target_pairs={{0,192},{8,200},{16,208},{24,216},{32,224},{40,232},{48,240},{56,2... | collective-permute-start | bytes 1572872 | tf_op jit(solution)/shard_map/ppermute | solution.py:209
  72.9 9.4 %collective-permute-done.4.refs_4_.down = bf16[2,1024,128]{2,1,0:T(8,128)(2,1)S(1)} collective-permute-done((bf16[2,1024,128]{2,1,0:T(8,128)(2,1)S(1)}, bf16[2,1024,128]{2,1,0:T(8,128)(2,1)S(1)}, u32[]{:S(2)}, u32[]{:S(2)}) %collective-permute-start.4) | collective-permute-done | bytes 524320 | tf_op jit(solution)/shard_map/ppermute | solution.py:206
  82.3 3.8 %collective-permute-start.8 = (bf16[1024,128]{1,0:T(8,128)(2,1)S(1)}, bf16[1024,128]{1,0:T(8,128)(2,1)S(1)}, u32[]{:S(2)}, u32[]{:S(2)}) collective-permute-start(bf16[1024,128]{1,0:T(8,128)(2,1)S(1)} %slice_bitcast_fusion), channel_id=1, source_target_pairs={{0,6},{1,7},{2,0},{3,1},{4,2},{5,3},{6,4},{7,5},{8,14},{9,15},{10,... | collective-permute-start | bytes 786440 | tf_op jit(solution)/shard_map/ppermute | solution.py:206
  86.1 0.1 collective-permute-start.7
  86.2 2.2 %collective-permute-start.6 = (bf16[1024,128]{1,0:T(8,128)(2,1)S(1)}, bf16[1024,128]{1,0:T(8,128)(2,1)S(1)}, u32[]{:S(2)}, u32[]{:S(2)}) collective-permute-start(bf16[1024,128]{1,0:T(8,128)(2,1)S(1)} %slice_bitcast_fusion.2), channel_id=1, source_target_pairs={{0,192},{8,200},{16,208},{24,216},{32,224},{40,232},{48,240},{56,2... | collective-permute-start | bytes 786440 | tf_op jit(solution)/shard_map/ppermute | solution.py:209
  88.5 1.4 %gram_near.1 = (bf16[2,384,1024]{2,1,0:T(8,128)(2,1)S(1)}, bf16[3,384,256]{2,1,0:T(8,128)(2,1)S(1)}, f32[3,384,256]{2,1,0:T(8,128)S(1)}) custom-call(bf16[2,1024,128]{2,1,0:T(8,128)(2,1)S(1)} %pad_maximum_fusion.refs_0_.own, bf16[2,1024,128]{2,1,0:T(8,128)(2,1)S(1)} %collective-permute-done.1.refs_1_, ...), custom_call_target="tpu_custom_call" | custom-call | flops 1207959552 | bytes 8388608 | tf_op jit(solution)/shard_map/gram_near/pallas_call | solution.py:123
  90.0 1.1 collective-permute-done.8.far_other
  91.1 3.5 %collective-permute-done.7.far_own = bf16[1024,128]{1,0:T(8,128)(2,1)S(1)} collective-permute-done((bf16[1024,128]{1,0:T(8,128)(2,1)S(1)}, bf16[1024,128]{1,0:T(8,128)(2,1)S(1)}, u32[]{:S(2)}, u32[]{:S(2)}) %collective-permute-start.7) | collective-permute-done | bytes 262176 | tf_op jit(solution)/shard_map/ppermute | solution.py:206
  94.6 2.1 %collective-permute-done.5.far_cols_0 = bf16[1024,128]{1,0:T(8,128)(2,1)S(1)} collective-permute-done((bf16[1024,128]{1,0:T(8,128)(2,1)S(1)}, bf16[1024,128]{1,0:T(8,128)(2,1)S(1)}, u32[]{:S(2)}, u32[]{:S(2)}) %collective-permute-start.5) | collective-permute-done | bytes 262176 | tf_op jit(solution)/shard_map/ppermute | solution.py:209
  96.7 1.3 gram_other.1
  98.0 0.1 collective-permute-start.9
  98.1 1.3 gram_own.1
  99.4 1.3 collective-permute-done.9
  100.7 0.2 add_convert_fusion
  100.9 33.3 %all_to_all.11.parts_ref = bf16[8,512,128]{2,1,0:T(8,128)(2,1)S(1)} all-to-all(bf16[8,512,128]{2,1,0:T(8,128)(2,1)S(1)} %add_convert_fusion), channel_id=1, replica_groups={{0,32,72,104,144,176,216,248},{8,40,80,112,152,184,192,224},{16,48,88,1..., dimensions={0} | all-to-all | bytes 2097152 | tf_op jit(solution)/shard_map/all_to_all | solution.py:229
  134.2 0.9 finish.1
  (17 shorter events, 0.3 us)
Async XLA Ops:
  0.1 1.6 %copy-start = (bf16[2048,512]{1,0:T(8,128)(2,1)S(1)}, bf16[2048,512]{1,0:T(8,128)(2,1)}, u32[]{:S(2)}) copy-start(bf16[2048,512]{1,0:T(8,128)(2,1)} %param.3) | copy-start | bytes 6291460
  1.7 0.7 copy-start.1
  3.4 60.0 %copy-start.2 = (s32[128]{0:T(128)S(1)}, s32[128]{0:T(128)}, u32[]{:S(2)}) copy-start(s32[128]{0:T(128)} %picks_ref.1) | copy-start | bytes 1540
  66.3 1.6 %collective-permute-start = (bf16[64,16,128]{2,1,0:T(8,128)(2,1)S(1)}, bf16[64,16,128]{2,1,0:T(8,128)(2,1)S(1)}, u32[]{:S(2)}, u32[]{:S(2)}) collective-permute-start(bf16[64,16,128]{2,1,0:T(8,128)(2,1)S(1)} %get-tuple-element.11), channel_id=1, source_target_pairs={{0,1},{1,0},{2,3},{3,2},{4,5},{5,4},{6,7},{7,6},{8,9},{9,8},{10,11... | collective-permute-start | bytes 786440 | tf_op jit(solution)/shard_map/ppermute | solution.py:212
  68.0 14.3 %collective-permute-start.4 = (bf16[2,1024,128]{2,1,0:T(8,128)(2,1)S(1)}, bf16[2,1024,128]{2,1,0:T(8,128)(2,1)S(1)}, u32[]{:S(2)}, u32[]{:S(2)}) collective-permute-start(bf16[2,1024,128]{2,1,0:T(8,128)(2,1)S(1)} %pad_maximum_fusion.refs_0_.own), channel_id=1, source_target_pairs={{0,6},{1,7},{2,0},{3,1},{4,2},{5,3},{6,4},{7,5},{8,14},{9,15},{10,... | collective-permute-start | bytes 1572872 | tf_op jit(solution)/shard_map/ppermute | solution.py:206
  70.8 15.3 %collective-permute-start.3 = (bf16[2,1024,128]{2,1,0:T(8,128)(2,1)S(1)}, bf16[2,1024,128]{2,1,0:T(8,128)(2,1)S(1)}, u32[]{:S(2)}, u32[]{:S(2)}) collective-permute-start(bf16[2,1024,128]{2,1,0:T(8,128)(2,1)S(1)} %pad_maximum_fusion.refs_0_.own), channel_id=1, source_target_pairs={{0,2},{1,3},{2,4},{3,5},{4,6},{5,7},{6,0},{7,1},{8,10},{9,11},{10,... | collective-permute-start | bytes 1572872 | tf_op jit(solution)/shard_map/ppermute | solution.py:206
  70.8 15.4 %collective-permute-start.2 = (bf16[2,1024,128]{2,1,0:T(8,128)(2,1)S(1)}, bf16[2,1024,128]{2,1,0:T(8,128)(2,1)S(1)}, u32[]{:S(2)}, u32[]{:S(2)}) collective-permute-start(bf16[2,1024,128]{2,1,0:T(8,128)(2,1)S(1)} %pad_maximum_fusion.refs_0_.own), channel_id=1, source_target_pairs={{0,192},{8,200},{16,208},{24,216},{32,224},{40,232},{48,240},{56,2... | collective-permute-start | bytes 1572872 | tf_op jit(solution)/shard_map/ppermute | solution.py:209
  72.9 15.5 %collective-permute-start.1 = (bf16[2,1024,128]{2,1,0:T(8,128)(2,1)S(1)}, bf16[2,1024,128]{2,1,0:T(8,128)(2,1)S(1)}, u32[]{:S(2)}, u32[]{:S(2)}) collective-permute-start(bf16[2,1024,128]{2,1,0:T(8,128)(2,1)S(1)} %pad_maximum_fusion.refs_0_.own), channel_id=1, source_target_pairs={{0,64},{8,72},{16,80},{24,88},{32,96},{40,104},{48,112},{56,120},{... | collective-permute-start | bytes 1572872 | tf_op jit(solution)/shard_map/ppermute | solution.py:209
  82.3 8.8 %collective-permute-start.8 = (bf16[1024,128]{1,0:T(8,128)(2,1)S(1)}, bf16[1024,128]{1,0:T(8,128)(2,1)S(1)}, u32[]{:S(2)}, u32[]{:S(2)}) collective-permute-start(bf16[1024,128]{1,0:T(8,128)(2,1)S(1)} %slice_bitcast_fusion), channel_id=1, source_target_pairs={{0,6},{1,7},{2,0},{3,1},{4,2},{5,3},{6,4},{7,5},{8,14},{9,15},{10,... | collective-permute-start | bytes 786440 | tf_op jit(solution)/shard_map/ppermute | solution.py:206
  86.1 8.5 %collective-permute-start.7 = (bf16[1024,128]{1,0:T(8,128)(2,1)S(1)}, bf16[1024,128]{1,0:T(8,128)(2,1)S(1)}, u32[]{:S(2)}, u32[]{:S(2)}) collective-permute-start(bf16[1024,128]{1,0:T(8,128)(2,1)S(1)} %slice_bitcast_fusion.1), channel_id=1, source_target_pairs={{0,2},{1,3},{2,4},{3,5},{4,6},{5,7},{6,0},{7,1},{8,10},{9,11},{10,... | collective-permute-start | bytes 786440 | tf_op jit(solution)/shard_map/ppermute | solution.py:206
  86.2 8.4 %collective-permute-start.6 = (bf16[1024,128]{1,0:T(8,128)(2,1)S(1)}, bf16[1024,128]{1,0:T(8,128)(2,1)S(1)}, u32[]{:S(2)}, u32[]{:S(2)}) collective-permute-start(bf16[1024,128]{1,0:T(8,128)(2,1)S(1)} %slice_bitcast_fusion.2), channel_id=1, source_target_pairs={{0,192},{8,200},{16,208},{24,216},{32,224},{40,232},{48,240},{56,2... | collective-permute-start | bytes 786440 | tf_op jit(solution)/shard_map/ppermute | solution.py:209
  88.4 8.2 %collective-permute-start.5 = (bf16[1024,128]{1,0:T(8,128)(2,1)S(1)}, bf16[1024,128]{1,0:T(8,128)(2,1)S(1)}, u32[]{:S(2)}, u32[]{:S(2)}) collective-permute-start(bf16[1024,128]{1,0:T(8,128)(2,1)S(1)} %slice_bitcast_fusion.3), channel_id=1, source_target_pairs={{0,64},{8,72},{16,80},{24,88},{32,96},{40,104},{48,112},{56,120},{... | collective-permute-start | bytes 786440 | tf_op jit(solution)/shard_map/ppermute | solution.py:209
  98.0 2.7 %collective-permute-start.9 = (bf16[8,512,128]{2,1,0:T(8,128)(2,1)S(1)}, bf16[8,512,128]{2,1,0:T(8,128)(2,1)S(1)}, u32[]{:S(2)}, u32[]{:S(2)}) collective-permute-start(bf16[8,512,128]{2,1,0:T(8,128)(2,1)S(1)} %gram_other.1), channel_id=1, source_target_pairs={{0,1},{1,0},{2,3},{3,2},{4,5},{5,4},{6,7},{7,6},{8,9},{9,8},{10,11... | collective-permute-start | bytes 3145736 | tf_op jit(solution)/shard_map/ppermute | solution.py:212

commit v5 on v2

--- a/solution.py
+++ b/solution.py
@@ -1,3 +1,5 @@
+import functools
+
 import jax
 import jax.numpy as jnp
 from jax import lax
@@ -59,14 +61,14 @@
 def mix_kernel(picks_ref, raw_ref, out_ref, work):
     half = N_BLOCKS // 2
 
-    @pl.loop(0, N_BLOCKS // 16)
+    @pl.loop(0, N_BLOCKS // 16, unroll=2)
     def _(d):
         base = d * 16
         parts = [raw_ref[base + b].astype(jnp.float32) for b in range(16)]
         for b, part in enumerate(hadamard(parts)):
             work[base + b] = part
 
-    @pl.loop(0, 32)
+    @pl.loop(0, 32, unroll=2)
     def _(i):
         base = lax.div(i, 16) * half + lax.rem(i, 16)
         parts = [work[base + 16 * e] for e in range(16)]
@@ -82,56 +84,125 @@
 
 
 def mix(raw, picks):
-    samples = picks.shape[0]
     return pl.pallas_call(
         mix_kernel,
         in_specs=[SCALARS, LOCAL],
         out_specs=LOCAL,
         scratch_shapes=[pltpu.VMEM((N_BLOCKS, CHUNK, LANES), jnp.float32)],
-        out_shape=jax.ShapeDtypeStruct((samples, CHUNK, LANES), jnp.bfloat16),
+        out_shape=jax.ShapeDtypeStruct((picks.shape[0], CHUNK, LANES), jnp.bfloat16),
         compiler_params=pltpu.CompilerParams(vmem_limit_bytes=16 * MIB),
         name="mix",
     )(picks, raw)
 
 
-PIECES = 5
-
-
-def gram_kernel(at, *refs):
-    cols, rows = refs[:PIECES], (refs[PIECES : 2 * PIECES], refs[2 * PIECES : 3 * PIECES])
-    out_ref, left = refs[3 * PIECES :]
-    half = cols[2].shape[0]
+NEAR = (0, 1, 3)
+
+
+def halves_kernel(*refs):
+    pieces, outs = refs[:4], refs[4:]
+    depth = outs[0].shape[0]
+    for i, out in enumerate(outs):
+        out[...] = pieces[i][pl.ds(i % 2 * depth, depth), :]
+
+
+def halves(*pieces):
+    part = jax.ShapeDtypeStruct((pieces[0].shape[0] // 2, LANES), pieces[0].dtype)
+    return pl.pallas_call(
+        halves_kernel,
+        in_specs=[LOCAL] * 4,
+        out_specs=[LOCAL] * 4,
+        out_shape=[part] * 4,
+        compiler_params=pltpu.CompilerParams(vmem_limit_bytes=16 * MIB),
+        cost_estimate=pl.CostEstimate(flops=0, bytes_accessed=2 * MIB, transcendentals=0),
+        name="halves",
+    )(*pieces)
+
+
+def pair_dot(left, own, other):
+    return jnp.dot(left, jnp.concatenate([own, other], axis=1), preferred_element_type=jnp.float32)
+
+
+def near_kernel(*refs):
+    cols, own, other, (left, out_ref) = refs[:3], refs[3:6], refs[6:9], refs[9:]
+    for j in range(len(NEAR)):
+        left[pl.ds(j * LANES, LANES), :] = cols[j][...].T
+    for j in range(len(NEAR)):
+        out_ref[j] = pair_dot(left[...], own[j][...], other[j][...]).astype(out_ref.dtype)
+
+
+def cost(depth, blocks):
+    flops = 2 * depth * blocks * LANES * NCORE * LANES
+    return pl.CostEstimate(flops=flops, bytes_accessed=8 * MIB, transcendentals=0)
+
+
+def gram_near(cols, own, other):
+    depth, near = cols[0].shape[0], len(NEAR)
+    return pl.pallas_call(
+        near_kernel,
+        in_specs=[LOCAL] * 9,
+        out_specs=[LOCAL] * 2,
+        out_shape=[
+            jax.ShapeDtypeStruct((near * LANES, depth), jnp.bfloat16),
+            jax.ShapeDtypeStruct((near, near * LANES, NCORE * LANES), jnp.bfloat16),
+        ],
+        compiler_params=pltpu.CompilerParams(vmem_limit_bytes=16 * MIB),
+        cost_estimate=cost(depth, near * near),
+        name="gram_near",
+    )(*cols, *own, *other)
+
+
+def side_kernel(*refs):
+    col, own, other, (last, out_ref) = refs[0], refs[1:4], refs[4:7], refs[7:]
+    last[...] = col[...].T
+    for j in range(len(NEAR)):
+        out_ref[j] = pair_dot(last[...], own[j][...], other[j][...]).astype(out_ref.dtype)
+
+
+def gram_side(col, own, other):
+    depth, near = col.shape[0], len(NEAR)
+    return pl.pallas_call(
+        side_kernel,
+        in_specs=[LOCAL] * 7,
+        out_specs=[LOCAL] * 2,
+        out_shape=[
+            jax.ShapeDtypeStruct((LANES, depth), jnp.bfloat16),
+            jax.ShapeDtypeStruct((near, LANES, NCORE * LANES), jnp.bfloat16),
+        ],
+        compiler_params=pltpu.CompilerParams(vmem_limit_bytes=16 * MIB),
+        cost_estimate=cost(depth, near),
+        name="gram_side",
+    )(col, *own, *other)
+
+
+def far_kernel(at, near_ref, side_ref, left, last, own, other, out_ref):
     x, core, turn = at[0], at[1], at[2]
-    spots = [(0, 0, 2 * half), (1, 0, 2 * half), (2, 0, half), (2, half, half), (3, 0, 2 * half)]
-    for p, (j, start, size) in enumerate(spots):
-        quarter = lax.rem(turn + j, NY)
-        where = pl.ds(pl.multiple_of(quarter * LANES, LANES), LANES)
-        left[where, pl.ds(start, size)] = cols[p][...].T
-    for pieces, j in (((0,), 0), ((1,), 1), ((4,), 3), ((2, 3), 2)):
-        panel = lax.rem(x + NX - j, NX) * NCORE
-        for m in range(2):
-            part = pl.ds(m * 2 * LANES, 2 * LANES)
-            block = None
-            for p in pieces:
-                pair = jnp.concatenate([rows[0][p][...], rows[1][p][...]], axis=1)
-                depth = pl.ds(spots[p][1], spots[p][2])
-                term = jnp.dot(left[part, depth], pair, preferred_element_type=jnp.float32)
-                block = term if block is None else block + term
-            block = block.astype(out_ref.dtype)
-            out_ref[panel + core, part, :] = block[:, :LANES]
-            out_ref[panel + 1 - core, part, :] = block[:, LANES:]
-
-
-def gram_part(at, cols, own, other):
-    return pl.pallas_call(
-        gram_kernel,
-        in_specs=[SCALARS] + [LOCAL] * (3 * PIECES),
+
+    def put(step_x, step_y, block):
+        panel = lax.rem(x + NX - step_x, NX) * NCORE
+        quarter = pl.multiple_of(lax.rem(turn + step_y, NY) * LANES, LANES)
+        out_ref[panel + core, pl.ds(quarter, LANES), :] = block[:, :LANES]
+        out_ref[panel + 1 - core, pl.ds(quarter, LANES), :] = block[:, LANES:]
+
+    block = pair_dot(left[...], own[...], other[...]).astype(out_ref.dtype)
+    for j, step in enumerate(NEAR):
+        put(2, step, block[j * LANES : (j + 1) * LANES])
+    put(2, 2, pair_dot(last[...], own[...], other[...]).astype(out_ref.dtype))
+    for i, step_x in enumerate(NEAR):
+        put(step_x, 2, side_ref[i])
+        for j, step_y in enumerate(NEAR):
+            put(step_x, step_y, near_ref[i, pl.ds(j * LANES, LANES), :])
+
+
+def gram_far(at, near, side, left, last, own, other):
+    return pl.pallas_call(
+        far_kernel,
+        in_specs=[SCALARS] + [LOCAL] * 6,
         out_specs=LOCAL,
-        scratch_shapes=[pltpu.VMEM((NY * LANES, cols[0].shape[0]), jnp.bfloat16)],
-        out_shape=jax.ShapeDtypeStruct((NX * NCORE, NY * LANES, LANES), jnp.bfloat16),
-        compiler_params=pltpu.CompilerParams(vmem_limit_bytes=24 * MIB),
-        name="gram_part",
-    )(at, *cols, *own, *other)
+        out_shape=jax.ShapeDtypeStruct((NX * NCORE, NY * LANES, LANES), near.dtype),
+        compiler_params=pltpu.CompilerParams(vmem_limit_bytes=16 * MIB),
+        cost_estimate=cost(own.shape[0], NY),
+        name="gram_far",
+    )(at, near, side, left, last, own, other)
 
 
 def finish_kernel(scale, parts_ref, out_ref):
@@ -172,15 +243,16 @@
     def swap(value):
         return lax.ppermute(value, "col", [(i, i ^ 1) for i in range(NX * NCORE)])
 
-    depth = sketch.shape[0] // 2
     x_up, x_down = along_x(sketch, 1), along_x(sketch, -1)
     y_up, y_down = along_y(sketch, 1), along_y(sketch, -1)
-    x_far = (along_x(x_up[:depth], 1), along_x(x_down[depth:], -1))
-    y_far = (along_y(y_up[:depth], 1), along_y(y_down[depth:], -1))
-    own = [sketch, x_up, *x_far, x_down]
-    cols = [sketch, y_up, *y_far, y_down]
-    other = [swap(piece) for piece in own]
-    partial = gram_part(at, cols, own, other)
+    x_low, x_high, y_low, y_high = halves(x_up, x_down, y_up, y_down)
+    x_far = jnp.concatenate([along_x(x_low, 1), along_x(x_high, -1)])
+    y_far = jnp.concatenate([along_y(y_low, 1), along_y(y_high, -1)])
+    own = (sketch, x_up, x_down)
+    other = tuple(swap(piece) for piece in own)
+    left, near = gram_near((sketch, y_up, y_down), own, other)
+    last, side = gram_side(y_far, own, other)
+    partial = gram_far(at, near, side, left, last, x_far, swap(x_far))
 
     groups = [
         [gy * NZ + (s + gy) % NY + NY * half for gy in range(NY) for half in range(NZ // NY)]

time: 136 us -> 136 us (level); the launches traced: 135 us -> 134 us
  blocking collectives: 94.3 us -> 91.9 us
    ppermute x4, waiting for transfers between devices: 9.35 us -> 13.3 us  [along_y(): lax.ppermute(value, 'dp', [(i, (i + NZ * step) % (NY * NZ)) for i in rang...]
    ppermute x4, waiting for transfers between devices: 8.68 us -> 5.27 us  [along_x(): lax.ppermute(value, 'col', [(i, (i + NCORE * step) % (NX * NCORE)) for i...]
    all_to_all x1, blocking collectives: 34.3 us -> 31.9 us  [on_device(): lax.all_to_all(partial, 'dp', split_axis=0, concat_axis=0, axis_index_gro...]
    pallas_call x1 -> x4, Pallas kernels: 3.45 us -> 3.5 us  [the longest x1 1.42 us: gram_near(): pl.pallas_call(near_kernel, in_specs=[LOCAL] * 9, out_specs=[LOCAL] * 2,...]
  transfers between devices with their start and end apart: 13 -> 12, of which waited for: 6 -> 6; matrix products, arithmetic and copies ran while one was open for 0% -> 0% of each run, Pallas kernels for 0% -> 2%
where the time goes in v5:
time: 136 us; the launch traced here: 134 us
  blocking collectives  91.9 us (68%)
  waiting for transfers between devices  18.6 us (14%)
  starting transfers between devices  12.1 us (9%)
  Pallas kernels  8.35 us (6%)
  local copies, waits for them, and re-layouts  2.35 us (2%)
    all_to_all x1, blocking collectives, on_device(): lax.all_to_all(outgoing, 'dp', split_axis=0, concat_axis=0, tiled=True)  60 us
    all_to_all x1, blocking collectives, on_device(): lax.all_to_all(partial, 'dp', split_axis=0, concat_axis=0, axis_index_gro...  31.9 us
    ppermute x4, waiting for transfers between devices, along_y(): lax.ppermute(value, 'dp', [(i, (i + NZ * step) % (NY * NZ)) for i in rang...  13.3 us
    ppermute x4, starting transfers between devices, along_x(): lax.ppermute(value, 'col', [(i, (i + NCORE * step) % (NX * NCORE)) for i...  6.55 us
    ppermute x4, starting transfers between devices, along_y(): lax.ppermute(value, 'dp', [(i, (i + NZ * step) % (NY * NZ)) for i in rang...  5.34 us
    ppermute x4, waiting for transfers between devices, along_x(): lax.ppermute(value, 'col', [(i, (i + NCORE * step) % (NX * NCORE)) for i...  5.27 us
    pallas_call x1, Pallas kernels, mix(): pl.pallas_call(mix_kernel, in_specs=[SCALARS, LOCAL], out_specs=LOCAL, sc...  2.94 us
  transfers between devices with their start and end apart: 12, of which 6 were waited for; matrix products, arithmetic and copies ran while one was open for 0% of the time, Pallas kernels for 2%

profile of v5, /device:TPU:64, one launch (start us, length us, event | category | flops | bytes accessed | tf_op | source)
XLA Modules:
  0.0 133.6 jit_solution(5588847663153581657)
XLA Ops:
  0.1 1.6 %copy-done = bf16[2048,512]{1,0:T(8,128)(2,1)S(1)} copy-done((bf16[2048,512]{1,0:T(8,128)(2,1)S(1)}, bf16[2048,512]{1,0:T(8,128)(2,1)}, u32[]{:S(2)}) %copy-start) | copy-done | bytes 2097176
  1.7 0.7 copy-done.1
  2.4 1.0 pack.1
  3.4 60.0 %all_to_all.10 = bf16[32,16,16,128]{3,2,1,0:T(8,128)(2,1)S(1)} all-to-all(bf16[32,16,16,128]{3,2,1,0:T(8,128)(2,1)S(1)} %bitcast.17), channel_id=1, replica_groups=mesh['dp'=32,'col'=8] {'dp'}, dimensions={0} | all-to-all | bytes 4194304 | tf_op jit(solution)/shard_map/all_to_all | solution.py:234
  63.4 2.9 %mix.1 = bf16[128,16,128]{2,1,0:T(8,128)(2,1)S(1)} custom-call(s32[128]{0:T(128)S(1)} %copy-done.2, bf16[512,16,128]{2,1,0:T(8,128)(2,1)S(1)} %bitcast.16), custom_call_target="tpu_custom_call" | custom-call | tf_op jit(solution)/shard_map/mix/pallas_call | solution.py:87
  66.3 0.6 collective-permute-start
  67.0 2.7 %collective-permute-start.1 = (bf16[2048,128]{1,0:T(8,128)(2,1)S(1)}, bf16[2048,128]{1,0:T(8,128)(2,1)S(1)}, u32[]{:S(2)}, u32[]{:S(2)}) collective-permute-start(bf16[2048,128]{1,0:T(8,128)(2,1)S(1)} %bitcast.9), channel_id=1, source_target_pairs={{0,192},{8,200},{16,208},{24,216},{32,224},{40,232},{48,240},{56,2... | collective-permute-start | bytes 1572872 | tf_op jit(solution)/shard_map/ppermute | solution.py:241
  69.6 1.5 %collective-permute-start.2 = (bf16[2048,128]{1,0:T(8,128)(2,1)S(1)}, bf16[2048,128]{1,0:T(8,128)(2,1)S(1)}, u32[]{:S(2)}, u32[]{:S(2)}) collective-permute-start(bf16[2048,128]{1,0:T(8,128)(2,1)S(1)} %bitcast.10), channel_id=1, source_target_pairs={{0,2},{1,3},{2,4},{3,5},{4,6},{5,7},{6,0},{7,1},{8,10},{9,11},{10,... | collective-permute-start | bytes 1572872 | tf_op jit(solution)/shard_map/ppermute | solution.py:238
  71.1 1.7 %collective-permute-start.3 = (bf16[2048,128]{1,0:T(8,128)(2,1)S(1)}, bf16[2048,128]{1,0:T(8,128)(2,1)S(1)}, u32[]{:S(2)}, u32[]{:S(2)}) collective-permute-start(bf16[2048,128]{1,0:T(8,128)(2,1)S(1)} %bitcast.11), channel_id=1, source_target_pairs={{0,6},{1,7},{2,0},{3,1},{4,2},{5,3},{6,4},{7,5},{8,14},{9,15},{10,... | collective-permute-start | bytes 1572872 | tf_op jit(solution)/shard_map/ppermute | solution.py:238
  72.9 6.8 %collective-permute-done.refs_1_.refs_2_ = bf16[2048,128]{1,0:T(8,128)(2,1)S(1)} collective-permute-done((bf16[2048,128]{1,0:T(8,128)(2,1)S(1)}, bf16[2048,128]{1,0:T(8,128)(2,1)S(1)}, u32[]{:S(2)}, u32[]{:S(2)}) %collective-permute-start) | collective-permute-done | bytes 524320 | tf_op jit(solution)/shard_map/ppermute | solution.py:241
  79.7 2.7 %collective-permute-done.2.refs_4_.refs_0_.refs_2_ = bf16[2048,128]{1,0:T(8,128)(2,1)S(1)} collective-permute-done((bf16[2048,128]{1,0:T(8,128)(2,1)S(1)}, bf16[2048,128]{1,0:T(8,128)(2,1)S(1)}, u32[]{:S(2)}, u32[]{:S(2)}) %collective-permute-start.2) | collective-permute-done | bytes 524320 | tf_op jit(solution)/shard_map/ppermute | solution.py:238
  82.4 1.6 %collective-permute-start.9 = (bf16[1024,128]{1,0:T(8,128)(2,1)S(1)}, bf16[1024,128]{1,0:T(8,128)(2,1)S(1)}, u32[]{:S(2)}, u32[]{:S(2)}) collective-permute-start(bf16[1024,128]{1,0:T(8,128)(2,1)S(1)} %get-tuple-element.19), channel_id=1, source_target_pairs={{0,2},{1,3},{2,4},{3,5},{4,6},{5,7},{6,0},{7,1},{8,10},{9,11},{10,... | collective-permute-start | bytes 786440 | tf_op jit(solution)/shard_map/ppermute | solution.py:238
  84.0 1.7 %collective-permute-start.10 = (bf16[1024,128]{1,0:T(8,128)(2,1)S(1)}, bf16[1024,128]{1,0:T(8,128)(2,1)S(1)}, u32[]{:S(2)}, u32[]{:S(2)}) collective-permute-start(bf16[1024,128]{1,0:T(8,128)(2,1)S(1)} %get-tuple-element.20), channel_id=1, source_target_pairs={{0,6},{1,7},{2,0},{3,1},{4,2},{5,3},{6,4},{7,5},{8,14},{9,15},{10,... | collective-permute-start | bytes 786440 | tf_op jit(solution)/shard_map/ppermute | solution.py:238
  85.7 1.5 %collective-permute-start.8 = (bf16[1024,128]{1,0:T(8,128)(2,1)S(1)}, bf16[1024,128]{1,0:T(8,128)(2,1)S(1)}, u32[]{:S(2)}, u32[]{:S(2)}) collective-permute-start(bf16[1024,128]{1,0:T(8,128)(2,1)S(1)} %get-tuple-element.15), channel_id=1, source_target_pairs={{0,192},{8,200},{16,208},{24,216},{32,224},{40,232},{48,240},{56,2... | collective-permute-start | bytes 786440 | tf_op jit(solution)/shard_map/ppermute | solution.py:241
  87.3 0.5 collective-permute-start.7
  87.8 2.3 %collective-permute-done.9 = bf16[1024,128]{1,0:T(8,128)(2,1)S(1)} collective-permute-done((bf16[1024,128]{1,0:T(8,128)(2,1)S(1)}, bf16[1024,128]{1,0:T(8,128)(2,1)S(1)}, u32[]{:S(2)}, u32[]{:S(2)}) %collective-permute-start.9) | collective-permute-done | bytes 262176 | tf_op jit(solution)/shard_map/ppermute | solution.py:238
  90.1 0.3 collective-permute-done.10
  90.7 1.4 %collective-permute-done.8 = bf16[1024,128]{1,0:T(8,128)(2,1)S(1)} collective-permute-done((bf16[1024,128]{1,0:T(8,128)(2,1)S(1)}, bf16[1024,128]{1,0:T(8,128)(2,1)S(1)}, u32[]{:S(2)}, u32[]{:S(2)}) %collective-permute-start.8) | collective-permute-done | bytes 262176 | tf_op jit(solution)/shard_map/ppermute | solution.py:241
  92.1 5.1 %collective-permute-done.7 = bf16[1024,128]{1,0:T(8,128)(2,1)S(1)} collective-permute-done((bf16[1024,128]{1,0:T(8,128)(2,1)S(1)}, bf16[1024,128]{1,0:T(8,128)(2,1)S(1)}, u32[]{:S(2)}, u32[]{:S(2)}) %collective-permute-start.7) | collective-permute-done | bytes 262176 | tf_op jit(solution)/shard_map/ppermute | solution.py:241
  97.3 0.6 gram_side.1
  97.9 1.4 %gram_near.1 = (bf16[384,2048]{1,0:T(8,128)(2,1)S(1)}, bf16[3,384,256]{2,1,0:T(8,128)(2,1)S(1)}) custom-call(bf16[2048,128]{1,0:T(8,128)(2,1)S(1)} %bitcast.14, bf16[2048,128]{1,0:T(8,128)(2,1)S(1)} %collective-permute-done.refs_1_.refs_2_, bf16[2048,128]{1,0:T(8,128)(2,1)S(1)} %collective-permute-done.1.refs_2_.refs_3_, bf16[2048,128]{1,0:T(8,128)(2,1)S(1)} %bitcast.15, ...), custom_call_target="tpu_custom_call" | custom-call | flops 1207959552 | bytes 8388608 | tf_op jit(solution)/shard_map/gram_near/pallas_call | solution.py:140
  99.3 1.4 %gram_far.1 = bf16[8,512,128]{2,1,0:T(8,128)(2,1)S(1)} custom-call(s32[3]{0:T(128)S(1)} %pad_add_fusion.at, bf16[3,384,256]{2,1,0:T(8,128)(2,1)S(1)} %get-tuple-element.13.near_ref, bf16[3,128,256]{2,1,0:T(8,128)(2,1)S(1)} %get-tuple-element.16.side_ref, bf16[384,2048]{1,0:T(8,128)(2,1)S(1)} %get-tuple-element.17.left, ...), custom_call_target="tpu_custom_call" | custom-call | flops 536870912 | bytes 8388608 | tf_op jit(solution)/shard_map/gram_far/pallas_call | solution.py:197
  100.7 31.9 %all_to_all.11.parts_ref = bf16[8,512,128]{2,1,0:T(8,128)(2,1)S(1)} all-to-all(bf16[8,512,128]{2,1,0:T(8,128)(2,1)S(1)} %gram_far.1), channel_id=1, replica_groups={{0,32,72,104,144,176,216,248},{8,40,80,112,152,184,192,224},{16,48,88,1..., dimensions={0} | all-to-all | bytes 2097152 | tf_op jit(solution)/shard_map/all_to_all | solution.py:261
  132.6 0.9 finish.1
  (19 shorter events, 0.5 us)
Async XLA Ops:
  0.1 1.6 %copy-start = (bf16[2048,512]{1,0:T(8,128)(2,1)S(1)}, bf16[2048,512]{1,0:T(8,128)(2,1)}, u32[]{:S(2)}) copy-start(bf16[2048,512]{1,0:T(8,128)(2,1)} %param.3) | copy-start | bytes 6291460
  1.7 0.7 copy-start.1
  3.4 60.0 %copy-start.2 = (s32[128]{0:T(128)S(1)}, s32[128]{0:T(128)}, u32[]{:S(2)}) copy-start(s32[128]{0:T(128)} %picks_ref.1) | copy-start | bytes 1540
  66.3 13.3 %collective-permute-start = (bf16[2048,128]{1,0:T(8,128)(2,1)S(1)}, bf16[2048,128]{1,0:T(8,128)(2,1)S(1)}, u32[]{:S(2)}, u32[]{:S(2)}) collective-permute-start(bf16[2048,128]{1,0:T(8,128)(2,1)S(1)} %bitcast.8), channel_id=1, source_target_pairs={{0,64},{8,72},{16,80},{24,88},{32,96},{40,104},{48,112},{56,120},{... | collective-permute-start | bytes 1572872 | tf_op jit(solution)/shard_map/ppermute | solution.py:241
  67.0 12.7 %collective-permute-start.1 = (bf16[2048,128]{1,0:T(8,128)(2,1)S(1)}, bf16[2048,128]{1,0:T(8,128)(2,1)S(1)}, u32[]{:S(2)}, u32[]{:S(2)}) collective-permute-start(bf16[2048,128]{1,0:T(8,128)(2,1)S(1)} %bitcast.9), channel_id=1, source_target_pairs={{0,192},{8,200},{16,208},{24,216},{32,224},{40,232},{48,240},{56,2... | collective-permute-start | bytes 1572872 | tf_op jit(solution)/shard_map/ppermute | solution.py:241
  69.6 12.7 %collective-permute-start.2 = (bf16[2048,128]{1,0:T(8,128)(2,1)S(1)}, bf16[2048,128]{1,0:T(8,128)(2,1)S(1)}, u32[]{:S(2)}, u32[]{:S(2)}) collective-permute-start(bf16[2048,128]{1,0:T(8,128)(2,1)S(1)} %bitcast.10), channel_id=1, source_target_pairs={{0,2},{1,3},{2,4},{3,5},{4,6},{5,7},{6,0},{7,1},{8,10},{9,11},{10,... | collective-permute-start | bytes 1572872 | tf_op jit(solution)/shard_map/ppermute | solution.py:238
  71.1 11.2 %collective-permute-start.3 = (bf16[2048,128]{1,0:T(8,128)(2,1)S(1)}, bf16[2048,128]{1,0:T(8,128)(2,1)S(1)}, u32[]{:S(2)}, u32[]{:S(2)}) collective-permute-start(bf16[2048,128]{1,0:T(8,128)(2,1)S(1)} %bitcast.11), channel_id=1, source_target_pairs={{0,6},{1,7},{2,0},{3,1},{4,2},{5,3},{6,4},{7,5},{8,14},{9,15},{10,... | collective-permute-start | bytes 1572872 | tf_op jit(solution)/shard_map/ppermute | solution.py:238
  82.4 7.7 %collective-permute-start.9 = (bf16[1024,128]{1,0:T(8,128)(2,1)S(1)}, bf16[1024,128]{1,0:T(8,128)(2,1)S(1)}, u32[]{:S(2)}, u32[]{:S(2)}) collective-permute-start(bf16[1024,128]{1,0:T(8,128)(2,1)S(1)} %get-tuple-element.19), channel_id=1, source_target_pairs={{0,2},{1,3},{2,4},{3,5},{4,6},{5,7},{6,0},{7,1},{8,10},{9,11},{10,... | collective-permute-start | bytes 786440 | tf_op jit(solution)/shard_map/ppermute | solution.py:238
  84.0 6.4 %collective-permute-start.10 = (bf16[1024,128]{1,0:T(8,128)(2,1)S(1)}, bf16[1024,128]{1,0:T(8,128)(2,1)S(1)}, u32[]{:S(2)}, u32[]{:S(2)}) collective-permute-start(bf16[1024,128]{1,0:T(8,128)(2,1)S(1)} %get-tuple-element.20), channel_id=1, source_target_pairs={{0,6},{1,7},{2,0},{3,1},{4,2},{5,3},{6,4},{7,5},{8,14},{9,15},{10,... | collective-permute-start | bytes 786440 | tf_op jit(solution)/shard_map/ppermute | solution.py:238
  85.7 6.4 %collective-permute-start.8 = (bf16[1024,128]{1,0:T(8,128)(2,1)S(1)}, bf16[1024,128]{1,0:T(8,128)(2,1)S(1)}, u32[]{:S(2)}, u32[]{:S(2)}) collective-permute-start(bf16[1024,128]{1,0:T(8,128)(2,1)S(1)} %get-tuple-element.15), channel_id=1, source_target_pairs={{0,192},{8,200},{16,208},{24,216},{32,224},{40,232},{48,240},{56,2... | collective-permute-start | bytes 786440 | tf_op jit(solution)/shard_map/ppermute | solution.py:241
  87.3 10.0 %collective-permute-start.4 = (bf16[2048,128]{1,0:T(8,128)(2,1)S(1)}, bf16[2048,128]{1,0:T(8,128)(2,1)S(1)}, u32[]{:S(2)}, u32[]{:S(2)}) collective-permute-start(bf16[2048,128]{1,0:T(8,128)(2,1)S(1)} %bitcast.12), channel_id=1, source_target_pairs={{0,1},{1,0},{2,3},{3,2},{4,5},{5,4},{6,7},{7,6},{8,9},{9,8},{10,11... | collective-permute-start | bytes 1572872 | tf_op jit(solution)/shard_map/ppermute | solution.py:244
  87.3 9.9 %collective-permute-start.7 = (bf16[1024,128]{1,0:T(8,128)(2,1)S(1)}, bf16[1024,128]{1,0:T(8,128)(2,1)S(1)}, u32[]{:S(2)}, u32[]{:S(2)}) collective-permute-start(bf16[1024,128]{1,0:T(8,128)(2,1)S(1)} %get-tuple-element.14), channel_id=1, source_target_pairs={{0,64},{8,72},{16,80},{24,88},{32,96},{40,104},{48,112},{56,120},{... | collective-permute-start | bytes 786440 | tf_op jit(solution)/shard_map/ppermute | solution.py:241
  90.1 7.2 %collective-permute-start.5 = (bf16[2048,128]{1,0:T(8,128)(2,1)S(1)}, bf16[2048,128]{1,0:T(8,128)(2,1)S(1)}, u32[]{:S(2)}, u32[]{:S(2)}) collective-permute-start(bf16[2048,128]{1,0:T(8,128)(2,1)S(1)} %collective-permute-done.2.refs_4_.refs_0_.refs_2_), channel_id=1, source_target_pairs={{0,1},{1,0},{2,3},{3,2},{4,5},{5,4},{6,7},{7,6},{8,9},{9,8},{10,11... | collective-permute-start | bytes 1572872 | tf_op jit(solution)/shard_map/ppermute | solution.py:244
  90.4 6.9 %collective-permute-start.6 = (bf16[2048,128]{1,0:T(8,128)(2,1)S(1)}, bf16[2048,128]{1,0:T(8,128)(2,1)S(1)}, u32[]{:S(2)}, u32[]{:S(2)}) collective-permute-start(bf16[2048,128]{1,0:T(8,128)(2,1)S(1)} %collective-permute-done.3.refs_5_.refs_1_.refs_3_), channel_id=1, source_target_pairs={{0,1},{1,0},{2,3},{3,2},{4,5},{5,4},{6,7},{7,6},{8,9},{9,8},{10,11... | collective-permute-start | bytes 1572872 | tf_op jit(solution)/shard_map/ppermute | solution.py:244
  92.1 7.2 %collective-permute-start.11 = (bf16[2048,128]{1,0:T(8,128)(2,1)S(1)}, bf16[2048,128]{1,0:T(8,128)(2,1)S(1)}, u32[]{:S(2)}, u32[]{:S(2)}) collective-permute-start(bf16[2048,128]{1,0:T(8,128)(2,1)S(1)} %constant_dynamic-update-slice_fusion.own), channel_id=1, source_target_pairs={{0,1},{1,0},{2,3},{3,2},{4,5},{5,4},{6,7},{7,6},{8,9},{9,8},{10,11... | collective-permute-start | bytes 1572872 | tf_op jit(solution)/shard_map/ppermute | solution.py:244

commit v6 on v5

--- a/solution.py
+++ b/solution.py
@@ -98,24 +98,20 @@
 NEAR = (0, 1, 3)
 
 
-def halves_kernel(*refs):
-    pieces, outs = refs[:4], refs[4:]
-    depth = outs[0].shape[0]
-    for i, out in enumerate(outs):
-        out[...] = pieces[i][pl.ds(i % 2 * depth, depth), :]
-
-
-def halves(*pieces):
-    part = jax.ShapeDtypeStruct((pieces[0].shape[0] // 2, LANES), pieces[0].dtype)
-    return pl.pallas_call(
-        halves_kernel,
-        in_specs=[LOCAL] * 4,
-        out_specs=[LOCAL] * 4,
-        out_shape=[part] * 4,
-        compiler_params=pltpu.CompilerParams(vmem_limit_bytes=16 * MIB),
-        cost_estimate=pl.CostEstimate(flops=0, bytes_accessed=2 * MIB, transcendentals=0),
-        name="halves",
-    )(*pieces)
+def after_kernel(value_ref, *refs):
+    refs[-1][...] = value_ref[...]
+
+
+def after(value, *others):
+    return pl.pallas_call(
+        after_kernel,
+        in_specs=[LOCAL] * (1 + len(others)),
+        out_specs=LOCAL,
+        out_shape=jax.ShapeDtypeStruct(value.shape, value.dtype),
+        compiler_params=pltpu.CompilerParams(vmem_limit_bytes=16 * MIB),
+        cost_estimate=pl.CostEstimate(flops=0, bytes_accessed=MIB, transcendentals=0),
+        name="after",
+    )(value, *others)
 
 
 def pair_dot(left, own, other):
@@ -152,7 +148,7 @@
 
 
 def side_kernel(*refs):
-    col, own, other, (last, out_ref) = refs[0], refs[1:4], refs[4:7], refs[7:]
+    other, own, col, (last, out_ref) = refs[:3], refs[3:6], refs[6], refs[7:]
     last[...] = col[...].T
     for j in range(len(NEAR)):
         out_ref[j] = pair_dot(last[...], own[j][...], other[j][...]).astype(out_ref.dtype)
@@ -171,10 +167,10 @@
         compiler_params=pltpu.CompilerParams(vmem_limit_bytes=16 * MIB),
         cost_estimate=cost(depth, near),
         name="gram_side",
-    )(col, *own, *other)
-
-
-def far_kernel(at, near_ref, side_ref, left, last, own, other, out_ref):
+    )(*other, *own, col)
+
+
+def far_kernel(at, last, side_ref, left, near_ref, own, other, out_ref):
     x, core, turn = at[0], at[1], at[2]
 
     def put(step_x, step_y, block):
@@ -193,7 +189,7 @@
             put(step_x, step_y, near_ref[i, pl.ds(j * LANES, LANES), :])
 
 
-def gram_far(at, near, side, left, last, own, other):
+def gram_far(at, last, side, left, near, own, other):
     return pl.pallas_call(
         far_kernel,
         in_specs=[SCALARS] + [LOCAL] * 6,
@@ -202,7 +198,7 @@
         compiler_params=pltpu.CompilerParams(vmem_limit_bytes=16 * MIB),
         cost_estimate=cost(own.shape[0], NY),
         name="gram_far",
-    )(at, near, side, left, last, own, other)
+    )(at, last, side, left, near, own, other)
 
 
 def finish_kernel(scale, parts_ref, out_ref):
@@ -245,14 +241,13 @@
 
     x_up, x_down = along_x(sketch, 1), along_x(sketch, -1)
     y_up, y_down = along_y(sketch, 1), along_y(sketch, -1)
-    x_low, x_high, y_low, y_high = halves(x_up, x_down, y_up, y_down)
-    x_far = jnp.concatenate([along_x(x_low, 1), along_x(x_high, -1)])
-    y_far = jnp.concatenate([along_y(y_low, 1), along_y(y_high, -1)])
+    x_far, y_far = along_x(sketch, 2), along_y(sketch, 2)
     own = (sketch, x_up, x_down)
-    other = tuple(swap(piece) for piece in own)
+    gate = after(sketch, y_up, y_down, x_up, x_down)
+    other = (swap(gate), swap(after(x_up, gate)), swap(after(x_down, gate)))
+    last, side = gram_side(y_far, own, other)
     left, near = gram_near((sketch, y_up, y_down), own, other)
-    last, side = gram_side(y_far, own, other)
-    partial = gram_far(at, near, side, left, last, x_far, swap(x_far))
+    partial = gram_far(at, last, side, left, near, x_far, swap(x_far))
 
     groups = [
         [gy * NZ + (s + gy) % NY + NY * half for gy in range(NY) for half in range(NZ // NY)]

time: 136 us -> 137 us (level)
  blocking collectives: 91.9 us -> 94.7 us
  starting transfers between devices: 12.1 us -> 10 us
    ppermute x4 -> x3, waiting for transfers between devices: 13.3 us -> 4.97 us  [along_y(): lax.ppermute(value, 'dp', [(i, (i + NZ * step) % (NY * NZ)) for i in rang...]
    ppermute x4 -> x3, waiting for transfers between devices: 5.27 us -> 13.1 us  [along_x(): lax.ppermute(value, 'col', [(i, (i + NCORE * step) % (NX * NCORE)) for i...]
    all_to_all x1, blocking collectives: 31.9 us -> 34.7 us  [on_device(): lax.all_to_all(partial, 'dp', split_axis=0, concat_axis=0, axis_index_gro...]
    ppermute x4, waiting for transfers between devices: 0.01 us -> 1.88 us  [swap(): return lax.ppermute(value, 'col', [(i, i ^ 1) for i in range(NX * NCORE)])]
    ppermute x4 -> x3, starting transfers between devices: 6.55 us -> 5.05 us  [along_x(): lax.ppermute(value, 'col', [(i, (i + NCORE * step) % (NX * NCORE)) for i...]
    ppermute x4 -> x3, starting transfers between devices: 5.34 us -> 4.22 us  [along_y(): lax.ppermute(value, 'dp', [(i, (i + NZ * step) % (NY * NZ)) for i in rang...]
  transfers between devices with their start and end apart: 12 -> 10, of which waited for: 6 -> 7; matrix products, arithmetic and copies ran while one was open for 0% -> 0% of each run, Pallas kernels for 2% -> 2%
where the time goes in v6:
time: 137 us; the launch traced here: 136 us
  blocking collectives  94.7 us (69%)
  waiting for transfers between devices  19.9 us (15%)
  starting transfers between devices  10 us (7%)
  Pallas kernels  8.39 us (6%)
  local copies, waits for them, and re-layouts  2.29 us (2%)
    all_to_all x1, blocking collectives, on_device(): lax.all_to_all(outgoing, 'dp', split_axis=0, concat_axis=0, tiled=True)  60 us
    all_to_all x1, blocking collectives, on_device(): lax.all_to_all(partial, 'dp', split_axis=0, concat_axis=0, axis_index_gro...  34.7 us
    ppermute x3, waiting for transfers between devices, along_x(): lax.ppermute(value, 'col', [(i, (i + NCORE * step) % (NX * NCORE)) for i...  13.1 us
    ppermute x3, starting transfers between devices, along_x(): lax.ppermute(value, 'col', [(i, (i + NCORE * step) % (NX * NCORE)) for i...  5.05 us
    ppermute x3, waiting for transfers between devices, along_y(): lax.ppermute(value, 'dp', [(i, (i + NZ * step) % (NY * NZ)) for i in rang...  4.97 us
    ppermute x3, starting transfers between devices, along_y(): lax.ppermute(value, 'dp', [(i, (i + NZ * step) % (NY * NZ)) for i in rang...  4.22 us
    pallas_call x1, Pallas kernels, mix(): pl.pallas_call(mix_kernel, in_specs=[SCALARS, LOCAL], out_specs=LOCAL, sc...  2.94 us
  transfers between devices with their start and end apart: 10, of which 7 were waited for; matrix products, arithmetic and copies ran while one was open for 0% of the time, Pallas kernels for 2%

profile of v6, /device:TPU:64, one launch (start us, length us, event | category | flops | bytes accessed | tf_op | source)
XLA Modules:
  0.0 135.5 jit_solution(3393332634049313664)
XLA Ops:
  0.1 1.6 %copy-done = bf16[2048,512]{1,0:T(8,128)(2,1)S(1)} copy-done((bf16[2048,512]{1,0:T(8,128)(2,1)S(1)}, bf16[2048,512]{1,0:T(8,128)(2,1)}, u32[]{:S(2)}) %copy-start) | copy-done | bytes 2097176
  1.7 0.7 copy-done.1
  2.4 1.0 pack.1
  3.4 60.0 %all_to_all.10 = bf16[32,16,16,128]{3,2,1,0:T(8,128)(2,1)S(1)} all-to-all(bf16[32,16,16,128]{3,2,1,0:T(8,128)(2,1)S(1)} %bitcast.19), channel_id=1, replica_groups=mesh['dp'=32,'col'=8] {'dp'}, dimensions={0} | all-to-all | bytes 4194304 | tf_op jit(solution)/shard_map/all_to_all | solution.py:230
  63.4 2.9 %mix.1 = bf16[128,16,128]{2,1,0:T(8,128)(2,1)S(1)} custom-call(s32[128]{0:T(128)S(1)} %copy-done.2, bf16[512,16,128]{2,1,0:T(8,128)(2,1)S(1)} %bitcast.18), custom_call_target="tpu_custom_call" | custom-call | tf_op jit(solution)/shard_map/mix/pallas_call | solution.py:87
  66.3 0.6 collective-permute-start
  67.0 2.7 %collective-permute-start.1 = (bf16[2048,128]{1,0:T(8,128)(2,1)S(1)}, bf16[2048,128]{1,0:T(8,128)(2,1)S(1)}, u32[]{:S(2)}, u32[]{:S(2)}) collective-permute-start(bf16[2048,128]{1,0:T(8,128)(2,1)S(1)} %bitcast.9), channel_id=1, source_target_pairs={{0,192},{8,200},{16,208},{24,216},{32,224},{40,232},{48,240},{56,2... | collective-permute-start | bytes 1572872 | tf_op jit(solution)/shard_map/ppermute | solution.py:237
  69.6 1.5 %collective-permute-start.2 = (bf16[2048,128]{1,0:T(8,128)(2,1)S(1)}, bf16[2048,128]{1,0:T(8,128)(2,1)S(1)}, u32[]{:S(2)}, u32[]{:S(2)}) collective-permute-start(bf16[2048,128]{1,0:T(8,128)(2,1)S(1)} %bitcast.10), channel_id=1, source_target_pairs={{0,2},{1,3},{2,4},{3,5},{4,6},{5,7},{6,0},{7,1},{8,10},{9,11},{10,... | collective-permute-start | bytes 1572872 | tf_op jit(solution)/shard_map/ppermute | solution.py:234
  71.1 1.7 %collective-permute-start.3 = (bf16[2048,128]{1,0:T(8,128)(2,1)S(1)}, bf16[2048,128]{1,0:T(8,128)(2,1)S(1)}, u32[]{:S(2)}, u32[]{:S(2)}) collective-permute-start(bf16[2048,128]{1,0:T(8,128)(2,1)S(1)} %bitcast.11), channel_id=1, source_target_pairs={{0,6},{1,7},{2,0},{3,1},{4,2},{5,3},{6,4},{7,5},{8,14},{9,15},{10,... | collective-permute-start | bytes 1572872 | tf_op jit(solution)/shard_map/ppermute | solution.py:234
  72.9 1.8 %collective-permute-start.8 = (bf16[2048,128]{1,0:T(8,128)(2,1)S(1)}, bf16[2048,128]{1,0:T(8,128)(2,1)S(1)}, u32[]{:S(2)}, u32[]{:S(2)}) collective-permute-start(bf16[2048,128]{1,0:T(8,128)(2,1)S(1)} %bitcast.12), channel_id=1, source_target_pairs={{0,4},{1,5},{2,6},{3,7},{4,0},{5,1},{6,2},{7,3},{8,12},{9,13},{10,... | collective-permute-start | bytes 1572872 | tf_op jit(solution)/shard_map/ppermute | solution.py:234
  74.7 5.0 %collective-permute-done.refs_0_.refs_1_ = bf16[2048,128]{1,0:T(8,128)(2,1)S(1)} collective-permute-done((bf16[2048,128]{1,0:T(8,128)(2,1)S(1)}, bf16[2048,128]{1,0:T(8,128)(2,1)S(1)}, u32[]{:S(2)}, u32[]{:S(2)}) %collective-permute-start) | collective-permute-done | bytes 524320 | tf_op jit(solution)/shard_map/ppermute | solution.py:237
  79.7 0.9 collective-permute-start.7
  80.6 4.2 %collective-permute-done.2.refs_2_.value_ref.refs_4_ = bf16[2048,128]{1,0:T(8,128)(2,1)S(1)} collective-permute-done((bf16[2048,128]{1,0:T(8,128)(2,1)S(1)}, bf16[2048,128]{1,0:T(8,128)(2,1)S(1)}, u32[]{:S(2)}, u32[]{:S(2)}) %collective-permute-start.2) | collective-permute-done | bytes 524320 | tf_op jit(solution)/shard_map/ppermute | solution.py:234
  84.7 8.1 %collective-permute-done.3.refs_3_.value_ref.refs_5_ = bf16[2048,128]{1,0:T(8,128)(2,1)S(1)} collective-permute-done((bf16[2048,128]{1,0:T(8,128)(2,1)S(1)}, bf16[2048,128]{1,0:T(8,128)(2,1)S(1)}, u32[]{:S(2)}, u32[]{:S(2)}) %collective-permute-start.3) | collective-permute-done | bytes 524320 | tf_op jit(solution)/shard_map/ppermute | solution.py:234
  93.1 0.6 collective-permute-start.5
  93.8 0.8 collective-permute-done.8.own
  94.6 0.4 collective-permute-done.6.refs_2_.refs_8_
  94.9 0.7 collective-permute-done.5.refs_1_.refs_7_
  95.7 0.7 collective-permute-done.4.refs_0_.refs_6_
  96.4 0.6 gram_side.1
  97.1 1.4 %gram_near.1 = (bf16[384,2048]{1,0:T(8,128)(2,1)S(1)}, bf16[3,384,256]{2,1,0:T(8,128)(2,1)S(1)}) custom-call(bf16[2048,128]{1,0:T(8,128)(2,1)S(1)} %bitcast.16, bf16[2048,128]{1,0:T(8,128)(2,1)S(1)} %collective-permute-done.refs_0_.refs_1_, bf16[2048,128]{1,0:T(8,128)(2,1)S(1)} %collective-permute-done.1.refs_1_.refs_2_, bf16[2048,128]{1,0:T(8,128)(2,1)S(1)} %bitcast.17, ...), custom_call_target="tpu_custom_call" | custom-call | flops 1207959552 | bytes 8388608 | tf_op jit(solution)/shard_map/gram_near/pallas_call | solution.py:136
  98.5 1.4 %gram_far.1 = bf16[8,512,128]{2,1,0:T(8,128)(2,1)S(1)} custom-call(s32[3]{0:T(128)S(1)} %pad_add_fusion.at, bf16[128,2048]{1,0:T(8,128)(2,1)S(1)} %get-tuple-element.9.last, bf16[3,128,256]{2,1,0:T(8,128)(2,1)S(1)} %get-tuple-element.10.side_ref, bf16[384,2048]{1,0:T(8,128)(2,1)S(1)} %get-tuple-element.11.left, ...), custom_call_target="tpu_custom_call" | custom-call | flops 536870912 | bytes 8388608 | tf_op jit(solution)/shard_map/gram_far/pallas_call | solution.py:193
  99.9 34.7 %all_to_all.11.parts_ref = bf16[8,512,128]{2,1,0:T(8,128)(2,1)S(1)} all-to-all(bf16[8,512,128]{2,1,0:T(8,128)(2,1)S(1)} %gram_far.1), channel_id=1, replica_groups={{0,32,72,104,144,176,216,248},{8,40,80,112,152,184,192,224},{16,48,88,1..., dimensions={0} | all-to-all | bytes 2097152 | tf_op jit(solution)/shard_map/all_to_all | solution.py:256
  134.6 0.9 finish.1
  (14 shorter events, 0.4 us)
Async XLA Ops:
  0.1 1.6 %copy-start = (bf16[2048,512]{1,0:T(8,128)(2,1)S(1)}, bf16[2048,512]{1,0:T(8,128)(2,1)}, u32[]{:S(2)}) copy-start(bf16[2048,512]{1,0:T(8,128)(2,1)} %param.3) | copy-start | bytes 6291460
  1.7 0.7 copy-start.1
  3.4 60.0 %copy-start.2 = (s32[128]{0:T(128)S(1)}, s32[128]{0:T(128)}, u32[]{:S(2)}) copy-start(s32[128]{0:T(128)} %picks_ref.1) | copy-start | bytes 1540
  66.3 13.3 %collective-permute-start = (bf16[2048,128]{1,0:T(8,128)(2,1)S(1)}, bf16[2048,128]{1,0:T(8,128)(2,1)S(1)}, u32[]{:S(2)}, u32[]{:S(2)}) collective-permute-start(bf16[2048,128]{1,0:T(8,128)(2,1)S(1)} %bitcast.8), channel_id=1, source_target_pairs={{0,64},{8,72},{16,80},{24,88},{32,96},{40,104},{48,112},{56,120},{... | collective-permute-start | bytes 1572872 | tf_op jit(solution)/shard_map/ppermute | solution.py:237
  67.0 13.6 %collective-permute-start.1 = (bf16[2048,128]{1,0:T(8,128)(2,1)S(1)}, bf16[2048,128]{1,0:T(8,128)(2,1)S(1)}, u32[]{:S(2)}, u32[]{:S(2)}) collective-permute-start(bf16[2048,128]{1,0:T(8,128)(2,1)S(1)} %bitcast.9), channel_id=1, source_target_pairs={{0,192},{8,200},{16,208},{24,216},{32,224},{40,232},{48,240},{56,2... | collective-permute-start | bytes 1572872 | tf_op jit(solution)/shard_map/ppermute | solution.py:237
  69.6 15.1 %collective-permute-start.2 = (bf16[2048,128]{1,0:T(8,128)(2,1)S(1)}, bf16[2048,128]{1,0:T(8,128)(2,1)S(1)}, u32[]{:S(2)}, u32[]{:S(2)}) collective-permute-start(bf16[2048,128]{1,0:T(8,128)(2,1)S(1)} %bitcast.10), channel_id=1, source_target_pairs={{0,2},{1,3},{2,4},{3,5},{4,6},{5,7},{6,0},{7,1},{8,10},{9,11},{10,... | collective-permute-start | bytes 1572872 | tf_op jit(solution)/shard_map/ppermute | solution.py:234
  71.1 21.7 %collective-permute-start.3 = (bf16[2048,128]{1,0:T(8,128)(2,1)S(1)}, bf16[2048,128]{1,0:T(8,128)(2,1)S(1)}, u32[]{:S(2)}, u32[]{:S(2)}) collective-permute-start(bf16[2048,128]{1,0:T(8,128)(2,1)S(1)} %bitcast.11), channel_id=1, source_target_pairs={{0,6},{1,7},{2,0},{3,1},{4,2},{5,3},{6,4},{7,5},{8,14},{9,15},{10,... | collective-permute-start | bytes 1572872 | tf_op jit(solution)/shard_map/ppermute | solution.py:234
  72.9 21.7 %collective-permute-start.8 = (bf16[2048,128]{1,0:T(8,128)(2,1)S(1)}, bf16[2048,128]{1,0:T(8,128)(2,1)S(1)}, u32[]{:S(2)}, u32[]{:S(2)}) collective-permute-start(bf16[2048,128]{1,0:T(8,128)(2,1)S(1)} %bitcast.12), channel_id=1, source_target_pairs={{0,4},{1,5},{2,6},{3,7},{4,0},{5,1},{6,2},{7,3},{8,12},{9,13},{10,... | collective-permute-start | bytes 1572872 | tf_op jit(solution)/shard_map/ppermute | solution.py:234
  79.7 14.9 %collective-permute-start.7 = (bf16[2048,128]{1,0:T(8,128)(2,1)S(1)}, bf16[2048,128]{1,0:T(8,128)(2,1)S(1)}, u32[]{:S(2)}, u32[]{:S(2)}) collective-permute-start(bf16[2048,128]{1,0:T(8,128)(2,1)S(1)} %bitcast.13), channel_id=1, source_target_pairs={{0,128},{8,136},{16,144},{24,152},{32,160},{40,168},{48,176},{56,1... | collective-permute-start | bytes 1572872 | tf_op jit(solution)/shard_map/ppermute | solution.py:237
  93.0 2.0 %collective-permute-start.6 = (bf16[2048,128]{1,0:T(8,128)(2,1)S(1)}, bf16[2048,128]{1,0:T(8,128)(2,1)S(1)}, u32[]{:S(2)}, u32[]{:S(2)}) collective-permute-start(bf16[2048,128]{1,0:T(8,128)(2,1)S(1)} %after.5), channel_id=1, source_target_pairs={{0,1},{1,0},{2,3},{3,2},{4,5},{5,4},{6,7},{7,6},{8,9},{9,8},{10,11... | collective-permute-start | bytes 1572872 | tf_op jit(solution)/shard_map/ppermute | solution.py:240
  93.1 2.6 %collective-permute-start.5 = (bf16[2048,128]{1,0:T(8,128)(2,1)S(1)}, bf16[2048,128]{1,0:T(8,128)(2,1)S(1)}, u32[]{:S(2)}, u32[]{:S(2)}) collective-permute-start(bf16[2048,128]{1,0:T(8,128)(2,1)S(1)} %after.4), channel_id=1, source_target_pairs={{0,1},{1,0},{2,3},{3,2},{4,5},{5,4},{6,7},{7,6},{8,9},{9,8},{10,11... | collective-permute-start | bytes 1572872 | tf_op jit(solution)/shard_map/ppermute | solution.py:240
  93.7 2.8 %collective-permute-start.4 = (bf16[2048,128]{1,0:T(8,128)(2,1)S(1)}, bf16[2048,128]{1,0:T(8,128)(2,1)S(1)}, u32[]{:S(2)}, u32[]{:S(2)}) collective-permute-start(bf16[2048,128]{1,0:T(8,128)(2,1)S(1)} %after.3.refs_0_), channel_id=1, source_target_pairs={{0,1},{1,0},{2,3},{3,2},{4,5},{5,4},{6,7},{7,6},{8,9},{9,8},{10,11... | collective-permute-start | bytes 1572872 | tf_op jit(solution)/shard_map/ppermute | solution.py:240
  94.6 4.0 %collective-permute-start.9 = (bf16[2048,128]{1,0:T(8,128)(2,1)S(1)}, bf16[2048,128]{1,0:T(8,128)(2,1)S(1)}, u32[]{:S(2)}, u32[]{:S(2)}) collective-permute-start(bf16[2048,128]{1,0:T(8,128)(2,1)S(1)} %collective-permute-done.8.own), channel_id=1, source_target_pairs={{0,1},{1,0},{2,3},{3,2},{4,5},{5,4},{6,7},{7,6},{8,9},{9,8},{10,11... | collective-permute-start | bytes 1572872 | tf_op jit(solution)/shard_map/ppermute | solution.py:240

commit v7 on v6

--- a/solution.py
+++ b/solution.py
@@ -98,20 +98,26 @@
 NEAR = (0, 1, 3)
 
 
-def after_kernel(value_ref, *refs):
-    refs[-1][...] = value_ref[...]
-
-
-def after(value, *others):
-    return pl.pallas_call(
-        after_kernel,
-        in_specs=[LOCAL] * (1 + len(others)),
-        out_specs=LOCAL,
-        out_shape=jax.ShapeDtypeStruct(value.shape, value.dtype),
-        compiler_params=pltpu.CompilerParams(vmem_limit_bytes=16 * MIB),
-        cost_estimate=pl.CostEstimate(flops=0, bytes_accessed=MIB, transcendentals=0),
-        name="after",
-    )(value, *others)
+def share_kernel(own, x_up, x_down, y_up, y_down, joined, *halves):
+    for j, piece in enumerate((own, x_up, x_down)):
+        joined[j] = piece[...]
+    half = halves[0].shape[0]
+    for i, piece in enumerate((x_up, x_down, y_up, y_down)):
+        halves[i][...] = piece[pl.ds(i % 2 * half, half), :]
+
+
+def share(own, x_up, x_down, y_up, y_down):
+    rows, width = own.shape
+    half = jax.ShapeDtypeStruct((rows // 2, width), own.dtype)
+    return pl.pallas_call(
+        share_kernel,
+        in_specs=[LOCAL] * 5,
+        out_specs=[LOCAL] * 5,
+        out_shape=[jax.ShapeDtypeStruct((len(NEAR), rows, width), own.dtype)] + [half] * 4,
+        compiler_params=pltpu.CompilerParams(vmem_limit_bytes=16 * MIB),
+        cost_estimate=pl.CostEstimate(flops=0, bytes_accessed=2 * MIB, transcendentals=0),
+        name="share",
+    )(own, x_up, x_down, y_up, y_down)
 
 
 def pair_dot(left, own, other):
@@ -119,11 +125,11 @@
 
 
 def near_kernel(*refs):
-    cols, own, other, (left, out_ref) = refs[:3], refs[3:6], refs[6:9], refs[9:]
+    cols, own, (other, left, out_ref) = refs[:3], refs[3:6], refs[6:]
     for j in range(len(NEAR)):
         left[pl.ds(j * LANES, LANES), :] = cols[j][...].T
     for j in range(len(NEAR)):
-        out_ref[j] = pair_dot(left[...], own[j][...], other[j][...]).astype(out_ref.dtype)
+        out_ref[j] = pair_dot(left[...], own[j][...], other[j]).astype(out_ref.dtype)
 
 
 def cost(depth, blocks):
@@ -135,7 +141,7 @@
     depth, near = cols[0].shape[0], len(NEAR)
     return pl.pallas_call(
         near_kernel,
-        in_specs=[LOCAL] * 9,
+        in_specs=[LOCAL] * 7,
         out_specs=[LOCAL] * 2,
         out_shape=[
             jax.ShapeDtypeStruct((near * LANES, depth), jnp.bfloat16),
@@ -144,21 +150,21 @@
         compiler_params=pltpu.CompilerParams(vmem_limit_bytes=16 * MIB),
         cost_estimate=cost(depth, near * near),
         name="gram_near",
-    )(*cols, *own, *other)
+    )(*cols, *own, other)
 
 
 def side_kernel(*refs):
-    other, own, col, (last, out_ref) = refs[:3], refs[3:6], refs[6], refs[7:]
+    other, own, (col, last, out_ref) = refs[0], refs[1:4], refs[4:]
     last[...] = col[...].T
     for j in range(len(NEAR)):
-        out_ref[j] = pair_dot(last[...], own[j][...], other[j][...]).astype(out_ref.dtype)
+        out_ref[j] = pair_dot(last[...], own[j][...], other[j]).astype(out_ref.dtype)
 
 
 def gram_side(col, own, other):
     depth, near = col.shape[0], len(NEAR)
     return pl.pallas_call(
         side_kernel,
-        in_specs=[LOCAL] * 7,
+        in_specs=[LOCAL] * 5,
         out_specs=[LOCAL] * 2,
         out_shape=[
             jax.ShapeDtypeStruct((LANES, depth), jnp.bfloat16),
@@ -167,7 +173,7 @@
         compiler_params=pltpu.CompilerParams(vmem_limit_bytes=16 * MIB),
         cost_estimate=cost(depth, near),
         name="gram_side",
-    )(*other, *own, col)
+    )(other, *own, col)
 
 
 def far_kernel(at, last, side_ref, left, near_ref, own, other, out_ref):
@@ -241,10 +247,10 @@
 
     x_up, x_down = along_x(sketch, 1), along_x(sketch, -1)
     y_up, y_down = along_y(sketch, 1), along_y(sketch, -1)
-    x_far, y_far = along_x(sketch, 2), along_y(sketch, 2)
-    own = (sketch, x_up, x_down)
-    gate = after(sketch, y_up, y_down, x_up, x_down)
-    other = (swap(gate), swap(after(x_up, gate)), swap(after(x_down, gate)))
+    joined, x_low, x_high, y_low, y_high = share(sketch, x_up, x_down, y_up, y_down)
+    x_far = jnp.concatenate([along_x(x_low, 1), along_x(x_high, -1)])
+    y_far = jnp.concatenate([along_y(y_low, 1), along_y(y_high, -1)])
+    own, other = (sketch, x_up, x_down), swap(joined)
     last, side = gram_side(y_far, own, other)
     left, near = gram_near((sketch, y_up, y_down), own, other)
     partial = gram_far(at, last, side, left, near, x_far, swap(x_far))

time: 137 us -> 136 us (level)
  starting transfers between devices: 10 us -> 13 us
  blocking collectives: 94.7 us -> 92.4 us
  waiting for transfers between devices: 19.9 us -> 18.3 us
    ppermute x3 -> x4, waiting for transfers between devices: 4.97 us -> 7.85 us  [along_y(): lax.ppermute(value, 'dp', [(i, (i + NZ * step) % (NY * NZ)) for i in rang...]
    ppermute x3 -> x4, waiting for transfers between devices: 13.1 us -> 10.4 us  [along_x(): lax.ppermute(value, 'col', [(i, (i + NCORE * step) % (NX * NCORE)) for i...]
    all_to_all x1, blocking collectives: 34.7 us -> 32.4 us  [on_device(): lax.all_to_all(partial, 'dp', split_axis=0, concat_axis=0, axis_index_gro...]
    ppermute x3 -> x4, starting transfers between devices: 4.22 us -> 6.19 us  [along_y(): lax.ppermute(value, 'dp', [(i, (i + NZ * step) % (NY * NZ)) for i in rang...]
    ppermute x4 -> x2, waiting for transfers between devices: 1.88 us -> 0.01 us  [swap(): return lax.ppermute(value, 'col', [(i, i ^ 1) for i in range(NX * NCORE)])]
    ppermute x3 -> x4, starting transfers between devices: 5.05 us -> 6.63 us  [along_x(): lax.ppermute(value, 'col', [(i, (i + NCORE * step) % (NX * NCORE)) for i...]
  transfers between devices with their start and end apart: 10 -> 10, of which waited for: 7 -> 5; matrix products, arithmetic and copies ran while one was open for 0% -> 0% of each run, Pallas kernels for 2% -> 2%
where the time goes in v7:
time: 136 us; the launch traced here: 135 us
  blocking collectives  92.4 us (68%)
  waiting for transfers between devices  18.3 us (13%)
  starting transfers between devices  13 us (10%)
  Pallas kernels  8.45 us (6%)
  local copies, waits for them, and re-layouts  2.35 us (2%)
    all_to_all x1, blocking collectives, on_device(): lax.all_to_all(outgoing, 'dp', split_axis=0, concat_axis=0, tiled=True)  60 us
    all_to_all x1, blocking collectives, on_device(): lax.all_to_all(partial, 'dp', split_axis=0, concat_axis=0, axis_index_gro...  32.4 us
    ppermute x4, waiting for transfers between devices, along_x(): lax.ppermute(value, 'col', [(i, (i + NCORE * step) % (NX * NCORE)) for i...  10.4 us
    ppermute x4, waiting for transfers between devices, along_y(): lax.ppermute(value, 'dp', [(i, (i + NZ * step) % (NY * NZ)) for i in rang...  7.85 us
    ppermute x4, starting transfers between devices, along_x(): lax.ppermute(value, 'col', [(i, (i + NCORE * step) % (NX * NCORE)) for i...  6.63 us
    ppermute x4, starting transfers between devices, along_y(): lax.ppermute(value, 'dp', [(i, (i + NZ * step) % (NY * NZ)) for i in rang...  6.19 us
    pallas_call x1, Pallas kernels, mix(): pl.pallas_call(mix_kernel, in_specs=[SCALARS, LOCAL], out_specs=LOCAL, sc...  2.94 us
  transfers between devices with their start and end apart: 10, of which 5 were waited for; matrix products, arithmetic and copies ran while one was open for 0% of the time, Pallas kernels for 2%

profile of v7, /device:TPU:64, one launch (start us, length us, event | category | flops | bytes accessed | tf_op | source)
XLA Modules:
  0.0 134.7 jit_solution(4982392568496827936)
XLA Ops:
  0.1 1.6 %copy-done = bf16[2048,512]{1,0:T(8,128)(2,1)S(1)} copy-done((bf16[2048,512]{1,0:T(8,128)(2,1)S(1)}, bf16[2048,512]{1,0:T(8,128)(2,1)}, u32[]{:S(2)}) %copy-start) | copy-done | bytes 2097176
  1.7 0.7 copy-done.1
  2.4 1.0 pack.1
  3.4 60.0 %all_to_all.10 = bf16[32,16,16,128]{3,2,1,0:T(8,128)(2,1)S(1)} all-to-all(bf16[32,16,16,128]{3,2,1,0:T(8,128)(2,1)S(1)} %bitcast.17), channel_id=1, replica_groups=mesh['dp'=32,'col'=8] {'dp'}, dimensions={0} | all-to-all | bytes 4194304 | tf_op jit(solution)/shard_map/all_to_all | solution.py:236
  63.4 2.9 %mix.1 = bf16[128,16,128]{2,1,0:T(8,128)(2,1)S(1)} custom-call(s32[128]{0:T(128)S(1)} %copy-done.2, bf16[512,16,128]{2,1,0:T(8,128)(2,1)S(1)} %bitcast.16), custom_call_target="tpu_custom_call" | custom-call | tf_op jit(solution)/shard_map/mix/pallas_call | solution.py:87
  66.3 1.6 %collective-permute-start = (bf16[2048,128]{1,0:T(8,128)(2,1)S(1)}, bf16[2048,128]{1,0:T(8,128)(2,1)S(1)}, u32[]{:S(2)}, u32[]{:S(2)}) collective-permute-start(bf16[2048,128]{1,0:T(8,128)(2,1)S(1)} %bitcast.8), channel_id=1, source_target_pairs={{0,2},{1,3},{2,4},{3,5},{4,6},{5,7},{6,0},{7,1},{8,10},{9,11},{10,... | collective-permute-start | bytes 1572872 | tf_op jit(solution)/shard_map/ppermute | solution.py:240
  67.9 1.7 %collective-permute-start.1 = (bf16[2048,128]{1,0:T(8,128)(2,1)S(1)}, bf16[2048,128]{1,0:T(8,128)(2,1)S(1)}, u32[]{:S(2)}, u32[]{:S(2)}) collective-permute-start(bf16[2048,128]{1,0:T(8,128)(2,1)S(1)} %bitcast.9), channel_id=1, source_target_pairs={{0,6},{1,7},{2,0},{3,1},{4,2},{5,3},{6,4},{7,5},{8,14},{9,15},{10,... | collective-permute-start | bytes 1572872 | tf_op jit(solution)/shard_map/ppermute | solution.py:240
  69.6 0.6 collective-permute-start.2
  70.2 2.7 %collective-permute-start.3 = (bf16[2048,128]{1,0:T(8,128)(2,1)S(1)}, bf16[2048,128]{1,0:T(8,128)(2,1)S(1)}, u32[]{:S(2)}, u32[]{:S(2)}) collective-permute-start(bf16[2048,128]{1,0:T(8,128)(2,1)S(1)} %bitcast.11), channel_id=1, source_target_pairs={{0,192},{8,200},{16,208},{24,216},{32,224},{40,232},{48,240},{56,2... | collective-permute-start | bytes 1572872 | tf_op jit(solution)/shard_map/ppermute | solution.py:243
  72.9 6.8 %collective-permute-done.x_up.refs_2_.refs_4_ = bf16[2048,128]{1,0:T(8,128)(2,1)S(1)} collective-permute-done((bf16[2048,128]{1,0:T(8,128)(2,1)S(1)}, bf16[2048,128]{1,0:T(8,128)(2,1)S(1)}, u32[]{:S(2)}, u32[]{:S(2)}) %collective-permute-start) | collective-permute-done | bytes 524320 | tf_op jit(solution)/shard_map/ppermute | solution.py:240
  79.7 2.7 %collective-permute-done.2.y_up.refs_1_ = bf16[2048,128]{1,0:T(8,128)(2,1)S(1)} collective-permute-done((bf16[2048,128]{1,0:T(8,128)(2,1)S(1)}, bf16[2048,128]{1,0:T(8,128)(2,1)S(1)}, u32[]{:S(2)}, u32[]{:S(2)}) %collective-permute-start.2) | collective-permute-done | bytes 524320 | tf_op jit(solution)/shard_map/ppermute | solution.py:243
  82.3 0.2 share.1
  82.5 0.1 collective-permute-start.4
  82.6 0.4 collective-permute-start.7
  83.0 3.0 %collective-permute-start.8 = (bf16[1024,128]{1,0:T(8,128)(2,1)S(1)}, bf16[1024,128]{1,0:T(8,128)(2,1)S(1)}, u32[]{:S(2)}, u32[]{:S(2)}) collective-permute-start(bf16[1024,128]{1,0:T(8,128)(2,1)S(1)} %get-tuple-element.22), channel_id=1, source_target_pairs={{0,6},{1,7},{2,0},{3,1},{4,2},{5,3},{6,4},{7,5},{8,14},{9,15},{10,... | collective-permute-start | bytes 786440 | tf_op jit(solution)/shard_map/ppermute | solution.py:240
  85.9 3.0 %collective-permute-start.6 = (bf16[1024,128]{1,0:T(8,128)(2,1)S(1)}, bf16[1024,128]{1,0:T(8,128)(2,1)S(1)}, u32[]{:S(2)}, u32[]{:S(2)}) collective-permute-start(bf16[1024,128]{1,0:T(8,128)(2,1)S(1)} %get-tuple-element.16), channel_id=1, source_target_pairs={{0,192},{8,200},{16,208},{24,216},{32,224},{40,232},{48,240},{56,2... | collective-permute-start | bytes 786440 | tf_op jit(solution)/shard_map/ppermute | solution.py:243
  88.9 3.7 %collective-permute-done.7 = bf16[1024,128]{1,0:T(8,128)(2,1)S(1)} collective-permute-done((bf16[1024,128]{1,0:T(8,128)(2,1)S(1)}, bf16[1024,128]{1,0:T(8,128)(2,1)S(1)}, u32[]{:S(2)}, u32[]{:S(2)}) %collective-permute-start.7) | collective-permute-done | bytes 262176 | tf_op jit(solution)/shard_map/ppermute | solution.py:240
  92.7 1.8 %collective-permute-done.6 = bf16[1024,128]{1,0:T(8,128)(2,1)S(1)} collective-permute-done((bf16[1024,128]{1,0:T(8,128)(2,1)S(1)}, bf16[1024,128]{1,0:T(8,128)(2,1)S(1)}, u32[]{:S(2)}, u32[]{:S(2)}) %collective-permute-start.6) | collective-permute-done | bytes 262176 | tf_op jit(solution)/shard_map/ppermute | solution.py:243
  94.5 3.4 %collective-permute-done.5 = bf16[1024,128]{1,0:T(8,128)(2,1)S(1)} collective-permute-done((bf16[1024,128]{1,0:T(8,128)(2,1)S(1)}, bf16[1024,128]{1,0:T(8,128)(2,1)S(1)}, u32[]{:S(2)}, u32[]{:S(2)}) %collective-permute-start.5) | collective-permute-done | bytes 262176 | tf_op jit(solution)/shard_map/ppermute | solution.py:243
  98.0 0.6 gram_side.1
  98.6 1.4 %gram_near.1 = (bf16[384,2048]{1,0:T(8,128)(2,1)S(1)}, bf16[3,384,256]{2,1,0:T(8,128)(2,1)S(1)}) custom-call(bf16[2048,128]{1,0:T(8,128)(2,1)S(1)} %bitcast.14, bf16[2048,128]{1,0:T(8,128)(2,1)S(1)} %collective-permute-done.2.y_up.refs_1_, bf16[2048,128]{1,0:T(8,128)(2,1)S(1)} %collective-permute-done.3.y_down.refs_2_, bf16[2048,128]{1,0:T(8,128)(2,1)S(1)} %bitcast.15, ...), custom_call_target="tpu_custom_call" | custom-call | flops 1207959552 | bytes 8388608 | tf_op jit(solution)/shard_map/gram_near/pallas_call | solution.py:142
  100.0 1.4 %gram_far.1 = bf16[8,512,128]{2,1,0:T(8,128)(2,1)S(1)} custom-call(s32[3]{0:T(128)S(1)} %pad_add_fusion.at, bf16[128,2048]{1,0:T(8,128)(2,1)S(1)} %get-tuple-element.17.last, bf16[3,128,256]{2,1,0:T(8,128)(2,1)S(1)} %get-tuple-element.18.side_ref, bf16[384,2048]{1,0:T(8,128)(2,1)S(1)} %get-tuple-element.19.left, ...), custom_call_target="tpu_custom_call" | custom-call | flops 536870912 | bytes 8388608 | tf_op jit(solution)/shard_map/gram_far/pallas_call | solution.py:199
  101.4 32.4 %all_to_all.11.parts_ref = bf16[8,512,128]{2,1,0:T(8,128)(2,1)S(1)} all-to-all(bf16[8,512,128]{2,1,0:T(8,128)(2,1)S(1)} %gram_far.1), channel_id=1, replica_groups={{0,32,72,104,144,176,216,248},{8,40,80,112,152,184,192,224},{16,48,88,1..., dimensions={0} | all-to-all | bytes 2097152 | tf_op jit(solution)/shard_map/all_to_all | solution.py:262
  133.8 0.9 finish.1
  (15 shorter events, 0.3 us)
Async XLA Ops:
  0.1 1.6 %copy-start = (bf16[2048,512]{1,0:T(8,128)(2,1)S(1)}, bf16[2048,512]{1,0:T(8,128)(2,1)}, u32[]{:S(2)}) copy-start(bf16[2048,512]{1,0:T(8,128)(2,1)} %param.3) | copy-start | bytes 6291460
  1.7 0.7 copy-start.1
  3.4 60.0 %copy-start.2 = (s32[128]{0:T(128)S(1)}, s32[128]{0:T(128)}, u32[]{:S(2)}) copy-start(s32[128]{0:T(128)} %picks_ref.1) | copy-start | bytes 1540
  66.3 13.3 %collective-permute-start = (bf16[2048,128]{1,0:T(8,128)(2,1)S(1)}, bf16[2048,128]{1,0:T(8,128)(2,1)S(1)}, u32[]{:S(2)}, u32[]{:S(2)}) collective-permute-start(bf16[2048,128]{1,0:T(8,128)(2,1)S(1)} %bitcast.8), channel_id=1, source_target_pairs={{0,2},{1,3},{2,4},{3,5},{4,6},{5,7},{6,0},{7,1},{8,10},{9,11},{10,... | collective-permute-start | bytes 1572872 | tf_op jit(solution)/shard_map/ppermute | solution.py:240
  67.9 11.8 %collective-permute-start.1 = (bf16[2048,128]{1,0:T(8,128)(2,1)S(1)}, bf16[2048,128]{1,0:T(8,128)(2,1)S(1)}, u32[]{:S(2)}, u32[]{:S(2)}) collective-permute-start(bf16[2048,128]{1,0:T(8,128)(2,1)S(1)} %bitcast.9), channel_id=1, source_target_pairs={{0,6},{1,7},{2,0},{3,1},{4,2},{5,3},{6,4},{7,5},{8,14},{9,15},{10,... | collective-permute-start | bytes 1572872 | tf_op jit(solution)/shard_map/ppermute | solution.py:240
  69.6 12.7 %collective-permute-start.2 = (bf16[2048,128]{1,0:T(8,128)(2,1)S(1)}, bf16[2048,128]{1,0:T(8,128)(2,1)S(1)}, u32[]{:S(2)}, u32[]{:S(2)}) collective-permute-start(bf16[2048,128]{1,0:T(8,128)(2,1)S(1)} %bitcast.10), channel_id=1, source_target_pairs={{0,64},{8,72},{16,80},{24,88},{32,96},{40,104},{48,112},{56,120},{... | collective-permute-start | bytes 1572872 | tf_op jit(solution)/shard_map/ppermute | solution.py:243
  70.2 12.1 %collective-permute-start.3 = (bf16[2048,128]{1,0:T(8,128)(2,1)S(1)}, bf16[2048,128]{1,0:T(8,128)(2,1)S(1)}, u32[]{:S(2)}, u32[]{:S(2)}) collective-permute-start(bf16[2048,128]{1,0:T(8,128)(2,1)S(1)} %bitcast.11), channel_id=1, source_target_pairs={{0,192},{8,200},{16,208},{24,216},{32,224},{40,232},{48,240},{56,2... | collective-permute-start | bytes 1572872 | tf_op jit(solution)/shard_map/ppermute | solution.py:243
  82.5 15.4 %collective-permute-start.4 = (bf16[3,2048,128]{2,1,0:T(8,128)(2,1)S(1)}, bf16[3,2048,128]{2,1,0:T(8,128)(2,1)S(1)}, u32[]{:S(2)}, u32[]{:S(2)}) collective-permute-start(bf16[3,2048,128]{2,1,0:T(8,128)(2,1)S(1)} %get-tuple-element.14), channel_id=1, source_target_pairs={{0,1},{1,0},{2,3},{3,2},{4,5},{5,4},{6,7},{7,6},{8,9},{9,8},{10,11... | collective-permute-start | bytes 4718600 | tf_op jit(solution)/shard_map/ppermute | solution.py:246
  82.6 9.9 %collective-permute-start.7 = (bf16[1024,128]{1,0:T(8,128)(2,1)S(1)}, bf16[1024,128]{1,0:T(8,128)(2,1)S(1)}, u32[]{:S(2)}, u32[]{:S(2)}) collective-permute-start(bf16[1024,128]{1,0:T(8,128)(2,1)S(1)} %get-tuple-element.21), channel_id=1, source_target_pairs={{0,2},{1,3},{2,4},{3,5},{4,6},{5,7},{6,0},{7,1},{8,10},{9,11},{10,... | collective-permute-start | bytes 786440 | tf_op jit(solution)/shard_map/ppermute | solution.py:240
  83.0 9.6 %collective-permute-start.8 = (bf16[1024,128]{1,0:T(8,128)(2,1)S(1)}, bf16[1024,128]{1,0:T(8,128)(2,1)S(1)}, u32[]{:S(2)}, u32[]{:S(2)}) collective-permute-start(bf16[1024,128]{1,0:T(8,128)(2,1)S(1)} %get-tuple-element.22), channel_id=1, source_target_pairs={{0,6},{1,7},{2,0},{3,1},{4,2},{5,3},{6,4},{7,5},{8,14},{9,15},{10,... | collective-permute-start | bytes 786440 | tf_op jit(solution)/shard_map/ppermute | solution.py:240
  85.9 8.6 %collective-permute-start.6 = (bf16[1024,128]{1,0:T(8,128)(2,1)S(1)}, bf16[1024,128]{1,0:T(8,128)(2,1)S(1)}, u32[]{:S(2)}, u32[]{:S(2)}) collective-permute-start(bf16[1024,128]{1,0:T(8,128)(2,1)S(1)} %get-tuple-element.16), channel_id=1, source_target_pairs={{0,192},{8,200},{16,208},{24,216},{32,224},{40,232},{48,240},{56,2... | collective-permute-start | bytes 786440 | tf_op jit(solution)/shard_map/ppermute | solution.py:243
  88.9 9.0 %collective-permute-start.5 = (bf16[1024,128]{1,0:T(8,128)(2,1)S(1)}, bf16[1024,128]{1,0:T(8,128)(2,1)S(1)}, u32[]{:S(2)}, u32[]{:S(2)}) collective-permute-start(bf16[1024,128]{1,0:T(8,128)(2,1)S(1)} %get-tuple-element.15), channel_id=1, source_target_pairs={{0,64},{8,72},{16,80},{24,88},{32,96},{40,104},{48,112},{56,120},{... | collective-permute-start | bytes 786440 | tf_op jit(solution)/shard_map/ppermute | solution.py:243
  92.6 7.4 %collective-permute-start.9 = (bf16[2048,128]{1,0:T(8,128)(2,1)S(1)}, bf16[2048,128]{1,0:T(8,128)(2,1)S(1)}, u32[]{:S(2)}, u32[]{:S(2)}) collective-permute-start(bf16[2048,128]{1,0:T(8,128)(2,1)S(1)} %constant_dynamic-update-slice_fusion.own), channel_id=1, source_target_pairs={{0,1},{1,0},{2,3},{3,2},{4,5},{5,4},{6,7},{7,6},{8,9},{9,8},{10,11... | collective-permute-start | bytes 1572872 | tf_op jit(solution)/shard_map/ppermute | solution.py:246

commit v8 on v5

--- a/solution.py
+++ b/solution.py
@@ -61,16 +61,11 @@
 def mix_kernel(picks_ref, raw_ref, out_ref, work):
     half = N_BLOCKS // 2
 
-    @pl.loop(0, N_BLOCKS // 16, unroll=2)
-    def _(d):
-        base = d * 16
+    for base in range(0, N_BLOCKS, 16):
         parts = [raw_ref[base + b].astype(jnp.float32) for b in range(16)]
         for b, part in enumerate(hadamard(parts)):
             work[base + b] = part
-
-    @pl.loop(0, 32, unroll=2)
-    def _(i):
-        base = lax.div(i, 16) * half + lax.rem(i, 16)
+    for base in [*range(16), *range(half, half + 16)]:
         parts = [work[base + 16 * e] for e in range(16)]
         for e, part in enumerate(hadamard(parts)):
             work[base + 16 * e] = part
@@ -95,39 +90,43 @@
     )(picks, raw)
 
 
-NEAR = (0, 1, 3)
-
-
-def halves_kernel(*refs):
-    pieces, outs = refs[:4], refs[4:]
-    depth = outs[0].shape[0]
-    for i, out in enumerate(outs):
-        out[...] = pieces[i][pl.ds(i % 2 * depth, depth), :]
-
-
-def halves(*pieces):
-    part = jax.ShapeDtypeStruct((pieces[0].shape[0] // 2, LANES), pieces[0].dtype)
-    return pl.pallas_call(
-        halves_kernel,
-        in_specs=[LOCAL] * 4,
-        out_specs=[LOCAL] * 4,
-        out_shape=[part] * 4,
+NEAR = 3
+
+
+def share_kernel(near_x, near_y, joined, far_x, far_y):
+    joined[0], joined[1], joined[2] = near_x[0], near_x[1], near_y[1]
+    far_x[...] = near_x[0]
+    far_y[...] = near_y[0]
+
+
+def share(near_x, near_y):
+    _, rows, width = near_x.shape
+    piece = jax.ShapeDtypeStruct((rows, width), near_x.dtype)
+    return pl.pallas_call(
+        share_kernel,
+        in_specs=[LOCAL] * 2,
+        out_specs=[LOCAL] * 3,
+        out_shape=[jax.ShapeDtypeStruct((3, rows, width), near_x.dtype), piece, piece],
         compiler_params=pltpu.CompilerParams(vmem_limit_bytes=16 * MIB),
         cost_estimate=pl.CostEstimate(flops=0, bytes_accessed=2 * MIB, transcendentals=0),
-        name="halves",
-    )(*pieces)
+        name="share",
+    )(near_x, near_y)
 
 
 def pair_dot(left, own, other):
-    return jnp.dot(left, jnp.concatenate([own, other], axis=1), preferred_element_type=jnp.float32)
-
-
-def near_kernel(*refs):
-    cols, own, other, (left, out_ref) = refs[:3], refs[3:6], refs[6:9], refs[9:]
-    for j in range(len(NEAR)):
-        left[pl.ds(j * LANES, LANES), :] = cols[j][...].T
-    for j in range(len(NEAR)):
-        out_ref[j] = pair_dot(left[...], own[j][...], other[j][...]).astype(out_ref.dtype)
+    pair = jnp.concatenate([own, other], axis=1)
+    return jnp.dot(left, pair, preferred_element_type=jnp.float32).astype(jnp.bfloat16)
+
+
+def row_pairs(home, near_x, swapped):
+    return (home[0], home[1]), (near_x[0], near_x[1]), (swapped[1], swapped[0])
+
+
+def near_kernel(home, near_x, near_y, swapped, left, out_ref):
+    for j, col in enumerate((home[0], near_y[0], swapped[2])):
+        left[pl.ds(j * LANES, LANES), :] = col.T
+    for j, pair in enumerate(row_pairs(home, near_x, swapped)):
+        out_ref[j] = pair_dot(left[...], *pair)
 
 
 def cost(depth, blocks):
@@ -135,47 +134,47 @@
     return pl.CostEstimate(flops=flops, bytes_accessed=8 * MIB, transcendentals=0)
 
 
-def gram_near(cols, own, other):
-    depth, near = cols[0].shape[0], len(NEAR)
+def gram_near(home, near_x, near_y, swapped):
+    depth = home.shape[1]
     return pl.pallas_call(
         near_kernel,
-        in_specs=[LOCAL] * 9,
+        in_specs=[LOCAL] * 4,
         out_specs=[LOCAL] * 2,
         out_shape=[
-            jax.ShapeDtypeStruct((near * LANES, depth), jnp.bfloat16),
-            jax.ShapeDtypeStruct((near, near * LANES, NCORE * LANES), jnp.bfloat16),
+            jax.ShapeDtypeStruct((NEAR * LANES, depth), jnp.bfloat16),
+            jax.ShapeDtypeStruct((NEAR, NEAR * LANES, NCORE * LANES), jnp.bfloat16),
         ],
         compiler_params=pltpu.CompilerParams(vmem_limit_bytes=16 * MIB),
-        cost_estimate=cost(depth, near * near),
+        cost_estimate=cost(depth, NEAR * NEAR),
         name="gram_near",
-    )(*cols, *own, *other)
-
-
-def side_kernel(*refs):
-    col, own, other, (last, out_ref) = refs[0], refs[1:4], refs[4:7], refs[7:]
+    )(home, near_x, near_y, swapped)
+
+
+def side_kernel(col, home, near_x, swapped, last, out_ref):
     last[...] = col[...].T
-    for j in range(len(NEAR)):
-        out_ref[j] = pair_dot(last[...], own[j][...], other[j][...]).astype(out_ref.dtype)
-
-
-def gram_side(col, own, other):
-    depth, near = col.shape[0], len(NEAR)
+    for j, pair in enumerate(row_pairs(home, near_x, swapped)):
+        out_ref[j] = pair_dot(last[...], *pair)
+
+
+def gram_side(col, home, near_x, swapped):
+    depth = col.shape[0]
     return pl.pallas_call(
         side_kernel,
-        in_specs=[LOCAL] * 7,
+        in_specs=[LOCAL] * 4,
         out_specs=[LOCAL] * 2,
         out_shape=[
             jax.ShapeDtypeStruct((LANES, depth), jnp.bfloat16),
-            jax.ShapeDtypeStruct((near, LANES, NCORE * LANES), jnp.bfloat16),
+            jax.ShapeDtypeStruct((NEAR, LANES, NCORE * LANES), jnp.bfloat16),
         ],
         compiler_params=pltpu.CompilerParams(vmem_limit_bytes=16 * MIB),
-        cost_estimate=cost(depth, near),
+        cost_estimate=cost(depth, NEAR),
         name="gram_side",
-    )(col, *own, *other)
+    )(col, home, near_x, swapped)
 
 
 def far_kernel(at, near_ref, side_ref, left, last, own, other, out_ref):
     x, core, turn = at[0], at[1], at[2]
+    steps = (0, 1 + 2 * core, 3 - 2 * core)
 
     def put(step_x, step_y, block):
         panel = lax.rem(x + NX - step_x, NX) * NCORE
@@ -183,13 +182,13 @@
         out_ref[panel + core, pl.ds(quarter, LANES), :] = block[:, :LANES]
         out_ref[panel + 1 - core, pl.ds(quarter, LANES), :] = block[:, LANES:]
 
-    block = pair_dot(left[...], own[...], other[...]).astype(out_ref.dtype)
-    for j, step in enumerate(NEAR):
+    block = pair_dot(left[...], own[...], other[...])
+    for j, step in enumerate(steps):
         put(2, step, block[j * LANES : (j + 1) * LANES])
-    put(2, 2, pair_dot(last[...], own[...], other[...]).astype(out_ref.dtype))
-    for i, step_x in enumerate(NEAR):
+    put(2, 2, pair_dot(last[...], own[...], other[...]))
+    for i, step_x in enumerate(steps):
         put(step_x, 2, side_ref[i])
-        for j, step_y in enumerate(NEAR):
+        for j, step_y in enumerate(steps):
             put(step_x, step_y, near_ref[i, pl.ds(j * LANES, LANES), :])
 
 
@@ -234,25 +233,29 @@
     raw = lax.all_to_all(outgoing, "dp", split_axis=0, concat_axis=0, tiled=True)
     sketch = mix(raw.reshape(N_BLOCKS, CHUNK, LANES), picks).reshape(-1, LANES)
 
-    def along_x(value, step):
-        return lax.ppermute(value, "col", [(i, (i + NCORE * step) % (NX * NCORE)) for i in range(NX * NCORE)])
-
-    def along_y(value, step):
-        return lax.ppermute(value, "dp", [(i, (i + NZ * step) % (NY * NZ)) for i in range(NY * NZ)])
+    def ring(value, axis):
+        pairs = []
+        for i in range(NY * NZ * NX * NCORE):
+            (here, rest), down = divmod(i, NZ * NX * NCORE), i % NCORE
+            step = 1 - 2 * down
+            if axis == "y":
+                to = (here + step) % NY * NZ * NX * NCORE + rest
+            else:
+                side = (i // NCORE % NX + step) % NX
+                to = i // (NX * NCORE) * (NX * NCORE) + side * NCORE + down
+            pairs.append((i, to))
+        return lax.ppermute(value, ("dp", "col"), pairs)
 
     def swap(value):
         return lax.ppermute(value, "col", [(i, i ^ 1) for i in range(NX * NCORE)])
 
-    x_up, x_down = along_x(sketch, 1), along_x(sketch, -1)
-    y_up, y_down = along_y(sketch, 1), along_y(sketch, -1)
-    x_low, x_high, y_low, y_high = halves(x_up, x_down, y_up, y_down)
-    x_far = jnp.concatenate([along_x(x_low, 1), along_x(x_high, -1)])
-    y_far = jnp.concatenate([along_y(y_low, 1), along_y(y_high, -1)])
-    own = (sketch, x_up, x_down)
-    other = tuple(swap(piece) for piece in own)
-    left, near = gram_near((sketch, y_up, y_down), own, other)
-    last, side = gram_side(y_far, own, other)
-    partial = gram_far(at, near, side, left, last, x_far, swap(x_far))
+    home = jnp.stack([sketch, swap(sketch)])
+    near_x, near_y = ring(home, "x"), ring(home, "y")
+    joined, far_x, far_y = share(near_x, near_y)
+    far_x, far_y, swapped = ring(far_x, "x"), ring(far_y, "y"), swap(joined)
+    left, near = gram_near(home, near_x, near_y, swapped)
+    last, side = gram_side(far_y, home, near_x, swapped)
+    partial = gram_far(at, near, side, left, last, far_x, swap(far_x))
 
     groups = [
         [gy * NZ + (s + gy) % NY + NY * half for gy in range(NY) for half in range(NZ // NY)]

time: 136 us -> 136 us (level); the launches traced: 134 us -> 136 us
  waiting for transfers between devices: 18.6 us -> 27.7 us
  starting transfers between devices: 12.1 us -> 3.9 us
  blocking collectives: 91.9 us -> 93.6 us
    ppermute x8 -> x4, starting transfers between devices: 11.9 us -> 3.71 us  [ring(): return lax.ppermute(value, ('dp', 'col'), pairs)]
    ppermute x8 -> x4, waiting for transfers between devices: 18.6 us -> 25.8 us  [ring(): return lax.ppermute(value, ('dp', 'col'), pairs)]
    ppermute x4 -> x3, waiting for transfers between devices: 0.01 us -> 1.9 us  [swap(): return lax.ppermute(value, 'col', [(i, i ^ 1) for i in range(NX * NCORE)])]
    all_to_all x1, blocking collectives: 31.9 us -> 33.6 us  [on_device(): lax.all_to_all(partial, 'dp', split_axis=0, concat_axis=0, axis_index_gro...]
  transfers between devices with their start and end apart: 12 -> 7, of which waited for: 6 -> 5; matrix products, arithmetic and copies ran while one was open for 0% -> 0% of each run, Pallas kernels for 2% -> 2%
where the time goes in v8:
time: 136 us
  blocking collectives  93.6 us (69%)
  waiting for transfers between devices  27.7 us (20%)
  Pallas kernels  8.07 us (6%)
  starting transfers between devices  3.9 us (3%)
  local copies, waits for them, and re-layouts  2.29 us (2%)
    all_to_all x1, blocking collectives, on_device(): lax.all_to_all(outgoing, 'dp', split_axis=0, concat_axis=0, tiled=True)  60 us
    all_to_all x1, blocking collectives, on_device(): lax.all_to_all(partial, 'dp', split_axis=0, concat_axis=0, axis_index_gro...  33.6 us
    ppermute x4, waiting for transfers between devices, ring(): return lax.ppermute(value, ('dp', 'col'), pairs)  25.8 us
    ppermute x4, starting transfers between devices, ring(): return lax.ppermute(value, ('dp', 'col'), pairs)  3.71 us
  transfers between devices with their start and end apart: 7, of which 5 were waited for; matrix products, arithmetic and copies ran while one was open for 0% of the time, Pallas kernels for 2%

profile of v8, /device:TPU:64, one launch (start us, length us, event | category | flops | bytes accessed | tf_op | source)
XLA Modules:
  0.0 135.8 jit_solution(15846924208371036285)
XLA Ops:
  0.0 0.1 pad_add_fusion.at
  0.1 1.6 %copy-done = bf16[2048,512]{1,0:T(8,128)(2,1)S(1)} copy-done((bf16[2048,512]{1,0:T(8,128)(2,1)S(1)}, bf16[2048,512]{1,0:T(8,128)(2,1)}, u32[]{:S(2)}) %copy-start) | copy-done | bytes 2097176
  1.7 0.7 copy-done.1
  2.4 1.0 pack.1
  3.4 0.0 copy-start.2
  3.4 60.0 %all_to_all.10 = bf16[32,16,16,128]{3,2,1,0:T(8,128)(2,1)S(1)} all-to-all(bf16[32,16,16,128]{3,2,1,0:T(8,128)(2,1)S(1)} %bitcast.11), channel_id=1, replica_groups=mesh['dp'=32,'col'=8] {'dp'}, dimensions={0} | all-to-all | bytes 4194304 | tf_op jit(solution)/shard_map/all_to_all | solution.py:233
  63.4 2.6 %mix.1 = bf16[128,16,128]{2,1,0:T(8,128)(2,1)S(1)} custom-call(s32[128]{0:T(128)S(1)} %copy-done.2, bf16[512,16,128]{2,1,0:T(8,128)(2,1)S(1)} %bitcast.10), custom_call_target="tpu_custom_call" | custom-call | tf_op jit(solution)/shard_map/mix/pallas_call | solution.py:82
  66.0 0.1 collective-permute-start
  66.1 1.9 %collective-permute-done = bf16[2048,128]{1,0:T(8,128)(2,1)S(1)} collective-permute-done((bf16[2048,128]{1,0:T(8,128)(2,1)S(1)}, bf16[2048,128]{1,0:T(8,128)(2,1)S(1)}, u32[]{:S(2)}, u32[]{:S(2)}) %collective-permute-start) | collective-permute-done | bytes 524320 | tf_op jit(solution)/shard_map/ppermute | solution.py:250
  68.0 0.1 pad_maximum_fusion.home
  68.1 1.6 %collective-permute-start.1 = (bf16[2,2048,128]{2,1,0:T(8,128)(2,1)S(1)}, bf16[2,2048,128]{2,1,0:T(8,128)(2,1)S(1)}, u32[]{:S(2)}, u32[]{:S(2)}) collective-permute-start(bf16[2,2048,128]{2,1,0:T(8,128)(2,1)S(1)} %pad_maximum_fusion.home), channel_id=1, source_target_pairs={{0,2},{1,7},{2,4},{3,1},{4,6},{5,3},{6,0},{7,5},{8,10},{9,15},{10,... | collective-permute-start | bytes 3145736 | tf_op jit(solution)/shard_map/ppermute | solution.py:247
  69.6 0.6 collective-permute-start.2
  70.2 13.9 %collective-permute-done.1.near_x = bf16[2,2048,128]{2,1,0:T(8,128)(2,1)S(1)} collective-permute-done((bf16[2,2048,128]{2,1,0:T(8,128)(2,1)S(1)}, bf16[2,2048,128]{2,1,0:T(8,128)(2,1)S(1)}, u32[]{:S(2)}, u32[]{:S(2)}) %collective-permute-start.1) | collective-permute-done | bytes 1048608 | tf_op jit(solution)/shard_map/ppermute | solution.py:247
  84.1 1.5 %collective-permute-done.2.near_y = bf16[2,2048,128]{2,1,0:T(8,128)(2,1)S(1)} collective-permute-done((bf16[2,2048,128]{2,1,0:T(8,128)(2,1)S(1)}, bf16[2,2048,128]{2,1,0:T(8,128)(2,1)S(1)}, u32[]{:S(2)}, u32[]{:S(2)}) %collective-permute-start.2) | collective-permute-done | bytes 1048608 | tf_op jit(solution)/shard_map/ppermute | solution.py:247
  85.6 0.2 share.1
  85.8 0.1 collective-permute-start.3
  85.9 1.6 %collective-permute-start.5 = (bf16[2048,128]{1,0:T(8,128)(2,1)S(1)}, bf16[2048,128]{1,0:T(8,128)(2,1)S(1)}, u32[]{:S(2)}, u32[]{:S(2)}) collective-permute-start(bf16[2048,128]{1,0:T(8,128)(2,1)S(1)} %get-tuple-element.18), channel_id=1, source_target_pairs={{0,2},{1,7},{2,4},{3,1},{4,6},{5,3},{6,0},{7,5},{8,10},{9,15},{10,... | collective-permute-start | bytes 1572872 | tf_op jit(solution)/shard_map/ppermute | solution.py:247
  87.5 8.9 %collective-permute-done.5.own = bf16[2048,128]{1,0:T(8,128)(2,1)S(1)} collective-permute-done((bf16[2048,128]{1,0:T(8,128)(2,1)S(1)}, bf16[2048,128]{1,0:T(8,128)(2,1)S(1)}, u32[]{:S(2)}, u32[]{:S(2)}) %collective-permute-start.5) | collective-permute-done | bytes 524320 | tf_op jit(solution)/shard_map/ppermute | solution.py:247
  96.4 1.5 %collective-permute-done.4.col = bf16[2048,128]{1,0:T(8,128)(2,1)S(1)} collective-permute-done((bf16[2048,128]{1,0:T(8,128)(2,1)S(1)}, bf16[2048,128]{1,0:T(8,128)(2,1)S(1)}, u32[]{:S(2)}, u32[]{:S(2)}) %collective-permute-start.4) | collective-permute-done | bytes 524320 | tf_op jit(solution)/shard_map/ppermute | solution.py:247
  97.9 0.6 gram_side.1
  98.5 1.4 %gram_near.1 = (bf16[384,2048]{1,0:T(8,128)(2,1)S(1)}, bf16[3,384,256]{2,1,0:T(8,128)(2,1)S(1)}) custom-call(bf16[2,2048,128]{2,1,0:T(8,128)(2,1)S(1)} %pad_maximum_fusion.home, bf16[2,2048,128]{2,1,0:T(8,128)(2,1)S(1)} %collective-permute-done.1.near_x, bf16[2,2048,128]{2,1,0:T(8,128)(2,1)S(1)} %collective-permute-done.2.near_y, ...), custom_call_target="tpu_custom_call" | custom-call | flops 1207959552 | bytes 8388608 | tf_op jit(solution)/shard_map/gram_near/pallas_call | solution.py:139
  99.9 1.4 %gram_far.1 = bf16[8,512,128]{2,1,0:T(8,128)(2,1)S(1)} custom-call(s32[3]{0:T(128)S(1)} %pad_add_fusion.at, bf16[3,384,256]{2,1,0:T(8,128)(2,1)S(1)} %get-tuple-element.13.near_ref, bf16[3,128,256]{2,1,0:T(8,128)(2,1)S(1)} %get-tuple-element.15.side_ref, bf16[384,2048]{1,0:T(8,128)(2,1)S(1)} %get-tuple-element.16.left, ...), custom_call_target="tpu_custom_call" | custom-call | flops 536870912 | bytes 8388608 | tf_op jit(solution)/shard_map/gram_far/pallas_call | solution.py:196
  101.3 33.6 %all_to_all.11.parts_ref = bf16[8,512,128]{2,1,0:T(8,128)(2,1)S(1)} all-to-all(bf16[8,512,128]{2,1,0:T(8,128)(2,1)S(1)} %gram_far.1), channel_id=1, replica_groups={{0,32,72,104,144,176,216,248},{8,40,80,112,152,184,192,224},{16,48,88,1..., dimensions={0} | all-to-all | bytes 2097152 | tf_op jit(solution)/shard_map/all_to_all | solution.py:264
  134.9 0.9 finish.1
  (7 shorter events, 0.0 us)
Async XLA Ops:
  0.1 1.6 %copy-start = (bf16[2048,512]{1,0:T(8,128)(2,1)S(1)}, bf16[2048,512]{1,0:T(8,128)(2,1)}, u32[]{:S(2)}) copy-start(bf16[2048,512]{1,0:T(8,128)(2,1)} %param.3) | copy-start | bytes 6291460
  1.7 0.7 copy-start.1
  3.4 60.0 %copy-start.2 = (s32[128]{0:T(128)S(1)}, s32[128]{0:T(128)}, u32[]{:S(2)}) copy-start(s32[128]{0:T(128)} %picks_ref.1) | copy-start | bytes 1540
  66.0 2.0 %collective-permute-start = (bf16[2048,128]{1,0:T(8,128)(2,1)S(1)}, bf16[2048,128]{1,0:T(8,128)(2,1)S(1)}, u32[]{:S(2)}, u32[]{:S(2)}) collective-permute-start(bf16[2048,128]{1,0:T(8,128)(2,1)S(1)} %bitcast.13), channel_id=1, source_target_pairs={{0,1},{1,0},{2,3},{3,2},{4,5},{5,4},{6,7},{7,6},{8,9},{9,8},{10,11... | collective-permute-start | bytes 1572872 | tf_op jit(solution)/shard_map/ppermute | solution.py:250
  68.1 16.1 %collective-permute-start.1 = (bf16[2,2048,128]{2,1,0:T(8,128)(2,1)S(1)}, bf16[2,2048,128]{2,1,0:T(8,128)(2,1)S(1)}, u32[]{:S(2)}, u32[]{:S(2)}) collective-permute-start(bf16[2,2048,128]{2,1,0:T(8,128)(2,1)S(1)} %pad_maximum_fusion.home), channel_id=1, source_target_pairs={{0,2},{1,7},{2,4},{3,1},{4,6},{5,3},{6,0},{7,5},{8,10},{9,15},{10,... | collective-permute-start | bytes 3145736 | tf_op jit(solution)/shard_map/ppermute | solution.py:247
  69.6 16.0 %collective-permute-start.2 = (bf16[2,2048,128]{2,1,0:T(8,128)(2,1)S(1)}, bf16[2,2048,128]{2,1,0:T(8,128)(2,1)S(1)}, u32[]{:S(2)}, u32[]{:S(2)}) collective-permute-start(bf16[2,2048,128]{2,1,0:T(8,128)(2,1)S(1)} %pad_maximum_fusion.home), channel_id=1, source_target_pairs={{0,64},{1,193},{2,66},{3,195},{4,68},{5,197},{6,70},{7,199},{8,72}... | collective-permute-start | bytes 3145736 | tf_op jit(solution)/shard_map/ppermute | solution.py:247
  85.8 12.1 %collective-permute-start.3 = (bf16[3,2048,128]{2,1,0:T(8,128)(2,1)S(1)}, bf16[3,2048,128]{2,1,0:T(8,128)(2,1)S(1)}, u32[]{:S(2)}, u32[]{:S(2)}) collective-permute-start(bf16[3,2048,128]{2,1,0:T(8,128)(2,1)S(1)} %get-tuple-element.12), channel_id=1, source_target_pairs={{0,1},{1,0},{2,3},{3,2},{4,5},{5,4},{6,7},{7,6},{8,9},{9,8},{10,11... | collective-permute-start | bytes 4718600 | tf_op jit(solution)/shard_map/ppermute | solution.py:250
  85.9 10.5 %collective-permute-start.5 = (bf16[2048,128]{1,0:T(8,128)(2,1)S(1)}, bf16[2048,128]{1,0:T(8,128)(2,1)S(1)}, u32[]{:S(2)}, u32[]{:S(2)}) collective-permute-start(bf16[2048,128]{1,0:T(8,128)(2,1)S(1)} %get-tuple-element.18), channel_id=1, source_target_pairs={{0,2},{1,7},{2,4},{3,1},{4,6},{5,3},{6,0},{7,5},{8,10},{9,15},{10,... | collective-permute-start | bytes 1572872 | tf_op jit(solution)/shard_map/ppermute | solution.py:247
  87.5 10.4 %collective-permute-start.4 = (bf16[2048,128]{1,0:T(8,128)(2,1)S(1)}, bf16[2048,128]{1,0:T(8,128)(2,1)S(1)}, u32[]{:S(2)}, u32[]{:S(2)}) collective-permute-start(bf16[2048,128]{1,0:T(8,128)(2,1)S(1)} %get-tuple-element.14), channel_id=1, source_target_pairs={{0,64},{1,193},{2,66},{3,195},{4,68},{5,197},{6,70},{7,199},{8,72}... | collective-permute-start | bytes 1572872 | tf_op jit(solution)/shard_map/ppermute | solution.py:247
  96.4 3.6 %collective-permute-start.6 = (bf16[2048,128]{1,0:T(8,128)(2,1)S(1)}, bf16[2048,128]{1,0:T(8,128)(2,1)S(1)}, u32[]{:S(2)}, u32[]{:S(2)}) collective-permute-start(bf16[2048,128]{1,0:T(8,128)(2,1)S(1)} %collective-permute-done.5.own), channel_id=1, source_target_pairs={{0,1},{1,0},{2,3},{3,2},{4,5},{5,4},{6,7},{7,6},{8,9},{9,8},{10,11... | collective-permute-start | bytes 1572872 | tf_op jit(solution)/shard_map/ppermute | solution.py:250

commit v9 on v5

--- a/solution.py
+++ b/solution.py
@@ -61,16 +61,11 @@
 def mix_kernel(picks_ref, raw_ref, out_ref, work):
     half = N_BLOCKS // 2
 
-    @pl.loop(0, N_BLOCKS // 16, unroll=2)
-    def _(d):
-        base = d * 16
+    for base in range(0, N_BLOCKS, 16):
         parts = [raw_ref[base + b].astype(jnp.float32) for b in range(16)]
         for b, part in enumerate(hadamard(parts)):
             work[base + b] = part
-
-    @pl.loop(0, 32, unroll=2)
-    def _(i):
-        base = lax.div(i, 16) * half + lax.rem(i, 16)
+    for base in [*range(16), *range(half, half + 16)]:
         parts = [work[base + 16 * e] for e in range(16)]
         for e, part in enumerate(hadamard(parts)):
             work[base + 16 * e] = part
@@ -99,23 +94,23 @@
 
 
 def halves_kernel(*refs):
-    pieces, outs = refs[:4], refs[4:]
+    pieces, outs = refs[:4], refs[-4:]
     depth = outs[0].shape[0]
     for i, out in enumerate(outs):
         out[...] = pieces[i][pl.ds(i % 2 * depth, depth), :]
 
 
-def halves(*pieces):
+def halves(pieces, after):
     part = jax.ShapeDtypeStruct((pieces[0].shape[0] // 2, LANES), pieces[0].dtype)
     return pl.pallas_call(
         halves_kernel,
-        in_specs=[LOCAL] * 4,
+        in_specs=[LOCAL] * (4 + len(after)),
         out_specs=[LOCAL] * 4,
         out_shape=[part] * 4,
         compiler_params=pltpu.CompilerParams(vmem_limit_bytes=16 * MIB),
         cost_estimate=pl.CostEstimate(flops=0, bytes_accessed=2 * MIB, transcendentals=0),
         name="halves",
-    )(*pieces)
+    )(*pieces, *after)
 
 
 def pair_dot(left, own, other):
@@ -245,11 +240,11 @@
 
     x_up, x_down = along_x(sketch, 1), along_x(sketch, -1)
     y_up, y_down = along_y(sketch, 1), along_y(sketch, -1)
-    x_low, x_high, y_low, y_high = halves(x_up, x_down, y_up, y_down)
+    home = swap(sketch)
+    x_low, x_high, y_low, y_high = halves((x_up, x_down, y_up, y_down), (home,))
     x_far = jnp.concatenate([along_x(x_low, 1), along_x(x_high, -1)])
     y_far = jnp.concatenate([along_y(y_low, 1), along_y(y_high, -1)])
-    own = (sketch, x_up, x_down)
-    other = tuple(swap(piece) for piece in own)
+    own, other = (sketch, x_up, x_down), (home, swap(x_up), swap(x_down))
     left, near = gram_near((sketch, y_up, y_down), own, other)
     last, side = gram_side(y_far, own, other)
     partial = gram_far(at, near, side, left, last, x_far, swap(x_far))

time: 136 us -> 131 us (0.963); the launches traced: 134 us -> 131 us
  waiting for transfers between devices: 18.6 us -> 15.9 us
    ppermute x4, waiting for transfers between devices: 13.3 us -> 10.7 us  [along_y(): lax.ppermute(value, 'dp', [(i, (i + NZ * step) % (NY * NZ)) for i in rang...]
where the time goes in v9:
time: 131 us
  blocking collectives  92.1 us (70%)
  waiting for transfers between devices  15.9 us (12%)
  starting transfers between devices  12.4 us (9%)
  Pallas kernels  7.99 us (6%)
  local copies, waits for them, and re-layouts  2.35 us (2%)
    all_to_all x1, blocking collectives, on_device(): lax.all_to_all(outgoing, 'dp', split_axis=0, concat_axis=0, tiled=True)  60 us
    all_to_all x1, blocking collectives, on_device(): lax.all_to_all(partial, 'dp', split_axis=0, concat_axis=0, axis_index_gro...  32.1 us
    ppermute x4, waiting for transfers between devices, along_y(): lax.ppermute(value, 'dp', [(i, (i + NZ * step) % (NY * NZ)) for i in rang...  10.7 us
    ppermute x4, starting transfers between devices, along_x(): lax.ppermute(value, 'col', [(i, (i + NCORE * step) % (NX * NCORE)) for i...  6.55 us
    ppermute x4, starting transfers between devices, along_y(): lax.ppermute(value, 'dp', [(i, (i + NZ * step) % (NY * NZ)) for i in rang...  5.34 us
    ppermute x4, waiting for transfers between devices, along_x(): lax.ppermute(value, 'col', [(i, (i + NCORE * step) % (NX * NCORE)) for i...  5.24 us
  transfers between devices with their start and end apart: 12, of which 6 were waited for; matrix products, arithmetic and copies ran while one was open for 0% of the time, Pallas kernels for 2%

profile of v9, /device:TPU:64, one launch (start us, length us, event | category | flops | bytes accessed | tf_op | source)
XLA Modules:
  0.0 131.0 jit_solution(18007935957842655904)
XLA Ops:
  0.1 1.6 %copy-done = bf16[2048,512]{1,0:T(8,128)(2,1)S(1)} copy-done((bf16[2048,512]{1,0:T(8,128)(2,1)S(1)}, bf16[2048,512]{1,0:T(8,128)(2,1)}, u32[]{:S(2)}) %copy-start) | copy-done | bytes 2097176
  1.7 0.7 copy-done.1
  2.4 1.0 pack.1
  3.4 60.0 %all_to_all.10 = bf16[32,16,16,128]{3,2,1,0:T(8,128)(2,1)S(1)} all-to-all(bf16[32,16,16,128]{3,2,1,0:T(8,128)(2,1)S(1)} %bitcast.17), channel_id=1, replica_groups=mesh['dp'=32,'col'=8] {'dp'}, dimensions={0} | all-to-all | bytes 4194304 | tf_op jit(solution)/shard_map/all_to_all | solution.py:229
  63.4 2.6 %mix.1 = bf16[128,16,128]{2,1,0:T(8,128)(2,1)S(1)} custom-call(s32[128]{0:T(128)S(1)} %copy-done.2, bf16[512,16,128]{2,1,0:T(8,128)(2,1)S(1)} %bitcast.16), custom_call_target="tpu_custom_call" | custom-call | tf_op jit(solution)/shard_map/mix/pallas_call | solution.py:82
  66.0 0.6 collective-permute-start
  66.6 2.7 %collective-permute-start.1 = (bf16[2048,128]{1,0:T(8,128)(2,1)S(1)}, bf16[2048,128]{1,0:T(8,128)(2,1)S(1)}, u32[]{:S(2)}, u32[]{:S(2)}) collective-permute-start(bf16[2048,128]{1,0:T(8,128)(2,1)S(1)} %bitcast.9), channel_id=1, source_target_pairs={{0,192},{8,200},{16,208},{24,216},{32,224},{40,232},{48,240},{56,2... | collective-permute-start | bytes 1572872 | tf_op jit(solution)/shard_map/ppermute | solution.py:236
  69.3 1.5 %collective-permute-start.2 = (bf16[2048,128]{1,0:T(8,128)(2,1)S(1)}, bf16[2048,128]{1,0:T(8,128)(2,1)S(1)}, u32[]{:S(2)}, u32[]{:S(2)}) collective-permute-start(bf16[2048,128]{1,0:T(8,128)(2,1)S(1)} %bitcast.10), channel_id=1, source_target_pairs={{0,2},{1,3},{2,4},{3,5},{4,6},{5,7},{6,0},{7,1},{8,10},{9,11},{10,... | collective-permute-start | bytes 1572872 | tf_op jit(solution)/shard_map/ppermute | solution.py:233
  70.8 1.7 %collective-permute-start.3 = (bf16[2048,128]{1,0:T(8,128)(2,1)S(1)}, bf16[2048,128]{1,0:T(8,128)(2,1)S(1)}, u32[]{:S(2)}, u32[]{:S(2)}) collective-permute-start(bf16[2048,128]{1,0:T(8,128)(2,1)S(1)} %bitcast.11), channel_id=1, source_target_pairs={{0,6},{1,7},{2,0},{3,1},{4,2},{5,3},{6,4},{7,5},{8,14},{9,15},{10,... | collective-permute-start | bytes 1572872 | tf_op jit(solution)/shard_map/ppermute | solution.py:233
  72.5 6.8 %collective-permute-done.refs_1_.refs_2_ = bf16[2048,128]{1,0:T(8,128)(2,1)S(1)} collective-permute-done((bf16[2048,128]{1,0:T(8,128)(2,1)S(1)}, bf16[2048,128]{1,0:T(8,128)(2,1)S(1)}, u32[]{:S(2)}, u32[]{:S(2)}) %collective-permute-start) | collective-permute-done | bytes 524320 | tf_op jit(solution)/shard_map/ppermute | solution.py:236
  79.3 2.7 %collective-permute-done.2.refs_4_.refs_0_.refs_2_ = bf16[2048,128]{1,0:T(8,128)(2,1)S(1)} collective-permute-done((bf16[2048,128]{1,0:T(8,128)(2,1)S(1)}, bf16[2048,128]{1,0:T(8,128)(2,1)S(1)}, u32[]{:S(2)}, u32[]{:S(2)}) %collective-permute-start.2) | collective-permute-done | bytes 524320 | tf_op jit(solution)/shard_map/ppermute | solution.py:233
  82.0 1.6 %collective-permute-start.9 = (bf16[1024,128]{1,0:T(8,128)(2,1)S(1)}, bf16[1024,128]{1,0:T(8,128)(2,1)S(1)}, u32[]{:S(2)}, u32[]{:S(2)}) collective-permute-start(bf16[1024,128]{1,0:T(8,128)(2,1)S(1)} %get-tuple-element.19), channel_id=1, source_target_pairs={{0,2},{1,3},{2,4},{3,5},{4,6},{5,7},{6,0},{7,1},{8,10},{9,11},{10,... | collective-permute-start | bytes 786440 | tf_op jit(solution)/shard_map/ppermute | solution.py:233
  83.6 1.7 %collective-permute-start.10 = (bf16[1024,128]{1,0:T(8,128)(2,1)S(1)}, bf16[1024,128]{1,0:T(8,128)(2,1)S(1)}, u32[]{:S(2)}, u32[]{:S(2)}) collective-permute-start(bf16[1024,128]{1,0:T(8,128)(2,1)S(1)} %get-tuple-element.20), channel_id=1, source_target_pairs={{0,6},{1,7},{2,0},{3,1},{4,2},{5,3},{6,4},{7,5},{8,14},{9,15},{10,... | collective-permute-start | bytes 786440 | tf_op jit(solution)/shard_map/ppermute | solution.py:233
  85.4 1.5 %collective-permute-start.8 = (bf16[1024,128]{1,0:T(8,128)(2,1)S(1)}, bf16[1024,128]{1,0:T(8,128)(2,1)S(1)}, u32[]{:S(2)}, u32[]{:S(2)}) collective-permute-start(bf16[1024,128]{1,0:T(8,128)(2,1)S(1)} %get-tuple-element.15), channel_id=1, source_target_pairs={{0,192},{8,200},{16,208},{24,216},{32,224},{40,232},{48,240},{56,2... | collective-permute-start | bytes 786440 | tf_op jit(solution)/shard_map/ppermute | solution.py:236
  86.9 0.5 collective-permute-start.7
  87.4 2.3 %collective-permute-done.9 = bf16[1024,128]{1,0:T(8,128)(2,1)S(1)} collective-permute-done((bf16[1024,128]{1,0:T(8,128)(2,1)S(1)}, bf16[1024,128]{1,0:T(8,128)(2,1)S(1)}, u32[]{:S(2)}, u32[]{:S(2)}) %collective-permute-start.9) | collective-permute-done | bytes 262176 | tf_op jit(solution)/shard_map/ppermute | solution.py:233
  90.0 0.5 collective-permute-start.11
  90.6 1.2 collective-permute-done.8
  91.7 2.7 %collective-permute-done.7 = bf16[1024,128]{1,0:T(8,128)(2,1)S(1)} collective-permute-done((bf16[1024,128]{1,0:T(8,128)(2,1)S(1)}, bf16[1024,128]{1,0:T(8,128)(2,1)S(1)}, u32[]{:S(2)}, u32[]{:S(2)}) %collective-permute-start.7) | collective-permute-done | bytes 262176 | tf_op jit(solution)/shard_map/ppermute | solution.py:236
  94.5 0.6 gram_side.1
  95.2 1.4 %gram_near.1 = (bf16[384,2048]{1,0:T(8,128)(2,1)S(1)}, bf16[3,384,256]{2,1,0:T(8,128)(2,1)S(1)}) custom-call(bf16[2048,128]{1,0:T(8,128)(2,1)S(1)} %bitcast.14, bf16[2048,128]{1,0:T(8,128)(2,1)S(1)} %collective-permute-done.refs_1_.refs_2_, bf16[2048,128]{1,0:T(8,128)(2,1)S(1)} %collective-permute-done.1.refs_2_.refs_3_, bf16[2048,128]{1,0:T(8,128)(2,1)S(1)} %bitcast.15, ...), custom_call_target="tpu_custom_call" | custom-call | flops 1207959552 | bytes 8388608 | tf_op jit(solution)/shard_map/gram_near/pallas_call | solution.py:135
  96.6 1.4 %gram_far.1 = bf16[8,512,128]{2,1,0:T(8,128)(2,1)S(1)} custom-call(s32[3]{0:T(128)S(1)} %pad_add_fusion.at, bf16[3,384,256]{2,1,0:T(8,128)(2,1)S(1)} %get-tuple-element.13.near_ref, bf16[3,128,256]{2,1,0:T(8,128)(2,1)S(1)} %get-tuple-element.16.side_ref, bf16[384,2048]{1,0:T(8,128)(2,1)S(1)} %get-tuple-element.17.left, ...), custom_call_target="tpu_custom_call" | custom-call | flops 536870912 | bytes 8388608 | tf_op jit(solution)/shard_map/gram_far/pallas_call | solution.py:192
  98.0 32.1 %all_to_all.11.parts_ref = bf16[8,512,128]{2,1,0:T(8,128)(2,1)S(1)} all-to-all(bf16[8,512,128]{2,1,0:T(8,128)(2,1)S(1)} %gram_far.1), channel_id=1, replica_groups={{0,32,72,104,144,176,216,248},{8,40,80,112,152,184,192,224},{16,48,88,1..., dimensions={0} | all-to-all | bytes 2097152 | tf_op jit(solution)/shard_map/all_to_all | solution.py:256
  130.1 0.9 finish.1
  (19 shorter events, 0.5 us)
Async XLA Ops:
  0.1 1.6 %copy-start = (bf16[2048,512]{1,0:T(8,128)(2,1)S(1)}, bf16[2048,512]{1,0:T(8,128)(2,1)}, u32[]{:S(2)}) copy-start(bf16[2048,512]{1,0:T(8,128)(2,1)} %param.3) | copy-start | bytes 6291460
  1.7 0.7 copy-start.1
  3.4 60.0 %copy-start.2 = (s32[128]{0:T(128)S(1)}, s32[128]{0:T(128)}, u32[]{:S(2)}) copy-start(s32[128]{0:T(128)} %picks_ref.1) | copy-start | bytes 1540
  66.0 13.3 %collective-permute-start = (bf16[2048,128]{1,0:T(8,128)(2,1)S(1)}, bf16[2048,128]{1,0:T(8,128)(2,1)S(1)}, u32[]{:S(2)}, u32[]{:S(2)}) collective-permute-start(bf16[2048,128]{1,0:T(8,128)(2,1)S(1)} %bitcast.8), channel_id=1, source_target_pairs={{0,64},{8,72},{16,80},{24,88},{32,96},{40,104},{48,112},{56,120},{... | collective-permute-start | bytes 1572872 | tf_op jit(solution)/shard_map/ppermute | solution.py:236
  66.6 12.7 %collective-permute-start.1 = (bf16[2048,128]{1,0:T(8,128)(2,1)S(1)}, bf16[2048,128]{1,0:T(8,128)(2,1)S(1)}, u32[]{:S(2)}, u32[]{:S(2)}) collective-permute-start(bf16[2048,128]{1,0:T(8,128)(2,1)S(1)} %bitcast.9), channel_id=1, source_target_pairs={{0,192},{8,200},{16,208},{24,216},{32,224},{40,232},{48,240},{56,2... | collective-permute-start | bytes 1572872 | tf_op jit(solution)/shard_map/ppermute | solution.py:236
  69.3 12.7 %collective-permute-start.2 = (bf16[2048,128]{1,0:T(8,128)(2,1)S(1)}, bf16[2048,128]{1,0:T(8,128)(2,1)S(1)}, u32[]{:S(2)}, u32[]{:S(2)}) collective-permute-start(bf16[2048,128]{1,0:T(8,128)(2,1)S(1)} %bitcast.10), channel_id=1, source_target_pairs={{0,2},{1,3},{2,4},{3,5},{4,6},{5,7},{6,0},{7,1},{8,10},{9,11},{10,... | collective-permute-start | bytes 1572872 | tf_op jit(solution)/shard_map/ppermute | solution.py:233
  70.8 11.2 %collective-permute-start.3 = (bf16[2048,128]{1,0:T(8,128)(2,1)S(1)}, bf16[2048,128]{1,0:T(8,128)(2,1)S(1)}, u32[]{:S(2)}, u32[]{:S(2)}) collective-permute-start(bf16[2048,128]{1,0:T(8,128)(2,1)S(1)} %bitcast.11), channel_id=1, source_target_pairs={{0,6},{1,7},{2,0},{3,1},{4,2},{5,3},{6,4},{7,5},{8,14},{9,15},{10,... | collective-permute-start | bytes 1572872 | tf_op jit(solution)/shard_map/ppermute | solution.py:233
  72.5 9.5 %collective-permute-start.4 = (bf16[2048,128]{1,0:T(8,128)(2,1)S(1)}, bf16[2048,128]{1,0:T(8,128)(2,1)S(1)}, u32[]{:S(2)}, u32[]{:S(2)}) collective-permute-start(bf16[2048,128]{1,0:T(8,128)(2,1)S(1)} %bitcast.12), channel_id=1, source_target_pairs={{0,1},{1,0},{2,3},{3,2},{4,5},{5,4},{6,7},{7,6},{8,9},{9,8},{10,11... | collective-permute-start | bytes 1572872 | tf_op jit(solution)/shard_map/ppermute | solution.py:239
  82.0 7.7 %collective-permute-start.9 = (bf16[1024,128]{1,0:T(8,128)(2,1)S(1)}, bf16[1024,128]{1,0:T(8,128)(2,1)S(1)}, u32[]{:S(2)}, u32[]{:S(2)}) collective-permute-start(bf16[1024,128]{1,0:T(8,128)(2,1)S(1)} %get-tuple-element.19), channel_id=1, source_target_pairs={{0,2},{1,3},{2,4},{3,5},{4,6},{5,7},{6,0},{7,1},{8,10},{9,11},{10,... | collective-permute-start | bytes 786440 | tf_op jit(solution)/shard_map/ppermute | solution.py:233
  83.6 6.4 %collective-permute-start.10 = (bf16[1024,128]{1,0:T(8,128)(2,1)S(1)}, bf16[1024,128]{1,0:T(8,128)(2,1)S(1)}, u32[]{:S(2)}, u32[]{:S(2)}) collective-permute-start(bf16[1024,128]{1,0:T(8,128)(2,1)S(1)} %get-tuple-element.20), channel_id=1, source_target_pairs={{0,6},{1,7},{2,0},{3,1},{4,2},{5,3},{6,4},{7,5},{8,14},{9,15},{10,... | collective-permute-start | bytes 786440 | tf_op jit(solution)/shard_map/ppermute | solution.py:233
  85.4 6.4 %collective-permute-start.8 = (bf16[1024,128]{1,0:T(8,128)(2,1)S(1)}, bf16[1024,128]{1,0:T(8,128)(2,1)S(1)}, u32[]{:S(2)}, u32[]{:S(2)}) collective-permute-start(bf16[1024,128]{1,0:T(8,128)(2,1)S(1)} %get-tuple-element.15), channel_id=1, source_target_pairs={{0,192},{8,200},{16,208},{24,216},{32,224},{40,232},{48,240},{56,2... | collective-permute-start | bytes 786440 | tf_op jit(solution)/shard_map/ppermute | solution.py:236
  86.9 7.6 %collective-permute-start.7 = (bf16[1024,128]{1,0:T(8,128)(2,1)S(1)}, bf16[1024,128]{1,0:T(8,128)(2,1)S(1)}, u32[]{:S(2)}, u32[]{:S(2)}) collective-permute-start(bf16[1024,128]{1,0:T(8,128)(2,1)S(1)} %get-tuple-element.14), channel_id=1, source_target_pairs={{0,64},{8,72},{16,80},{24,88},{32,96},{40,104},{48,112},{56,120},{... | collective-permute-start | bytes 786440 | tf_op jit(solution)/shard_map/ppermute | solution.py:236
  87.4 7.1 %collective-permute-start.5 = (bf16[2048,128]{1,0:T(8,128)(2,1)S(1)}, bf16[2048,128]{1,0:T(8,128)(2,1)S(1)}, u32[]{:S(2)}, u32[]{:S(2)}) collective-permute-start(bf16[2048,128]{1,0:T(8,128)(2,1)S(1)} %collective-permute-done.2.refs_4_.refs_0_.refs_2_), channel_id=1, source_target_pairs={{0,1},{1,0},{2,3},{3,2},{4,5},{5,4},{6,7},{7,6},{8,9},{9,8},{10,11... | collective-permute-start | bytes 1572872 | tf_op jit(solution)/shard_map/ppermute | solution.py:239
  89.7 4.8 %collective-permute-start.6 = (bf16[2048,128]{1,0:T(8,128)(2,1)S(1)}, bf16[2048,128]{1,0:T(8,128)(2,1)S(1)}, u32[]{:S(2)}, u32[]{:S(2)}) collective-permute-start(bf16[2048,128]{1,0:T(8,128)(2,1)S(1)} %collective-permute-done.3.refs_5_.refs_1_.refs_3_), channel_id=1, source_target_pairs={{0,1},{1,0},{2,3},{3,2},{4,5},{5,4},{6,7},{7,6},{8,9},{9,8},{10,11... | collective-permute-start | bytes 1572872 | tf_op jit(solution)/shard_map/ppermute | solution.py:239
  90.0 6.6 %collective-permute-start.11 = (bf16[2048,128]{1,0:T(8,128)(2,1)S(1)}, bf16[2048,128]{1,0:T(8,128)(2,1)S(1)}, u32[]{:S(2)}, u32[]{:S(2)}) collective-permute-start(bf16[2048,128]{1,0:T(8,128)(2,1)S(1)} %constant_dynamic-update-slice_fusion.own), channel_id=1, source_target_pairs={{0,1},{1,0},{2,3},{3,2},{4,5},{5,4},{6,7},{7,6},{8,9},{9,8},{10,11... | collective-permute-start | bytes 1572872 | tf_op jit(solution)/shard_map/ppermute | solution.py:239

commit v10 on v9

--- a/solution.py
+++ b/solution.py
@@ -93,24 +93,24 @@
 NEAR = (0, 1, 3)
 
 
-def halves_kernel(*refs):
-    pieces, outs = refs[:4], refs[-4:]
-    depth = outs[0].shape[0]
-    for i, out in enumerate(outs):
-        out[...] = pieces[i][pl.ds(i % 2 * depth, depth), :]
-
-
-def halves(pieces, after):
-    part = jax.ShapeDtypeStruct((pieces[0].shape[0] // 2, LANES), pieces[0].dtype)
+def halves_kernel(up, down, *refs):
+    low, high = refs[-2:]
+    depth = low.shape[0]
+    low[...] = up[pl.ds(0, depth), :]
+    high[...] = down[pl.ds(depth, depth), :]
+
+
+def halves(up, down, after):
+    part = jax.ShapeDtypeStruct((up.shape[0] // 2, LANES), up.dtype)
     return pl.pallas_call(
         halves_kernel,
-        in_specs=[LOCAL] * (4 + len(after)),
-        out_specs=[LOCAL] * 4,
-        out_shape=[part] * 4,
-        compiler_params=pltpu.CompilerParams(vmem_limit_bytes=16 * MIB),
-        cost_estimate=pl.CostEstimate(flops=0, bytes_accessed=2 * MIB, transcendentals=0),
+        in_specs=[LOCAL] * 3,
+        out_specs=[LOCAL] * 2,
+        out_shape=[part] * 2,
+        compiler_params=pltpu.CompilerParams(vmem_limit_bytes=16 * MIB),
+        cost_estimate=pl.CostEstimate(flops=0, bytes_accessed=MIB, transcendentals=0),
         name="halves",
-    )(*pieces, *after)
+    )(up, down, after)
 
 
 def pair_dot(left, own, other):
@@ -118,7 +118,7 @@
 
 
 def near_kernel(*refs):
-    cols, own, other, (left, out_ref) = refs[:3], refs[3:6], refs[6:9], refs[9:]
+    own, other, cols, (left, out_ref) = refs[:3], refs[3:6], refs[6:9], refs[9:]
     for j in range(len(NEAR)):
         left[pl.ds(j * LANES, LANES), :] = cols[j][...].T
     for j in range(len(NEAR)):
@@ -143,21 +143,21 @@
         compiler_params=pltpu.CompilerParams(vmem_limit_bytes=16 * MIB),
         cost_estimate=cost(depth, near * near),
         name="gram_near",
-    )(*cols, *own, *other)
+    )(*own, *other, *cols)
 
 
 def side_kernel(*refs):
-    col, own, other, (last, out_ref) = refs[0], refs[1:4], refs[4:7], refs[7:]
+    own, other, col, (last, out_ref) = refs[:3], refs[3:6], refs[6], refs[-2:]
     last[...] = col[...].T
     for j in range(len(NEAR)):
         out_ref[j] = pair_dot(last[...], own[j][...], other[j][...]).astype(out_ref.dtype)
 
 
-def gram_side(col, own, other):
+def gram_side(col, own, other, left):
     depth, near = col.shape[0], len(NEAR)
     return pl.pallas_call(
         side_kernel,
-        in_specs=[LOCAL] * 7,
+        in_specs=[LOCAL] * 8,
         out_specs=[LOCAL] * 2,
         out_shape=[
             jax.ShapeDtypeStruct((LANES, depth), jnp.bfloat16),
@@ -166,7 +166,7 @@
         compiler_params=pltpu.CompilerParams(vmem_limit_bytes=16 * MIB),
         cost_estimate=cost(depth, near),
         name="gram_side",
-    )(col, *own, *other)
+    )(*own, *other, col, left)
 
 
 def far_kernel(at, near_ref, side_ref, left, last, own, other, out_ref):
@@ -241,12 +241,13 @@
     x_up, x_down = along_x(sketch, 1), along_x(sketch, -1)
     y_up, y_down = along_y(sketch, 1), along_y(sketch, -1)
     home = swap(sketch)
-    x_low, x_high, y_low, y_high = halves((x_up, x_down, y_up, y_down), (home,))
+    x_low, x_high = halves(x_up, x_down, home)
+    y_low, y_high = halves(y_up, y_down, x_low)
     x_far = jnp.concatenate([along_x(x_low, 1), along_x(x_high, -1)])
     y_far = jnp.concatenate([along_y(y_low, 1), along_y(y_high, -1)])
     own, other = (sketch, x_up, x_down), (home, swap(x_up), swap(x_down))
     left, near = gram_near((sketch, y_up, y_down), own, other)
-    last, side = gram_side(y_far, own, other)
+    last, side = gram_side(y_far, own, other, left)
     partial = gram_far(at, near, side, left, last, x_far, swap(x_far))
 
     groups = [

time: 131 us -> 134 us (1.023)
  starting transfers between devices: 12.4 us -> 13.8 us
    ppermute x4, waiting for transfers between devices: 5.24 us -> 6.78 us  [along_x(): lax.ppermute(value, 'col', [(i, (i + NCORE * step) % (NX * NCORE)) for i...]
  transfers between devices with their start and end apart: 12 -> 12, of which waited for: 6 -> 4; matrix products, arithmetic and copies ran while one was open for 0% -> 0% of each run, Pallas kernels for 2% -> 2%
where the time goes in v10:
time: 134 us; the launch traced here: 133 us
  blocking collectives  92.4 us (69%)
  waiting for transfers between devices  16.6 us (12%)
  starting transfers between devices  13.8 us (10%)
  Pallas kernels  7.98 us (6%)
  local copies, waits for them, and re-layouts  2.35 us (2%)
    all_to_all x1, blocking collectives, on_device(): lax.all_to_all(outgoing, 'dp', split_axis=0, concat_axis=0, tiled=True)  60 us
    all_to_all x1, blocking collectives, on_device(): lax.all_to_all(partial, 'dp', split_axis=0, concat_axis=0, axis_index_gro...  32.4 us
    ppermute x4, waiting for transfers between devices, along_y(): lax.ppermute(value, 'dp', [(i, (i + NZ * step) % (NY * NZ)) for i in rang...  9.77 us
    ppermute x4, waiting for transfers between devices, along_x(): lax.ppermute(value, 'col', [(i, (i + NCORE * step) % (NX * NCORE)) for i...  6.78 us
    ppermute x4, starting transfers between devices, along_x(): lax.ppermute(value, 'col', [(i, (i + NCORE * step) % (NX * NCORE)) for i...  6.63 us
    ppermute x4, starting transfers between devices, along_y(): lax.ppermute(value, 'dp', [(i, (i + NZ * step) % (NY * NZ)) for i in rang...  6.27 us
  transfers between devices with their start and end apart: 12, of which 4 were waited for; matrix products, arithmetic and copies ran while one was open for 0% of the time, Pallas kernels for 2%

profile of v10, /device:TPU:64, one launch (start us, length us, event | category | flops | bytes accessed | tf_op | source)
XLA Modules:
  0.0 133.3 jit_solution(8014467667525440125)
XLA Ops:
  0.0 0.1 pad_add_fusion.at
  0.1 1.6 %copy-done = bf16[2048,512]{1,0:T(8,128)(2,1)S(1)} copy-done((bf16[2048,512]{1,0:T(8,128)(2,1)S(1)}, bf16[2048,512]{1,0:T(8,128)(2,1)}, u32[]{:S(2)}) %copy-start) | copy-done | bytes 2097176
  1.7 0.7 copy-done.1
  2.4 1.0 pack.1
  3.4 60.0 %all_to_all.10 = bf16[32,16,16,128]{3,2,1,0:T(8,128)(2,1)S(1)} all-to-all(bf16[32,16,16,128]{3,2,1,0:T(8,128)(2,1)S(1)} %bitcast.17), channel_id=1, replica_groups=mesh['dp'=32,'col'=8] {'dp'}, dimensions={0} | all-to-all | bytes 4194304 | tf_op jit(solution)/shard_map/all_to_all | solution.py:229
  63.4 2.6 %mix.1 = bf16[128,16,128]{2,1,0:T(8,128)(2,1)S(1)} custom-call(s32[128]{0:T(128)S(1)} %copy-done.2, bf16[512,16,128]{2,1,0:T(8,128)(2,1)S(1)} %bitcast.16), custom_call_target="tpu_custom_call" | custom-call | tf_op jit(solution)/shard_map/mix/pallas_call | solution.py:82
  66.0 1.6 %collective-permute-start = (bf16[2048,128]{1,0:T(8,128)(2,1)S(1)}, bf16[2048,128]{1,0:T(8,128)(2,1)S(1)}, u32[]{:S(2)}, u32[]{:S(2)}) collective-permute-start(bf16[2048,128]{1,0:T(8,128)(2,1)S(1)} %bitcast.8), channel_id=1, source_target_pairs={{0,2},{1,3},{2,4},{3,5},{4,6},{5,7},{6,0},{7,1},{8,10},{9,11},{10,... | collective-permute-start | bytes 1572872 | tf_op jit(solution)/shard_map/ppermute | solution.py:233
  67.5 1.7 %collective-permute-start.1 = (bf16[2048,128]{1,0:T(8,128)(2,1)S(1)}, bf16[2048,128]{1,0:T(8,128)(2,1)S(1)}, u32[]{:S(2)}, u32[]{:S(2)}) collective-permute-start(bf16[2048,128]{1,0:T(8,128)(2,1)S(1)} %bitcast.9), channel_id=1, source_target_pairs={{0,6},{1,7},{2,0},{3,1},{4,2},{5,3},{6,4},{7,5},{8,14},{9,15},{10,... | collective-permute-start | bytes 1572872 | tf_op jit(solution)/shard_map/ppermute | solution.py:233
  69.3 0.6 collective-permute-start.5
  69.8 2.7 %collective-permute-start.6 = (bf16[2048,128]{1,0:T(8,128)(2,1)S(1)}, bf16[2048,128]{1,0:T(8,128)(2,1)S(1)}, u32[]{:S(2)}, u32[]{:S(2)}) collective-permute-start(bf16[2048,128]{1,0:T(8,128)(2,1)S(1)} %bitcast.12), channel_id=1, source_target_pairs={{0,192},{8,200},{16,208},{24,216},{32,224},{40,232},{48,240},{56,2... | collective-permute-start | bytes 1572872 | tf_op jit(solution)/shard_map/ppermute | solution.py:236
  72.5 6.8 %collective-permute-done.refs_1_.up = bf16[2048,128]{1,0:T(8,128)(2,1)S(1)} collective-permute-done((bf16[2048,128]{1,0:T(8,128)(2,1)S(1)}, bf16[2048,128]{1,0:T(8,128)(2,1)S(1)}, u32[]{:S(2)}, u32[]{:S(2)}) %collective-permute-start) | collective-permute-done | bytes 524320 | tf_op jit(solution)/shard_map/ppermute | solution.py:233
  79.3 1.6 %collective-permute-start.9 = (bf16[1024,128]{1,0:T(8,128)(2,1)S(1)}, bf16[1024,128]{1,0:T(8,128)(2,1)S(1)}, u32[]{:S(2)}, u32[]{:S(2)}) collective-permute-start(bf16[1024,128]{1,0:T(8,128)(2,1)S(1)} %get-tuple-element.14.refs_0_), channel_id=1, source_target_pairs={{0,2},{1,3},{2,4},{3,5},{4,6},{5,7},{6,0},{7,1},{8,10},{9,11},{10,... | collective-permute-start | bytes 786440 | tf_op jit(solution)/shard_map/ppermute | solution.py:233
  80.9 1.7 %collective-permute-start.10 = (bf16[1024,128]{1,0:T(8,128)(2,1)S(1)}, bf16[1024,128]{1,0:T(8,128)(2,1)S(1)}, u32[]{:S(2)}, u32[]{:S(2)}) collective-permute-start(bf16[1024,128]{1,0:T(8,128)(2,1)S(1)} %get-tuple-element.20), channel_id=1, source_target_pairs={{0,6},{1,7},{2,0},{3,1},{4,2},{5,3},{6,4},{7,5},{8,14},{9,15},{10,... | collective-permute-start | bytes 786440 | tf_op jit(solution)/shard_map/ppermute | solution.py:233
  82.7 2.2 %collective-permute-done.5.refs_7_.up = bf16[2048,128]{1,0:T(8,128)(2,1)S(1)} collective-permute-done((bf16[2048,128]{1,0:T(8,128)(2,1)S(1)}, bf16[2048,128]{1,0:T(8,128)(2,1)S(1)}, u32[]{:S(2)}, u32[]{:S(2)}) %collective-permute-start.5) | collective-permute-done | bytes 524320 | tf_op jit(solution)/shard_map/ppermute | solution.py:236
  84.9 3.0 %collective-permute-start.8 = (bf16[1024,128]{1,0:T(8,128)(2,1)S(1)}, bf16[1024,128]{1,0:T(8,128)(2,1)S(1)}, u32[]{:S(2)}, u32[]{:S(2)}) collective-permute-start(bf16[1024,128]{1,0:T(8,128)(2,1)S(1)} %get-tuple-element.16), channel_id=1, source_target_pairs={{0,192},{8,200},{16,208},{24,216},{32,224},{40,232},{48,240},{56,2... | collective-permute-start | bytes 786440 | tf_op jit(solution)/shard_map/ppermute | solution.py:236
  87.9 0.5 collective-permute-start.4
  88.5 0.4 collective-permute-start.11
  88.8 4.2 %collective-permute-done.8 = bf16[1024,128]{1,0:T(8,128)(2,1)S(1)} collective-permute-done((bf16[1024,128]{1,0:T(8,128)(2,1)S(1)}, bf16[1024,128]{1,0:T(8,128)(2,1)S(1)}, u32[]{:S(2)}, u32[]{:S(2)}) %collective-permute-start.8) | collective-permute-done | bytes 262176 | tf_op jit(solution)/shard_map/ppermute | solution.py:236
  93.0 3.4 %collective-permute-done.7 = bf16[1024,128]{1,0:T(8,128)(2,1)S(1)} collective-permute-done((bf16[1024,128]{1,0:T(8,128)(2,1)S(1)}, bf16[1024,128]{1,0:T(8,128)(2,1)S(1)}, u32[]{:S(2)}, u32[]{:S(2)}) %collective-permute-start.7) | collective-permute-done | bytes 262176 | tf_op jit(solution)/shard_map/ppermute | solution.py:236
  96.5 1.4 %gram_near.1 = (bf16[384,2048]{1,0:T(8,128)(2,1)S(1)}, bf16[3,384,256]{2,1,0:T(8,128)(2,1)S(1)}) custom-call(bf16[2048,128]{1,0:T(8,128)(2,1)S(1)} %bitcast.13, bf16[2048,128]{1,0:T(8,128)(2,1)S(1)} %collective-permute-done.refs_1_.up, bf16[2048,128]{1,0:T(8,128)(2,1)S(1)} %collective-permute-done.1.refs_2_.down, ...), custom_call_target="tpu_custom_call" | custom-call | flops 1207959552 | bytes 8388608 | tf_op jit(solution)/shard_map/gram_near/pallas_call | solution.py:135
  97.9 0.6 gram_side.1
  98.6 1.4 %gram_far.1 = bf16[8,512,128]{2,1,0:T(8,128)(2,1)S(1)} custom-call(s32[3]{0:T(128)S(1)} %pad_add_fusion.at, bf16[3,384,256]{2,1,0:T(8,128)(2,1)S(1)} %get-tuple-element.13.near_ref, bf16[3,128,256]{2,1,0:T(8,128)(2,1)S(1)} %get-tuple-element.18.side_ref, bf16[384,2048]{1,0:T(8,128)(2,1)S(1)} %get-tuple-element.17.refs_7_.left, ...), custom_call_target="tpu_custom_call" | custom-call | flops 536870912 | bytes 8388608 | tf_op jit(solution)/shard_map/gram_far/pallas_call | solution.py:192
  100.0 32.4 %all_to_all.11.parts_ref = bf16[8,512,128]{2,1,0:T(8,128)(2,1)S(1)} all-to-all(bf16[8,512,128]{2,1,0:T(8,128)(2,1)S(1)} %gram_far.1), channel_id=1, replica_groups={{0,32,72,104,144,176,216,248},{8,40,80,112,152,184,192,224},{16,48,88,1..., dimensions={0} | all-to-all | bytes 2097152 | tf_op jit(solution)/shard_map/all_to_all | solution.py:257
  132.4 0.9 finish.1
  (20 shorter events, 0.2 us)
Async XLA Ops:
  0.1 1.6 %copy-start = (bf16[2048,512]{1,0:T(8,128)(2,1)S(1)}, bf16[2048,512]{1,0:T(8,128)(2,1)}, u32[]{:S(2)}) copy-start(bf16[2048,512]{1,0:T(8,128)(2,1)} %param.3) | copy-start | bytes 6291460
  1.7 0.7 copy-start.1
  3.4 60.0 %copy-start.2 = (s32[128]{0:T(128)S(1)}, s32[128]{0:T(128)}, u32[]{:S(2)}) copy-start(s32[128]{0:T(128)} %picks_ref.1) | copy-start | bytes 1540
  66.0 13.3 %collective-permute-start = (bf16[2048,128]{1,0:T(8,128)(2,1)S(1)}, bf16[2048,128]{1,0:T(8,128)(2,1)S(1)}, u32[]{:S(2)}, u32[]{:S(2)}) collective-permute-start(bf16[2048,128]{1,0:T(8,128)(2,1)S(1)} %bitcast.8), channel_id=1, source_target_pairs={{0,2},{1,3},{2,4},{3,5},{4,6},{5,7},{6,0},{7,1},{8,10},{9,11},{10,... | collective-permute-start | bytes 1572872 | tf_op jit(solution)/shard_map/ppermute | solution.py:233
  67.5 11.8 %collective-permute-start.1 = (bf16[2048,128]{1,0:T(8,128)(2,1)S(1)}, bf16[2048,128]{1,0:T(8,128)(2,1)S(1)}, u32[]{:S(2)}, u32[]{:S(2)}) collective-permute-start(bf16[2048,128]{1,0:T(8,128)(2,1)S(1)} %bitcast.9), channel_id=1, source_target_pairs={{0,6},{1,7},{2,0},{3,1},{4,2},{5,3},{6,4},{7,5},{8,14},{9,15},{10,... | collective-permute-start | bytes 1572872 | tf_op jit(solution)/shard_map/ppermute | solution.py:233
  69.3 10.0 %collective-permute-start.2 = (bf16[2048,128]{1,0:T(8,128)(2,1)S(1)}, bf16[2048,128]{1,0:T(8,128)(2,1)S(1)}, u32[]{:S(2)}, u32[]{:S(2)}) collective-permute-start(bf16[2048,128]{1,0:T(8,128)(2,1)S(1)} %bitcast.10), channel_id=1, source_target_pairs={{0,1},{1,0},{2,3},{3,2},{4,5},{5,4},{6,7},{7,6},{8,9},{9,8},{10,11... | collective-permute-start | bytes 1572872 | tf_op jit(solution)/shard_map/ppermute | solution.py:239
  69.3 15.5 %collective-permute-start.5 = (bf16[2048,128]{1,0:T(8,128)(2,1)S(1)}, bf16[2048,128]{1,0:T(8,128)(2,1)S(1)}, u32[]{:S(2)}, u32[]{:S(2)}) collective-permute-start(bf16[2048,128]{1,0:T(8,128)(2,1)S(1)} %bitcast.11), channel_id=1, source_target_pairs={{0,64},{8,72},{16,80},{24,88},{32,96},{40,104},{48,112},{56,120},{... | collective-permute-start | bytes 1572872 | tf_op jit(solution)/shard_map/ppermute | solution.py:236
  69.8 15.0 %collective-permute-start.6 = (bf16[2048,128]{1,0:T(8,128)(2,1)S(1)}, bf16[2048,128]{1,0:T(8,128)(2,1)S(1)}, u32[]{:S(2)}, u32[]{:S(2)}) collective-permute-start(bf16[2048,128]{1,0:T(8,128)(2,1)S(1)} %bitcast.12), channel_id=1, source_target_pairs={{0,192},{8,200},{16,208},{24,216},{32,224},{40,232},{48,240},{56,2... | collective-permute-start | bytes 1572872 | tf_op jit(solution)/shard_map/ppermute | solution.py:236
  79.3 8.6 %collective-permute-start.9 = (bf16[1024,128]{1,0:T(8,128)(2,1)S(1)}, bf16[1024,128]{1,0:T(8,128)(2,1)S(1)}, u32[]{:S(2)}, u32[]{:S(2)}) collective-permute-start(bf16[1024,128]{1,0:T(8,128)(2,1)S(1)} %get-tuple-element.14.refs_0_), channel_id=1, source_target_pairs={{0,2},{1,3},{2,4},{3,5},{4,6},{5,7},{6,0},{7,1},{8,10},{9,11},{10,... | collective-permute-start | bytes 786440 | tf_op jit(solution)/shard_map/ppermute | solution.py:233
  80.9 7.5 %collective-permute-start.10 = (bf16[1024,128]{1,0:T(8,128)(2,1)S(1)}, bf16[1024,128]{1,0:T(8,128)(2,1)S(1)}, u32[]{:S(2)}, u32[]{:S(2)}) collective-permute-start(bf16[1024,128]{1,0:T(8,128)(2,1)S(1)} %get-tuple-element.20), channel_id=1, source_target_pairs={{0,6},{1,7},{2,0},{3,1},{4,2},{5,3},{6,4},{7,5},{8,14},{9,15},{10,... | collective-permute-start | bytes 786440 | tf_op jit(solution)/shard_map/ppermute | solution.py:233
  84.9 8.2 %collective-permute-start.8 = (bf16[1024,128]{1,0:T(8,128)(2,1)S(1)}, bf16[1024,128]{1,0:T(8,128)(2,1)S(1)}, u32[]{:S(2)}, u32[]{:S(2)}) collective-permute-start(bf16[1024,128]{1,0:T(8,128)(2,1)S(1)} %get-tuple-element.16), channel_id=1, source_target_pairs={{0,192},{8,200},{16,208},{24,216},{32,224},{40,232},{48,240},{56,2... | collective-permute-start | bytes 786440 | tf_op jit(solution)/shard_map/ppermute | solution.py:236
  87.9 8.5 %collective-permute-start.7 = (bf16[1024,128]{1,0:T(8,128)(2,1)S(1)}, bf16[1024,128]{1,0:T(8,128)(2,1)S(1)}, u32[]{:S(2)}, u32[]{:S(2)}) collective-permute-start(bf16[1024,128]{1,0:T(8,128)(2,1)S(1)} %get-tuple-element.15), channel_id=1, source_target_pairs={{0,64},{8,72},{16,80},{24,88},{32,96},{40,104},{48,112},{56,120},{... | collective-permute-start | bytes 786440 | tf_op jit(solution)/shard_map/ppermute | solution.py:236
  87.9 8.6 %collective-permute-start.3 = (bf16[2048,128]{1,0:T(8,128)(2,1)S(1)}, bf16[2048,128]{1,0:T(8,128)(2,1)S(1)}, u32[]{:S(2)}, u32[]{:S(2)}) collective-permute-start(bf16[2048,128]{1,0:T(8,128)(2,1)S(1)} %collective-permute-done.refs_1_.up), channel_id=1, source_target_pairs={{0,1},{1,0},{2,3},{3,2},{4,5},{5,4},{6,7},{7,6},{8,9},{9,8},{10,11... | collective-permute-start | bytes 1572872 | tf_op jit(solution)/shard_map/ppermute | solution.py:239
  87.9 8.6 %collective-permute-start.4 = (bf16[2048,128]{1,0:T(8,128)(2,1)S(1)}, bf16[2048,128]{1,0:T(8,128)(2,1)S(1)}, u32[]{:S(2)}, u32[]{:S(2)}) collective-permute-start(bf16[2048,128]{1,0:T(8,128)(2,1)S(1)} %collective-permute-done.1.refs_2_.down), channel_id=1, source_target_pairs={{0,1},{1,0},{2,3},{3,2},{4,5},{5,4},{6,7},{7,6},{8,9},{9,8},{10,11... | collective-permute-start | bytes 1572872 | tf_op jit(solution)/shard_map/ppermute | solution.py:239
  88.5 10.1 %collective-permute-start.11 = (bf16[2048,128]{1,0:T(8,128)(2,1)S(1)}, bf16[2048,128]{1,0:T(8,128)(2,1)S(1)}, u32[]{:S(2)}, u32[]{:S(2)}) collective-permute-start(bf16[2048,128]{1,0:T(8,128)(2,1)S(1)} %constant_dynamic-update-slice_fusion.own), channel_id=1, source_target_pairs={{0,1},{1,0},{2,3},{3,2},{4,5},{5,4},{6,7},{7,6},{8,9},{9,8},{10,11... | collective-permute-start | bytes 1572872 | tf_op jit(solution)/shard_map/ppermute | solution.py:239

commit v11 on v9

--- a/solution.py
+++ b/solution.py
@@ -93,24 +93,29 @@
 NEAR = (0, 1, 3)
 
 
-def halves_kernel(*refs):
-    pieces, outs = refs[:4], refs[-4:]
-    depth = outs[0].shape[0]
-    for i, out in enumerate(outs):
-        out[...] = pieces[i][pl.ds(i % 2 * depth, depth), :]
-
-
-def halves(pieces, after):
-    part = jax.ShapeDtypeStruct((pieces[0].shape[0] // 2, LANES), pieces[0].dtype)
-    return pl.pallas_call(
-        halves_kernel,
-        in_specs=[LOCAL] * (4 + len(after)),
-        out_specs=[LOCAL] * 4,
-        out_shape=[part] * 4,
+def onward_kernel(at, x_up, x_down, y_up, y_down, home, far_x, far_y):
+    @pl.when(at[1] == 0)
+    def _():
+        far_x[...] = x_up[...]
+        far_y[...] = y_up[...]
+
+    @pl.when(at[1] != 0)
+    def _():
+        far_x[...] = x_down[...]
+        far_y[...] = y_down[...]
+
+
+def onward(at, x_up, x_down, y_up, y_down, home):
+    piece = jax.ShapeDtypeStruct(x_up.shape, x_up.dtype)
+    return pl.pallas_call(
+        onward_kernel,
+        in_specs=[SCALARS] + [LOCAL] * 5,
+        out_specs=[LOCAL] * 2,
+        out_shape=[piece] * 2,
         compiler_params=pltpu.CompilerParams(vmem_limit_bytes=16 * MIB),
         cost_estimate=pl.CostEstimate(flops=0, bytes_accessed=2 * MIB, transcendentals=0),
-        name="halves",
-    )(*pieces, *after)
+        name="onward",
+    )(at, x_up, x_down, y_up, y_down, home)
 
 
 def pair_dot(left, own, other):
@@ -147,26 +152,38 @@
 
 
 def side_kernel(*refs):
-    col, own, other, (last, out_ref) = refs[0], refs[1:4], refs[4:7], refs[7:]
-    last[...] = col[...].T
+    last, own, other, out_ref = refs[0], refs[1:4], refs[4:7], refs[7]
     for j in range(len(NEAR)):
         out_ref[j] = pair_dot(last[...], own[j][...], other[j][...]).astype(out_ref.dtype)
 
 
-def gram_side(col, own, other):
-    depth, near = col.shape[0], len(NEAR)
+def gram_side(last, own, other):
+    depth, near = last.shape[1], len(NEAR)
     return pl.pallas_call(
         side_kernel,
         in_specs=[LOCAL] * 7,
-        out_specs=[LOCAL] * 2,
-        out_shape=[
-            jax.ShapeDtypeStruct((LANES, depth), jnp.bfloat16),
-            jax.ShapeDtypeStruct((near, LANES, NCORE * LANES), jnp.bfloat16),
-        ],
+        out_specs=LOCAL,
+        out_shape=jax.ShapeDtypeStruct((near, LANES, NCORE * LANES), jnp.bfloat16),
         compiler_params=pltpu.CompilerParams(vmem_limit_bytes=16 * MIB),
         cost_estimate=cost(depth, near),
         name="gram_side",
-    )(col, *own, *other)
+    )(last, *own, *other)
+
+
+def turn_kernel(col, out_ref):
+    out_ref[...] = col[...].T
+
+
+def turn(col):
+    return pl.pallas_call(
+        turn_kernel,
+        in_specs=[LOCAL],
+        out_specs=LOCAL,
+        out_shape=jax.ShapeDtypeStruct(col.shape[::-1], col.dtype),
+        compiler_params=pltpu.CompilerParams(vmem_limit_bytes=16 * MIB),
+        cost_estimate=pl.CostEstimate(flops=0, bytes_accessed=MIB, transcendentals=0),
+        name="turn",
+    )(col)
 
 
 def far_kernel(at, near_ref, side_ref, left, last, own, other, out_ref):
@@ -235,18 +252,31 @@
     def along_y(value, step):
         return lax.ppermute(value, "dp", [(i, (i + NZ * step) % (NY * NZ)) for i in range(NY * NZ)])
 
+    def ring(value, axis):
+        pairs = []
+        for i in range(NY * NZ * NX * NCORE):
+            (here, rest), down = divmod(i, NZ * NX * NCORE), i % NCORE
+            step = 1 - 2 * down
+            if axis == "y":
+                to = (here + step) % NY * NZ * NX * NCORE + rest
+            else:
+                side = (i // NCORE % NX + step) % NX
+                to = i // (NX * NCORE) * (NX * NCORE) + side * NCORE + down
+            pairs.append((i, to))
+        return lax.ppermute(value, ("dp", "col"), pairs)
+
     def swap(value):
         return lax.ppermute(value, "col", [(i, i ^ 1) for i in range(NX * NCORE)])
 
     x_up, x_down = along_x(sketch, 1), along_x(sketch, -1)
     y_up, y_down = along_y(sketch, 1), along_y(sketch, -1)
     home = swap(sketch)
-    x_low, x_high, y_low, y_high = halves((x_up, x_down, y_up, y_down), (home,))
-    x_far = jnp.concatenate([along_x(x_low, 1), along_x(x_high, -1)])
-    y_far = jnp.concatenate([along_y(y_low, 1), along_y(y_high, -1)])
+    far_x, far_y = onward(at, x_up, x_down, y_up, y_down, home)
+    x_far, y_far = ring(far_x, "x"), ring(far_y, "y")
     own, other = (sketch, x_up, x_down), (home, swap(x_up), swap(x_down))
     left, near = gram_near((sketch, y_up, y_down), own, other)
-    last, side = gram_side(y_far, own, other)
+    last = turn(y_far)
+    side = gram_side(last, own, other)
     partial = gram_far(at, near, side, left, last, x_far, swap(x_far))
 
     groups = [

time: 131 us -> 133 us (1.015)
  starting transfers between devices: 12.4 us -> 8.81 us
  waiting for transfers between devices: 15.9 us -> 19.3 us
    ppermute x0 -> x2, waiting for transfers between devices: none -> 9.87 us  [ring(): return lax.ppermute(value, ('dp', 'col'), pairs)]
    ppermute x4 -> x2, waiting for transfers between devices: 10.7 us -> 6.78 us  [along_y(): lax.ppermute(value, 'dp', [(i, (i + NZ * step) % (NY * NZ)) for i in rang...]
    ppermute x4 -> x2, starting transfers between devices: 6.55 us -> 3.24 us  [along_x(): lax.ppermute(value, 'col', [(i, (i + NCORE * step) % (NX * NCORE)) for i...]
    ppermute x4 -> x2, waiting for transfers between devices: 5.24 us -> 2.68 us  [along_x(): lax.ppermute(value, 'col', [(i, (i + NCORE * step) % (NX * NCORE)) for i...]
    ppermute x4 -> x2, starting transfers between devices: 5.34 us -> 3.31 us  [along_y(): lax.ppermute(value, 'dp', [(i, (i + NZ * step) % (NY * NZ)) for i in rang...]
    ppermute x0 -> x2, starting transfers between devices: none -> 1.74 us  [ring(): return lax.ppermute(value, ('dp', 'col'), pairs)]
    all_to_all x1, blocking collectives: 32.1 us -> 33.4 us  [on_device(): lax.all_to_all(partial, 'dp', split_axis=0, concat_axis=0, axis_index_gro...]
  transfers between devices with their start and end apart: 12 -> 10, of which waited for: 6 -> 4; matrix products, arithmetic and copies ran while one was open for 0% -> 0% of each run, Pallas kernels for 2% -> 2%
where the time goes in v11:
time: 133 us
  blocking collectives  93.4 us (70%)
  waiting for transfers between devices  19.3 us (15%)
  starting transfers between devices  8.81 us (7%)
  Pallas kernels  8.67 us (7%)
  local copies, waits for them, and re-layouts  2.29 us (2%)
    all_to_all x1, blocking collectives, on_device(): lax.all_to_all(outgoing, 'dp', split_axis=0, concat_axis=0, tiled=True)  60 us
    all_to_all x1, blocking collectives, on_device(): lax.all_to_all(partial, 'dp', split_axis=0, concat_axis=0, axis_index_gro...  33.4 us
    ppermute x2, waiting for transfers between devices, ring(): return lax.ppermute(value, ('dp', 'col'), pairs)  9.87 us
    ppermute x2, waiting for transfers between devices, along_y(): lax.ppermute(value, 'dp', [(i, (i + NZ * step) % (NY * NZ)) for i in rang...  6.78 us
    ppermute x2, starting transfers between devices, along_y(): lax.ppermute(value, 'dp', [(i, (i + NZ * step) % (NY * NZ)) for i in rang...  3.31 us
    ppermute x2, starting transfers between devices, along_x(): lax.ppermute(value, 'col', [(i, (i + NCORE * step) % (NX * NCORE)) for i...  3.24 us
    ppermute x2, waiting for transfers between devices, along_x(): lax.ppermute(value, 'col', [(i, (i + NCORE * step) % (NX * NCORE)) for i...  2.68 us
  transfers between devices with their start and end apart: 10, of which 4 were waited for; matrix products, arithmetic and copies ran while one was open for 0% of the time, Pallas kernels for 2%

profile of v11, /device:TPU:64, one launch (start us, length us, event | category | flops | bytes accessed | tf_op | source)
XLA Modules:
  0.0 132.7 jit_solution(2302287636152689312)
XLA Ops:
  0.0 0.1 pad_add_fusion.at
  0.1 1.6 %copy-done = bf16[2048,512]{1,0:T(8,128)(2,1)S(1)} copy-done((bf16[2048,512]{1,0:T(8,128)(2,1)S(1)}, bf16[2048,512]{1,0:T(8,128)(2,1)}, u32[]{:S(2)}) %copy-start) | copy-done | bytes 2097176
  1.7 0.7 copy-done.1
  2.4 1.0 pack.1
  3.4 0.0 copy-start.2
  3.4 60.0 %all_to_all.10 = bf16[32,16,16,128]{3,2,1,0:T(8,128)(2,1)S(1)} all-to-all(bf16[32,16,16,128]{3,2,1,0:T(8,128)(2,1)S(1)} %bitcast.9), channel_id=1, replica_groups=mesh['dp'=32,'col'=8] {'dp'}, dimensions={0} | all-to-all | bytes 4194304 | tf_op jit(solution)/shard_map/all_to_all | solution.py:246
  63.4 2.6 %mix.1 = bf16[128,16,128]{2,1,0:T(8,128)(2,1)S(1)} custom-call(s32[128]{0:T(128)S(1)} %copy-done.2, bf16[512,16,128]{2,1,0:T(8,128)(2,1)S(1)} %bitcast.8), custom_call_target="tpu_custom_call" | custom-call | tf_op jit(solution)/shard_map/mix/pallas_call | solution.py:82
  66.0 0.6 collective-permute-start
  66.6 2.7 %collective-permute-start.1 = (bf16[2048,128]{1,0:T(8,128)(2,1)S(1)}, bf16[2048,128]{1,0:T(8,128)(2,1)S(1)}, u32[]{:S(2)}, u32[]{:S(2)}) collective-permute-start(bf16[2048,128]{1,0:T(8,128)(2,1)S(1)} %bitcast.11), channel_id=1, source_target_pairs={{0,192},{8,200},{16,208},{24,216},{32,224},{40,232},{48,240},{56,2... | collective-permute-start | bytes 1572872 | tf_op jit(solution)/shard_map/ppermute | solution.py:253
  69.3 1.5 %collective-permute-start.2 = (bf16[2048,128]{1,0:T(8,128)(2,1)S(1)}, bf16[2048,128]{1,0:T(8,128)(2,1)S(1)}, u32[]{:S(2)}, u32[]{:S(2)}) collective-permute-start(bf16[2048,128]{1,0:T(8,128)(2,1)S(1)} %bitcast.12), channel_id=1, source_target_pairs={{0,2},{1,3},{2,4},{3,5},{4,6},{5,7},{6,0},{7,1},{8,10},{9,11},{10,... | collective-permute-start | bytes 1572872 | tf_op jit(solution)/shard_map/ppermute | solution.py:250
  70.8 1.7 %collective-permute-start.3 = (bf16[2048,128]{1,0:T(8,128)(2,1)S(1)}, bf16[2048,128]{1,0:T(8,128)(2,1)S(1)}, u32[]{:S(2)}, u32[]{:S(2)}) collective-permute-start(bf16[2048,128]{1,0:T(8,128)(2,1)S(1)} %bitcast.13), channel_id=1, source_target_pairs={{0,6},{1,7},{2,0},{3,1},{4,2},{5,3},{6,4},{7,5},{8,14},{9,15},{10,... | collective-permute-start | bytes 1572872 | tf_op jit(solution)/shard_map/ppermute | solution.py:250
  72.5 6.8 %collective-permute-done.refs_1_.y_up = bf16[2048,128]{1,0:T(8,128)(2,1)S(1)} collective-permute-done((bf16[2048,128]{1,0:T(8,128)(2,1)S(1)}, bf16[2048,128]{1,0:T(8,128)(2,1)S(1)}, u32[]{:S(2)}, u32[]{:S(2)}) %collective-permute-start) | collective-permute-done | bytes 524320 | tf_op jit(solution)/shard_map/ppermute | solution.py:253
  79.3 2.7 %collective-permute-done.2.refs_4_.x_up.refs_2_ = bf16[2048,128]{1,0:T(8,128)(2,1)S(1)} collective-permute-done((bf16[2048,128]{1,0:T(8,128)(2,1)S(1)}, bf16[2048,128]{1,0:T(8,128)(2,1)S(1)}, u32[]{:S(2)}, u32[]{:S(2)}) %collective-permute-start.2) | collective-permute-done | bytes 524320 | tf_op jit(solution)/shard_map/ppermute | solution.py:250
  82.0 0.6 onward.1
  82.6 1.7 %collective-permute-start.8 = (bf16[2048,128]{1,0:T(8,128)(2,1)S(1)}, bf16[2048,128]{1,0:T(8,128)(2,1)S(1)}, u32[]{:S(2)}, u32[]{:S(2)}) collective-permute-start(bf16[2048,128]{1,0:T(8,128)(2,1)S(1)} %get-tuple-element.12), channel_id=1, source_target_pairs={{0,2},{1,7},{2,4},{3,1},{4,6},{5,3},{6,0},{7,5},{8,10},{9,15},{10,... | collective-permute-start | bytes 1572872 | tf_op jit(solution)/shard_map/ppermute | solution.py:266
  84.4 0.5 collective-permute-start.6
  84.9 8.2 %collective-permute-done.8.own = bf16[2048,128]{1,0:T(8,128)(2,1)S(1)} collective-permute-done((bf16[2048,128]{1,0:T(8,128)(2,1)S(1)}, bf16[2048,128]{1,0:T(8,128)(2,1)S(1)}, u32[]{:S(2)}, u32[]{:S(2)}) %collective-permute-start.8) | collective-permute-done | bytes 524320 | tf_op jit(solution)/shard_map/ppermute | solution.py:266
  93.1 1.7 %collective-permute-done.7.col = bf16[2048,128]{1,0:T(8,128)(2,1)S(1)} collective-permute-done((bf16[2048,128]{1,0:T(8,128)(2,1)S(1)}, bf16[2048,128]{1,0:T(8,128)(2,1)S(1)}, u32[]{:S(2)}, u32[]{:S(2)}) %collective-permute-start.7) | collective-permute-done | bytes 524320 | tf_op jit(solution)/shard_map/ppermute | solution.py:266
  94.7 0.2 turn.1.refs_0_.last
  94.9 0.6 gram_side.1.side_ref
  95.5 1.4 %gram_near.1 = (bf16[384,2048]{1,0:T(8,128)(2,1)S(1)}, bf16[3,384,256]{2,1,0:T(8,128)(2,1)S(1)}) custom-call(bf16[2048,128]{1,0:T(8,128)(2,1)S(1)} %bitcast.16, bf16[2048,128]{1,0:T(8,128)(2,1)S(1)} %collective-permute-done.refs_1_.y_up, bf16[2048,128]{1,0:T(8,128)(2,1)S(1)} %collective-permute-done.1.refs_2_.y_down, bf16[2048,128]{1,0:T(8,128)(2,1)S(1)} %bitcast.17, ...), custom_call_target="tpu_custom_call" | custom-call | flops 1207959552 | bytes 8388608 | tf_op jit(solution)/shard_map/gram_near/pallas_call | solution.py:140
  97.0 1.4 %gram_far.1 = bf16[8,512,128]{2,1,0:T(8,128)(2,1)S(1)} custom-call(s32[3]{0:T(128)S(1)} %pad_add_fusion.at, bf16[3,384,256]{2,1,0:T(8,128)(2,1)S(1)} %get-tuple-element.9.near_ref, bf16[3,128,256]{2,1,0:T(8,128)(2,1)S(1)} %gram_side.1.side_ref, bf16[384,2048]{1,0:T(8,128)(2,1)S(1)} %get-tuple-element.11.left, bf16[128,2048]{1,0:T(8,128)(2,1)S(1)} %turn.1.refs_0_.last, ...), custom_call_target="tpu_custom_call" | custom-call | flops 536870912 | bytes 8388608 | tf_op jit(solution)/shard_map/gram_far/pallas_call | solution.py:209
  98.4 33.4 %all_to_all.11.parts_ref = bf16[8,512,128]{2,1,0:T(8,128)(2,1)S(1)} all-to-all(bf16[8,512,128]{2,1,0:T(8,128)(2,1)S(1)} %gram_far.1), channel_id=1, replica_groups={{0,32,72,104,144,176,216,248},{8,40,80,112,152,184,192,224},{16,48,88,1..., dimensions={0} | all-to-all | bytes 2097152 | tf_op jit(solution)/shard_map/all_to_all | solution.py:286
  131.8 0.9 finish.1
  (13 shorter events, 0.0 us)
Async XLA Ops:
  0.1 1.6 %copy-start = (bf16[2048,512]{1,0:T(8,128)(2,1)S(1)}, bf16[2048,512]{1,0:T(8,128)(2,1)}, u32[]{:S(2)}) copy-start(bf16[2048,512]{1,0:T(8,128)(2,1)} %param.3) | copy-start | bytes 6291460
  1.7 0.7 copy-start.1
  3.4 60.0 %copy-start.2 = (s32[128]{0:T(128)S(1)}, s32[128]{0:T(128)}, u32[]{:S(2)}) copy-start(s32[128]{0:T(128)} %picks_ref.1) | copy-start | bytes 1540
  66.0 13.3 %collective-permute-start = (bf16[2048,128]{1,0:T(8,128)(2,1)S(1)}, bf16[2048,128]{1,0:T(8,128)(2,1)S(1)}, u32[]{:S(2)}, u32[]{:S(2)}) collective-permute-start(bf16[2048,128]{1,0:T(8,128)(2,1)S(1)} %bitcast.10), channel_id=1, source_target_pairs={{0,64},{8,72},{16,80},{24,88},{32,96},{40,104},{48,112},{56,120},{... | collective-permute-start | bytes 1572872 | tf_op jit(solution)/shard_map/ppermute | solution.py:253
  66.6 12.7 %collective-permute-start.1 = (bf16[2048,128]{1,0:T(8,128)(2,1)S(1)}, bf16[2048,128]{1,0:T(8,128)(2,1)S(1)}, u32[]{:S(2)}, u32[]{:S(2)}) collective-permute-start(bf16[2048,128]{1,0:T(8,128)(2,1)S(1)} %bitcast.11), channel_id=1, source_target_pairs={{0,192},{8,200},{16,208},{24,216},{32,224},{40,232},{48,240},{56,2... | collective-permute-start | bytes 1572872 | tf_op jit(solution)/shard_map/ppermute | solution.py:253
  69.3 12.7 %collective-permute-start.2 = (bf16[2048,128]{1,0:T(8,128)(2,1)S(1)}, bf16[2048,128]{1,0:T(8,128)(2,1)S(1)}, u32[]{:S(2)}, u32[]{:S(2)}) collective-permute-start(bf16[2048,128]{1,0:T(8,128)(2,1)S(1)} %bitcast.12), channel_id=1, source_target_pairs={{0,2},{1,3},{2,4},{3,5},{4,6},{5,7},{6,0},{7,1},{8,10},{9,11},{10,... | collective-permute-start | bytes 1572872 | tf_op jit(solution)/shard_map/ppermute | solution.py:250
  70.8 11.2 %collective-permute-start.3 = (bf16[2048,128]{1,0:T(8,128)(2,1)S(1)}, bf16[2048,128]{1,0:T(8,128)(2,1)S(1)}, u32[]{:S(2)}, u32[]{:S(2)}) collective-permute-start(bf16[2048,128]{1,0:T(8,128)(2,1)S(1)} %bitcast.13), channel_id=1, source_target_pairs={{0,6},{1,7},{2,0},{3,1},{4,2},{5,3},{6,4},{7,5},{8,14},{9,15},{10,... | collective-permute-start | bytes 1572872 | tf_op jit(solution)/shard_map/ppermute | solution.py:250
  72.5 9.5 %collective-permute-start.4 = (bf16[2048,128]{1,0:T(8,128)(2,1)S(1)}, bf16[2048,128]{1,0:T(8,128)(2,1)S(1)}, u32[]{:S(2)}, u32[]{:S(2)}) collective-permute-start(bf16[2048,128]{1,0:T(8,128)(2,1)S(1)} %bitcast.14), channel_id=1, source_target_pairs={{0,1},{1,0},{2,3},{3,2},{4,5},{5,4},{6,7},{7,6},{8,9},{9,8},{10,11... | collective-permute-start | bytes 1572872 | tf_op jit(solution)/shard_map/ppermute | solution.py:269
  82.6 10.5 %collective-permute-start.8 = (bf16[2048,128]{1,0:T(8,128)(2,1)S(1)}, bf16[2048,128]{1,0:T(8,128)(2,1)S(1)}, u32[]{:S(2)}, u32[]{:S(2)}) collective-permute-start(bf16[2048,128]{1,0:T(8,128)(2,1)S(1)} %get-tuple-element.12), channel_id=1, source_target_pairs={{0,2},{1,7},{2,4},{3,1},{4,6},{5,3},{6,0},{7,5},{8,10},{9,15},{10,... | collective-permute-start | bytes 1572872 | tf_op jit(solution)/shard_map/ppermute | solution.py:266
  84.3 10.4 %collective-permute-start.7 = (bf16[2048,128]{1,0:T(8,128)(2,1)S(1)}, bf16[2048,128]{1,0:T(8,128)(2,1)S(1)}, u32[]{:S(2)}, u32[]{:S(2)}) collective-permute-start(bf16[2048,128]{1,0:T(8,128)(2,1)S(1)} %get-tuple-element.10), channel_id=1, source_target_pairs={{0,64},{1,193},{2,66},{3,195},{4,68},{5,197},{6,70},{7,199},{8,72}... | collective-permute-start | bytes 1572872 | tf_op jit(solution)/shard_map/ppermute | solution.py:266
  84.3 10.6 %collective-permute-start.5 = (bf16[2048,128]{1,0:T(8,128)(2,1)S(1)}, bf16[2048,128]{1,0:T(8,128)(2,1)S(1)}, u32[]{:S(2)}, u32[]{:S(2)}) collective-permute-start(bf16[2048,128]{1,0:T(8,128)(2,1)S(1)} %collective-permute-done.2.refs_4_.x_up.refs_2_), channel_id=1, source_target_pairs={{0,1},{1,0},{2,3},{3,2},{4,5},{5,4},{6,7},{7,6},{8,9},{9,8},{10,11... | collective-permute-start | bytes 1572872 | tf_op jit(solution)/shard_map/ppermute | solution.py:269
  84.4 10.6 %collective-permute-start.6 = (bf16[2048,128]{1,0:T(8,128)(2,1)S(1)}, bf16[2048,128]{1,0:T(8,128)(2,1)S(1)}, u32[]{:S(2)}, u32[]{:S(2)}) collective-permute-start(bf16[2048,128]{1,0:T(8,128)(2,1)S(1)} %collective-permute-done.3.refs_5_.x_down.refs_3_), channel_id=1, source_target_pairs={{0,1},{1,0},{2,3},{3,2},{4,5},{5,4},{6,7},{7,6},{8,9},{9,8},{10,11... | collective-permute-start | bytes 1572872 | tf_op jit(solution)/shard_map/ppermute | solution.py:269
  93.1 3.9 %collective-permute-start.9 = (bf16[2048,128]{1,0:T(8,128)(2,1)S(1)}, bf16[2048,128]{1,0:T(8,128)(2,1)S(1)}, u32[]{:S(2)}, u32[]{:S(2)}) collective-permute-start(bf16[2048,128]{1,0:T(8,128)(2,1)S(1)} %collective-permute-done.8.own), channel_id=1, source_target_pairs={{0,1},{1,0},{2,3},{3,2},{4,5},{5,4},{6,7},{7,6},{8,9},{9,8},{10,11... | collective-permute-start | bytes 1572872 | tf_op jit(solution)/shard_map/ppermute | solution.py:269

commit v12 on v9

--- a/solution.py
+++ b/solution.py
@@ -113,6 +113,24 @@
     )(*pieces, *after)
 
 
+def join_kernel(first, second, *refs):
+    joined, depth = refs[-1], first.shape[0]
+    joined[pl.ds(0, depth), :] = first[...]
+    joined[pl.ds(depth, depth), :] = second[...]
+
+
+def join(first, second, *after):
+    return pl.pallas_call(
+        join_kernel,
+        in_specs=[LOCAL] * (2 + len(after)),
+        out_specs=LOCAL,
+        out_shape=jax.ShapeDtypeStruct((2 * first.shape[0], LANES), first.dtype),
+        compiler_params=pltpu.CompilerParams(vmem_limit_bytes=16 * MIB),
+        cost_estimate=pl.CostEstimate(flops=0, bytes_accessed=MIB, transcendentals=0),
+        name="join",
+    )(first, second, *after)
+
+
 def pair_dot(left, own, other):
     return jnp.dot(left, jnp.concatenate([own, other], axis=1), preferred_element_type=jnp.float32)
 
@@ -242,10 +260,10 @@
     y_up, y_down = along_y(sketch, 1), along_y(sketch, -1)
     home = swap(sketch)
     x_low, x_high, y_low, y_high = halves((x_up, x_down, y_up, y_down), (home,))
-    x_far = jnp.concatenate([along_x(x_low, 1), along_x(x_high, -1)])
     y_far = jnp.concatenate([along_y(y_low, 1), along_y(y_high, -1)])
     own, other = (sketch, x_up, x_down), (home, swap(x_up), swap(x_down))
     left, near = gram_near((sketch, y_up, y_down), own, other)
+    x_far = join(along_x(x_low, 1), along_x(x_high, -1), left)
     last, side = gram_side(y_far, own, other)
     partial = gram_far(at, near, side, left, last, x_far, swap(x_far))
 

time: 131 us -> 132 us (level); the launches traced: 131 us -> 130 us
    ppermute x4, waiting for transfers between devices: 10.7 us -> 8.15 us  [along_y(): lax.ppermute(value, 'dp', [(i, (i + NZ * step) % (NY * NZ)) for i in rang...]
    ppermute x4, waiting for transfers between devices: 5.24 us -> 6.78 us  [along_x(): lax.ppermute(value, 'col', [(i, (i + NCORE * step) % (NX * NCORE)) for i...]
  transfers between devices with their start and end apart: 12 -> 12, of which waited for: 6 -> 4; matrix products, arithmetic and copies ran while one was open for 0% -> 0% of each run, Pallas kernels for 2% -> 2%
where the time goes in v12:
time: 132 us; the launch traced here: 130 us
  blocking collectives  91 us (69%)
  waiting for transfers between devices  14.9 us (11%)
  starting transfers between devices  13.4 us (10%)
  Pallas kernels  8.02 us (6%)
  local copies, waits for them, and re-layouts  2.29 us (2%)
    all_to_all x1, blocking collectives, on_device(): lax.all_to_all(outgoing, 'dp', split_axis=0, concat_axis=0, tiled=True)  60 us
    all_to_all x1, blocking collectives, on_device(): lax.all_to_all(partial, 'dp', split_axis=0, concat_axis=0, axis_index_gro...  31 us
    ppermute x4, waiting for transfers between devices, along_y(): lax.ppermute(value, 'dp', [(i, (i + NZ * step) % (NY * NZ)) for i in rang...  8.15 us
    ppermute x4, waiting for transfers between devices, along_x(): lax.ppermute(value, 'col', [(i, (i + NCORE * step) % (NX * NCORE)) for i...  6.78 us
    ppermute x4, starting transfers between devices, along_x(): lax.ppermute(value, 'col', [(i, (i + NCORE * step) % (NX * NCORE)) for i...  6.63 us
    ppermute x4, starting transfers between devices, along_y(): lax.ppermute(value, 'dp', [(i, (i + NZ * step) % (NY * NZ)) for i in rang...  6.19 us
  transfers between devices with their start and end apart: 12, of which 4 were waited for; matrix products, arithmetic and copies ran while one was open for 0% of the time, Pallas kernels for 2%

profile of v12, /device:TPU:64, one launch (start us, length us, event | category | flops | bytes accessed | tf_op | source)
XLA Modules:
  0.0 129.9 jit_solution(15720538525627342352)
XLA Ops:
  0.0 0.1 pad_add_fusion.at
  0.1 1.6 %copy-done = bf16[2048,512]{1,0:T(8,128)(2,1)S(1)} copy-done((bf16[2048,512]{1,0:T(8,128)(2,1)S(1)}, bf16[2048,512]{1,0:T(8,128)(2,1)}, u32[]{:S(2)}) %copy-start) | copy-done | bytes 2097176
  1.7 0.7 copy-done.1
  2.4 1.0 pack.1
  3.4 60.0 %all_to_all.10 = bf16[32,16,16,128]{3,2,1,0:T(8,128)(2,1)S(1)} all-to-all(bf16[32,16,16,128]{3,2,1,0:T(8,128)(2,1)S(1)} %bitcast.17), channel_id=1, replica_groups=mesh['dp'=32,'col'=8] {'dp'}, dimensions={0} | all-to-all | bytes 4194304 | tf_op jit(solution)/shard_map/all_to_all | solution.py:247
  63.4 2.6 %mix.1 = bf16[128,16,128]{2,1,0:T(8,128)(2,1)S(1)} custom-call(s32[128]{0:T(128)S(1)} %copy-done.2, bf16[512,16,128]{2,1,0:T(8,128)(2,1)S(1)} %bitcast.16), custom_call_target="tpu_custom_call" | custom-call | tf_op jit(solution)/shard_map/mix/pallas_call | solution.py:82
  66.0 1.6 %collective-permute-start.2 = (bf16[2048,128]{1,0:T(8,128)(2,1)S(1)}, bf16[2048,128]{1,0:T(8,128)(2,1)S(1)}, u32[]{:S(2)}, u32[]{:S(2)}) collective-permute-start(bf16[2048,128]{1,0:T(8,128)(2,1)S(1)} %bitcast.8), channel_id=1, source_target_pairs={{0,2},{1,3},{2,4},{3,5},{4,6},{5,7},{6,0},{7,1},{8,10},{9,11},{10,... | collective-permute-start | bytes 1572872 | tf_op jit(solution)/shard_map/ppermute | solution.py:251
  67.5 1.7 %collective-permute-start.3 = (bf16[2048,128]{1,0:T(8,128)(2,1)S(1)}, bf16[2048,128]{1,0:T(8,128)(2,1)S(1)}, u32[]{:S(2)}, u32[]{:S(2)}) collective-permute-start(bf16[2048,128]{1,0:T(8,128)(2,1)S(1)} %bitcast.9), channel_id=1, source_target_pairs={{0,6},{1,7},{2,0},{3,1},{4,2},{5,3},{6,4},{7,5},{8,14},{9,15},{10,... | collective-permute-start | bytes 1572872 | tf_op jit(solution)/shard_map/ppermute | solution.py:251
  69.3 0.6 collective-permute-start
  69.8 2.7 %collective-permute-start.1 = (bf16[2048,128]{1,0:T(8,128)(2,1)S(1)}, bf16[2048,128]{1,0:T(8,128)(2,1)S(1)}, u32[]{:S(2)}, u32[]{:S(2)}) collective-permute-start(bf16[2048,128]{1,0:T(8,128)(2,1)S(1)} %bitcast.11), channel_id=1, source_target_pairs={{0,192},{8,200},{16,208},{24,216},{32,224},{40,232},{48,240},{56,2... | collective-permute-start | bytes 1572872 | tf_op jit(solution)/shard_map/ppermute | solution.py:254
  72.5 6.8 %collective-permute-done.2.refs_4_.refs_0_.refs_2_ = bf16[2048,128]{1,0:T(8,128)(2,1)S(1)} collective-permute-done((bf16[2048,128]{1,0:T(8,128)(2,1)S(1)}, bf16[2048,128]{1,0:T(8,128)(2,1)S(1)}, u32[]{:S(2)}, u32[]{:S(2)}) %collective-permute-start.2) | collective-permute-done | bytes 524320 | tf_op jit(solution)/shard_map/ppermute | solution.py:251
  79.3 0.5 collective-permute-start.6
  79.8 2.2 %collective-permute-done.refs_1_.refs_2_ = bf16[2048,128]{1,0:T(8,128)(2,1)S(1)} collective-permute-done((bf16[2048,128]{1,0:T(8,128)(2,1)S(1)}, bf16[2048,128]{1,0:T(8,128)(2,1)S(1)}, u32[]{:S(2)}, u32[]{:S(2)}) %collective-permute-start) | collective-permute-done | bytes 524320 | tf_op jit(solution)/shard_map/ppermute | solution.py:254
  82.0 0.4 collective-permute-start.9
  82.4 3.0 %collective-permute-start.10 = (bf16[1024,128]{1,0:T(8,128)(2,1)S(1)}, bf16[1024,128]{1,0:T(8,128)(2,1)S(1)}, u32[]{:S(2)}, u32[]{:S(2)}) collective-permute-start(bf16[1024,128]{1,0:T(8,128)(2,1)S(1)} %get-tuple-element.20), channel_id=1, source_target_pairs={{0,6},{1,7},{2,0},{3,1},{4,2},{5,3},{6,4},{7,5},{8,14},{9,15},{10,... | collective-permute-start | bytes 786440 | tf_op jit(solution)/shard_map/ppermute | solution.py:251
  85.4 3.0 %collective-permute-start.8 = (bf16[1024,128]{1,0:T(8,128)(2,1)S(1)}, bf16[1024,128]{1,0:T(8,128)(2,1)S(1)}, u32[]{:S(2)}, u32[]{:S(2)}) collective-permute-start(bf16[1024,128]{1,0:T(8,128)(2,1)S(1)} %get-tuple-element.15), channel_id=1, source_target_pairs={{0,192},{8,200},{16,208},{24,216},{32,224},{40,232},{48,240},{56,2... | collective-permute-start | bytes 786440 | tf_op jit(solution)/shard_map/ppermute | solution.py:254
  88.3 1.4 %gram_near.1 = (bf16[384,2048]{1,0:T(8,128)(2,1)S(1)}, bf16[3,384,256]{2,1,0:T(8,128)(2,1)S(1)}) custom-call(bf16[2048,128]{1,0:T(8,128)(2,1)S(1)} %bitcast.13, bf16[2048,128]{1,0:T(8,128)(2,1)S(1)} %collective-permute-done.refs_1_.refs_2_, bf16[2048,128]{1,0:T(8,128)(2,1)S(1)} %collective-permute-done.1.refs_2_.refs_3_, bf16[2048,128]{1,0:T(8,128)(2,1)S(1)} %bitcast.14, ...), custom_call_target="tpu_custom_call" | custom-call | flops 1207959552 | bytes 8388608 | tf_op jit(solution)/shard_map/gram_near/pallas_call | solution.py:153
  89.8 0.1 collective-permute-start.11
  89.9 2.3 %collective-permute-done.8 = bf16[1024,128]{1,0:T(8,128)(2,1)S(1)} collective-permute-done((bf16[1024,128]{1,0:T(8,128)(2,1)S(1)}, bf16[1024,128]{1,0:T(8,128)(2,1)S(1)}, u32[]{:S(2)}, u32[]{:S(2)}) %collective-permute-start.8) | collective-permute-done | bytes 262176 | tf_op jit(solution)/shard_map/ppermute | solution.py:254
  92.2 3.7 %collective-permute-done.7 = bf16[1024,128]{1,0:T(8,128)(2,1)S(1)} collective-permute-done((bf16[1024,128]{1,0:T(8,128)(2,1)S(1)}, bf16[1024,128]{1,0:T(8,128)(2,1)S(1)}, u32[]{:S(2)}, u32[]{:S(2)}) %collective-permute-start.7) | collective-permute-done | bytes 262176 | tf_op jit(solution)/shard_map/ppermute | solution.py:254
  95.9 0.6 gram_side.1
  96.6 1.4 %gram_far.1 = bf16[8,512,128]{2,1,0:T(8,128)(2,1)S(1)} custom-call(s32[3]{0:T(128)S(1)} %pad_add_fusion.at, bf16[3,384,256]{2,1,0:T(8,128)(2,1)S(1)} %get-tuple-element.13.near_ref, bf16[3,128,256]{2,1,0:T(8,128)(2,1)S(1)} %get-tuple-element.16.side_ref, bf16[384,2048]{1,0:T(8,128)(2,1)S(1)} %get-tuple-element.17.refs_0_.left, ...), custom_call_target="tpu_custom_call" | custom-call | flops 536870912 | bytes 8388608 | tf_op jit(solution)/shard_map/gram_far/pallas_call | solution.py:210
  98.0 31.0 %all_to_all.11.parts_ref = bf16[8,512,128]{2,1,0:T(8,128)(2,1)S(1)} all-to-all(bf16[8,512,128]{2,1,0:T(8,128)(2,1)S(1)} %gram_far.1), channel_id=1, replica_groups={{0,32,72,104,144,176,216,248},{8,40,80,112,152,184,192,224},{16,48,88,1..., dimensions={0} | all-to-all | bytes 2097152 | tf_op jit(solution)/shard_map/all_to_all | solution.py:274
  129.0 0.9 finish.1
  (18 shorter events, 0.2 us)
Async XLA Ops:
  0.1 1.6 %copy-start = (bf16[2048,512]{1,0:T(8,128)(2,1)S(1)}, bf16[2048,512]{1,0:T(8,128)(2,1)}, u32[]{:S(2)}) copy-start(bf16[2048,512]{1,0:T(8,128)(2,1)} %param.3) | copy-start | bytes 6291460
  1.7 0.7 copy-start.1
  3.4 60.0 %copy-start.2 = (s32[128]{0:T(128)S(1)}, s32[128]{0:T(128)}, u32[]{:S(2)}) copy-start(s32[128]{0:T(128)} %picks_ref.1) | copy-start | bytes 1540
  66.0 13.3 %collective-permute-start.2 = (bf16[2048,128]{1,0:T(8,128)(2,1)S(1)}, bf16[2048,128]{1,0:T(8,128)(2,1)S(1)}, u32[]{:S(2)}, u32[]{:S(2)}) collective-permute-start(bf16[2048,128]{1,0:T(8,128)(2,1)S(1)} %bitcast.8), channel_id=1, source_target_pairs={{0,2},{1,3},{2,4},{3,5},{4,6},{5,7},{6,0},{7,1},{8,10},{9,11},{10,... | collective-permute-start | bytes 1572872 | tf_op jit(solution)/shard_map/ppermute | solution.py:251
  67.5 11.8 %collective-permute-start.3 = (bf16[2048,128]{1,0:T(8,128)(2,1)S(1)}, bf16[2048,128]{1,0:T(8,128)(2,1)S(1)}, u32[]{:S(2)}, u32[]{:S(2)}) collective-permute-start(bf16[2048,128]{1,0:T(8,128)(2,1)S(1)} %bitcast.9), channel_id=1, source_target_pairs={{0,6},{1,7},{2,0},{3,1},{4,2},{5,3},{6,4},{7,5},{8,14},{9,15},{10,... | collective-permute-start | bytes 1572872 | tf_op jit(solution)/shard_map/ppermute | solution.py:251
  69.3 12.7 %collective-permute-start = (bf16[2048,128]{1,0:T(8,128)(2,1)S(1)}, bf16[2048,128]{1,0:T(8,128)(2,1)S(1)}, u32[]{:S(2)}, u32[]{:S(2)}) collective-permute-start(bf16[2048,128]{1,0:T(8,128)(2,1)S(1)} %bitcast.10), channel_id=1, source_target_pairs={{0,64},{8,72},{16,80},{24,88},{32,96},{40,104},{48,112},{56,120},{... | collective-permute-start | bytes 1572872 | tf_op jit(solution)/shard_map/ppermute | solution.py:254
  69.8 12.1 %collective-permute-start.1 = (bf16[2048,128]{1,0:T(8,128)(2,1)S(1)}, bf16[2048,128]{1,0:T(8,128)(2,1)S(1)}, u32[]{:S(2)}, u32[]{:S(2)}) collective-permute-start(bf16[2048,128]{1,0:T(8,128)(2,1)S(1)} %bitcast.11), channel_id=1, source_target_pairs={{0,192},{8,200},{16,208},{24,216},{32,224},{40,232},{48,240},{56,2... | collective-permute-start | bytes 1572872 | tf_op jit(solution)/shard_map/ppermute | solution.py:254
  72.5 9.5 %collective-permute-start.4 = (bf16[2048,128]{1,0:T(8,128)(2,1)S(1)}, bf16[2048,128]{1,0:T(8,128)(2,1)S(1)}, u32[]{:S(2)}, u32[]{:S(2)}) collective-permute-start(bf16[2048,128]{1,0:T(8,128)(2,1)S(1)} %bitcast.12), channel_id=1, source_target_pairs={{0,1},{1,0},{2,3},{3,2},{4,5},{5,4},{6,7},{7,6},{8,9},{9,8},{10,11... | collective-permute-start | bytes 1572872 | tf_op jit(solution)/shard_map/ppermute | solution.py:257
  79.3 9.0 %collective-permute-start.5 = (bf16[2048,128]{1,0:T(8,128)(2,1)S(1)}, bf16[2048,128]{1,0:T(8,128)(2,1)S(1)}, u32[]{:S(2)}, u32[]{:S(2)}) collective-permute-start(bf16[2048,128]{1,0:T(8,128)(2,1)S(1)} %collective-permute-done.2.refs_4_.refs_0_.refs_2_), channel_id=1, source_target_pairs={{0,1},{1,0},{2,3},{3,2},{4,5},{5,4},{6,7},{7,6},{8,9},{9,8},{10,11... | collective-permute-start | bytes 1572872 | tf_op jit(solution)/shard_map/ppermute | solution.py:257
  79.3 9.0 %collective-permute-start.6 = (bf16[2048,128]{1,0:T(8,128)(2,1)S(1)}, bf16[2048,128]{1,0:T(8,128)(2,1)S(1)}, u32[]{:S(2)}, u32[]{:S(2)}) collective-permute-start(bf16[2048,128]{1,0:T(8,128)(2,1)S(1)} %collective-permute-done.3.refs_5_.refs_1_.refs_3_), channel_id=1, source_target_pairs={{0,1},{1,0},{2,3},{3,2},{4,5},{5,4},{6,7},{7,6},{8,9},{9,8},{10,11... | collective-permute-start | bytes 1572872 | tf_op jit(solution)/shard_map/ppermute | solution.py:257
  82.0 7.7 %collective-permute-start.9 = (bf16[1024,128]{1,0:T(8,128)(2,1)S(1)}, bf16[1024,128]{1,0:T(8,128)(2,1)S(1)}, u32[]{:S(2)}, u32[]{:S(2)}) collective-permute-start(bf16[1024,128]{1,0:T(8,128)(2,1)S(1)} %get-tuple-element.19), channel_id=1, source_target_pairs={{0,2},{1,3},{2,4},{3,5},{4,6},{5,7},{6,0},{7,1},{8,10},{9,11},{10,... | collective-permute-start | bytes 786440 | tf_op jit(solution)/shard_map/ppermute | solution.py:251
  82.4 7.4 %collective-permute-start.10 = (bf16[1024,128]{1,0:T(8,128)(2,1)S(1)}, bf16[1024,128]{1,0:T(8,128)(2,1)S(1)}, u32[]{:S(2)}, u32[]{:S(2)}) collective-permute-start(bf16[1024,128]{1,0:T(8,128)(2,1)S(1)} %get-tuple-element.20), channel_id=1, source_target_pairs={{0,6},{1,7},{2,0},{3,1},{4,2},{5,3},{6,4},{7,5},{8,14},{9,15},{10,... | collective-permute-start | bytes 786440 | tf_op jit(solution)/shard_map/ppermute | solution.py:251
  85.4 6.8 %collective-permute-start.8 = (bf16[1024,128]{1,0:T(8,128)(2,1)S(1)}, bf16[1024,128]{1,0:T(8,128)(2,1)S(1)}, u32[]{:S(2)}, u32[]{:S(2)}) collective-permute-start(bf16[1024,128]{1,0:T(8,128)(2,1)S(1)} %get-tuple-element.15), channel_id=1, source_target_pairs={{0,192},{8,200},{16,208},{24,216},{32,224},{40,232},{48,240},{56,2... | collective-permute-start | bytes 786440 | tf_op jit(solution)/shard_map/ppermute | solution.py:254
  88.3 7.6 %collective-permute-start.7 = (bf16[1024,128]{1,0:T(8,128)(2,1)S(1)}, bf16[1024,128]{1,0:T(8,128)(2,1)S(1)}, u32[]{:S(2)}, u32[]{:S(2)}) collective-permute-start(bf16[1024,128]{1,0:T(8,128)(2,1)S(1)} %get-tuple-element.14), channel_id=1, source_target_pairs={{0,64},{8,72},{16,80},{24,88},{32,96},{40,104},{48,112},{56,120},{... | collective-permute-start | bytes 786440 | tf_op jit(solution)/shard_map/ppermute | solution.py:254
  89.8 6.8 %collective-permute-start.11 = (bf16[2048,128]{1,0:T(8,128)(2,1)S(1)}, bf16[2048,128]{1,0:T(8,128)(2,1)S(1)}, u32[]{:S(2)}, u32[]{:S(2)}) collective-permute-start(bf16[2048,128]{1,0:T(8,128)(2,1)S(1)} %join.1.own), channel_id=1, source_target_pairs={{0,1},{1,0},{2,3},{3,2},{4,5},{5,4},{6,7},{7,6},{8,9},{9,8},{10,11... | collective-permute-start | bytes 1572872 | tf_op jit(solution)/shard_map/ppermute | solution.py:257

commit v13 on v12

--- a/solution.py
+++ b/solution.py
@@ -188,13 +188,14 @@
 
 
 def far_kernel(at, near_ref, side_ref, left, last, own, other, out_ref):
-    x, core, turn = at[0], at[1], at[2]
+    x, core, turn, group = at[0], at[1], at[2], at[3]
 
     def put(step_x, step_y, block):
-        panel = lax.rem(x + NX - step_x, NX) * NCORE
+        panel = lax.rem(x + NX - step_x, NX)
+        flip = lax.rem(core + lax.div(group + panel, NY), NCORE)
         quarter = pl.multiple_of(lax.rem(turn + step_y, NY) * LANES, LANES)
-        out_ref[panel + core, pl.ds(quarter, LANES), :] = block[:, :LANES]
-        out_ref[panel + 1 - core, pl.ds(quarter, LANES), :] = block[:, LANES:]
+        out_ref[panel * NCORE + flip, pl.ds(quarter, LANES), :] = block[:, :LANES]
+        out_ref[panel * NCORE + 1 - flip, pl.ds(quarter, LANES), :] = block[:, LANES:]
 
     block = pair_dot(left[...], own[...], other[...]).astype(out_ref.dtype)
     for j, step in enumerate(NEAR):
@@ -241,7 +242,7 @@
     dp, col = lax.axis_index("dp"), lax.axis_index("col")
     y, z = lax.div(dp, NZ), lax.rem(dp, NZ)
     x, core = lax.div(col, NCORE), lax.rem(col, NCORE)
-    at = jnp.stack([x, core, lax.rem(z - y + x + NY, NY)])
+    at = jnp.stack([x, core, lax.rem(z - y + x + NY, NY), lax.rem(z - y + NY, NY)])
 
     outgoing = pack(grads, signs, at).reshape(NY * NZ, PER_DEV, CHUNK, LANES)
     raw = lax.all_to_all(outgoing, "dp", split_axis=0, concat_axis=0, tiled=True)
@@ -268,7 +269,7 @@
     partial = gram_far(at, near, side, left, last, x_far, swap(x_far))
 
     groups = [
-        [gy * NZ + (s + gy) % NY + NY * half for gy in range(NY) for half in range(NZ // NY)]
+        [gy * NZ + (s + gy + NY * h) % NZ for gy in range(NY) for h in range(NZ // NY)]
         for s in range(NY)
     ]
     parts = lax.all_to_all(

time: 132 us -> 131 us (level)
  no operation moved by 1% of the time
where the time goes in v13:
time: 131 us; the launch traced here: 130 us
  blocking collectives  91.1 us (70%)
  waiting for transfers between devices  14.9 us (11%)
  starting transfers between devices  13.4 us (10%)
  Pallas kernels  8.03 us (6%)
  local copies, waits for them, and re-layouts  2.29 us (2%)
    all_to_all x1, blocking collectives, on_device(): lax.all_to_all(outgoing, 'dp', split_axis=0, concat_axis=0, tiled=True)  60 us
    all_to_all x1, blocking collectives, on_device(): lax.all_to_all(partial, 'dp', split_axis=0, concat_axis=0, axis_index_gro...  31.1 us
    ppermute x4, waiting for transfers between devices, along_y(): lax.ppermute(value, 'dp', [(i, (i + NZ * step) % (NY * NZ)) for i in rang...  8.14 us
    ppermute x4, waiting for transfers between devices, along_x(): lax.ppermute(value, 'col', [(i, (i + NCORE * step) % (NX * NCORE)) for i...  6.78 us
    ppermute x4, starting transfers between devices, along_x(): lax.ppermute(value, 'col', [(i, (i + NCORE * step) % (NX * NCORE)) for i...  6.63 us
    ppermute x4, starting transfers between devices, along_y(): lax.ppermute(value, 'dp', [(i, (i + NZ * step) % (NY * NZ)) for i in rang...  6.19 us
  transfers between devices with their start and end apart: 12, of which 4 were waited for; matrix products, arithmetic and copies ran while one was open for 0% of the time, Pallas kernels for 2%

profile of v13, /device:TPU:64, one launch (start us, length us, event | category | flops | bytes accessed | tf_op | source)
XLA Modules:
  0.0 130.0 jit_solution(15970579668475087080)
XLA Ops:
  0.0 0.1 pad_add_fusion.at
  0.1 1.6 %copy-done = bf16[2048,512]{1,0:T(8,128)(2,1)S(1)} copy-done((bf16[2048,512]{1,0:T(8,128)(2,1)S(1)}, bf16[2048,512]{1,0:T(8,128)(2,1)}, u32[]{:S(2)}) %copy-start) | copy-done | bytes 2097176
  1.7 0.7 copy-done.1
  2.4 1.0 pack.1
  3.4 60.0 %all_to_all.10 = bf16[32,16,16,128]{3,2,1,0:T(8,128)(2,1)S(1)} all-to-all(bf16[32,16,16,128]{3,2,1,0:T(8,128)(2,1)S(1)} %bitcast.18), channel_id=1, replica_groups=mesh['dp'=32,'col'=8] {'dp'}, dimensions={0} | all-to-all | bytes 4194304 | tf_op jit(solution)/shard_map/all_to_all | solution.py:248
  63.4 2.6 %mix.1 = bf16[128,16,128]{2,1,0:T(8,128)(2,1)S(1)} custom-call(s32[128]{0:T(128)S(1)} %copy-done.2, bf16[512,16,128]{2,1,0:T(8,128)(2,1)S(1)} %bitcast.17), custom_call_target="tpu_custom_call" | custom-call | tf_op jit(solution)/shard_map/mix/pallas_call | solution.py:82
  66.0 1.6 %collective-permute-start.2 = (bf16[2048,128]{1,0:T(8,128)(2,1)S(1)}, bf16[2048,128]{1,0:T(8,128)(2,1)S(1)}, u32[]{:S(2)}, u32[]{:S(2)}) collective-permute-start(bf16[2048,128]{1,0:T(8,128)(2,1)S(1)} %bitcast.9), channel_id=1, source_target_pairs={{0,2},{1,3},{2,4},{3,5},{4,6},{5,7},{6,0},{7,1},{8,10},{9,11},{10,... | collective-permute-start | bytes 1572872 | tf_op jit(solution)/shard_map/ppermute | solution.py:252
  67.5 1.7 %collective-permute-start.3 = (bf16[2048,128]{1,0:T(8,128)(2,1)S(1)}, bf16[2048,128]{1,0:T(8,128)(2,1)S(1)}, u32[]{:S(2)}, u32[]{:S(2)}) collective-permute-start(bf16[2048,128]{1,0:T(8,128)(2,1)S(1)} %bitcast.10), channel_id=1, source_target_pairs={{0,6},{1,7},{2,0},{3,1},{4,2},{5,3},{6,4},{7,5},{8,14},{9,15},{10,... | collective-permute-start | bytes 1572872 | tf_op jit(solution)/shard_map/ppermute | solution.py:252
  69.3 0.6 collective-permute-start
  69.8 2.7 %collective-permute-start.1 = (bf16[2048,128]{1,0:T(8,128)(2,1)S(1)}, bf16[2048,128]{1,0:T(8,128)(2,1)S(1)}, u32[]{:S(2)}, u32[]{:S(2)}) collective-permute-start(bf16[2048,128]{1,0:T(8,128)(2,1)S(1)} %bitcast.12), channel_id=1, source_target_pairs={{0,192},{8,200},{16,208},{24,216},{32,224},{40,232},{48,240},{56,2... | collective-permute-start | bytes 1572872 | tf_op jit(solution)/shard_map/ppermute | solution.py:255
  72.5 6.8 %collective-permute-done.2.refs_4_.refs_0_.refs_2_ = bf16[2048,128]{1,0:T(8,128)(2,1)S(1)} collective-permute-done((bf16[2048,128]{1,0:T(8,128)(2,1)S(1)}, bf16[2048,128]{1,0:T(8,128)(2,1)S(1)}, u32[]{:S(2)}, u32[]{:S(2)}) %collective-permute-start.2) | collective-permute-done | bytes 524320 | tf_op jit(solution)/shard_map/ppermute | solution.py:252
  79.3 0.5 collective-permute-start.6
  79.8 2.2 %collective-permute-done.refs_1_.refs_2_ = bf16[2048,128]{1,0:T(8,128)(2,1)S(1)} collective-permute-done((bf16[2048,128]{1,0:T(8,128)(2,1)S(1)}, bf16[2048,128]{1,0:T(8,128)(2,1)S(1)}, u32[]{:S(2)}, u32[]{:S(2)}) %collective-permute-start) | collective-permute-done | bytes 524320 | tf_op jit(solution)/shard_map/ppermute | solution.py:255
  82.0 0.4 collective-permute-start.9
  82.4 3.0 %collective-permute-start.10 = (bf16[1024,128]{1,0:T(8,128)(2,1)S(1)}, bf16[1024,128]{1,0:T(8,128)(2,1)S(1)}, u32[]{:S(2)}, u32[]{:S(2)}) collective-permute-start(bf16[1024,128]{1,0:T(8,128)(2,1)S(1)} %get-tuple-element.20), channel_id=1, source_target_pairs={{0,6},{1,7},{2,0},{3,1},{4,2},{5,3},{6,4},{7,5},{8,14},{9,15},{10,... | collective-permute-start | bytes 786440 | tf_op jit(solution)/shard_map/ppermute | solution.py:252
  85.4 3.0 %collective-permute-start.8 = (bf16[1024,128]{1,0:T(8,128)(2,1)S(1)}, bf16[1024,128]{1,0:T(8,128)(2,1)S(1)}, u32[]{:S(2)}, u32[]{:S(2)}) collective-permute-start(bf16[1024,128]{1,0:T(8,128)(2,1)S(1)} %get-tuple-element.15), channel_id=1, source_target_pairs={{0,192},{8,200},{16,208},{24,216},{32,224},{40,232},{48,240},{56,2... | collective-permute-start | bytes 786440 | tf_op jit(solution)/shard_map/ppermute | solution.py:255
  88.3 1.4 %gram_near.1 = (bf16[384,2048]{1,0:T(8,128)(2,1)S(1)}, bf16[3,384,256]{2,1,0:T(8,128)(2,1)S(1)}) custom-call(bf16[2048,128]{1,0:T(8,128)(2,1)S(1)} %bitcast.14, bf16[2048,128]{1,0:T(8,128)(2,1)S(1)} %collective-permute-done.refs_1_.refs_2_, bf16[2048,128]{1,0:T(8,128)(2,1)S(1)} %collective-permute-done.1.refs_2_.refs_3_, bf16[2048,128]{1,0:T(8,128)(2,1)S(1)} %bitcast.15, ...), custom_call_target="tpu_custom_call" | custom-call | flops 1207959552 | bytes 8388608 | tf_op jit(solution)/shard_map/gram_near/pallas_call | solution.py:153
  89.8 0.1 collective-permute-start.11
  89.9 2.3 %collective-permute-done.8 = bf16[1024,128]{1,0:T(8,128)(2,1)S(1)} collective-permute-done((bf16[1024,128]{1,0:T(8,128)(2,1)S(1)}, bf16[1024,128]{1,0:T(8,128)(2,1)S(1)}, u32[]{:S(2)}, u32[]{:S(2)}) %collective-permute-start.8) | collective-permute-done | bytes 262176 | tf_op jit(solution)/shard_map/ppermute | solution.py:255
  92.2 3.7 %collective-permute-done.7 = bf16[1024,128]{1,0:T(8,128)(2,1)S(1)} collective-permute-done((bf16[1024,128]{1,0:T(8,128)(2,1)S(1)}, bf16[1024,128]{1,0:T(8,128)(2,1)S(1)}, u32[]{:S(2)}, u32[]{:S(2)}) %collective-permute-start.7) | collective-permute-done | bytes 262176 | tf_op jit(solution)/shard_map/ppermute | solution.py:255
  95.9 0.6 gram_side.1
  96.6 1.4 %gram_far.1 = bf16[8,512,128]{2,1,0:T(8,128)(2,1)S(1)} custom-call(s32[4]{0:T(128)S(1)} %pad_add_fusion.at, bf16[3,384,256]{2,1,0:T(8,128)(2,1)S(1)} %get-tuple-element.13.near_ref, bf16[3,128,256]{2,1,0:T(8,128)(2,1)S(1)} %get-tuple-element.16.side_ref, bf16[384,2048]{1,0:T(8,128)(2,1)S(1)} %get-tuple-element.17.refs_0_.left, ...), custom_call_target="tpu_custom_call" | custom-call | flops 536870912 | bytes 8388608 | tf_op jit(solution)/shard_map/gram_far/pallas_call | solution.py:211
  98.0 31.1 %all_to_all.11.parts_ref = bf16[8,512,128]{2,1,0:T(8,128)(2,1)S(1)} all-to-all(bf16[8,512,128]{2,1,0:T(8,128)(2,1)S(1)} %gram_far.1), channel_id=1, replica_groups={{0,32,72,104,144,176,216,248},{8,40,80,112,152,184,224,192},{16,48,88,1..., dimensions={0} | all-to-all | bytes 2097152 | tf_op jit(solution)/shard_map/all_to_all | solution.py:275
  129.1 0.9 finish.1
  (18 shorter events, 0.2 us)
Async XLA Ops:
  0.1 1.6 %copy-start = (bf16[2048,512]{1,0:T(8,128)(2,1)S(1)}, bf16[2048,512]{1,0:T(8,128)(2,1)}, u32[]{:S(2)}) copy-start(bf16[2048,512]{1,0:T(8,128)(2,1)} %param.3) | copy-start | bytes 6291460
  1.7 0.7 copy-start.1
  3.4 60.0 %copy-start.2 = (s32[128]{0:T(128)S(1)}, s32[128]{0:T(128)}, u32[]{:S(2)}) copy-start(s32[128]{0:T(128)} %picks_ref.1) | copy-start | bytes 1540
  66.0 13.3 %collective-permute-start.2 = (bf16[2048,128]{1,0:T(8,128)(2,1)S(1)}, bf16[2048,128]{1,0:T(8,128)(2,1)S(1)}, u32[]{:S(2)}, u32[]{:S(2)}) collective-permute-start(bf16[2048,128]{1,0:T(8,128)(2,1)S(1)} %bitcast.9), channel_id=1, source_target_pairs={{0,2},{1,3},{2,4},{3,5},{4,6},{5,7},{6,0},{7,1},{8,10},{9,11},{10,... | collective-permute-start | bytes 1572872 | tf_op jit(solution)/shard_map/ppermute | solution.py:252
  67.5 11.8 %collective-permute-start.3 = (bf16[2048,128]{1,0:T(8,128)(2,1)S(1)}, bf16[2048,128]{1,0:T(8,128)(2,1)S(1)}, u32[]{:S(2)}, u32[]{:S(2)}) collective-permute-start(bf16[2048,128]{1,0:T(8,128)(2,1)S(1)} %bitcast.10), channel_id=1, source_target_pairs={{0,6},{1,7},{2,0},{3,1},{4,2},{5,3},{6,4},{7,5},{8,14},{9,15},{10,... | collective-permute-start | bytes 1572872 | tf_op jit(solution)/shard_map/ppermute | solution.py:252
  69.3 12.7 %collective-permute-start = (bf16[2048,128]{1,0:T(8,128)(2,1)S(1)}, bf16[2048,128]{1,0:T(8,128)(2,1)S(1)}, u32[]{:S(2)}, u32[]{:S(2)}) collective-permute-start(bf16[2048,128]{1,0:T(8,128)(2,1)S(1)} %bitcast.11), channel_id=1, source_target_pairs={{0,64},{8,72},{16,80},{24,88},{32,96},{40,104},{48,112},{56,120},{... | collective-permute-start | bytes 1572872 | tf_op jit(solution)/shard_map/ppermute | solution.py:255
  69.8 12.1 %collective-permute-start.1 = (bf16[2048,128]{1,0:T(8,128)(2,1)S(1)}, bf16[2048,128]{1,0:T(8,128)(2,1)S(1)}, u32[]{:S(2)}, u32[]{:S(2)}) collective-permute-start(bf16[2048,128]{1,0:T(8,128)(2,1)S(1)} %bitcast.12), channel_id=1, source_target_pairs={{0,192},{8,200},{16,208},{24,216},{32,224},{40,232},{48,240},{56,2... | collective-permute-start | bytes 1572872 | tf_op jit(solution)/shard_map/ppermute | solution.py:255
  72.5 9.5 %collective-permute-start.4 = (bf16[2048,128]{1,0:T(8,128)(2,1)S(1)}, bf16[2048,128]{1,0:T(8,128)(2,1)S(1)}, u32[]{:S(2)}, u32[]{:S(2)}) collective-permute-start(bf16[2048,128]{1,0:T(8,128)(2,1)S(1)} %bitcast.13), channel_id=1, source_target_pairs={{0,1},{1,0},{2,3},{3,2},{4,5},{5,4},{6,7},{7,6},{8,9},{9,8},{10,11... | collective-permute-start | bytes 1572872 | tf_op jit(solution)/shard_map/ppermute | solution.py:258
  79.3 9.0 %collective-permute-start.5 = (bf16[2048,128]{1,0:T(8,128)(2,1)S(1)}, bf16[2048,128]{1,0:T(8,128)(2,1)S(1)}, u32[]{:S(2)}, u32[]{:S(2)}) collective-permute-start(bf16[2048,128]{1,0:T(8,128)(2,1)S(1)} %collective-permute-done.2.refs_4_.refs_0_.refs_2_), channel_id=1, source_target_pairs={{0,1},{1,0},{2,3},{3,2},{4,5},{5,4},{6,7},{7,6},{8,9},{9,8},{10,11... | collective-permute-start | bytes 1572872 | tf_op jit(solution)/shard_map/ppermute | solution.py:258
  79.3 9.0 %collective-permute-start.6 = (bf16[2048,128]{1,0:T(8,128)(2,1)S(1)}, bf16[2048,128]{1,0:T(8,128)(2,1)S(1)}, u32[]{:S(2)}, u32[]{:S(2)}) collective-permute-start(bf16[2048,128]{1,0:T(8,128)(2,1)S(1)} %collective-permute-done.3.refs_5_.refs_1_.refs_3_), channel_id=1, source_target_pairs={{0,1},{1,0},{2,3},{3,2},{4,5},{5,4},{6,7},{7,6},{8,9},{9,8},{10,11... | collective-permute-start | bytes 1572872 | tf_op jit(solution)/shard_map/ppermute | solution.py:258
  82.0 7.7 %collective-permute-start.9 = (bf16[1024,128]{1,0:T(8,128)(2,1)S(1)}, bf16[1024,128]{1,0:T(8,128)(2,1)S(1)}, u32[]{:S(2)}, u32[]{:S(2)}) collective-permute-start(bf16[1024,128]{1,0:T(8,128)(2,1)S(1)} %get-tuple-element.19), channel_id=1, source_target_pairs={{0,2},{1,3},{2,4},{3,5},{4,6},{5,7},{6,0},{7,1},{8,10},{9,11},{10,... | collective-permute-start | bytes 786440 | tf_op jit(solution)/shard_map/ppermute | solution.py:252
  82.4 7.4 %collective-permute-start.10 = (bf16[1024,128]{1,0:T(8,128)(2,1)S(1)}, bf16[1024,128]{1,0:T(8,128)(2,1)S(1)}, u32[]{:S(2)}, u32[]{:S(2)}) collective-permute-start(bf16[1024,128]{1,0:T(8,128)(2,1)S(1)} %get-tuple-element.20), channel_id=1, source_target_pairs={{0,6},{1,7},{2,0},{3,1},{4,2},{5,3},{6,4},{7,5},{8,14},{9,15},{10,... | collective-permute-start | bytes 786440 | tf_op jit(solution)/shard_map/ppermute | solution.py:252
  85.4 6.8 %collective-permute-start.8 = (bf16[1024,128]{1,0:T(8,128)(2,1)S(1)}, bf16[1024,128]{1,0:T(8,128)(2,1)S(1)}, u32[]{:S(2)}, u32[]{:S(2)}) collective-permute-start(bf16[1024,128]{1,0:T(8,128)(2,1)S(1)} %get-tuple-element.15), channel_id=1, source_target_pairs={{0,192},{8,200},{16,208},{24,216},{32,224},{40,232},{48,240},{56,2... | collective-permute-start | bytes 786440 | tf_op jit(solution)/shard_map/ppermute | solution.py:255
  88.3 7.6 %collective-permute-start.7 = (bf16[1024,128]{1,0:T(8,128)(2,1)S(1)}, bf16[1024,128]{1,0:T(8,128)(2,1)S(1)}, u32[]{:S(2)}, u32[]{:S(2)}) collective-permute-start(bf16[1024,128]{1,0:T(8,128)(2,1)S(1)} %get-tuple-element.14), channel_id=1, source_target_pairs={{0,64},{8,72},{16,80},{24,88},{32,96},{40,104},{48,112},{56,120},{... | collective-permute-start | bytes 786440 | tf_op jit(solution)/shard_map/ppermute | solution.py:255
  89.8 6.8 %collective-permute-start.11 = (bf16[2048,128]{1,0:T(8,128)(2,1)S(1)}, bf16[2048,128]{1,0:T(8,128)(2,1)S(1)}, u32[]{:S(2)}, u32[]{:S(2)}) collective-permute-start(bf16[2048,128]{1,0:T(8,128)(2,1)S(1)} %join.1.own), channel_id=1, source_target_pairs={{0,1},{1,0},{2,3},{3,2},{4,5},{5,4},{6,7},{7,6},{8,9},{9,8},{10,11... | collective-permute-start | bytes 1572872 | tf_op jit(solution)/shard_map/ppermute | solution.py:258

commit v14 on v13

--- a/solution.py
+++ b/solution.py
@@ -14,35 +14,40 @@
 N_BLOCKS = 512
 CHUNK = BLOCK // NZ
 MIB = 1 << 20
+PIECES = 4
 
 
 SCALARS = pl.BlockSpec(memory_space=pltpu.SMEM)
 LOCAL = pl.BlockSpec(memory_space=pltpu.VMEM)
 
 
-def pack_kernel(at, grads_ref, signs_ref, out_ref):
+def pack_kernel(at, signs_ref, *refs):
+    pieces, out_ref = refs[:-1], refs[-1]
     columns = signs_ref[...].astype(jnp.float32).T
-    for z in range(NZ):
-        for y in range(NY):
-            quarter = lax.rem(z - y + at[0] + NY, NY)
-            lanes = pl.ds(pl.multiple_of(quarter * LANES, LANES), LANES)
-            for b in range(PER_DEV):
-                sign = columns[z * CHUNK : (z + 1) * CHUNK, b : b + 1]
-                sign = jnp.broadcast_to(sign, (CHUNK, LANES)).astype(jnp.bfloat16)
-                rows = pl.ds(z * CHUNK, CHUNK)
-                out_ref[y, z, b] = grads_ref[b, rows, lanes] * sign
+    count = pieces[0].shape[0]
+    for b in range(PER_DEV):
+        for z in range(NZ):
+            sign = columns[z * CHUNK : (z + 1) * CHUNK, b : b + 1]
+            sign = jnp.broadcast_to(sign, (CHUNK, LANES)).astype(jnp.bfloat16)
+            rows = pl.ds(z * CHUNK, CHUNK)
+            for y in range(NY):
+                quarter = lax.rem(z - y + at[0] + NY, NY)
+                lanes = pl.ds(pl.multiple_of(quarter * LANES, LANES), LANES)
+                out_ref[y, z, b] = pieces[b // count][b % count, rows, lanes] * sign
 
 
 def pack(grads, signs, at):
     blocks = grads.reshape(PER_DEV, BLOCK, NY * LANES)
+    count = PER_DEV // PIECES
+    pieces = [blocks[i * count : (i + 1) * count] for i in range(PIECES)]
     return pl.pallas_call(
         pack_kernel,
-        in_specs=[SCALARS, LOCAL, LOCAL],
+        in_specs=[SCALARS] + [LOCAL] * (1 + PIECES),
         out_specs=LOCAL,
         out_shape=jax.ShapeDtypeStruct((NY, NZ, PER_DEV, CHUNK, LANES), jnp.bfloat16),
         compiler_params=pltpu.CompilerParams(vmem_limit_bytes=16 * MIB),
         name="pack",
-    )(at, blocks, signs.reshape(PER_DEV, BLOCK))
+    )(at, signs.reshape(PER_DEV, BLOCK), *pieces)
 
 
 def hadamard(parts):
@@ -93,24 +98,24 @@
 NEAR = (0, 1, 3)
 
 
-def halves_kernel(*refs):
-    pieces, outs = refs[:4], refs[-4:]
-    depth = outs[0].shape[0]
-    for i, out in enumerate(outs):
-        out[...] = pieces[i][pl.ds(i % 2 * depth, depth), :]
-
-
-def halves(pieces, after):
-    part = jax.ShapeDtypeStruct((pieces[0].shape[0] // 2, LANES), pieces[0].dtype)
+def halves_kernel(up, down, *refs):
+    low, high = refs[-2:]
+    depth = low.shape[0]
+    low[...] = up[pl.ds(0, depth), :]
+    high[...] = down[pl.ds(depth, depth), :]
+
+
+def halves(up, down, *after):
+    part = jax.ShapeDtypeStruct((up.shape[0] // 2, LANES), up.dtype)
     return pl.pallas_call(
         halves_kernel,
-        in_specs=[LOCAL] * (4 + len(after)),
-        out_specs=[LOCAL] * 4,
-        out_shape=[part] * 4,
-        compiler_params=pltpu.CompilerParams(vmem_limit_bytes=16 * MIB),
-        cost_estimate=pl.CostEstimate(flops=0, bytes_accessed=2 * MIB, transcendentals=0),
+        in_specs=[LOCAL] * (2 + len(after)),
+        out_specs=[LOCAL] * 2,
+        out_shape=[part] * 2,
+        compiler_params=pltpu.CompilerParams(vmem_limit_bytes=16 * MIB),
+        cost_estimate=pl.CostEstimate(flops=0, bytes_accessed=MIB, transcendentals=0),
         name="halves",
-    )(*pieces, *after)
+    )(up, down, *after)
 
 
 def join_kernel(first, second, *refs):
@@ -260,7 +265,8 @@
     x_up, x_down = along_x(sketch, 1), along_x(sketch, -1)
     y_up, y_down = along_y(sketch, 1), along_y(sketch, -1)
     home = swap(sketch)
-    x_low, x_high, y_low, y_high = halves((x_up, x_down, y_up, y_down), (home,))
+    x_low, x_high = halves(x_up, x_down)
+    y_low, y_high = halves(y_up, y_down, home, x_low)
     y_far = jnp.concatenate([along_y(y_low, 1), along_y(y_high, -1)])
     own, other = (sketch, x_up, x_down), (home, swap(x_up), swap(x_down))
     left, near = gram_near((sketch, y_up, y_down), own, other)

time: 131 us -> 129 us (0.985)
    unnamed x6 -> x4, local copies, waits for them, and re-layouts: 2.29 us -> 0.01 us
    slice x0 -> x1, local copies, waits for them, and re-layouts: none -> 1.66 us  [pack(): pieces = [blocks[i * count:(i + 1) * count] for i in range(PIECES)]]
  transfers between devices with their start and end apart: 12 -> 12, of which waited for: 4 -> 5; matrix products, arithmetic and copies ran while one was open for 0% -> 0% of each run, Pallas kernels for 2% -> 2%
where the time goes in v14:
time: 129 us
  blocking collectives  91.1 us (71%)
  waiting for transfers between devices  14.7 us (11%)
  starting transfers between devices  12.5 us (10%)
  Pallas kernels  8.29 us (6%)
  local copies, waits for them, and re-layouts  1.67 us (1%)
    all_to_all x1, blocking collectives, on_device(): lax.all_to_all(outgoing, 'dp', split_axis=0, concat_axis=0, tiled=True)  60 us
    all_to_all x1, blocking collectives, on_device(): lax.all_to_all(partial, 'dp', split_axis=0, concat_axis=0, axis_index_gro...  31.1 us
    ppermute x4, waiting for transfers between devices, along_x(): lax.ppermute(value, 'col', [(i, (i + NCORE * step) % (NX * NCORE)) for i...  7.55 us
    ppermute x4, waiting for transfers between devices, along_y(): lax.ppermute(value, 'dp', [(i, (i + NZ * step) % (NY * NZ)) for i in rang...  7.14 us
    ppermute x4, starting transfers between devices, along_x(): lax.ppermute(value, 'col', [(i, (i + NCORE * step) % (NX * NCORE)) for i...  6.55 us
    ppermute x4, starting transfers between devices, along_y(): lax.ppermute(value, 'dp', [(i, (i + NZ * step) % (NY * NZ)) for i in rang...  5.34 us
  transfers between devices with their start and end apart: 12, of which 5 were waited for; matrix products, arithmetic and copies ran while one was open for 0% of the time, Pallas kernels for 2%

profile of v14, /device:TPU:64, one launch (start us, length us, event | category | flops | bytes accessed | tf_op | source)
XLA Modules:
  0.0 128.5 jit_solution(10367103040337471809)
XLA Ops:
  0.0 1.7 %fusion = (bf16[512,512]{1,0:T(8,128)(2,1)S(1)}, bf16[512,512]{1,0:T(8,128)(2,1)S(1)}, bf16[512,512]{1,0:T(8,128)(2,1)S(1)}, bf16[512,512]{1,0:T(8,128)(2,1)S(1)}) fusion(bf16[2048,512]{1,0:T(8,128)(2,1)} %param.3), kind=kLoop, calls=%fused_computation.2 | loop fusion | bytes 4194304 | tf_op jit(solution)/shard_map/slice | solution.py:42
  1.8 1.3 pack.1
  3.0 60.0 %all_to_all.10 = bf16[32,16,16,128]{3,2,1,0:T(8,128)(2,1)S(1)} all-to-all(bf16[32,16,16,128]{3,2,1,0:T(8,128)(2,1)S(1)} %bitcast.20), channel_id=1, replica_groups=mesh['dp'=32,'col'=8] {'dp'}, dimensions={0} | all-to-all | bytes 4194304 | tf_op jit(solution)/shard_map/all_to_all | solution.py:253
  63.0 2.6 %mix.1 = bf16[128,16,128]{2,1,0:T(8,128)(2,1)S(1)} custom-call(s32[128]{0:T(128)S(1)} %copy-done.1, bf16[512,16,128]{2,1,0:T(8,128)(2,1)S(1)} %bitcast.21), custom_call_target="tpu_custom_call" | custom-call | tf_op jit(solution)/shard_map/mix/pallas_call | solution.py:87
  65.6 1.6 %collective-permute-start.2 = (bf16[2048,128]{1,0:T(8,128)(2,1)S(1)}, bf16[2048,128]{1,0:T(8,128)(2,1)S(1)}, u32[]{:S(2)}, u32[]{:S(2)}) collective-permute-start(bf16[2048,128]{1,0:T(8,128)(2,1)S(1)} %bitcast.12), channel_id=1, source_target_pairs={{0,2},{1,3},{2,4},{3,5},{4,6},{5,7},{6,0},{7,1},{8,10},{9,11},{10,... | collective-permute-start | bytes 1572872 | tf_op jit(solution)/shard_map/ppermute | solution.py:257
  67.2 1.7 %collective-permute-start.3 = (bf16[2048,128]{1,0:T(8,128)(2,1)S(1)}, bf16[2048,128]{1,0:T(8,128)(2,1)S(1)}, u32[]{:S(2)}, u32[]{:S(2)}) collective-permute-start(bf16[2048,128]{1,0:T(8,128)(2,1)S(1)} %bitcast.13), channel_id=1, source_target_pairs={{0,6},{1,7},{2,0},{3,1},{4,2},{5,3},{6,4},{7,5},{8,14},{9,15},{10,... | collective-permute-start | bytes 1572872 | tf_op jit(solution)/shard_map/ppermute | solution.py:257
  68.9 0.6 collective-permute-start
  69.5 2.7 %collective-permute-start.1 = (bf16[2048,128]{1,0:T(8,128)(2,1)S(1)}, bf16[2048,128]{1,0:T(8,128)(2,1)S(1)}, u32[]{:S(2)}, u32[]{:S(2)}) collective-permute-start(bf16[2048,128]{1,0:T(8,128)(2,1)S(1)} %bitcast.15), channel_id=1, source_target_pairs={{0,192},{8,200},{16,208},{24,216},{32,224},{40,232},{48,240},{56,2... | collective-permute-start | bytes 1572872 | tf_op jit(solution)/shard_map/ppermute | solution.py:260
  72.2 6.8 %collective-permute-done.2.refs_4_.up.refs_2_ = bf16[2048,128]{1,0:T(8,128)(2,1)S(1)} collective-permute-done((bf16[2048,128]{1,0:T(8,128)(2,1)S(1)}, bf16[2048,128]{1,0:T(8,128)(2,1)S(1)}, u32[]{:S(2)}, u32[]{:S(2)}) %collective-permute-start.2) | collective-permute-done | bytes 524320 | tf_op jit(solution)/shard_map/ppermute | solution.py:257
  79.0 0.5 collective-permute-start.6
  79.5 2.1 %collective-permute-done.refs_1_.up = bf16[2048,128]{1,0:T(8,128)(2,1)S(1)} collective-permute-done((bf16[2048,128]{1,0:T(8,128)(2,1)S(1)}, bf16[2048,128]{1,0:T(8,128)(2,1)S(1)}, u32[]{:S(2)}, u32[]{:S(2)}) %collective-permute-start) | collective-permute-done | bytes 524320 | tf_op jit(solution)/shard_map/ppermute | solution.py:260
  81.6 0.3 collective-permute-start.9
  81.9 3.0 %collective-permute-start.10 = (bf16[1024,128]{1,0:T(8,128)(2,1)S(1)}, bf16[1024,128]{1,0:T(8,128)(2,1)S(1)}, u32[]{:S(2)}, u32[]{:S(2)}) collective-permute-start(bf16[1024,128]{1,0:T(8,128)(2,1)S(1)} %get-tuple-element.20), channel_id=1, source_target_pairs={{0,6},{1,7},{2,0},{3,1},{4,2},{5,3},{6,4},{7,5},{8,14},{9,15},{10,... | collective-permute-start | bytes 786440 | tf_op jit(solution)/shard_map/ppermute | solution.py:257
  84.9 1.6 %collective-permute-start.8 = (bf16[1024,128]{1,0:T(8,128)(2,1)S(1)}, bf16[1024,128]{1,0:T(8,128)(2,1)S(1)}, u32[]{:S(2)}, u32[]{:S(2)}) collective-permute-start(bf16[1024,128]{1,0:T(8,128)(2,1)S(1)} %get-tuple-element.16), channel_id=1, source_target_pairs={{0,192},{8,200},{16,208},{24,216},{32,224},{40,232},{48,240},{56,2... | collective-permute-start | bytes 786440 | tf_op jit(solution)/shard_map/ppermute | solution.py:260
  86.5 0.5 collective-permute-start.7
  87.0 1.4 %gram_near.1 = (bf16[384,2048]{1,0:T(8,128)(2,1)S(1)}, bf16[3,384,256]{2,1,0:T(8,128)(2,1)S(1)}) custom-call(bf16[2048,128]{1,0:T(8,128)(2,1)S(1)} %bitcast.17, bf16[2048,128]{1,0:T(8,128)(2,1)S(1)} %collective-permute-done.refs_1_.up, bf16[2048,128]{1,0:T(8,128)(2,1)S(1)} %collective-permute-done.1.refs_2_.down, bf16[2048,128]{1,0:T(8,128)(2,1)S(1)} %bitcast.18, ...), custom_call_target="tpu_custom_call" | custom-call | flops 1207959552 | bytes 8388608 | tf_op jit(solution)/shard_map/gram_near/pallas_call | solution.py:158
  88.4 0.8 collective-permute-done.9.first
  89.2 0.1 collective-permute-start.11
  89.4 2.0 %collective-permute-done.8 = bf16[1024,128]{1,0:T(8,128)(2,1)S(1)} collective-permute-done((bf16[1024,128]{1,0:T(8,128)(2,1)S(1)}, bf16[1024,128]{1,0:T(8,128)(2,1)S(1)}, u32[]{:S(2)}, u32[]{:S(2)}) %collective-permute-start.8) | collective-permute-done | bytes 262176 | tf_op jit(solution)/shard_map/ppermute | solution.py:260
  91.4 3.0 %collective-permute-done.7 = bf16[1024,128]{1,0:T(8,128)(2,1)S(1)} collective-permute-done((bf16[1024,128]{1,0:T(8,128)(2,1)S(1)}, bf16[1024,128]{1,0:T(8,128)(2,1)S(1)}, u32[]{:S(2)}, u32[]{:S(2)}) %collective-permute-start.7) | collective-permute-done | bytes 262176 | tf_op jit(solution)/shard_map/ppermute | solution.py:260
  94.4 0.6 gram_side.1
  95.1 1.4 %gram_far.1 = bf16[8,512,128]{2,1,0:T(8,128)(2,1)S(1)} custom-call(s32[4]{0:T(128)S(1)} %pad_add_fusion.at, bf16[3,384,256]{2,1,0:T(8,128)(2,1)S(1)} %get-tuple-element.13.near_ref, bf16[3,128,256]{2,1,0:T(8,128)(2,1)S(1)} %get-tuple-element.17.side_ref, bf16[384,2048]{1,0:T(8,128)(2,1)S(1)} %get-tuple-element.18.refs_0_.left, ...), custom_call_target="tpu_custom_call" | custom-call | flops 536870912 | bytes 8388608 | tf_op jit(solution)/shard_map/gram_far/pallas_call | solution.py:216
  96.4 31.1 %all_to_all.11.parts_ref = bf16[8,512,128]{2,1,0:T(8,128)(2,1)S(1)} all-to-all(bf16[8,512,128]{2,1,0:T(8,128)(2,1)S(1)} %gram_far.1), channel_id=1, replica_groups={{0,32,72,104,144,176,216,248},{8,40,80,112,152,184,224,192},{16,48,88,1..., dimensions={0} | all-to-all | bytes 2097152 | tf_op jit(solution)/shard_map/all_to_all | solution.py:281
  127.6 0.9 finish.1
  (18 shorter events, 0.3 us)
Async XLA Ops:
  0.0 1.8 %copy-start = (s32[2048]{0:T(1024)S(1)}, s32[2048]{0:T(1024)}, u32[]{:S(2)}) copy-start(s32[2048]{0:T(1024)} %param.4) | copy-start | bytes 24580
  3.0 60.0 %copy-start.1 = (s32[128]{0:T(128)S(1)}, s32[128]{0:T(128)}, u32[]{:S(2)}) copy-start(s32[128]{0:T(128)} %picks_ref.1) | copy-start | bytes 1540
  65.6 13.3 %collective-permute-start.2 = (bf16[2048,128]{1,0:T(8,128)(2,1)S(1)}, bf16[2048,128]{1,0:T(8,128)(2,1)S(1)}, u32[]{:S(2)}, u32[]{:S(2)}) collective-permute-start(bf16[2048,128]{1,0:T(8,128)(2,1)S(1)} %bitcast.12), channel_id=1, source_target_pairs={{0,2},{1,3},{2,4},{3,5},{4,6},{5,7},{6,0},{7,1},{8,10},{9,11},{10,... | collective-permute-start | bytes 1572872 | tf_op jit(solution)/shard_map/ppermute | solution.py:257
  67.2 11.8 %collective-permute-start.3 = (bf16[2048,128]{1,0:T(8,128)(2,1)S(1)}, bf16[2048,128]{1,0:T(8,128)(2,1)S(1)}, u32[]{:S(2)}, u32[]{:S(2)}) collective-permute-start(bf16[2048,128]{1,0:T(8,128)(2,1)S(1)} %bitcast.13), channel_id=1, source_target_pairs={{0,6},{1,7},{2,0},{3,1},{4,2},{5,3},{6,4},{7,5},{8,14},{9,15},{10,... | collective-permute-start | bytes 1572872 | tf_op jit(solution)/shard_map/ppermute | solution.py:257
  68.9 12.7 %collective-permute-start = (bf16[2048,128]{1,0:T(8,128)(2,1)S(1)}, bf16[2048,128]{1,0:T(8,128)(2,1)S(1)}, u32[]{:S(2)}, u32[]{:S(2)}) collective-permute-start(bf16[2048,128]{1,0:T(8,128)(2,1)S(1)} %bitcast.14), channel_id=1, source_target_pairs={{0,64},{8,72},{16,80},{24,88},{32,96},{40,104},{48,112},{56,120},{... | collective-permute-start | bytes 1572872 | tf_op jit(solution)/shard_map/ppermute | solution.py:260
  69.5 12.4 %collective-permute-start.1 = (bf16[2048,128]{1,0:T(8,128)(2,1)S(1)}, bf16[2048,128]{1,0:T(8,128)(2,1)S(1)}, u32[]{:S(2)}, u32[]{:S(2)}) collective-permute-start(bf16[2048,128]{1,0:T(8,128)(2,1)S(1)} %bitcast.15), channel_id=1, source_target_pairs={{0,192},{8,200},{16,208},{24,216},{32,224},{40,232},{48,240},{56,2... | collective-permute-start | bytes 1572872 | tf_op jit(solution)/shard_map/ppermute | solution.py:260
  72.2 12.7 %collective-permute-start.4 = (bf16[2048,128]{1,0:T(8,128)(2,1)S(1)}, bf16[2048,128]{1,0:T(8,128)(2,1)S(1)}, u32[]{:S(2)}, u32[]{:S(2)}) collective-permute-start(bf16[2048,128]{1,0:T(8,128)(2,1)S(1)} %bitcast.16), channel_id=1, source_target_pairs={{0,1},{1,0},{2,3},{3,2},{4,5},{5,4},{6,7},{7,6},{8,9},{9,8},{10,11... | collective-permute-start | bytes 1572872 | tf_op jit(solution)/shard_map/ppermute | solution.py:263
  78.9 7.6 %collective-permute-start.5 = (bf16[2048,128]{1,0:T(8,128)(2,1)S(1)}, bf16[2048,128]{1,0:T(8,128)(2,1)S(1)}, u32[]{:S(2)}, u32[]{:S(2)}) collective-permute-start(bf16[2048,128]{1,0:T(8,128)(2,1)S(1)} %collective-permute-done.2.refs_4_.up.refs_2_), channel_id=1, source_target_pairs={{0,1},{1,0},{2,3},{3,2},{4,5},{5,4},{6,7},{7,6},{8,9},{9,8},{10,11... | collective-permute-start | bytes 1572872 | tf_op jit(solution)/shard_map/ppermute | solution.py:263
  79.0 8.1 %collective-permute-start.6 = (bf16[2048,128]{1,0:T(8,128)(2,1)S(1)}, bf16[2048,128]{1,0:T(8,128)(2,1)S(1)}, u32[]{:S(2)}, u32[]{:S(2)}) collective-permute-start(bf16[2048,128]{1,0:T(8,128)(2,1)S(1)} %collective-permute-done.3.refs_5_.down.refs_3_), channel_id=1, source_target_pairs={{0,1},{1,0},{2,3},{3,2},{4,5},{5,4},{6,7},{7,6},{8,9},{9,8},{10,11... | collective-permute-start | bytes 1572872 | tf_op jit(solution)/shard_map/ppermute | solution.py:263
  81.6 7.6 %collective-permute-start.9 = (bf16[1024,128]{1,0:T(8,128)(2,1)S(1)}, bf16[1024,128]{1,0:T(8,128)(2,1)S(1)}, u32[]{:S(2)}, u32[]{:S(2)}) collective-permute-start(bf16[1024,128]{1,0:T(8,128)(2,1)S(1)} %get-tuple-element.14.refs_1_), channel_id=1, source_target_pairs={{0,2},{1,3},{2,4},{3,5},{4,6},{5,7},{6,0},{7,1},{8,10},{9,11},{10,... | collective-permute-start | bytes 786440 | tf_op jit(solution)/shard_map/ppermute | solution.py:257
  81.9 7.3 %collective-permute-start.10 = (bf16[1024,128]{1,0:T(8,128)(2,1)S(1)}, bf16[1024,128]{1,0:T(8,128)(2,1)S(1)}, u32[]{:S(2)}, u32[]{:S(2)}) collective-permute-start(bf16[1024,128]{1,0:T(8,128)(2,1)S(1)} %get-tuple-element.20), channel_id=1, source_target_pairs={{0,6},{1,7},{2,0},{3,1},{4,2},{5,3},{6,4},{7,5},{8,14},{9,15},{10,... | collective-permute-start | bytes 786440 | tf_op jit(solution)/shard_map/ppermute | solution.py:257
  84.9 6.4 %collective-permute-start.8 = (bf16[1024,128]{1,0:T(8,128)(2,1)S(1)}, bf16[1024,128]{1,0:T(8,128)(2,1)S(1)}, u32[]{:S(2)}, u32[]{:S(2)}) collective-permute-start(bf16[1024,128]{1,0:T(8,128)(2,1)S(1)} %get-tuple-element.16), channel_id=1, source_target_pairs={{0,192},{8,200},{16,208},{24,216},{32,224},{40,232},{48,240},{56,2... | collective-permute-start | bytes 786440 | tf_op jit(solution)/shard_map/ppermute | solution.py:260
  86.5 7.8 %collective-permute-start.7 = (bf16[1024,128]{1,0:T(8,128)(2,1)S(1)}, bf16[1024,128]{1,0:T(8,128)(2,1)S(1)}, u32[]{:S(2)}, u32[]{:S(2)}) collective-permute-start(bf16[1024,128]{1,0:T(8,128)(2,1)S(1)} %get-tuple-element.15), channel_id=1, source_target_pairs={{0,64},{8,72},{16,80},{24,88},{32,96},{40,104},{48,112},{56,120},{... | collective-permute-start | bytes 786440 | tf_op jit(solution)/shard_map/ppermute | solution.py:260
  89.2 5.8 %collective-permute-start.11 = (bf16[2048,128]{1,0:T(8,128)(2,1)S(1)}, bf16[2048,128]{1,0:T(8,128)(2,1)S(1)}, u32[]{:S(2)}, u32[]{:S(2)}) collective-permute-start(bf16[2048,128]{1,0:T(8,128)(2,1)S(1)} %join.1.own), channel_id=1, source_target_pairs={{0,1},{1,0},{2,3},{3,2},{4,5},{5,4},{6,7},{7,6},{8,9},{9,8},{10,11... | collective-permute-start | bytes 1572872 | tf_op jit(solution)/shard_map/ppermute | solution.py:263

commit v15 on v14

--- a/solution.py
+++ b/solution.py
@@ -25,14 +25,14 @@
     pieces, out_ref = refs[:-1], refs[-1]
     columns = signs_ref[...].astype(jnp.float32).T
     count = pieces[0].shape[0]
-    for b in range(PER_DEV):
-        for z in range(NZ):
-            sign = columns[z * CHUNK : (z + 1) * CHUNK, b : b + 1]
-            sign = jnp.broadcast_to(sign, (CHUNK, LANES)).astype(jnp.bfloat16)
-            rows = pl.ds(z * CHUNK, CHUNK)
-            for y in range(NY):
-                quarter = lax.rem(z - y + at[0] + NY, NY)
-                lanes = pl.ds(pl.multiple_of(quarter * LANES, LANES), LANES)
+    for z in range(NZ):
+        rows = pl.ds(z * CHUNK, CHUNK)
+        for y in range(NY):
+            quarter = lax.rem(z - y + at[0] + NY, NY)
+            lanes = pl.ds(pl.multiple_of(quarter * LANES, LANES), LANES)
+            for b in range(PER_DEV):
+                sign = columns[z * CHUNK : (z + 1) * CHUNK, b : b + 1]
+                sign = jnp.broadcast_to(sign, (CHUNK, LANES)).astype(jnp.bfloat16)
                 out_ref[y, z, b] = pieces[b // count][b % count, rows, lanes] * sign
 
 
@@ -202,10 +202,10 @@
         out_ref[panel * NCORE + flip, pl.ds(quarter, LANES), :] = block[:, :LANES]
         out_ref[panel * NCORE + 1 - flip, pl.ds(quarter, LANES), :] = block[:, LANES:]
 
-    block = pair_dot(left[...], own[...], other[...]).astype(out_ref.dtype)
-    for j, step in enumerate(NEAR):
+    whole = jnp.concatenate([left[...], last[...]], axis=0)
+    block = pair_dot(whole, own[...], other[...]).astype(out_ref.dtype)
+    for j, step in enumerate((*NEAR, 2)):
         put(2, step, block[j * LANES : (j + 1) * LANES])
-    put(2, 2, pair_dot(last[...], own[...], other[...]).astype(out_ref.dtype))
     for i, step_x in enumerate(NEAR):
         put(step_x, 2, side_ref[i])
         for j, step_y in enumerate(NEAR):

time: 129 us -> 129 us (level)
  no operation moved by 1% of the time
where the time goes in v15:
time: 129 us; the launch traced here: 128 us
  blocking collectives  91.1 us (71%)
  waiting for transfers between devices  14.7 us (11%)
  starting transfers between devices  12.5 us (10%)
  Pallas kernels  8.02 us (6%)
  local copies, waits for them, and re-layouts  1.67 us (1%)
    all_to_all x1, blocking collectives, on_device(): lax.all_to_all(outgoing, 'dp', split_axis=0, concat_axis=0, tiled=True)  60 us
    all_to_all x1, blocking collectives, on_device(): lax.all_to_all(partial, 'dp', split_axis=0, concat_axis=0, axis_index_gro...  31.1 us
    ppermute x4, waiting for transfers between devices, along_x(): lax.ppermute(value, 'col', [(i, (i + NCORE * step) % (NX * NCORE)) for i...  7.55 us
    ppermute x4, waiting for transfers between devices, along_y(): lax.ppermute(value, 'dp', [(i, (i + NZ * step) % (NY * NZ)) for i in rang...  7.14 us
    ppermute x4, starting transfers between devices, along_x(): lax.ppermute(value, 'col', [(i, (i + NCORE * step) % (NX * NCORE)) for i...  6.55 us
    ppermute x4, starting transfers between devices, along_y(): lax.ppermute(value, 'dp', [(i, (i + NZ * step) % (NY * NZ)) for i in rang...  5.34 us
  transfers between devices with their start and end apart: 12, of which 5 were waited for; matrix products, arithmetic and copies ran while one was open for 0% of the time, Pallas kernels for 2%

profile of v15, /device:TPU:64, one launch (start us, length us, event | category | flops | bytes accessed | tf_op | source)
XLA Modules:
  0.0 128.2 jit_solution(5096893359494154466)
XLA Ops:
  0.0 1.7 %fusion = (bf16[512,512]{1,0:T(8,128)(2,1)S(1)}, bf16[512,512]{1,0:T(8,128)(2,1)S(1)}, bf16[512,512]{1,0:T(8,128)(2,1)S(1)}, bf16[512,512]{1,0:T(8,128)(2,1)S(1)}) fusion(bf16[2048,512]{1,0:T(8,128)(2,1)} %param.3), kind=kLoop, calls=%fused_computation.2 | loop fusion | bytes 4194304 | tf_op jit(solution)/shard_map/slice | solution.py:42
  1.8 1.0 pack.1
  2.8 60.0 %all_to_all.10 = bf16[32,16,16,128]{3,2,1,0:T(8,128)(2,1)S(1)} all-to-all(bf16[32,16,16,128]{3,2,1,0:T(8,128)(2,1)S(1)} %bitcast.20), channel_id=1, replica_groups=mesh['dp'=32,'col'=8] {'dp'}, dimensions={0} | all-to-all | bytes 4194304 | tf_op jit(solution)/shard_map/all_to_all | solution.py:253
  62.8 2.6 %mix.1 = bf16[128,16,128]{2,1,0:T(8,128)(2,1)S(1)} custom-call(s32[128]{0:T(128)S(1)} %copy-done.1, bf16[512,16,128]{2,1,0:T(8,128)(2,1)S(1)} %bitcast.21), custom_call_target="tpu_custom_call" | custom-call | tf_op jit(solution)/shard_map/mix/pallas_call | solution.py:87
  65.4 1.6 %collective-permute-start.2 = (bf16[2048,128]{1,0:T(8,128)(2,1)S(1)}, bf16[2048,128]{1,0:T(8,128)(2,1)S(1)}, u32[]{:S(2)}, u32[]{:S(2)}) collective-permute-start(bf16[2048,128]{1,0:T(8,128)(2,1)S(1)} %bitcast.12), channel_id=1, source_target_pairs={{0,2},{1,3},{2,4},{3,5},{4,6},{5,7},{6,0},{7,1},{8,10},{9,11},{10,... | collective-permute-start | bytes 1572872 | tf_op jit(solution)/shard_map/ppermute | solution.py:257
  66.9 1.7 %collective-permute-start.3 = (bf16[2048,128]{1,0:T(8,128)(2,1)S(1)}, bf16[2048,128]{1,0:T(8,128)(2,1)S(1)}, u32[]{:S(2)}, u32[]{:S(2)}) collective-permute-start(bf16[2048,128]{1,0:T(8,128)(2,1)S(1)} %bitcast.13), channel_id=1, source_target_pairs={{0,6},{1,7},{2,0},{3,1},{4,2},{5,3},{6,4},{7,5},{8,14},{9,15},{10,... | collective-permute-start | bytes 1572872 | tf_op jit(solution)/shard_map/ppermute | solution.py:257
  68.7 0.6 collective-permute-start
  69.2 2.7 %collective-permute-start.1 = (bf16[2048,128]{1,0:T(8,128)(2,1)S(1)}, bf16[2048,128]{1,0:T(8,128)(2,1)S(1)}, u32[]{:S(2)}, u32[]{:S(2)}) collective-permute-start(bf16[2048,128]{1,0:T(8,128)(2,1)S(1)} %bitcast.15), channel_id=1, source_target_pairs={{0,192},{8,200},{16,208},{24,216},{32,224},{40,232},{48,240},{56,2... | collective-permute-start | bytes 1572872 | tf_op jit(solution)/shard_map/ppermute | solution.py:260
  71.9 6.8 %collective-permute-done.2.refs_4_.up.refs_2_ = bf16[2048,128]{1,0:T(8,128)(2,1)S(1)} collective-permute-done((bf16[2048,128]{1,0:T(8,128)(2,1)S(1)}, bf16[2048,128]{1,0:T(8,128)(2,1)S(1)}, u32[]{:S(2)}, u32[]{:S(2)}) %collective-permute-start.2) | collective-permute-done | bytes 524320 | tf_op jit(solution)/shard_map/ppermute | solution.py:257
  78.7 0.5 collective-permute-start.6
  79.2 2.1 %collective-permute-done.refs_1_.up = bf16[2048,128]{1,0:T(8,128)(2,1)S(1)} collective-permute-done((bf16[2048,128]{1,0:T(8,128)(2,1)S(1)}, bf16[2048,128]{1,0:T(8,128)(2,1)S(1)}, u32[]{:S(2)}, u32[]{:S(2)}) %collective-permute-start) | collective-permute-done | bytes 524320 | tf_op jit(solution)/shard_map/ppermute | solution.py:260
  81.4 0.3 collective-permute-start.9
  81.7 3.0 %collective-permute-start.10 = (bf16[1024,128]{1,0:T(8,128)(2,1)S(1)}, bf16[1024,128]{1,0:T(8,128)(2,1)S(1)}, u32[]{:S(2)}, u32[]{:S(2)}) collective-permute-start(bf16[1024,128]{1,0:T(8,128)(2,1)S(1)} %get-tuple-element.20), channel_id=1, source_target_pairs={{0,6},{1,7},{2,0},{3,1},{4,2},{5,3},{6,4},{7,5},{8,14},{9,15},{10,... | collective-permute-start | bytes 786440 | tf_op jit(solution)/shard_map/ppermute | solution.py:257
  84.7 1.6 %collective-permute-start.8 = (bf16[1024,128]{1,0:T(8,128)(2,1)S(1)}, bf16[1024,128]{1,0:T(8,128)(2,1)S(1)}, u32[]{:S(2)}, u32[]{:S(2)}) collective-permute-start(bf16[1024,128]{1,0:T(8,128)(2,1)S(1)} %get-tuple-element.16), channel_id=1, source_target_pairs={{0,192},{8,200},{16,208},{24,216},{32,224},{40,232},{48,240},{56,2... | collective-permute-start | bytes 786440 | tf_op jit(solution)/shard_map/ppermute | solution.py:260
  86.3 0.5 collective-permute-start.7
  86.8 1.4 %gram_near.1 = (bf16[384,2048]{1,0:T(8,128)(2,1)S(1)}, bf16[3,384,256]{2,1,0:T(8,128)(2,1)S(1)}) custom-call(bf16[2048,128]{1,0:T(8,128)(2,1)S(1)} %bitcast.17, bf16[2048,128]{1,0:T(8,128)(2,1)S(1)} %collective-permute-done.refs_1_.up, bf16[2048,128]{1,0:T(8,128)(2,1)S(1)} %collective-permute-done.1.refs_2_.down, bf16[2048,128]{1,0:T(8,128)(2,1)S(1)} %bitcast.18, ...), custom_call_target="tpu_custom_call" | custom-call | flops 1207959552 | bytes 8388608 | tf_op jit(solution)/shard_map/gram_near/pallas_call | solution.py:158
  88.2 0.8 collective-permute-done.9.first
  89.0 0.1 collective-permute-start.11
  89.1 2.0 %collective-permute-done.8 = bf16[1024,128]{1,0:T(8,128)(2,1)S(1)} collective-permute-done((bf16[1024,128]{1,0:T(8,128)(2,1)S(1)}, bf16[1024,128]{1,0:T(8,128)(2,1)S(1)}, u32[]{:S(2)}, u32[]{:S(2)}) %collective-permute-start.8) | collective-permute-done | bytes 262176 | tf_op jit(solution)/shard_map/ppermute | solution.py:260
  91.1 3.0 %collective-permute-done.7 = bf16[1024,128]{1,0:T(8,128)(2,1)S(1)} collective-permute-done((bf16[1024,128]{1,0:T(8,128)(2,1)S(1)}, bf16[1024,128]{1,0:T(8,128)(2,1)S(1)}, u32[]{:S(2)}, u32[]{:S(2)}) %collective-permute-start.7) | collective-permute-done | bytes 262176 | tf_op jit(solution)/shard_map/ppermute | solution.py:260
  94.1 0.6 gram_side.1
  94.8 1.4 %gram_far.1 = bf16[8,512,128]{2,1,0:T(8,128)(2,1)S(1)} custom-call(s32[4]{0:T(128)S(1)} %pad_add_fusion.at, bf16[3,384,256]{2,1,0:T(8,128)(2,1)S(1)} %get-tuple-element.13.near_ref, bf16[3,128,256]{2,1,0:T(8,128)(2,1)S(1)} %get-tuple-element.17.side_ref, bf16[384,2048]{1,0:T(8,128)(2,1)S(1)} %get-tuple-element.18.refs_0_.left, ...), custom_call_target="tpu_custom_call" | custom-call | flops 536870912 | bytes 8388608 | tf_op jit(solution)/shard_map/gram_far/pallas_call | solution.py:216
  96.2 31.1 %all_to_all.11.parts_ref = bf16[8,512,128]{2,1,0:T(8,128)(2,1)S(1)} all-to-all(bf16[8,512,128]{2,1,0:T(8,128)(2,1)S(1)} %gram_far.1), channel_id=1, replica_groups={{0,32,72,104,144,176,216,248},{8,40,80,112,152,184,224,192},{16,48,88,1..., dimensions={0} | all-to-all | bytes 2097152 | tf_op jit(solution)/shard_map/all_to_all | solution.py:281
  127.3 0.9 finish.1
  (18 shorter events, 0.3 us)
Async XLA Ops:
  0.0 1.8 %copy-start = (s32[2048]{0:T(1024)S(1)}, s32[2048]{0:T(1024)}, u32[]{:S(2)}) copy-start(s32[2048]{0:T(1024)} %param.4) | copy-start | bytes 24580
  2.8 60.0 %copy-start.1 = (s32[128]{0:T(128)S(1)}, s32[128]{0:T(128)}, u32[]{:S(2)}) copy-start(s32[128]{0:T(128)} %picks_ref.1) | copy-start | bytes 1540
  65.4 13.3 %collective-permute-start.2 = (bf16[2048,128]{1,0:T(8,128)(2,1)S(1)}, bf16[2048,128]{1,0:T(8,128)(2,1)S(1)}, u32[]{:S(2)}, u32[]{:S(2)}) collective-permute-start(bf16[2048,128]{1,0:T(8,128)(2,1)S(1)} %bitcast.12), channel_id=1, source_target_pairs={{0,2},{1,3},{2,4},{3,5},{4,6},{5,7},{6,0},{7,1},{8,10},{9,11},{10,... | collective-permute-start | bytes 1572872 | tf_op jit(solution)/shard_map/ppermute | solution.py:257
  66.9 11.8 %collective-permute-start.3 = (bf16[2048,128]{1,0:T(8,128)(2,1)S(1)}, bf16[2048,128]{1,0:T(8,128)(2,1)S(1)}, u32[]{:S(2)}, u32[]{:S(2)}) collective-permute-start(bf16[2048,128]{1,0:T(8,128)(2,1)S(1)} %bitcast.13), channel_id=1, source_target_pairs={{0,6},{1,7},{2,0},{3,1},{4,2},{5,3},{6,4},{7,5},{8,14},{9,15},{10,... | collective-permute-start | bytes 1572872 | tf_op jit(solution)/shard_map/ppermute | solution.py:257
  68.7 12.7 %collective-permute-start = (bf16[2048,128]{1,0:T(8,128)(2,1)S(1)}, bf16[2048,128]{1,0:T(8,128)(2,1)S(1)}, u32[]{:S(2)}, u32[]{:S(2)}) collective-permute-start(bf16[2048,128]{1,0:T(8,128)(2,1)S(1)} %bitcast.14), channel_id=1, source_target_pairs={{0,64},{8,72},{16,80},{24,88},{32,96},{40,104},{48,112},{56,120},{... | collective-permute-start | bytes 1572872 | tf_op jit(solution)/shard_map/ppermute | solution.py:260
  69.2 12.4 %collective-permute-start.1 = (bf16[2048,128]{1,0:T(8,128)(2,1)S(1)}, bf16[2048,128]{1,0:T(8,128)(2,1)S(1)}, u32[]{:S(2)}, u32[]{:S(2)}) collective-permute-start(bf16[2048,128]{1,0:T(8,128)(2,1)S(1)} %bitcast.15), channel_id=1, source_target_pairs={{0,192},{8,200},{16,208},{24,216},{32,224},{40,232},{48,240},{56,2... | collective-permute-start | bytes 1572872 | tf_op jit(solution)/shard_map/ppermute | solution.py:260
  71.9 12.7 %collective-permute-start.4 = (bf16[2048,128]{1,0:T(8,128)(2,1)S(1)}, bf16[2048,128]{1,0:T(8,128)(2,1)S(1)}, u32[]{:S(2)}, u32[]{:S(2)}) collective-permute-start(bf16[2048,128]{1,0:T(8,128)(2,1)S(1)} %bitcast.16), channel_id=1, source_target_pairs={{0,1},{1,0},{2,3},{3,2},{4,5},{5,4},{6,7},{7,6},{8,9},{9,8},{10,11... | collective-permute-start | bytes 1572872 | tf_op jit(solution)/shard_map/ppermute | solution.py:263
  78.7 7.6 %collective-permute-start.5 = (bf16[2048,128]{1,0:T(8,128)(2,1)S(1)}, bf16[2048,128]{1,0:T(8,128)(2,1)S(1)}, u32[]{:S(2)}, u32[]{:S(2)}) collective-permute-start(bf16[2048,128]{1,0:T(8,128)(2,1)S(1)} %collective-permute-done.2.refs_4_.up.refs_2_), channel_id=1, source_target_pairs={{0,1},{1,0},{2,3},{3,2},{4,5},{5,4},{6,7},{7,6},{8,9},{9,8},{10,11... | collective-permute-start | bytes 1572872 | tf_op jit(solution)/shard_map/ppermute | solution.py:263
  78.7 8.1 %collective-permute-start.6 = (bf16[2048,128]{1,0:T(8,128)(2,1)S(1)}, bf16[2048,128]{1,0:T(8,128)(2,1)S(1)}, u32[]{:S(2)}, u32[]{:S(2)}) collective-permute-start(bf16[2048,128]{1,0:T(8,128)(2,1)S(1)} %collective-permute-done.3.refs_5_.down.refs_3_), channel_id=1, source_target_pairs={{0,1},{1,0},{2,3},{3,2},{4,5},{5,4},{6,7},{7,6},{8,9},{9,8},{10,11... | collective-permute-start | bytes 1572872 | tf_op jit(solution)/shard_map/ppermute | solution.py:263
  81.4 7.6 %collective-permute-start.9 = (bf16[1024,128]{1,0:T(8,128)(2,1)S(1)}, bf16[1024,128]{1,0:T(8,128)(2,1)S(1)}, u32[]{:S(2)}, u32[]{:S(2)}) collective-permute-start(bf16[1024,128]{1,0:T(8,128)(2,1)S(1)} %get-tuple-element.14.refs_1_), channel_id=1, source_target_pairs={{0,2},{1,3},{2,4},{3,5},{4,6},{5,7},{6,0},{7,1},{8,10},{9,11},{10,... | collective-permute-start | bytes 786440 | tf_op jit(solution)/shard_map/ppermute | solution.py:257
  81.7 7.3 %collective-permute-start.10 = (bf16[1024,128]{1,0:T(8,128)(2,1)S(1)}, bf16[1024,128]{1,0:T(8,128)(2,1)S(1)}, u32[]{:S(2)}, u32[]{:S(2)}) collective-permute-start(bf16[1024,128]{1,0:T(8,128)(2,1)S(1)} %get-tuple-element.20), channel_id=1, source_target_pairs={{0,6},{1,7},{2,0},{3,1},{4,2},{5,3},{6,4},{7,5},{8,14},{9,15},{10,... | collective-permute-start | bytes 786440 | tf_op jit(solution)/shard_map/ppermute | solution.py:257
  84.7 6.4 %collective-permute-start.8 = (bf16[1024,128]{1,0:T(8,128)(2,1)S(1)}, bf16[1024,128]{1,0:T(8,128)(2,1)S(1)}, u32[]{:S(2)}, u32[]{:S(2)}) collective-permute-start(bf16[1024,128]{1,0:T(8,128)(2,1)S(1)} %get-tuple-element.16), channel_id=1, source_target_pairs={{0,192},{8,200},{16,208},{24,216},{32,224},{40,232},{48,240},{56,2... | collective-permute-start | bytes 786440 | tf_op jit(solution)/shard_map/ppermute | solution.py:260
  86.3 7.8 %collective-permute-start.7 = (bf16[1024,128]{1,0:T(8,128)(2,1)S(1)}, bf16[1024,128]{1,0:T(8,128)(2,1)S(1)}, u32[]{:S(2)}, u32[]{:S(2)}) collective-permute-start(bf16[1024,128]{1,0:T(8,128)(2,1)S(1)} %get-tuple-element.15), channel_id=1, source_target_pairs={{0,64},{8,72},{16,80},{24,88},{32,96},{40,104},{48,112},{56,120},{... | collective-permute-start | bytes 786440 | tf_op jit(solution)/shard_map/ppermute | solution.py:260
  89.0 5.8 %collective-permute-start.11 = (bf16[2048,128]{1,0:T(8,128)(2,1)S(1)}, bf16[2048,128]{1,0:T(8,128)(2,1)S(1)}, u32[]{:S(2)}, u32[]{:S(2)}) collective-permute-start(bf16[2048,128]{1,0:T(8,128)(2,1)S(1)} %join.1.own), channel_id=1, source_target_pairs={{0,1},{1,0},{2,3},{3,2},{4,5},{5,4},{6,7},{7,6},{8,9},{9,8},{10,11... | collective-permute-start | bytes 1572872 | tf_op jit(solution)/shard_map/ppermute | solution.py:263

commit v16 on v15

--- a/solution.py
+++ b/solution.py
@@ -98,24 +98,27 @@
 NEAR = (0, 1, 3)
 
 
-def halves_kernel(up, down, *refs):
-    low, high = refs[-2:]
-    depth = low.shape[0]
-    low[...] = up[pl.ds(0, depth), :]
-    high[...] = down[pl.ds(depth, depth), :]
-
-
-def halves(up, down, *after):
-    part = jax.ShapeDtypeStruct((up.shape[0] // 2, LANES), up.dtype)
-    return pl.pallas_call(
-        halves_kernel,
-        in_specs=[LOCAL] * (2 + len(after)),
-        out_specs=[LOCAL] * 2,
-        out_shape=[part] * 2,
+def share_kernel(*refs):
+    pieces, outs, joined = refs[:4], refs[-5:-1], refs[-1]
+    depth = outs[0].shape[0]
+    for i, out in enumerate(outs):
+        out[...] = pieces[i][pl.ds(i % 2 * depth, depth), :]
+    for i in range(2):
+        joined[pl.ds(i * 2 * depth, 2 * depth), :] = pieces[i][...]
+
+
+def share(pieces, *after):
+    rows = pieces[0].shape[0]
+    part = jax.ShapeDtypeStruct((rows // 2, LANES), pieces[0].dtype)
+    return pl.pallas_call(
+        share_kernel,
+        in_specs=[LOCAL] * (4 + len(after)),
+        out_specs=[LOCAL] * 5,
+        out_shape=[part] * 4 + [jax.ShapeDtypeStruct((2 * rows, LANES), part.dtype)],
         compiler_params=pltpu.CompilerParams(vmem_limit_bytes=16 * MIB),
         cost_estimate=pl.CostEstimate(flops=0, bytes_accessed=MIB, transcendentals=0),
-        name="halves",
-    )(up, down, *after)
+        name="share",
+    )(*pieces, *after)
 
 
 def join_kernel(first, second, *refs):
@@ -140,12 +143,17 @@
     return jnp.dot(left, jnp.concatenate([own, other], axis=1), preferred_element_type=jnp.float32)
 
 
+def others(home, swapped):
+    half = home.shape[0]
+    return home[...], swapped[pl.ds(0, half), :], swapped[pl.ds(half, half), :]
+
+
 def near_kernel(*refs):
-    cols, own, other, (left, out_ref) = refs[:3], refs[3:6], refs[6:9], refs[9:]
+    cols, own, other, (left, out_ref) = refs[:3], refs[3:6], others(*refs[6:8]), refs[8:]
     for j in range(len(NEAR)):
         left[pl.ds(j * LANES, LANES), :] = cols[j][...].T
     for j in range(len(NEAR)):
-        out_ref[j] = pair_dot(left[...], own[j][...], other[j][...]).astype(out_ref.dtype)
+        out_ref[j] = pair_dot(left[...], own[j][...], other[j]).astype(out_ref.dtype)
 
 
 def cost(depth, blocks):
@@ -157,7 +165,7 @@
     depth, near = cols[0].shape[0], len(NEAR)
     return pl.pallas_call(
         near_kernel,
-        in_specs=[LOCAL] * 9,
+        in_specs=[LOCAL] * 8,
         out_specs=[LOCAL] * 2,
         out_shape=[
             jax.ShapeDtypeStruct((near * LANES, depth), jnp.bfloat16),
@@ -170,17 +178,17 @@
 
 
 def side_kernel(*refs):
-    col, own, other, (last, out_ref) = refs[0], refs[1:4], refs[4:7], refs[7:]
+    col, own, other, (last, out_ref) = refs[0], refs[1:4], others(*refs[4:6]), refs[6:]
     last[...] = col[...].T
     for j in range(len(NEAR)):
-        out_ref[j] = pair_dot(last[...], own[j][...], other[j][...]).astype(out_ref.dtype)
+        out_ref[j] = pair_dot(last[...], own[j][...], other[j]).astype(out_ref.dtype)
 
 
 def gram_side(col, own, other):
     depth, near = col.shape[0], len(NEAR)
     return pl.pallas_call(
         side_kernel,
-        in_specs=[LOCAL] * 7,
+        in_specs=[LOCAL] * 6,
         out_specs=[LOCAL] * 2,
         out_shape=[
             jax.ShapeDtypeStruct((LANES, depth), jnp.bfloat16),
@@ -265,10 +273,9 @@
     x_up, x_down = along_x(sketch, 1), along_x(sketch, -1)
     y_up, y_down = along_y(sketch, 1), along_y(sketch, -1)
     home = swap(sketch)
-    x_low, x_high = halves(x_up, x_down)
-    y_low, y_high = halves(y_up, y_down, home, x_low)
+    x_low, x_high, y_low, y_high, joined = share((x_up, x_down, y_up, y_down), home)
     y_far = jnp.concatenate([along_y(y_low, 1), along_y(y_high, -1)])
-    own, other = (sketch, x_up, x_down), (home, swap(x_up), swap(x_down))
+    own, other = (sketch, x_up, x_down), (home, swap(joined))
     left, near = gram_near((sketch, y_up, y_down), own, other)
     x_far = join(along_x(x_low, 1), along_x(x_high, -1), left)
     last, side = gram_side(y_far, own, other)

time: 129 us -> 131 us (1.016)
  waiting for transfers between devices: 14.7 us -> 16.4 us
    ppermute x4, waiting for transfers between devices: 7.14 us -> 10.6 us  [along_y(): lax.ppermute(value, 'dp', [(i, (i + NZ * step) % (NY * NZ)) for i in rang...]
    ppermute x4, waiting for transfers between devices: 7.55 us -> 5.84 us  [along_x(): lax.ppermute(value, 'col', [(i, (i + NCORE * step) % (NX * NCORE)) for i...]
  transfers between devices with their start and end apart: 12 -> 11, of which waited for: 5 -> 5; matrix products, arithmetic and copies ran while one was open for 0% -> 0% of each run, Pallas kernels for 2% -> 2%
where the time goes in v16:
time: 131 us; the launch traced here: 130 us
  blocking collectives  92 us (70%)
  waiting for transfers between devices  16.4 us (13%)
  starting transfers between devices  12.1 us (9%)
  Pallas kernels  8.09 us (6%)
  local copies, waits for them, and re-layouts  1.67 us (1%)
    all_to_all x1, blocking collectives, on_device(): lax.all_to_all(outgoing, 'dp', split_axis=0, concat_axis=0, tiled=True)  60 us
    all_to_all x1, blocking collectives, on_device(): lax.all_to_all(partial, 'dp', split_axis=0, concat_axis=0, axis_index_gro...  32 us
    ppermute x4, waiting for transfers between devices, along_y(): lax.ppermute(value, 'dp', [(i, (i + NZ * step) % (NY * NZ)) for i in rang...  10.6 us
    ppermute x4, starting transfers between devices, along_x(): lax.ppermute(value, 'col', [(i, (i + NCORE * step) % (NX * NCORE)) for i...  6.55 us
    ppermute x4, waiting for transfers between devices, along_x(): lax.ppermute(value, 'col', [(i, (i + NCORE * step) % (NX * NCORE)) for i...  5.84 us
    ppermute x4, starting transfers between devices, along_y(): lax.ppermute(value, 'dp', [(i, (i + NZ * step) % (NY * NZ)) for i in rang...  5.34 us
  transfers between devices with their start and end apart: 11, of which 5 were waited for; matrix products, arithmetic and copies ran while one was open for 0% of the time, Pallas kernels for 2%

profile of v16, /device:TPU:64, one launch (start us, length us, event | category | flops | bytes accessed | tf_op | source)
XLA Modules:
  0.0 130.4 jit_solution(1253242257901956751)
XLA Ops:
  0.0 1.7 %fusion = (bf16[512,512]{1,0:T(8,128)(2,1)S(1)}, bf16[512,512]{1,0:T(8,128)(2,1)S(1)}, bf16[512,512]{1,0:T(8,128)(2,1)S(1)}, bf16[512,512]{1,0:T(8,128)(2,1)S(1)}) fusion(bf16[2048,512]{1,0:T(8,128)(2,1)} %param.3), kind=kLoop, calls=%fused_computation.2 | loop fusion | bytes 4194304 | tf_op jit(solution)/shard_map/slice | solution.py:42
  1.8 1.0 pack.1
  2.8 60.0 %all_to_all.10 = bf16[32,16,16,128]{3,2,1,0:T(8,128)(2,1)S(1)} all-to-all(bf16[32,16,16,128]{3,2,1,0:T(8,128)(2,1)S(1)} %bitcast.20), channel_id=1, replica_groups=mesh['dp'=32,'col'=8] {'dp'}, dimensions={0} | all-to-all | bytes 4194304 | tf_op jit(solution)/shard_map/all_to_all | solution.py:261
  62.8 2.6 %mix.1 = bf16[128,16,128]{2,1,0:T(8,128)(2,1)S(1)} custom-call(s32[128]{0:T(128)S(1)} %copy-done.1, bf16[512,16,128]{2,1,0:T(8,128)(2,1)S(1)} %bitcast.21), custom_call_target="tpu_custom_call" | custom-call | tf_op jit(solution)/shard_map/mix/pallas_call | solution.py:87
  65.4 0.6 collective-permute-start
  66.0 2.7 %collective-permute-start.1 = (bf16[2048,128]{1,0:T(8,128)(2,1)S(1)}, bf16[2048,128]{1,0:T(8,128)(2,1)S(1)}, u32[]{:S(2)}, u32[]{:S(2)}) collective-permute-start(bf16[2048,128]{1,0:T(8,128)(2,1)S(1)} %bitcast.13), channel_id=1, source_target_pairs={{0,192},{8,200},{16,208},{24,216},{32,224},{40,232},{48,240},{56,2... | collective-permute-start | bytes 1572872 | tf_op jit(solution)/shard_map/ppermute | solution.py:268
  68.7 1.5 %collective-permute-start.2 = (bf16[2048,128]{1,0:T(8,128)(2,1)S(1)}, bf16[2048,128]{1,0:T(8,128)(2,1)S(1)}, u32[]{:S(2)}, u32[]{:S(2)}) collective-permute-start(bf16[2048,128]{1,0:T(8,128)(2,1)S(1)} %bitcast.14), channel_id=1, source_target_pairs={{0,2},{1,3},{2,4},{3,5},{4,6},{5,7},{6,0},{7,1},{8,10},{9,11},{10,... | collective-permute-start | bytes 1572872 | tf_op jit(solution)/shard_map/ppermute | solution.py:265
  70.2 1.7 %collective-permute-start.3 = (bf16[2048,128]{1,0:T(8,128)(2,1)S(1)}, bf16[2048,128]{1,0:T(8,128)(2,1)S(1)}, u32[]{:S(2)}, u32[]{:S(2)}) collective-permute-start(bf16[2048,128]{1,0:T(8,128)(2,1)S(1)} %bitcast.15), channel_id=1, source_target_pairs={{0,6},{1,7},{2,0},{3,1},{4,2},{5,3},{6,4},{7,5},{8,14},{9,15},{10,... | collective-permute-start | bytes 1572872 | tf_op jit(solution)/shard_map/ppermute | solution.py:265
  71.9 6.8 %collective-permute-done.refs_2_.refs_1_ = bf16[2048,128]{1,0:T(8,128)(2,1)S(1)} collective-permute-done((bf16[2048,128]{1,0:T(8,128)(2,1)S(1)}, bf16[2048,128]{1,0:T(8,128)(2,1)S(1)}, u32[]{:S(2)}, u32[]{:S(2)}) %collective-permute-start) | collective-permute-done | bytes 524320 | tf_op jit(solution)/shard_map/ppermute | solution.py:268
  78.7 2.7 %collective-permute-done.2.refs_0_.refs_4_.refs_2_ = bf16[2048,128]{1,0:T(8,128)(2,1)S(1)} collective-permute-done((bf16[2048,128]{1,0:T(8,128)(2,1)S(1)}, bf16[2048,128]{1,0:T(8,128)(2,1)S(1)}, u32[]{:S(2)}, u32[]{:S(2)}) %collective-permute-start.2) | collective-permute-done | bytes 524320 | tf_op jit(solution)/shard_map/ppermute | solution.py:265
  81.4 0.1 share.1
  81.5 0.1 collective-permute-start.5
  81.6 1.6 %collective-permute-start.8 = (bf16[1024,128]{1,0:T(8,128)(2,1)S(1)}, bf16[1024,128]{1,0:T(8,128)(2,1)S(1)}, u32[]{:S(2)}, u32[]{:S(2)}) collective-permute-start(bf16[1024,128]{1,0:T(8,128)(2,1)S(1)} %get-tuple-element.21), channel_id=1, source_target_pairs={{0,2},{1,3},{2,4},{3,5},{4,6},{5,7},{6,0},{7,1},{8,10},{9,11},{10,... | collective-permute-start | bytes 786440 | tf_op jit(solution)/shard_map/ppermute | solution.py:265
  83.2 1.7 %collective-permute-start.9 = (bf16[1024,128]{1,0:T(8,128)(2,1)S(1)}, bf16[1024,128]{1,0:T(8,128)(2,1)S(1)}, u32[]{:S(2)}, u32[]{:S(2)}) collective-permute-start(bf16[1024,128]{1,0:T(8,128)(2,1)S(1)} %get-tuple-element.22), channel_id=1, source_target_pairs={{0,6},{1,7},{2,0},{3,1},{4,2},{5,3},{6,4},{7,5},{8,14},{9,15},{10,... | collective-permute-start | bytes 786440 | tf_op jit(solution)/shard_map/ppermute | solution.py:265
  84.9 1.5 %collective-permute-start.7 = (bf16[1024,128]{1,0:T(8,128)(2,1)S(1)}, bf16[1024,128]{1,0:T(8,128)(2,1)S(1)}, u32[]{:S(2)}, u32[]{:S(2)}) collective-permute-start(bf16[1024,128]{1,0:T(8,128)(2,1)S(1)} %get-tuple-element.17), channel_id=1, source_target_pairs={{0,192},{8,200},{16,208},{24,216},{32,224},{40,232},{48,240},{56,2... | collective-permute-start | bytes 786440 | tf_op jit(solution)/shard_map/ppermute | solution.py:268
  86.5 0.5 collective-permute-start.6
  87.0 1.4 %gram_near.1 = (bf16[384,2048]{1,0:T(8,128)(2,1)S(1)}, bf16[3,384,256]{2,1,0:T(8,128)(2,1)S(1)}) custom-call(bf16[2048,128]{1,0:T(8,128)(2,1)S(1)} %bitcast.17, bf16[2048,128]{1,0:T(8,128)(2,1)S(1)} %collective-permute-done.refs_2_.refs_1_, bf16[2048,128]{1,0:T(8,128)(2,1)S(1)} %collective-permute-done.1.refs_3_.refs_2_, bf16[2048,128]{1,0:T(8,128)(2,1)S(1)} %bitcast.18, ...), custom_call_target="tpu_custom_call" | custom-call | flops 1207959552 | bytes 8388608 | tf_op jit(solution)/shard_map/gram_near/pallas_call | solution.py:166
  88.4 3.2 %collective-permute-done.8.first = bf16[1024,128]{1,0:T(8,128)(2,1)S(1)} collective-permute-done((bf16[1024,128]{1,0:T(8,128)(2,1)S(1)}, bf16[1024,128]{1,0:T(8,128)(2,1)S(1)}, u32[]{:S(2)}, u32[]{:S(2)}) %collective-permute-start.8) | collective-permute-done | bytes 262176 | tf_op jit(solution)/shard_map/ppermute | solution.py:265
  91.7 1.3 %collective-permute-done.7 = bf16[1024,128]{1,0:T(8,128)(2,1)S(1)} collective-permute-done((bf16[1024,128]{1,0:T(8,128)(2,1)S(1)}, bf16[1024,128]{1,0:T(8,128)(2,1)S(1)}, u32[]{:S(2)}, u32[]{:S(2)}) %collective-permute-start.7) | collective-permute-done | bytes 262176 | tf_op jit(solution)/shard_map/ppermute | solution.py:268
  93.0 2.5 %collective-permute-done.6 = bf16[1024,128]{1,0:T(8,128)(2,1)S(1)} collective-permute-done((bf16[1024,128]{1,0:T(8,128)(2,1)S(1)}, bf16[1024,128]{1,0:T(8,128)(2,1)S(1)}, u32[]{:S(2)}, u32[]{:S(2)}) %collective-permute-start.6) | collective-permute-done | bytes 262176 | tf_op jit(solution)/shard_map/ppermute | solution.py:268
  95.5 0.6 gram_side.1
  96.2 1.4 %gram_far.1 = bf16[8,512,128]{2,1,0:T(8,128)(2,1)S(1)} custom-call(s32[4]{0:T(128)S(1)} %pad_add_fusion.at, bf16[3,384,256]{2,1,0:T(8,128)(2,1)S(1)} %get-tuple-element.15.near_ref, bf16[3,128,256]{2,1,0:T(8,128)(2,1)S(1)} %get-tuple-element.18.side_ref, bf16[384,2048]{1,0:T(8,128)(2,1)S(1)} %get-tuple-element.19.refs_0_.left, ...), custom_call_target="tpu_custom_call" | custom-call | flops 536870912 | bytes 8388608 | tf_op jit(solution)/shard_map/gram_far/pallas_call | solution.py:224
  97.5 32.0 %all_to_all.11.parts_ref = bf16[8,512,128]{2,1,0:T(8,128)(2,1)S(1)} all-to-all(bf16[8,512,128]{2,1,0:T(8,128)(2,1)S(1)} %gram_far.1), channel_id=1, replica_groups={{0,32,72,104,144,176,216,248},{8,40,80,112,152,184,224,192},{16,48,88,1..., dimensions={0} | all-to-all | bytes 2097152 | tf_op jit(solution)/shard_map/all_to_all | solution.py:288
  129.5 0.9 finish.1
  (15 shorter events, 0.3 us)
Async XLA Ops:
  0.0 1.8 %copy-start = (s32[2048]{0:T(1024)S(1)}, s32[2048]{0:T(1024)}, u32[]{:S(2)}) copy-start(s32[2048]{0:T(1024)} %param.4) | copy-start | bytes 24580
  2.8 60.0 %copy-start.1 = (s32[128]{0:T(128)S(1)}, s32[128]{0:T(128)}, u32[]{:S(2)}) copy-start(s32[128]{0:T(128)} %picks_ref.1) | copy-start | bytes 1540
  65.4 13.3 %collective-permute-start = (bf16[2048,128]{1,0:T(8,128)(2,1)S(1)}, bf16[2048,128]{1,0:T(8,128)(2,1)S(1)}, u32[]{:S(2)}, u32[]{:S(2)}) collective-permute-start(bf16[2048,128]{1,0:T(8,128)(2,1)S(1)} %bitcast.12), channel_id=1, source_target_pairs={{0,64},{8,72},{16,80},{24,88},{32,96},{40,104},{48,112},{56,120},{... | collective-permute-start | bytes 1572872 | tf_op jit(solution)/shard_map/ppermute | solution.py:268
  66.0 12.7 %collective-permute-start.1 = (bf16[2048,128]{1,0:T(8,128)(2,1)S(1)}, bf16[2048,128]{1,0:T(8,128)(2,1)S(1)}, u32[]{:S(2)}, u32[]{:S(2)}) collective-permute-start(bf16[2048,128]{1,0:T(8,128)(2,1)S(1)} %bitcast.13), channel_id=1, source_target_pairs={{0,192},{8,200},{16,208},{24,216},{32,224},{40,232},{48,240},{56,2... | collective-permute-start | bytes 1572872 | tf_op jit(solution)/shard_map/ppermute | solution.py:268
  68.7 12.7 %collective-permute-start.2 = (bf16[2048,128]{1,0:T(8,128)(2,1)S(1)}, bf16[2048,128]{1,0:T(8,128)(2,1)S(1)}, u32[]{:S(2)}, u32[]{:S(2)}) collective-permute-start(bf16[2048,128]{1,0:T(8,128)(2,1)S(1)} %bitcast.14), channel_id=1, source_target_pairs={{0,2},{1,3},{2,4},{3,5},{4,6},{5,7},{6,0},{7,1},{8,10},{9,11},{10,... | collective-permute-start | bytes 1572872 | tf_op jit(solution)/shard_map/ppermute | solution.py:265
  70.2 11.2 %collective-permute-start.3 = (bf16[2048,128]{1,0:T(8,128)(2,1)S(1)}, bf16[2048,128]{1,0:T(8,128)(2,1)S(1)}, u32[]{:S(2)}, u32[]{:S(2)}) collective-permute-start(bf16[2048,128]{1,0:T(8,128)(2,1)S(1)} %bitcast.15), channel_id=1, source_target_pairs={{0,6},{1,7},{2,0},{3,1},{4,2},{5,3},{6,4},{7,5},{8,14},{9,15},{10,... | collective-permute-start | bytes 1572872 | tf_op jit(solution)/shard_map/ppermute | solution.py:265
  71.9 9.5 %collective-permute-start.4 = (bf16[2048,128]{1,0:T(8,128)(2,1)S(1)}, bf16[2048,128]{1,0:T(8,128)(2,1)S(1)}, u32[]{:S(2)}, u32[]{:S(2)}) collective-permute-start(bf16[2048,128]{1,0:T(8,128)(2,1)S(1)} %bitcast.16), channel_id=1, source_target_pairs={{0,1},{1,0},{2,3},{3,2},{4,5},{5,4},{6,7},{7,6},{8,9},{9,8},{10,11... | collective-permute-start | bytes 1572872 | tf_op jit(solution)/shard_map/ppermute | solution.py:271
  81.5 5.4 %collective-permute-start.5 = (bf16[4096,128]{1,0:T(8,128)(2,1)S(1)}, bf16[4096,128]{1,0:T(8,128)(2,1)S(1)}, u32[]{:S(2)}, u32[]{:S(2)}) collective-permute-start(bf16[4096,128]{1,0:T(8,128)(2,1)S(1)} %get-tuple-element.14), channel_id=1, source_target_pairs={{0,1},{1,0},{2,3},{3,2},{4,5},{5,4},{6,7},{7,6},{8,9},{9,8},{10,11... | collective-permute-start | bytes 3145736 | tf_op jit(solution)/shard_map/ppermute | solution.py:271
  81.6 9.9 %collective-permute-start.8 = (bf16[1024,128]{1,0:T(8,128)(2,1)S(1)}, bf16[1024,128]{1,0:T(8,128)(2,1)S(1)}, u32[]{:S(2)}, u32[]{:S(2)}) collective-permute-start(bf16[1024,128]{1,0:T(8,128)(2,1)S(1)} %get-tuple-element.21), channel_id=1, source_target_pairs={{0,2},{1,3},{2,4},{3,5},{4,6},{5,7},{6,0},{7,1},{8,10},{9,11},{10,... | collective-permute-start | bytes 786440 | tf_op jit(solution)/shard_map/ppermute | solution.py:265
  83.2 8.4 %collective-permute-start.9 = (bf16[1024,128]{1,0:T(8,128)(2,1)S(1)}, bf16[1024,128]{1,0:T(8,128)(2,1)S(1)}, u32[]{:S(2)}, u32[]{:S(2)}) collective-permute-start(bf16[1024,128]{1,0:T(8,128)(2,1)S(1)} %get-tuple-element.22), channel_id=1, source_target_pairs={{0,6},{1,7},{2,0},{3,1},{4,2},{5,3},{6,4},{7,5},{8,14},{9,15},{10,... | collective-permute-start | bytes 786440 | tf_op jit(solution)/shard_map/ppermute | solution.py:265
  84.9 8.1 %collective-permute-start.7 = (bf16[1024,128]{1,0:T(8,128)(2,1)S(1)}, bf16[1024,128]{1,0:T(8,128)(2,1)S(1)}, u32[]{:S(2)}, u32[]{:S(2)}) collective-permute-start(bf16[1024,128]{1,0:T(8,128)(2,1)S(1)} %get-tuple-element.17), channel_id=1, source_target_pairs={{0,192},{8,200},{16,208},{24,216},{32,224},{40,232},{48,240},{56,2... | collective-permute-start | bytes 786440 | tf_op jit(solution)/shard_map/ppermute | solution.py:268
  86.5 9.0 %collective-permute-start.6 = (bf16[1024,128]{1,0:T(8,128)(2,1)S(1)}, bf16[1024,128]{1,0:T(8,128)(2,1)S(1)}, u32[]{:S(2)}, u32[]{:S(2)}) collective-permute-start(bf16[1024,128]{1,0:T(8,128)(2,1)S(1)} %get-tuple-element.16), channel_id=1, source_target_pairs={{0,64},{8,72},{16,80},{24,88},{32,96},{40,104},{48,112},{56,120},{... | collective-permute-start | bytes 786440 | tf_op jit(solution)/shard_map/ppermute | solution.py:268
  91.6 4.6 %collective-permute-start.10 = (bf16[2048,128]{1,0:T(8,128)(2,1)S(1)}, bf16[2048,128]{1,0:T(8,128)(2,1)S(1)}, u32[]{:S(2)}, u32[]{:S(2)}) collective-permute-start(bf16[2048,128]{1,0:T(8,128)(2,1)S(1)} %join.1.own), channel_id=1, source_target_pairs={{0,1},{1,0},{2,3},{3,2},{4,5},{5,4},{6,7},{7,6},{8,9},{9,8},{10,11... | collective-permute-start | bytes 1572872 | tf_op jit(solution)/shard_map/ppermute | solution.py:271

commit v17 on v15

--- a/solution.py
+++ b/solution.py
@@ -75,11 +75,11 @@
         for e, part in enumerate(hadamard(parts)):
             work[base + 16 * e] = part
 
-    @pl.loop(0, out_ref.shape[0], unroll=4)
+    @pl.loop(0, out_ref.shape[0], unroll=16)
     def _(k):
         pick = picks_ref[k]
-        low = lax.rem(pick, half)
-        side = (1 - 2 * lax.div(pick, half)).astype(jnp.float32)
+        low = jnp.bitwise_and(pick, half - 1)
+        side = jnp.where(pick < half, 1.0, -1.0).astype(jnp.float32)
         out_ref[k] = (work[low] + side * work[low + half]).astype(out_ref.dtype)
 
 

time: 129 us -> 129 us (level)
  no operation moved by 1% of the time
where the time goes in v17:
time: 129 us; the launch traced here: 128 us
  blocking collectives  91.3 us (71%)
  waiting for transfers between devices  14.7 us (11%)
  starting transfers between devices  12.5 us (10%)
  Pallas kernels  7.59 us (6%)
  local copies, waits for them, and re-layouts  1.67 us (1%)
    all_to_all x1, blocking collectives, on_device(): lax.all_to_all(outgoing, 'dp', split_axis=0, concat_axis=0, tiled=True)  60 us
    all_to_all x1, blocking collectives, on_device(): lax.all_to_all(partial, 'dp', split_axis=0, concat_axis=0, axis_index_gro...  31.3 us
    ppermute x4, waiting for transfers between devices, along_x(): lax.ppermute(value, 'col', [(i, (i + NCORE * step) % (NX * NCORE)) for i...  7.55 us
    ppermute x4, waiting for transfers between devices, along_y(): lax.ppermute(value, 'dp', [(i, (i + NZ * step) % (NY * NZ)) for i in rang...  7.14 us
    ppermute x4, starting transfers between devices, along_x(): lax.ppermute(value, 'col', [(i, (i + NCORE * step) % (NX * NCORE)) for i...  6.55 us
    ppermute x4, starting transfers between devices, along_y(): lax.ppermute(value, 'dp', [(i, (i + NZ * step) % (NY * NZ)) for i in rang...  5.34 us
  transfers between devices with their start and end apart: 12, of which 5 were waited for; matrix products, arithmetic and copies ran while one was open for 0% of the time, Pallas kernels for 2%

profile of v17, /device:TPU:64, one launch (start us, length us, event | category | flops | bytes accessed | tf_op | source)
XLA Modules:
  0.0 127.9 jit_solution(8289525620515500319)
XLA Ops:
  0.0 1.7 %fusion = (bf16[512,512]{1,0:T(8,128)(2,1)S(1)}, bf16[512,512]{1,0:T(8,128)(2,1)S(1)}, bf16[512,512]{1,0:T(8,128)(2,1)S(1)}, bf16[512,512]{1,0:T(8,128)(2,1)S(1)}) fusion(bf16[2048,512]{1,0:T(8,128)(2,1)} %param.3), kind=kLoop, calls=%fused_computation.2 | loop fusion | bytes 4194304 | tf_op jit(solution)/shard_map/slice | solution.py:42
  1.8 1.0 pack.1
  2.8 60.0 %all_to_all.10 = bf16[32,16,16,128]{3,2,1,0:T(8,128)(2,1)S(1)} all-to-all(bf16[32,16,16,128]{3,2,1,0:T(8,128)(2,1)S(1)} %bitcast.20), channel_id=1, replica_groups=mesh['dp'=32,'col'=8] {'dp'}, dimensions={0} | all-to-all | bytes 4194304 | tf_op jit(solution)/shard_map/all_to_all | solution.py:253
  62.8 2.1 %mix.1 = bf16[128,16,128]{2,1,0:T(8,128)(2,1)S(1)} custom-call(s32[128]{0:T(128)S(1)} %copy-done.1, bf16[512,16,128]{2,1,0:T(8,128)(2,1)S(1)} %bitcast.21), custom_call_target="tpu_custom_call" | custom-call | tf_op jit(solution)/shard_map/mix/pallas_call | solution.py:87
  64.9 1.6 %collective-permute-start.2 = (bf16[2048,128]{1,0:T(8,128)(2,1)S(1)}, bf16[2048,128]{1,0:T(8,128)(2,1)S(1)}, u32[]{:S(2)}, u32[]{:S(2)}) collective-permute-start(bf16[2048,128]{1,0:T(8,128)(2,1)S(1)} %bitcast.12), channel_id=1, source_target_pairs={{0,2},{1,3},{2,4},{3,5},{4,6},{5,7},{6,0},{7,1},{8,10},{9,11},{10,... | collective-permute-start | bytes 1572872 | tf_op jit(solution)/shard_map/ppermute | solution.py:257
  66.5 1.7 %collective-permute-start.3 = (bf16[2048,128]{1,0:T(8,128)(2,1)S(1)}, bf16[2048,128]{1,0:T(8,128)(2,1)S(1)}, u32[]{:S(2)}, u32[]{:S(2)}) collective-permute-start(bf16[2048,128]{1,0:T(8,128)(2,1)S(1)} %bitcast.13), channel_id=1, source_target_pairs={{0,6},{1,7},{2,0},{3,1},{4,2},{5,3},{6,4},{7,5},{8,14},{9,15},{10,... | collective-permute-start | bytes 1572872 | tf_op jit(solution)/shard_map/ppermute | solution.py:257
  68.2 0.6 collective-permute-start
  68.8 2.7 %collective-permute-start.1 = (bf16[2048,128]{1,0:T(8,128)(2,1)S(1)}, bf16[2048,128]{1,0:T(8,128)(2,1)S(1)}, u32[]{:S(2)}, u32[]{:S(2)}) collective-permute-start(bf16[2048,128]{1,0:T(8,128)(2,1)S(1)} %bitcast.15), channel_id=1, source_target_pairs={{0,192},{8,200},{16,208},{24,216},{32,224},{40,232},{48,240},{56,2... | collective-permute-start | bytes 1572872 | tf_op jit(solution)/shard_map/ppermute | solution.py:260
  71.5 6.8 %collective-permute-done.2.refs_4_.up.refs_2_ = bf16[2048,128]{1,0:T(8,128)(2,1)S(1)} collective-permute-done((bf16[2048,128]{1,0:T(8,128)(2,1)S(1)}, bf16[2048,128]{1,0:T(8,128)(2,1)S(1)}, u32[]{:S(2)}, u32[]{:S(2)}) %collective-permute-start.2) | collective-permute-done | bytes 524320 | tf_op jit(solution)/shard_map/ppermute | solution.py:257
  78.3 0.5 collective-permute-start.6
  78.8 2.1 %collective-permute-done.refs_1_.up = bf16[2048,128]{1,0:T(8,128)(2,1)S(1)} collective-permute-done((bf16[2048,128]{1,0:T(8,128)(2,1)S(1)}, bf16[2048,128]{1,0:T(8,128)(2,1)S(1)}, u32[]{:S(2)}, u32[]{:S(2)}) %collective-permute-start) | collective-permute-done | bytes 524320 | tf_op jit(solution)/shard_map/ppermute | solution.py:260
  80.9 0.3 collective-permute-start.9
  81.2 3.0 %collective-permute-start.10 = (bf16[1024,128]{1,0:T(8,128)(2,1)S(1)}, bf16[1024,128]{1,0:T(8,128)(2,1)S(1)}, u32[]{:S(2)}, u32[]{:S(2)}) collective-permute-start(bf16[1024,128]{1,0:T(8,128)(2,1)S(1)} %get-tuple-element.20), channel_id=1, source_target_pairs={{0,6},{1,7},{2,0},{3,1},{4,2},{5,3},{6,4},{7,5},{8,14},{9,15},{10,... | collective-permute-start | bytes 786440 | tf_op jit(solution)/shard_map/ppermute | solution.py:257
  84.2 1.6 %collective-permute-start.8 = (bf16[1024,128]{1,0:T(8,128)(2,1)S(1)}, bf16[1024,128]{1,0:T(8,128)(2,1)S(1)}, u32[]{:S(2)}, u32[]{:S(2)}) collective-permute-start(bf16[1024,128]{1,0:T(8,128)(2,1)S(1)} %get-tuple-element.16), channel_id=1, source_target_pairs={{0,192},{8,200},{16,208},{24,216},{32,224},{40,232},{48,240},{56,2... | collective-permute-start | bytes 786440 | tf_op jit(solution)/shard_map/ppermute | solution.py:260
  85.8 0.5 collective-permute-start.7
  86.3 1.4 %gram_near.1 = (bf16[384,2048]{1,0:T(8,128)(2,1)S(1)}, bf16[3,384,256]{2,1,0:T(8,128)(2,1)S(1)}) custom-call(bf16[2048,128]{1,0:T(8,128)(2,1)S(1)} %bitcast.17, bf16[2048,128]{1,0:T(8,128)(2,1)S(1)} %collective-permute-done.refs_1_.up, bf16[2048,128]{1,0:T(8,128)(2,1)S(1)} %collective-permute-done.1.refs_2_.down, bf16[2048,128]{1,0:T(8,128)(2,1)S(1)} %bitcast.18, ...), custom_call_target="tpu_custom_call" | custom-call | flops 1207959552 | bytes 8388608 | tf_op jit(solution)/shard_map/gram_near/pallas_call | solution.py:158
  87.8 0.8 collective-permute-done.9.first
  88.6 0.1 collective-permute-start.11
  88.7 2.0 %collective-permute-done.8 = bf16[1024,128]{1,0:T(8,128)(2,1)S(1)} collective-permute-done((bf16[1024,128]{1,0:T(8,128)(2,1)S(1)}, bf16[1024,128]{1,0:T(8,128)(2,1)S(1)}, u32[]{:S(2)}, u32[]{:S(2)}) %collective-permute-start.8) | collective-permute-done | bytes 262176 | tf_op jit(solution)/shard_map/ppermute | solution.py:260
  90.7 3.0 %collective-permute-done.7 = bf16[1024,128]{1,0:T(8,128)(2,1)S(1)} collective-permute-done((bf16[1024,128]{1,0:T(8,128)(2,1)S(1)}, bf16[1024,128]{1,0:T(8,128)(2,1)S(1)}, u32[]{:S(2)}, u32[]{:S(2)}) %collective-permute-start.7) | collective-permute-done | bytes 262176 | tf_op jit(solution)/shard_map/ppermute | solution.py:260
  93.7 0.6 gram_side.1
  94.4 1.4 %gram_far.1 = bf16[8,512,128]{2,1,0:T(8,128)(2,1)S(1)} custom-call(s32[4]{0:T(128)S(1)} %pad_add_fusion.at, bf16[3,384,256]{2,1,0:T(8,128)(2,1)S(1)} %get-tuple-element.13.near_ref, bf16[3,128,256]{2,1,0:T(8,128)(2,1)S(1)} %get-tuple-element.17.side_ref, bf16[384,2048]{1,0:T(8,128)(2,1)S(1)} %get-tuple-element.18.refs_0_.left, ...), custom_call_target="tpu_custom_call" | custom-call | flops 536870912 | bytes 8388608 | tf_op jit(solution)/shard_map/gram_far/pallas_call | solution.py:216
  95.8 31.3 %all_to_all.11.parts_ref = bf16[8,512,128]{2,1,0:T(8,128)(2,1)S(1)} all-to-all(bf16[8,512,128]{2,1,0:T(8,128)(2,1)S(1)} %gram_far.1), channel_id=1, replica_groups={{0,32,72,104,144,176,216,248},{8,40,80,112,152,184,224,192},{16,48,88,1..., dimensions={0} | all-to-all | bytes 2097152 | tf_op jit(solution)/shard_map/all_to_all | solution.py:281
  127.0 0.9 finish.1
  (18 shorter events, 0.3 us)
Async XLA Ops:
  0.0 1.8 %copy-start = (s32[2048]{0:T(1024)S(1)}, s32[2048]{0:T(1024)}, u32[]{:S(2)}) copy-start(s32[2048]{0:T(1024)} %param.4) | copy-start | bytes 24580
  2.8 60.0 %copy-start.1 = (s32[128]{0:T(128)S(1)}, s32[128]{0:T(128)}, u32[]{:S(2)}) copy-start(s32[128]{0:T(128)} %picks_ref.1) | copy-start | bytes 1540
  64.9 13.3 %collective-permute-start.2 = (bf16[2048,128]{1,0:T(8,128)(2,1)S(1)}, bf16[2048,128]{1,0:T(8,128)(2,1)S(1)}, u32[]{:S(2)}, u32[]{:S(2)}) collective-permute-start(bf16[2048,128]{1,0:T(8,128)(2,1)S(1)} %bitcast.12), channel_id=1, source_target_pairs={{0,2},{1,3},{2,4},{3,5},{4,6},{5,7},{6,0},{7,1},{8,10},{9,11},{10,... | collective-permute-start | bytes 1572872 | tf_op jit(solution)/shard_map/ppermute | solution.py:257
  66.5 11.8 %collective-permute-start.3 = (bf16[2048,128]{1,0:T(8,128)(2,1)S(1)}, bf16[2048,128]{1,0:T(8,128)(2,1)S(1)}, u32[]{:S(2)}, u32[]{:S(2)}) collective-permute-start(bf16[2048,128]{1,0:T(8,128)(2,1)S(1)} %bitcast.13), channel_id=1, source_target_pairs={{0,6},{1,7},{2,0},{3,1},{4,2},{5,3},{6,4},{7,5},{8,14},{9,15},{10,... | collective-permute-start | bytes 1572872 | tf_op jit(solution)/shard_map/ppermute | solution.py:257
  68.2 12.7 %collective-permute-start = (bf16[2048,128]{1,0:T(8,128)(2,1)S(1)}, bf16[2048,128]{1,0:T(8,128)(2,1)S(1)}, u32[]{:S(2)}, u32[]{:S(2)}) collective-permute-start(bf16[2048,128]{1,0:T(8,128)(2,1)S(1)} %bitcast.14), channel_id=1, source_target_pairs={{0,64},{8,72},{16,80},{24,88},{32,96},{40,104},{48,112},{56,120},{... | collective-permute-start | bytes 1572872 | tf_op jit(solution)/shard_map/ppermute | solution.py:260
  68.8 12.4 %collective-permute-start.1 = (bf16[2048,128]{1,0:T(8,128)(2,1)S(1)}, bf16[2048,128]{1,0:T(8,128)(2,1)S(1)}, u32[]{:S(2)}, u32[]{:S(2)}) collective-permute-start(bf16[2048,128]{1,0:T(8,128)(2,1)S(1)} %bitcast.15), channel_id=1, source_target_pairs={{0,192},{8,200},{16,208},{24,216},{32,224},{40,232},{48,240},{56,2... | collective-permute-start | bytes 1572872 | tf_op jit(solution)/shard_map/ppermute | solution.py:260
  71.5 12.7 %collective-permute-start.4 = (bf16[2048,128]{1,0:T(8,128)(2,1)S(1)}, bf16[2048,128]{1,0:T(8,128)(2,1)S(1)}, u32[]{:S(2)}, u32[]{:S(2)}) collective-permute-start(bf16[2048,128]{1,0:T(8,128)(2,1)S(1)} %bitcast.16), channel_id=1, source_target_pairs={{0,1},{1,0},{2,3},{3,2},{4,5},{5,4},{6,7},{7,6},{8,9},{9,8},{10,11... | collective-permute-start | bytes 1572872 | tf_op jit(solution)/shard_map/ppermute | solution.py:263
  78.3 7.6 %collective-permute-start.5 = (bf16[2048,128]{1,0:T(8,128)(2,1)S(1)}, bf16[2048,128]{1,0:T(8,128)(2,1)S(1)}, u32[]{:S(2)}, u32[]{:S(2)}) collective-permute-start(bf16[2048,128]{1,0:T(8,128)(2,1)S(1)} %collective-permute-done.2.refs_4_.up.refs_2_), channel_id=1, source_target_pairs={{0,1},{1,0},{2,3},{3,2},{4,5},{5,4},{6,7},{7,6},{8,9},{9,8},{10,11... | collective-permute-start | bytes 1572872 | tf_op jit(solution)/shard_map/ppermute | solution.py:263
  78.3 8.1 %collective-permute-start.6 = (bf16[2048,128]{1,0:T(8,128)(2,1)S(1)}, bf16[2048,128]{1,0:T(8,128)(2,1)S(1)}, u32[]{:S(2)}, u32[]{:S(2)}) collective-permute-start(bf16[2048,128]{1,0:T(8,128)(2,1)S(1)} %collective-permute-done.3.refs_5_.down.refs_3_), channel_id=1, source_target_pairs={{0,1},{1,0},{2,3},{3,2},{4,5},{5,4},{6,7},{7,6},{8,9},{9,8},{10,11... | collective-permute-start | bytes 1572872 | tf_op jit(solution)/shard_map/ppermute | solution.py:263
  80.9 7.6 %collective-permute-start.9 = (bf16[1024,128]{1,0:T(8,128)(2,1)S(1)}, bf16[1024,128]{1,0:T(8,128)(2,1)S(1)}, u32[]{:S(2)}, u32[]{:S(2)}) collective-permute-start(bf16[1024,128]{1,0:T(8,128)(2,1)S(1)} %get-tuple-element.14.refs_1_), channel_id=1, source_target_pairs={{0,2},{1,3},{2,4},{3,5},{4,6},{5,7},{6,0},{7,1},{8,10},{9,11},{10,... | collective-permute-start | bytes 786440 | tf_op jit(solution)/shard_map/ppermute | solution.py:257
  81.2 7.3 %collective-permute-start.10 = (bf16[1024,128]{1,0:T(8,128)(2,1)S(1)}, bf16[1024,128]{1,0:T(8,128)(2,1)S(1)}, u32[]{:S(2)}, u32[]{:S(2)}) collective-permute-start(bf16[1024,128]{1,0:T(8,128)(2,1)S(1)} %get-tuple-element.20), channel_id=1, source_target_pairs={{0,6},{1,7},{2,0},{3,1},{4,2},{5,3},{6,4},{7,5},{8,14},{9,15},{10,... | collective-permute-start | bytes 786440 | tf_op jit(solution)/shard_map/ppermute | solution.py:257
  84.2 6.4 %collective-permute-start.8 = (bf16[1024,128]{1,0:T(8,128)(2,1)S(1)}, bf16[1024,128]{1,0:T(8,128)(2,1)S(1)}, u32[]{:S(2)}, u32[]{:S(2)}) collective-permute-start(bf16[1024,128]{1,0:T(8,128)(2,1)S(1)} %get-tuple-element.16), channel_id=1, source_target_pairs={{0,192},{8,200},{16,208},{24,216},{32,224},{40,232},{48,240},{56,2... | collective-permute-start | bytes 786440 | tf_op jit(solution)/shard_map/ppermute | solution.py:260
  85.8 7.8 %collective-permute-start.7 = (bf16[1024,128]{1,0:T(8,128)(2,1)S(1)}, bf16[1024,128]{1,0:T(8,128)(2,1)S(1)}, u32[]{:S(2)}, u32[]{:S(2)}) collective-permute-start(bf16[1024,128]{1,0:T(8,128)(2,1)S(1)} %get-tuple-element.15), channel_id=1, source_target_pairs={{0,64},{8,72},{16,80},{24,88},{32,96},{40,104},{48,112},{56,120},{... | collective-permute-start | bytes 786440 | tf_op jit(solution)/shard_map/ppermute | solution.py:260
  88.6 5.8 %collective-permute-start.11 = (bf16[2048,128]{1,0:T(8,128)(2,1)S(1)}, bf16[2048,128]{1,0:T(8,128)(2,1)S(1)}, u32[]{:S(2)}, u32[]{:S(2)}) collective-permute-start(bf16[2048,128]{1,0:T(8,128)(2,1)S(1)} %join.1.own), channel_id=1, source_target_pairs={{0,1},{1,0},{2,3},{3,2},{4,5},{5,4},{6,7},{7,6},{8,9},{9,8},{10,11... | collective-permute-start | bytes 1572872 | tf_op jit(solution)/shard_map/ppermute | solution.py:263

commit v18 on v17

--- a/solution.py
+++ b/solution.py
@@ -96,6 +96,7 @@
 
 
 NEAR = (0, 1, 3)
+NEAR_Y = (0, 3, 1)
 
 
 def halves_kernel(up, down, *refs):
@@ -204,11 +205,11 @@
 
     whole = jnp.concatenate([left[...], last[...]], axis=0)
     block = pair_dot(whole, own[...], other[...]).astype(out_ref.dtype)
-    for j, step in enumerate((*NEAR, 2)):
+    for j, step in enumerate((*NEAR_Y, 2)):
         put(2, step, block[j * LANES : (j + 1) * LANES])
     for i, step_x in enumerate(NEAR):
         put(step_x, 2, side_ref[i])
-        for j, step_y in enumerate(NEAR):
+        for j, step_y in enumerate(NEAR_Y):
             put(step_x, step_y, near_ref[i, pl.ds(j * LANES, LANES), :])
 
 
@@ -269,7 +270,7 @@
     y_low, y_high = halves(y_up, y_down, home, x_low)
     y_far = jnp.concatenate([along_y(y_low, 1), along_y(y_high, -1)])
     own, other = (sketch, x_up, x_down), (home, swap(x_up), swap(x_down))
-    left, near = gram_near((sketch, y_up, y_down), own, other)
+    left, near = gram_near((sketch, y_down, y_up), own, other)
     x_far = join(along_x(x_low, 1), along_x(x_high, -1), left)
     last, side = gram_side(y_far, own, other)
     partial = gram_far(at, near, side, left, last, x_far, swap(x_far))

time: 129 us -> 129 us (level)
  waiting for transfers between devices: 14.7 us -> 18.2 us
  starting transfers between devices: 12.5 us -> 9.97 us
    ppermute x4, waiting for transfers between devices: 7.14 us -> 9.02 us  [along_y(): lax.ppermute(value, 'dp', [(i, (i + NZ * step) % (NY * NZ)) for i in rang...]
    ppermute x4, waiting for transfers between devices: 7.55 us -> 9.14 us  [along_x(): lax.ppermute(value, 'col', [(i, (i + NCORE * step) % (NX * NCORE)) for i...]
    ppermute x4, starting transfers between devices: 6.55 us -> 5.14 us  [along_x(): lax.ppermute(value, 'col', [(i, (i + NCORE * step) % (NX * NCORE)) for i...]
  transfers between devices with their start and end apart: 12 -> 12, of which waited for: 5 -> 6; matrix products, arithmetic and copies ran while one was open for 0% -> 0% of each run, Pallas kernels for 2% -> 2%
where the time goes in v18:
time: 129 us; the launch traced here: 128 us
  blocking collectives  90.9 us (70%)
  waiting for transfers between devices  18.2 us (14%)
  starting transfers between devices  9.97 us (8%)
  Pallas kernels  7.59 us (6%)
  local copies, waits for them, and re-layouts  1.67 us (1%)
    all_to_all x1, blocking collectives, on_device(): lax.all_to_all(outgoing, 'dp', split_axis=0, concat_axis=0, tiled=True)  60 us
    all_to_all x1, blocking collectives, on_device(): lax.all_to_all(partial, 'dp', split_axis=0, concat_axis=0, axis_index_gro...  30.9 us
    ppermute x4, waiting for transfers between devices, along_x(): lax.ppermute(value, 'col', [(i, (i + NCORE * step) % (NX * NCORE)) for i...  9.14 us
    ppermute x4, waiting for transfers between devices, along_y(): lax.ppermute(value, 'dp', [(i, (i + NZ * step) % (NY * NZ)) for i in rang...  9.02 us
    ppermute x4, starting transfers between devices, along_x(): lax.ppermute(value, 'col', [(i, (i + NCORE * step) % (NX * NCORE)) for i...  5.14 us
    ppermute x4, starting transfers between devices, along_y(): lax.ppermute(value, 'dp', [(i, (i + NZ * step) % (NY * NZ)) for i in rang...  4.22 us
  transfers between devices with their start and end apart: 12, of which 6 were waited for; matrix products, arithmetic and copies ran while one was open for 0% of the time, Pallas kernels for 2%

profile of v18, /device:TPU:64, one launch (start us, length us, event | category | flops | bytes accessed | tf_op | source)
XLA Modules:
  0.0 128.5 jit_solution(12190369729007372769)
XLA Ops:
  0.0 1.7 %fusion = (bf16[512,512]{1,0:T(8,128)(2,1)S(1)}, bf16[512,512]{1,0:T(8,128)(2,1)S(1)}, bf16[512,512]{1,0:T(8,128)(2,1)S(1)}, bf16[512,512]{1,0:T(8,128)(2,1)S(1)}) fusion(bf16[2048,512]{1,0:T(8,128)(2,1)} %param.3), kind=kLoop, calls=%fused_computation.2 | loop fusion | bytes 4194304 | tf_op jit(solution)/shard_map/slice | solution.py:42
  1.7 0.1 pad_add_fusion.at
  1.8 1.0 pack.1
  2.8 60.0 %all_to_all.10 = bf16[32,16,16,128]{3,2,1,0:T(8,128)(2,1)S(1)} all-to-all(bf16[32,16,16,128]{3,2,1,0:T(8,128)(2,1)S(1)} %bitcast.20), channel_id=1, replica_groups=mesh['dp'=32,'col'=8] {'dp'}, dimensions={0} | all-to-all | bytes 4194304 | tf_op jit(solution)/shard_map/all_to_all | solution.py:254
  62.8 2.1 %mix.1 = bf16[128,16,128]{2,1,0:T(8,128)(2,1)S(1)} custom-call(s32[128]{0:T(128)S(1)} %copy-done.1, bf16[512,16,128]{2,1,0:T(8,128)(2,1)S(1)} %bitcast.21), custom_call_target="tpu_custom_call" | custom-call | tf_op jit(solution)/shard_map/mix/pallas_call | solution.py:87
  64.9 1.6 %collective-permute-start.2 = (bf16[2048,128]{1,0:T(8,128)(2,1)S(1)}, bf16[2048,128]{1,0:T(8,128)(2,1)S(1)}, u32[]{:S(2)}, u32[]{:S(2)}) collective-permute-start(bf16[2048,128]{1,0:T(8,128)(2,1)S(1)} %bitcast.12), channel_id=1, source_target_pairs={{0,2},{1,3},{2,4},{3,5},{4,6},{5,7},{6,0},{7,1},{8,10},{9,11},{10,... | collective-permute-start | bytes 1572872 | tf_op jit(solution)/shard_map/ppermute | solution.py:258
  66.5 1.7 %collective-permute-start.3 = (bf16[2048,128]{1,0:T(8,128)(2,1)S(1)}, bf16[2048,128]{1,0:T(8,128)(2,1)S(1)}, u32[]{:S(2)}, u32[]{:S(2)}) collective-permute-start(bf16[2048,128]{1,0:T(8,128)(2,1)S(1)} %bitcast.13), channel_id=1, source_target_pairs={{0,6},{1,7},{2,0},{3,1},{4,2},{5,3},{6,4},{7,5},{8,14},{9,15},{10,... | collective-permute-start | bytes 1572872 | tf_op jit(solution)/shard_map/ppermute | solution.py:258
  68.2 2.1 %collective-permute-start = (bf16[2048,128]{1,0:T(8,128)(2,1)S(1)}, bf16[2048,128]{1,0:T(8,128)(2,1)S(1)}, u32[]{:S(2)}, u32[]{:S(2)}) collective-permute-start(bf16[2048,128]{1,0:T(8,128)(2,1)S(1)} %bitcast.14), channel_id=1, source_target_pairs={{0,192},{8,200},{16,208},{24,216},{32,224},{40,232},{48,240},{56,2... | collective-permute-start | bytes 1572872 | tf_op jit(solution)/shard_map/ppermute | solution.py:261
  70.4 7.9 %collective-permute-done.2.refs_4_.up.refs_2_ = bf16[2048,128]{1,0:T(8,128)(2,1)S(1)} collective-permute-done((bf16[2048,128]{1,0:T(8,128)(2,1)S(1)}, bf16[2048,128]{1,0:T(8,128)(2,1)S(1)}, u32[]{:S(2)}, u32[]{:S(2)}) %collective-permute-start.2) | collective-permute-done | bytes 524320 | tf_op jit(solution)/shard_map/ppermute | solution.py:258
  78.3 0.5 collective-permute-start.6
  78.8 1.2 collective-permute-done.refs_1_.down
  80.0 0.3 collective-permute-start.9
  80.3 3.1 %collective-permute-done.1.refs_2_.up = bf16[2048,128]{1,0:T(8,128)(2,1)S(1)} collective-permute-done((bf16[2048,128]{1,0:T(8,128)(2,1)S(1)}, bf16[2048,128]{1,0:T(8,128)(2,1)S(1)}, u32[]{:S(2)}, u32[]{:S(2)}) %collective-permute-start.1) | collective-permute-done | bytes 524320 | tf_op jit(solution)/shard_map/ppermute | solution.py:261
  83.4 1.5 %collective-permute-start.10 = (bf16[1024,128]{1,0:T(8,128)(2,1)S(1)}, bf16[1024,128]{1,0:T(8,128)(2,1)S(1)}, u32[]{:S(2)}, u32[]{:S(2)}) collective-permute-start(bf16[1024,128]{1,0:T(8,128)(2,1)S(1)} %get-tuple-element.20), channel_id=1, source_target_pairs={{0,6},{1,7},{2,0},{3,1},{4,2},{5,3},{6,4},{7,5},{8,14},{9,15},{10,... | collective-permute-start | bytes 786440 | tf_op jit(solution)/shard_map/ppermute | solution.py:258
  85.0 2.0 %collective-permute-start.8 = (bf16[1024,128]{1,0:T(8,128)(2,1)S(1)}, bf16[1024,128]{1,0:T(8,128)(2,1)S(1)}, u32[]{:S(2)}, u32[]{:S(2)}) collective-permute-start(bf16[1024,128]{1,0:T(8,128)(2,1)S(1)} %get-tuple-element.16), channel_id=1, source_target_pairs={{0,192},{8,200},{16,208},{24,216},{32,224},{40,232},{48,240},{56,2... | collective-permute-start | bytes 786440 | tf_op jit(solution)/shard_map/ppermute | solution.py:261
  87.1 1.4 %gram_near.1 = (bf16[384,2048]{1,0:T(8,128)(2,1)S(1)}, bf16[3,384,256]{2,1,0:T(8,128)(2,1)S(1)}) custom-call(bf16[2048,128]{1,0:T(8,128)(2,1)S(1)} %bitcast.17, bf16[2048,128]{1,0:T(8,128)(2,1)S(1)} %collective-permute-done.refs_1_.down, bf16[2048,128]{1,0:T(8,128)(2,1)S(1)} %collective-permute-done.1.refs_2_.up, bf16[2048,128]{1,0:T(8,128)(2,1)S(1)} %bitcast.18, ...), custom_call_target="tpu_custom_call" | custom-call | flops 1207959552 | bytes 8388608 | tf_op jit(solution)/shard_map/gram_near/pallas_call | solution.py:159
  88.5 1.2 collective-permute-done.10.second
  89.8 0.1 collective-permute-start.11
  89.9 1.5 %collective-permute-done.8 = bf16[1024,128]{1,0:T(8,128)(2,1)S(1)} collective-permute-done((bf16[1024,128]{1,0:T(8,128)(2,1)S(1)}, bf16[1024,128]{1,0:T(8,128)(2,1)S(1)}, u32[]{:S(2)}, u32[]{:S(2)}) %collective-permute-start.8) | collective-permute-done | bytes 262176 | tf_op jit(solution)/shard_map/ppermute | solution.py:261
  91.4 3.2 %collective-permute-done.7 = bf16[1024,128]{1,0:T(8,128)(2,1)S(1)} collective-permute-done((bf16[1024,128]{1,0:T(8,128)(2,1)S(1)}, bf16[1024,128]{1,0:T(8,128)(2,1)S(1)}, u32[]{:S(2)}, u32[]{:S(2)}) %collective-permute-start.7) | collective-permute-done | bytes 262176 | tf_op jit(solution)/shard_map/ppermute | solution.py:261
  94.7 0.6 gram_side.1
  95.3 1.4 %gram_far.1 = bf16[8,512,128]{2,1,0:T(8,128)(2,1)S(1)} custom-call(s32[4]{0:T(128)S(1)} %pad_add_fusion.at, bf16[3,384,256]{2,1,0:T(8,128)(2,1)S(1)} %get-tuple-element.13.near_ref, bf16[3,128,256]{2,1,0:T(8,128)(2,1)S(1)} %get-tuple-element.17.side_ref, bf16[384,2048]{1,0:T(8,128)(2,1)S(1)} %get-tuple-element.18.refs_0_.left, ...), custom_call_target="tpu_custom_call" | custom-call | flops 536870912 | bytes 8388608 | tf_op jit(solution)/shard_map/gram_far/pallas_call | solution.py:217
  96.7 30.9 %all_to_all.11.parts_ref = bf16[8,512,128]{2,1,0:T(8,128)(2,1)S(1)} all-to-all(bf16[8,512,128]{2,1,0:T(8,128)(2,1)S(1)} %gram_far.1), channel_id=1, replica_groups={{0,32,72,104,144,176,216,248},{8,40,80,112,152,184,224,192},{16,48,88,1..., dimensions={0} | all-to-all | bytes 2097152 | tf_op jit(solution)/shard_map/all_to_all | solution.py:282
  127.6 0.9 finish.1
  (18 shorter events, 0.2 us)
Async XLA Ops:
  0.0 1.8 %copy-start = (s32[2048]{0:T(1024)S(1)}, s32[2048]{0:T(1024)}, u32[]{:S(2)}) copy-start(s32[2048]{0:T(1024)} %param.4) | copy-start | bytes 24580
  2.8 60.0 %copy-start.1 = (s32[128]{0:T(128)S(1)}, s32[128]{0:T(128)}, u32[]{:S(2)}) copy-start(s32[128]{0:T(128)} %picks_ref.1) | copy-start | bytes 1540
  64.9 13.3 %collective-permute-start.2 = (bf16[2048,128]{1,0:T(8,128)(2,1)S(1)}, bf16[2048,128]{1,0:T(8,128)(2,1)S(1)}, u32[]{:S(2)}, u32[]{:S(2)}) collective-permute-start(bf16[2048,128]{1,0:T(8,128)(2,1)S(1)} %bitcast.12), channel_id=1, source_target_pairs={{0,2},{1,3},{2,4},{3,5},{4,6},{5,7},{6,0},{7,1},{8,10},{9,11},{10,... | collective-permute-start | bytes 1572872 | tf_op jit(solution)/shard_map/ppermute | solution.py:258
  66.5 11.8 %collective-permute-start.3 = (bf16[2048,128]{1,0:T(8,128)(2,1)S(1)}, bf16[2048,128]{1,0:T(8,128)(2,1)S(1)}, u32[]{:S(2)}, u32[]{:S(2)}) collective-permute-start(bf16[2048,128]{1,0:T(8,128)(2,1)S(1)} %bitcast.13), channel_id=1, source_target_pairs={{0,6},{1,7},{2,0},{3,1},{4,2},{5,3},{6,4},{7,5},{8,14},{9,15},{10,... | collective-permute-start | bytes 1572872 | tf_op jit(solution)/shard_map/ppermute | solution.py:258
  68.2 11.7 %collective-permute-start = (bf16[2048,128]{1,0:T(8,128)(2,1)S(1)}, bf16[2048,128]{1,0:T(8,128)(2,1)S(1)}, u32[]{:S(2)}, u32[]{:S(2)}) collective-permute-start(bf16[2048,128]{1,0:T(8,128)(2,1)S(1)} %bitcast.14), channel_id=1, source_target_pairs={{0,192},{8,200},{16,208},{24,216},{32,224},{40,232},{48,240},{56,2... | collective-permute-start | bytes 1572872 | tf_op jit(solution)/shard_map/ppermute | solution.py:261
  70.4 13.0 %collective-permute-start.1 = (bf16[2048,128]{1,0:T(8,128)(2,1)S(1)}, bf16[2048,128]{1,0:T(8,128)(2,1)S(1)}, u32[]{:S(2)}, u32[]{:S(2)}) collective-permute-start(bf16[2048,128]{1,0:T(8,128)(2,1)S(1)} %bitcast.15), channel_id=1, source_target_pairs={{0,64},{8,72},{16,80},{24,88},{32,96},{40,104},{48,112},{56,120},{... | collective-permute-start | bytes 1572872 | tf_op jit(solution)/shard_map/ppermute | solution.py:261
  70.4 14.6 %collective-permute-start.4 = (bf16[2048,128]{1,0:T(8,128)(2,1)S(1)}, bf16[2048,128]{1,0:T(8,128)(2,1)S(1)}, u32[]{:S(2)}, u32[]{:S(2)}) collective-permute-start(bf16[2048,128]{1,0:T(8,128)(2,1)S(1)} %bitcast.16), channel_id=1, source_target_pairs={{0,1},{1,0},{2,3},{3,2},{4,5},{5,4},{6,7},{7,6},{8,9},{9,8},{10,11... | collective-permute-start | bytes 1572872 | tf_op jit(solution)/shard_map/ppermute | solution.py:264
  78.3 8.8 %collective-permute-start.5 = (bf16[2048,128]{1,0:T(8,128)(2,1)S(1)}, bf16[2048,128]{1,0:T(8,128)(2,1)S(1)}, u32[]{:S(2)}, u32[]{:S(2)}) collective-permute-start(bf16[2048,128]{1,0:T(8,128)(2,1)S(1)} %collective-permute-done.2.refs_4_.up.refs_2_), channel_id=1, source_target_pairs={{0,1},{1,0},{2,3},{3,2},{4,5},{5,4},{6,7},{7,6},{8,9},{9,8},{10,11... | collective-permute-start | bytes 1572872 | tf_op jit(solution)/shard_map/ppermute | solution.py:264
  78.3 8.8 %collective-permute-start.6 = (bf16[2048,128]{1,0:T(8,128)(2,1)S(1)}, bf16[2048,128]{1,0:T(8,128)(2,1)S(1)}, u32[]{:S(2)}, u32[]{:S(2)}) collective-permute-start(bf16[2048,128]{1,0:T(8,128)(2,1)S(1)} %collective-permute-done.3.refs_5_.down.refs_3_), channel_id=1, source_target_pairs={{0,1},{1,0},{2,3},{3,2},{4,5},{5,4},{6,7},{7,6},{8,9},{9,8},{10,11... | collective-permute-start | bytes 1572872 | tf_op jit(solution)/shard_map/ppermute | solution.py:264
  80.0 8.5 %collective-permute-start.9 = (bf16[1024,128]{1,0:T(8,128)(2,1)S(1)}, bf16[1024,128]{1,0:T(8,128)(2,1)S(1)}, u32[]{:S(2)}, u32[]{:S(2)}) collective-permute-start(bf16[1024,128]{1,0:T(8,128)(2,1)S(1)} %get-tuple-element.14.refs_1_), channel_id=1, source_target_pairs={{0,2},{1,3},{2,4},{3,5},{4,6},{5,7},{6,0},{7,1},{8,10},{9,11},{10,... | collective-permute-start | bytes 786440 | tf_op jit(solution)/shard_map/ppermute | solution.py:258
  83.4 6.4 %collective-permute-start.10 = (bf16[1024,128]{1,0:T(8,128)(2,1)S(1)}, bf16[1024,128]{1,0:T(8,128)(2,1)S(1)}, u32[]{:S(2)}, u32[]{:S(2)}) collective-permute-start(bf16[1024,128]{1,0:T(8,128)(2,1)S(1)} %get-tuple-element.20), channel_id=1, source_target_pairs={{0,6},{1,7},{2,0},{3,1},{4,2},{5,3},{6,4},{7,5},{8,14},{9,15},{10,... | collective-permute-start | bytes 786440 | tf_op jit(solution)/shard_map/ppermute | solution.py:258
  85.0 6.4 %collective-permute-start.8 = (bf16[1024,128]{1,0:T(8,128)(2,1)S(1)}, bf16[1024,128]{1,0:T(8,128)(2,1)S(1)}, u32[]{:S(2)}, u32[]{:S(2)}) collective-permute-start(bf16[1024,128]{1,0:T(8,128)(2,1)S(1)} %get-tuple-element.16), channel_id=1, source_target_pairs={{0,192},{8,200},{16,208},{24,216},{32,224},{40,232},{48,240},{56,2... | collective-permute-start | bytes 786440 | tf_op jit(solution)/shard_map/ppermute | solution.py:261
  87.0 7.6 %collective-permute-start.7 = (bf16[1024,128]{1,0:T(8,128)(2,1)S(1)}, bf16[1024,128]{1,0:T(8,128)(2,1)S(1)}, u32[]{:S(2)}, u32[]{:S(2)}) collective-permute-start(bf16[1024,128]{1,0:T(8,128)(2,1)S(1)} %get-tuple-element.15), channel_id=1, source_target_pairs={{0,64},{8,72},{16,80},{24,88},{32,96},{40,104},{48,112},{56,120},{... | collective-permute-start | bytes 786440 | tf_op jit(solution)/shard_map/ppermute | solution.py:261
  89.8 5.5 %collective-permute-start.11 = (bf16[2048,128]{1,0:T(8,128)(2,1)S(1)}, bf16[2048,128]{1,0:T(8,128)(2,1)S(1)}, u32[]{:S(2)}, u32[]{:S(2)}) collective-permute-start(bf16[2048,128]{1,0:T(8,128)(2,1)S(1)} %join.1.own), channel_id=1, source_target_pairs={{0,1},{1,0},{2,3},{3,2},{4,5},{5,4},{6,7},{7,6},{8,9},{9,8},{10,11... | collective-permute-start | bytes 1572872 | tf_op jit(solution)/shard_map/ppermute | solution.py:264

commit v19 on v18

--- a/solution.py
+++ b/solution.py
@@ -225,20 +225,32 @@
     )(at, near, side, left, last, own, other)
 
 
-def finish_kernel(scale, parts_ref, out_ref):
-    for i in range(out_ref.shape[1] // LANES):
+def finish_kernel(scale, parts_ref, out_ref, done, sems):
+    copies = []
+    for i in range(done.shape[0]):
         part = pl.ds(i * LANES, LANES)
         total = parts_ref[0, part].astype(jnp.float32)
         for k in range(1, parts_ref.shape[0]):
             total = total + parts_ref[k, part].astype(jnp.float32)
-        out_ref[:, part] = (total * scale).T
+        done[i] = (total * scale).T
+        copies.append(pltpu.make_async_copy(done.at[i], out_ref.at[:, part], sems.at[i]))
+        copies[-1].start()
+    for copy in copies:
+        copy.wait()
 
 
 def finish(parts, scale):
     count, width, rows = parts.shape
-    return pl.pallas_call(
-        lambda parts_ref, out_ref: finish_kernel(scale, parts_ref, out_ref),
+    pieces = width // LANES
+    return pl.pallas_call(
+        functools.partial(finish_kernel, scale),
+        in_specs=[LOCAL],
+        out_specs=pl.BlockSpec(memory_space=pl.ANY),
         out_shape=jax.ShapeDtypeStruct((rows, width), jnp.float32),
+        scratch_shapes=[
+            pltpu.VMEM((pieces, rows, LANES), jnp.float32),
+            pltpu.SemaphoreType.DMA((pieces,)),
+        ],
         compiler_params=pltpu.CompilerParams(vmem_limit_bytes=16 * MIB),
         name="finish",
     )(parts)

time: 129 us -> 129 us (level)
  no operation moved by 1% of the time
where the time goes in v19:
time: 129 us; the launch traced here: 128 us
  blocking collectives  90.9 us (70%)
  waiting for transfers between devices  18.2 us (14%)
  starting transfers between devices  9.97 us (8%)
  Pallas kernels  7.57 us (6%)
  local copies, waits for them, and re-layouts  1.67 us (1%)
    all_to_all x1, blocking collectives, on_device(): lax.all_to_all(outgoing, 'dp', split_axis=0, concat_axis=0, tiled=True)  60 us
    all_to_all x1, blocking collectives, on_device(): lax.all_to_all(partial, 'dp', split_axis=0, concat_axis=0, axis_index_gro...  30.9 us
    ppermute x4, waiting for transfers between devices, along_x(): lax.ppermute(value, 'col', [(i, (i + NCORE * step) % (NX * NCORE)) for i...  9.14 us
    ppermute x4, waiting for transfers between devices, along_y(): lax.ppermute(value, 'dp', [(i, (i + NZ * step) % (NY * NZ)) for i in rang...  9.02 us
    ppermute x4, starting transfers between devices, along_x(): lax.ppermute(value, 'col', [(i, (i + NCORE * step) % (NX * NCORE)) for i...  5.14 us
    ppermute x4, starting transfers between devices, along_y(): lax.ppermute(value, 'dp', [(i, (i + NZ * step) % (NY * NZ)) for i in rang...  4.22 us
  transfers between devices with their start and end apart: 12, of which 6 were waited for; matrix products, arithmetic and copies ran while one was open for 0% of the time, Pallas kernels for 2%

profile of v19, /device:TPU:64, one launch (start us, length us, event | category | flops | bytes accessed | tf_op | source)
XLA Modules:
  0.0 128.5 jit_solution(1747637703783738428)
XLA Ops:
  0.0 1.7 %fusion = (bf16[512,512]{1,0:T(8,128)(2,1)S(1)}, bf16[512,512]{1,0:T(8,128)(2,1)S(1)}, bf16[512,512]{1,0:T(8,128)(2,1)S(1)}, bf16[512,512]{1,0:T(8,128)(2,1)S(1)}) fusion(bf16[2048,512]{1,0:T(8,128)(2,1)} %param.3), kind=kLoop, calls=%fused_computation.2 | loop fusion | bytes 4194304 | tf_op jit(solution)/shard_map/slice | solution.py:42
  1.7 0.1 pad_add_fusion.at
  1.8 1.0 pack.1
  2.8 60.0 %all_to_all.10 = bf16[32,16,16,128]{3,2,1,0:T(8,128)(2,1)S(1)} all-to-all(bf16[32,16,16,128]{3,2,1,0:T(8,128)(2,1)S(1)} %bitcast.20), channel_id=1, replica_groups=mesh['dp'=32,'col'=8] {'dp'}, dimensions={0} | all-to-all | bytes 4194304 | tf_op jit(solution)/shard_map/all_to_all | solution.py:266
  62.8 2.1 %mix.1 = bf16[128,16,128]{2,1,0:T(8,128)(2,1)S(1)} custom-call(s32[128]{0:T(128)S(1)} %copy-done.1, bf16[512,16,128]{2,1,0:T(8,128)(2,1)S(1)} %bitcast.21), custom_call_target="tpu_custom_call" | custom-call | tf_op jit(solution)/shard_map/mix/pallas_call | solution.py:87
  64.9 1.6 %collective-permute-start.2 = (bf16[2048,128]{1,0:T(8,128)(2,1)S(1)}, bf16[2048,128]{1,0:T(8,128)(2,1)S(1)}, u32[]{:S(2)}, u32[]{:S(2)}) collective-permute-start(bf16[2048,128]{1,0:T(8,128)(2,1)S(1)} %bitcast.12), channel_id=1, source_target_pairs={{0,2},{1,3},{2,4},{3,5},{4,6},{5,7},{6,0},{7,1},{8,10},{9,11},{10,... | collective-permute-start | bytes 1572872 | tf_op jit(solution)/shard_map/ppermute | solution.py:270
  66.5 1.7 %collective-permute-start.3 = (bf16[2048,128]{1,0:T(8,128)(2,1)S(1)}, bf16[2048,128]{1,0:T(8,128)(2,1)S(1)}, u32[]{:S(2)}, u32[]{:S(2)}) collective-permute-start(bf16[2048,128]{1,0:T(8,128)(2,1)S(1)} %bitcast.13), channel_id=1, source_target_pairs={{0,6},{1,7},{2,0},{3,1},{4,2},{5,3},{6,4},{7,5},{8,14},{9,15},{10,... | collective-permute-start | bytes 1572872 | tf_op jit(solution)/shard_map/ppermute | solution.py:270
  68.2 2.1 %collective-permute-start = (bf16[2048,128]{1,0:T(8,128)(2,1)S(1)}, bf16[2048,128]{1,0:T(8,128)(2,1)S(1)}, u32[]{:S(2)}, u32[]{:S(2)}) collective-permute-start(bf16[2048,128]{1,0:T(8,128)(2,1)S(1)} %bitcast.14), channel_id=1, source_target_pairs={{0,192},{8,200},{16,208},{24,216},{32,224},{40,232},{48,240},{56,2... | collective-permute-start | bytes 1572872 | tf_op jit(solution)/shard_map/ppermute | solution.py:273
  70.4 7.9 %collective-permute-done.2.refs_4_.up.refs_2_ = bf16[2048,128]{1,0:T(8,128)(2,1)S(1)} collective-permute-done((bf16[2048,128]{1,0:T(8,128)(2,1)S(1)}, bf16[2048,128]{1,0:T(8,128)(2,1)S(1)}, u32[]{:S(2)}, u32[]{:S(2)}) %collective-permute-start.2) | collective-permute-done | bytes 524320 | tf_op jit(solution)/shard_map/ppermute | solution.py:270
  78.3 0.5 collective-permute-start.6
  78.8 1.2 collective-permute-done.refs_1_.down
  80.0 0.3 collective-permute-start.9
  80.3 3.1 %collective-permute-done.1.refs_2_.up = bf16[2048,128]{1,0:T(8,128)(2,1)S(1)} collective-permute-done((bf16[2048,128]{1,0:T(8,128)(2,1)S(1)}, bf16[2048,128]{1,0:T(8,128)(2,1)S(1)}, u32[]{:S(2)}, u32[]{:S(2)}) %collective-permute-start.1) | collective-permute-done | bytes 524320 | tf_op jit(solution)/shard_map/ppermute | solution.py:273
  83.4 1.5 %collective-permute-start.10 = (bf16[1024,128]{1,0:T(8,128)(2,1)S(1)}, bf16[1024,128]{1,0:T(8,128)(2,1)S(1)}, u32[]{:S(2)}, u32[]{:S(2)}) collective-permute-start(bf16[1024,128]{1,0:T(8,128)(2,1)S(1)} %get-tuple-element.20), channel_id=1, source_target_pairs={{0,6},{1,7},{2,0},{3,1},{4,2},{5,3},{6,4},{7,5},{8,14},{9,15},{10,... | collective-permute-start | bytes 786440 | tf_op jit(solution)/shard_map/ppermute | solution.py:270
  85.0 2.0 %collective-permute-start.8 = (bf16[1024,128]{1,0:T(8,128)(2,1)S(1)}, bf16[1024,128]{1,0:T(8,128)(2,1)S(1)}, u32[]{:S(2)}, u32[]{:S(2)}) collective-permute-start(bf16[1024,128]{1,0:T(8,128)(2,1)S(1)} %get-tuple-element.16), channel_id=1, source_target_pairs={{0,192},{8,200},{16,208},{24,216},{32,224},{40,232},{48,240},{56,2... | collective-permute-start | bytes 786440 | tf_op jit(solution)/shard_map/ppermute | solution.py:273
  87.1 1.4 %gram_near.1 = (bf16[384,2048]{1,0:T(8,128)(2,1)S(1)}, bf16[3,384,256]{2,1,0:T(8,128)(2,1)S(1)}) custom-call(bf16[2048,128]{1,0:T(8,128)(2,1)S(1)} %bitcast.17, bf16[2048,128]{1,0:T(8,128)(2,1)S(1)} %collective-permute-done.refs_1_.down, bf16[2048,128]{1,0:T(8,128)(2,1)S(1)} %collective-permute-done.1.refs_2_.up, bf16[2048,128]{1,0:T(8,128)(2,1)S(1)} %bitcast.18, ...), custom_call_target="tpu_custom_call" | custom-call | flops 1207959552 | bytes 8388608 | tf_op jit(solution)/shard_map/gram_near/pallas_call | solution.py:159
  88.5 1.2 collective-permute-done.10.second
  89.8 0.1 collective-permute-start.11
  89.9 1.5 %collective-permute-done.8 = bf16[1024,128]{1,0:T(8,128)(2,1)S(1)} collective-permute-done((bf16[1024,128]{1,0:T(8,128)(2,1)S(1)}, bf16[1024,128]{1,0:T(8,128)(2,1)S(1)}, u32[]{:S(2)}, u32[]{:S(2)}) %collective-permute-start.8) | collective-permute-done | bytes 262176 | tf_op jit(solution)/shard_map/ppermute | solution.py:273
  91.4 3.2 %collective-permute-done.7 = bf16[1024,128]{1,0:T(8,128)(2,1)S(1)} collective-permute-done((bf16[1024,128]{1,0:T(8,128)(2,1)S(1)}, bf16[1024,128]{1,0:T(8,128)(2,1)S(1)}, u32[]{:S(2)}, u32[]{:S(2)}) %collective-permute-start.7) | collective-permute-done | bytes 262176 | tf_op jit(solution)/shard_map/ppermute | solution.py:273
  94.7 0.6 gram_side.1
  95.3 1.4 %gram_far.1 = bf16[8,512,128]{2,1,0:T(8,128)(2,1)S(1)} custom-call(s32[4]{0:T(128)S(1)} %pad_add_fusion.at, bf16[3,384,256]{2,1,0:T(8,128)(2,1)S(1)} %get-tuple-element.13.near_ref, bf16[3,128,256]{2,1,0:T(8,128)(2,1)S(1)} %get-tuple-element.17.side_ref, bf16[384,2048]{1,0:T(8,128)(2,1)S(1)} %get-tuple-element.18.refs_0_.left, ...), custom_call_target="tpu_custom_call" | custom-call | flops 536870912 | bytes 8388608 | tf_op jit(solution)/shard_map/gram_far/pallas_call | solution.py:217
  96.7 30.9 %all_to_all.11.parts_ref = bf16[8,512,128]{2,1,0:T(8,128)(2,1)S(1)} all-to-all(bf16[8,512,128]{2,1,0:T(8,128)(2,1)S(1)} %gram_far.1), channel_id=1, replica_groups={{0,32,72,104,144,176,216,248},{8,40,80,112,152,184,224,192},{16,48,88,1..., dimensions={0} | all-to-all | bytes 2097152 | tf_op jit(solution)/shard_map/all_to_all | solution.py:294
  127.6 0.9 finish.1
  (18 shorter events, 0.2 us)
Async XLA Ops:
  0.0 1.8 %copy-start = (s32[2048]{0:T(1024)S(1)}, s32[2048]{0:T(1024)}, u32[]{:S(2)}) copy-start(s32[2048]{0:T(1024)} %param.4) | copy-start | bytes 24580
  2.8 60.0 %copy-start.1 = (s32[128]{0:T(128)S(1)}, s32[128]{0:T(128)}, u32[]{:S(2)}) copy-start(s32[128]{0:T(128)} %picks_ref.1) | copy-start | bytes 1540
  64.9 13.3 %collective-permute-start.2 = (bf16[2048,128]{1,0:T(8,128)(2,1)S(1)}, bf16[2048,128]{1,0:T(8,128)(2,1)S(1)}, u32[]{:S(2)}, u32[]{:S(2)}) collective-permute-start(bf16[2048,128]{1,0:T(8,128)(2,1)S(1)} %bitcast.12), channel_id=1, source_target_pairs={{0,2},{1,3},{2,4},{3,5},{4,6},{5,7},{6,0},{7,1},{8,10},{9,11},{10,... | collective-permute-start | bytes 1572872 | tf_op jit(solution)/shard_map/ppermute | solution.py:270
  66.5 11.8 %collective-permute-start.3 = (bf16[2048,128]{1,0:T(8,128)(2,1)S(1)}, bf16[2048,128]{1,0:T(8,128)(2,1)S(1)}, u32[]{:S(2)}, u32[]{:S(2)}) collective-permute-start(bf16[2048,128]{1,0:T(8,128)(2,1)S(1)} %bitcast.13), channel_id=1, source_target_pairs={{0,6},{1,7},{2,0},{3,1},{4,2},{5,3},{6,4},{7,5},{8,14},{9,15},{10,... | collective-permute-start | bytes 1572872 | tf_op jit(solution)/shard_map/ppermute | solution.py:270
  68.2 11.7 %collective-permute-start = (bf16[2048,128]{1,0:T(8,128)(2,1)S(1)}, bf16[2048,128]{1,0:T(8,128)(2,1)S(1)}, u32[]{:S(2)}, u32[]{:S(2)}) collective-permute-start(bf16[2048,128]{1,0:T(8,128)(2,1)S(1)} %bitcast.14), channel_id=1, source_target_pairs={{0,192},{8,200},{16,208},{24,216},{32,224},{40,232},{48,240},{56,2... | collective-permute-start | bytes 1572872 | tf_op jit(solution)/shard_map/ppermute | solution.py:273
  70.4 13.0 %collective-permute-start.1 = (bf16[2048,128]{1,0:T(8,128)(2,1)S(1)}, bf16[2048,128]{1,0:T(8,128)(2,1)S(1)}, u32[]{:S(2)}, u32[]{:S(2)}) collective-permute-start(bf16[2048,128]{1,0:T(8,128)(2,1)S(1)} %bitcast.15), channel_id=1, source_target_pairs={{0,64},{8,72},{16,80},{24,88},{32,96},{40,104},{48,112},{56,120},{... | collective-permute-start | bytes 1572872 | tf_op jit(solution)/shard_map/ppermute | solution.py:273
  70.4 14.6 %collective-permute-start.4 = (bf16[2048,128]{1,0:T(8,128)(2,1)S(1)}, bf16[2048,128]{1,0:T(8,128)(2,1)S(1)}, u32[]{:S(2)}, u32[]{:S(2)}) collective-permute-start(bf16[2048,128]{1,0:T(8,128)(2,1)S(1)} %bitcast.16), channel_id=1, source_target_pairs={{0,1},{1,0},{2,3},{3,2},{4,5},{5,4},{6,7},{7,6},{8,9},{9,8},{10,11... | collective-permute-start | bytes 1572872 | tf_op jit(solution)/shard_map/ppermute | solution.py:276
  78.3 8.8 %collective-permute-start.5 = (bf16[2048,128]{1,0:T(8,128)(2,1)S(1)}, bf16[2048,128]{1,0:T(8,128)(2,1)S(1)}, u32[]{:S(2)}, u32[]{:S(2)}) collective-permute-start(bf16[2048,128]{1,0:T(8,128)(2,1)S(1)} %collective-permute-done.2.refs_4_.up.refs_2_), channel_id=1, source_target_pairs={{0,1},{1,0},{2,3},{3,2},{4,5},{5,4},{6,7},{7,6},{8,9},{9,8},{10,11... | collective-permute-start | bytes 1572872 | tf_op jit(solution)/shard_map/ppermute | solution.py:276
  78.3 8.8 %collective-permute-start.6 = (bf16[2048,128]{1,0:T(8,128)(2,1)S(1)}, bf16[2048,128]{1,0:T(8,128)(2,1)S(1)}, u32[]{:S(2)}, u32[]{:S(2)}) collective-permute-start(bf16[2048,128]{1,0:T(8,128)(2,1)S(1)} %collective-permute-done.3.refs_5_.down.refs_3_), channel_id=1, source_target_pairs={{0,1},{1,0},{2,3},{3,2},{4,5},{5,4},{6,7},{7,6},{8,9},{9,8},{10,11... | collective-permute-start | bytes 1572872 | tf_op jit(solution)/shard_map/ppermute | solution.py:276
  80.0 8.5 %collective-permute-start.9 = (bf16[1024,128]{1,0:T(8,128)(2,1)S(1)}, bf16[1024,128]{1,0:T(8,128)(2,1)S(1)}, u32[]{:S(2)}, u32[]{:S(2)}) collective-permute-start(bf16[1024,128]{1,0:T(8,128)(2,1)S(1)} %get-tuple-element.14.refs_1_), channel_id=1, source_target_pairs={{0,2},{1,3},{2,4},{3,5},{4,6},{5,7},{6,0},{7,1},{8,10},{9,11},{10,... | collective-permute-start | bytes 786440 | tf_op jit(solution)/shard_map/ppermute | solution.py:270
  83.4 6.4 %collective-permute-start.10 = (bf16[1024,128]{1,0:T(8,128)(2,1)S(1)}, bf16[1024,128]{1,0:T(8,128)(2,1)S(1)}, u32[]{:S(2)}, u32[]{:S(2)}) collective-permute-start(bf16[1024,128]{1,0:T(8,128)(2,1)S(1)} %get-tuple-element.20), channel_id=1, source_target_pairs={{0,6},{1,7},{2,0},{3,1},{4,2},{5,3},{6,4},{7,5},{8,14},{9,15},{10,... | collective-permute-start | bytes 786440 | tf_op jit(solution)/shard_map/ppermute | solution.py:270
  85.0 6.4 %collective-permute-start.8 = (bf16[1024,128]{1,0:T(8,128)(2,1)S(1)}, bf16[1024,128]{1,0:T(8,128)(2,1)S(1)}, u32[]{:S(2)}, u32[]{:S(2)}) collective-permute-start(bf16[1024,128]{1,0:T(8,128)(2,1)S(1)} %get-tuple-element.16), channel_id=1, source_target_pairs={{0,192},{8,200},{16,208},{24,216},{32,224},{40,232},{48,240},{56,2... | collective-permute-start | bytes 786440 | tf_op jit(solution)/shard_map/ppermute | solution.py:273
  87.0 7.6 %collective-permute-start.7 = (bf16[1024,128]{1,0:T(8,128)(2,1)S(1)}, bf16[1024,128]{1,0:T(8,128)(2,1)S(1)}, u32[]{:S(2)}, u32[]{:S(2)}) collective-permute-start(bf16[1024,128]{1,0:T(8,128)(2,1)S(1)} %get-tuple-element.15), channel_id=1, source_target_pairs={{0,64},{8,72},{16,80},{24,88},{32,96},{40,104},{48,112},{56,120},{... | collective-permute-start | bytes 786440 | tf_op jit(solution)/shard_map/ppermute | solution.py:273
  89.8 5.5 %collective-permute-start.11 = (bf16[2048,128]{1,0:T(8,128)(2,1)S(1)}, bf16[2048,128]{1,0:T(8,128)(2,1)S(1)}, u32[]{:S(2)}, u32[]{:S(2)}) collective-permute-start(bf16[2048,128]{1,0:T(8,128)(2,1)S(1)} %join.1.own), channel_id=1, source_target_pairs={{0,1},{1,0},{2,3},{3,2},{4,5},{5,4},{6,7},{7,6},{8,9},{9,8},{10,11... | collective-permute-start | bytes 1572872 | tf_op jit(solution)/shard_map/ppermute | solution.py:276

commit v20 on v17

--- a/solution.py
+++ b/solution.py
@@ -95,7 +95,7 @@
     )(picks, raw)
 
 
-NEAR = (0, 1, 3)
+NEAR = (0, 3, 1)
 
 
 def halves_kernel(up, down, *refs):
@@ -268,8 +268,8 @@
     x_low, x_high = halves(x_up, x_down)
     y_low, y_high = halves(y_up, y_down, home, x_low)
     y_far = jnp.concatenate([along_y(y_low, 1), along_y(y_high, -1)])
-    own, other = (sketch, x_up, x_down), (home, swap(x_up), swap(x_down))
-    left, near = gram_near((sketch, y_up, y_down), own, other)
+    own, other = (sketch, x_down, x_up), (home, swap(x_down), swap(x_up))
+    left, near = gram_near((sketch, y_down, y_up), own, other)
     x_far = join(along_x(x_low, 1), along_x(x_high, -1), left)
     last, side = gram_side(y_far, own, other)
     partial = gram_far(at, near, side, left, last, x_far, swap(x_far))

time: 129 us -> 132 us (1.023)
  waiting for transfers between devices: 14.7 us -> 19.4 us
  starting transfers between devices: 12.5 us -> 10.2 us
    ppermute x4, waiting for transfers between devices: 7.55 us -> 11.9 us  [along_x(): lax.ppermute(value, 'col', [(i, (i + NCORE * step) % (NX * NCORE)) for i...]
  transfers between devices with their start and end apart: 12 -> 12, of which waited for: 5 -> 6; matrix products, arithmetic and copies ran while one was open for 0% -> 0% of each run, Pallas kernels for 2% -> 2%
where the time goes in v20:
time: 132 us; the launch traced here: 131 us
  blocking collectives  92.1 us (70%)
  waiting for transfers between devices  19.4 us (15%)
  starting transfers between devices  10.2 us (8%)
  Pallas kernels  7.59 us (6%)
  local copies, waits for them, and re-layouts  1.67 us (1%)
    all_to_all x1, blocking collectives, on_device(): lax.all_to_all(outgoing, 'dp', split_axis=0, concat_axis=0, tiled=True)  60 us
    all_to_all x1, blocking collectives, on_device(): lax.all_to_all(partial, 'dp', split_axis=0, concat_axis=0, axis_index_gro...  32.1 us
    ppermute x4, waiting for transfers between devices, along_x(): lax.ppermute(value, 'col', [(i, (i + NCORE * step) % (NX * NCORE)) for i...  11.9 us
    ppermute x4, waiting for transfers between devices, along_y(): lax.ppermute(value, 'dp', [(i, (i + NZ * step) % (NY * NZ)) for i in rang...  7.44 us
    ppermute x4, starting transfers between devices, along_x(): lax.ppermute(value, 'col', [(i, (i + NCORE * step) % (NX * NCORE)) for i...  5.88 us
    ppermute x4, starting transfers between devices, along_y(): lax.ppermute(value, 'dp', [(i, (i + NZ * step) % (NY * NZ)) for i in rang...  4.22 us
  transfers between devices with their start and end apart: 12, of which 6 were waited for; matrix products, arithmetic and copies ran while one was open for 0% of the time, Pallas kernels for 2%

profile of v20, /device:TPU:64, one launch (start us, length us, event | category | flops | bytes accessed | tf_op | source)
XLA Modules:
  0.0 131.1 jit_solution(9207557306570518996)
XLA Ops:
  0.0 1.7 %fusion = (bf16[512,512]{1,0:T(8,128)(2,1)S(1)}, bf16[512,512]{1,0:T(8,128)(2,1)S(1)}, bf16[512,512]{1,0:T(8,128)(2,1)S(1)}, bf16[512,512]{1,0:T(8,128)(2,1)S(1)}) fusion(bf16[2048,512]{1,0:T(8,128)(2,1)} %param.3), kind=kLoop, calls=%fused_computation.2 | loop fusion | bytes 4194304 | tf_op jit(solution)/shard_map/slice | solution.py:42
  1.7 0.1 pad_add_fusion.at
  1.8 1.0 pack.1
  2.8 0.0 copy-start.1
  2.8 60.0 %all_to_all.10 = bf16[32,16,16,128]{3,2,1,0:T(8,128)(2,1)S(1)} all-to-all(bf16[32,16,16,128]{3,2,1,0:T(8,128)(2,1)S(1)} %bitcast.20), channel_id=1, replica_groups=mesh['dp'=32,'col'=8] {'dp'}, dimensions={0} | all-to-all | bytes 4194304 | tf_op jit(solution)/shard_map/all_to_all | solution.py:253
  62.8 2.1 %mix.1 = bf16[128,16,128]{2,1,0:T(8,128)(2,1)S(1)} custom-call(s32[128]{0:T(128)S(1)} %copy-done.1, bf16[512,16,128]{2,1,0:T(8,128)(2,1)S(1)} %bitcast.21), custom_call_target="tpu_custom_call" | custom-call | tf_op jit(solution)/shard_map/mix/pallas_call | solution.py:87
  64.9 2.8 %collective-permute-start.2 = (bf16[2048,128]{1,0:T(8,128)(2,1)S(1)}, bf16[2048,128]{1,0:T(8,128)(2,1)S(1)}, u32[]{:S(2)}, u32[]{:S(2)}) collective-permute-start(bf16[2048,128]{1,0:T(8,128)(2,1)S(1)} %bitcast.12), channel_id=1, source_target_pairs={{0,6},{1,7},{2,0},{3,1},{4,2},{5,3},{6,4},{7,5},{8,14},{9,15},{10,... | collective-permute-start | bytes 1572872 | tf_op jit(solution)/shard_map/ppermute | solution.py:257
  67.8 2.1 %collective-permute-start = (bf16[2048,128]{1,0:T(8,128)(2,1)S(1)}, bf16[2048,128]{1,0:T(8,128)(2,1)S(1)}, u32[]{:S(2)}, u32[]{:S(2)}) collective-permute-start(bf16[2048,128]{1,0:T(8,128)(2,1)S(1)} %bitcast.14), channel_id=1, source_target_pairs={{0,192},{8,200},{16,208},{24,216},{32,224},{40,232},{48,240},{56,2... | collective-permute-start | bytes 1572872 | tf_op jit(solution)/shard_map/ppermute | solution.py:260
  69.9 7.4 %collective-permute-done.2.refs_4_.down.refs_2_ = bf16[2048,128]{1,0:T(8,128)(2,1)S(1)} collective-permute-done((bf16[2048,128]{1,0:T(8,128)(2,1)S(1)}, bf16[2048,128]{1,0:T(8,128)(2,1)S(1)}, u32[]{:S(2)}, u32[]{:S(2)}) %collective-permute-start.2) | collective-permute-done | bytes 524320 | tf_op jit(solution)/shard_map/ppermute | solution.py:257
  77.3 3.4 %collective-permute-done.3.refs_5_.up.refs_3_ = bf16[2048,128]{1,0:T(8,128)(2,1)S(1)} collective-permute-done((bf16[2048,128]{1,0:T(8,128)(2,1)S(1)}, bf16[2048,128]{1,0:T(8,128)(2,1)S(1)}, u32[]{:S(2)}, u32[]{:S(2)}) %collective-permute-start.3) | collective-permute-done | bytes 524320 | tf_op jit(solution)/shard_map/ppermute | solution.py:257
  80.8 0.1 collective-permute-start.9
  80.9 2.3 %collective-permute-done.1.refs_2_.up = bf16[2048,128]{1,0:T(8,128)(2,1)S(1)} collective-permute-done((bf16[2048,128]{1,0:T(8,128)(2,1)S(1)}, bf16[2048,128]{1,0:T(8,128)(2,1)S(1)}, u32[]{:S(2)}, u32[]{:S(2)}) %collective-permute-start.1) | collective-permute-done | bytes 524320 | tf_op jit(solution)/shard_map/ppermute | solution.py:260
  83.2 3.0 %collective-permute-start.10 = (bf16[1024,128]{1,0:T(8,128)(2,1)S(1)}, bf16[1024,128]{1,0:T(8,128)(2,1)S(1)}, u32[]{:S(2)}, u32[]{:S(2)}) collective-permute-start(bf16[1024,128]{1,0:T(8,128)(2,1)S(1)} %get-tuple-element.20), channel_id=1, source_target_pairs={{0,6},{1,7},{2,0},{3,1},{4,2},{5,3},{6,4},{7,5},{8,14},{9,15},{10,... | collective-permute-start | bytes 786440 | tf_op jit(solution)/shard_map/ppermute | solution.py:257
  86.2 0.8 collective-permute-start.8
  87.0 1.3 %collective-permute-start.7 = (bf16[1024,128]{1,0:T(8,128)(2,1)S(1)}, bf16[1024,128]{1,0:T(8,128)(2,1)S(1)}, u32[]{:S(2)}, u32[]{:S(2)}) collective-permute-start(bf16[1024,128]{1,0:T(8,128)(2,1)S(1)} %get-tuple-element.15), channel_id=1, source_target_pairs={{0,64},{8,72},{16,80},{24,88},{32,96},{40,104},{48,112},{56,120},{... | collective-permute-start | bytes 786440 | tf_op jit(solution)/shard_map/ppermute | solution.py:260
  88.3 1.4 %gram_near.1 = (bf16[384,2048]{1,0:T(8,128)(2,1)S(1)}, bf16[3,384,256]{2,1,0:T(8,128)(2,1)S(1)}) custom-call(bf16[2048,128]{1,0:T(8,128)(2,1)S(1)} %bitcast.17, bf16[2048,128]{1,0:T(8,128)(2,1)S(1)} %collective-permute-done.refs_1_.down, bf16[2048,128]{1,0:T(8,128)(2,1)S(1)} %collective-permute-done.1.refs_2_.up, bf16[2048,128]{1,0:T(8,128)(2,1)S(1)} %bitcast.18, ...), custom_call_target="tpu_custom_call" | custom-call | flops 1207959552 | bytes 8388608 | tf_op jit(solution)/shard_map/gram_near/pallas_call | solution.py:158
  89.7 1.1 collective-permute-done.9.first
  90.8 0.1 collective-permute-start.11
  90.9 1.7 %collective-permute-done.8 = bf16[1024,128]{1,0:T(8,128)(2,1)S(1)} collective-permute-done((bf16[1024,128]{1,0:T(8,128)(2,1)S(1)}, bf16[1024,128]{1,0:T(8,128)(2,1)S(1)}, u32[]{:S(2)}, u32[]{:S(2)}) %collective-permute-start.8) | collective-permute-done | bytes 262176 | tf_op jit(solution)/shard_map/ppermute | solution.py:260
  92.7 3.4 %collective-permute-done.7 = bf16[1024,128]{1,0:T(8,128)(2,1)S(1)} collective-permute-done((bf16[1024,128]{1,0:T(8,128)(2,1)S(1)}, bf16[1024,128]{1,0:T(8,128)(2,1)S(1)}, u32[]{:S(2)}, u32[]{:S(2)}) %collective-permute-start.7) | collective-permute-done | bytes 262176 | tf_op jit(solution)/shard_map/ppermute | solution.py:260
  96.1 0.6 gram_side.1
  96.8 1.4 %gram_far.1 = bf16[8,512,128]{2,1,0:T(8,128)(2,1)S(1)} custom-call(s32[4]{0:T(128)S(1)} %pad_add_fusion.at, bf16[3,384,256]{2,1,0:T(8,128)(2,1)S(1)} %get-tuple-element.13.near_ref, bf16[3,128,256]{2,1,0:T(8,128)(2,1)S(1)} %get-tuple-element.17.side_ref, bf16[384,2048]{1,0:T(8,128)(2,1)S(1)} %get-tuple-element.18.refs_0_.left, ...), custom_call_target="tpu_custom_call" | custom-call | flops 536870912 | bytes 8388608 | tf_op jit(solution)/shard_map/gram_far/pallas_call | solution.py:216
  98.1 32.1 %all_to_all.11.parts_ref = bf16[8,512,128]{2,1,0:T(8,128)(2,1)S(1)} all-to-all(bf16[8,512,128]{2,1,0:T(8,128)(2,1)S(1)} %gram_far.1), channel_id=1, replica_groups={{0,32,72,104,144,176,216,248},{8,40,80,112,152,184,224,192},{16,48,88,1..., dimensions={0} | all-to-all | bytes 2097152 | tf_op jit(solution)/shard_map/all_to_all | solution.py:281
  130.2 0.9 finish.1
  (18 shorter events, 0.2 us)
Async XLA Ops:
  0.0 1.8 %copy-start = (s32[2048]{0:T(1024)S(1)}, s32[2048]{0:T(1024)}, u32[]{:S(2)}) copy-start(s32[2048]{0:T(1024)} %param.4) | copy-start | bytes 24580
  2.8 60.0 %copy-start.1 = (s32[128]{0:T(128)S(1)}, s32[128]{0:T(128)}, u32[]{:S(2)}) copy-start(s32[128]{0:T(128)} %picks_ref.1) | copy-start | bytes 1540
  64.9 12.4 %collective-permute-start.2 = (bf16[2048,128]{1,0:T(8,128)(2,1)S(1)}, bf16[2048,128]{1,0:T(8,128)(2,1)S(1)}, u32[]{:S(2)}, u32[]{:S(2)}) collective-permute-start(bf16[2048,128]{1,0:T(8,128)(2,1)S(1)} %bitcast.12), channel_id=1, source_target_pairs={{0,6},{1,7},{2,0},{3,1},{4,2},{5,3},{6,4},{7,5},{8,14},{9,15},{10,... | collective-permute-start | bytes 1572872 | tf_op jit(solution)/shard_map/ppermute | solution.py:257
  67.8 13.0 %collective-permute-start.3 = (bf16[2048,128]{1,0:T(8,128)(2,1)S(1)}, bf16[2048,128]{1,0:T(8,128)(2,1)S(1)}, u32[]{:S(2)}, u32[]{:S(2)}) collective-permute-start(bf16[2048,128]{1,0:T(8,128)(2,1)S(1)} %bitcast.13), channel_id=1, source_target_pairs={{0,2},{1,3},{2,4},{3,5},{4,6},{5,7},{6,0},{7,1},{8,10},{9,11},{10,... | collective-permute-start | bytes 1572872 | tf_op jit(solution)/shard_map/ppermute | solution.py:257
  67.8 13.0 %collective-permute-start = (bf16[2048,128]{1,0:T(8,128)(2,1)S(1)}, bf16[2048,128]{1,0:T(8,128)(2,1)S(1)}, u32[]{:S(2)}, u32[]{:S(2)}) collective-permute-start(bf16[2048,128]{1,0:T(8,128)(2,1)S(1)} %bitcast.14), channel_id=1, source_target_pairs={{0,192},{8,200},{16,208},{24,216},{32,224},{40,232},{48,240},{56,2... | collective-permute-start | bytes 1572872 | tf_op jit(solution)/shard_map/ppermute | solution.py:260
  69.9 13.3 %collective-permute-start.1 = (bf16[2048,128]{1,0:T(8,128)(2,1)S(1)}, bf16[2048,128]{1,0:T(8,128)(2,1)S(1)}, u32[]{:S(2)}, u32[]{:S(2)}) collective-permute-start(bf16[2048,128]{1,0:T(8,128)(2,1)S(1)} %bitcast.15), channel_id=1, source_target_pairs={{0,64},{8,72},{16,80},{24,88},{32,96},{40,104},{48,112},{56,120},{... | collective-permute-start | bytes 1572872 | tf_op jit(solution)/shard_map/ppermute | solution.py:260
  69.9 16.3 %collective-permute-start.4 = (bf16[2048,128]{1,0:T(8,128)(2,1)S(1)}, bf16[2048,128]{1,0:T(8,128)(2,1)S(1)}, u32[]{:S(2)}, u32[]{:S(2)}) collective-permute-start(bf16[2048,128]{1,0:T(8,128)(2,1)S(1)} %bitcast.16), channel_id=1, source_target_pairs={{0,1},{1,0},{2,3},{3,2},{4,5},{5,4},{6,7},{7,6},{8,9},{9,8},{10,11... | collective-permute-start | bytes 1572872 | tf_op jit(solution)/shard_map/ppermute | solution.py:263
  77.3 9.6 %collective-permute-start.5 = (bf16[2048,128]{1,0:T(8,128)(2,1)S(1)}, bf16[2048,128]{1,0:T(8,128)(2,1)S(1)}, u32[]{:S(2)}, u32[]{:S(2)}) collective-permute-start(bf16[2048,128]{1,0:T(8,128)(2,1)S(1)} %collective-permute-done.2.refs_4_.down.refs_2_), channel_id=1, source_target_pairs={{0,1},{1,0},{2,3},{3,2},{4,5},{5,4},{6,7},{7,6},{8,9},{9,8},{10,11... | collective-permute-start | bytes 1572872 | tf_op jit(solution)/shard_map/ppermute | solution.py:263
  80.7 7.6 %collective-permute-start.6 = (bf16[2048,128]{1,0:T(8,128)(2,1)S(1)}, bf16[2048,128]{1,0:T(8,128)(2,1)S(1)}, u32[]{:S(2)}, u32[]{:S(2)}) collective-permute-start(bf16[2048,128]{1,0:T(8,128)(2,1)S(1)} %collective-permute-done.3.refs_5_.up.refs_3_), channel_id=1, source_target_pairs={{0,1},{1,0},{2,3},{3,2},{4,5},{5,4},{6,7},{7,6},{8,9},{9,8},{10,11... | collective-permute-start | bytes 1572872 | tf_op jit(solution)/shard_map/ppermute | solution.py:263
  80.8 10.0 %collective-permute-start.9 = (bf16[1024,128]{1,0:T(8,128)(2,1)S(1)}, bf16[1024,128]{1,0:T(8,128)(2,1)S(1)}, u32[]{:S(2)}, u32[]{:S(2)}) collective-permute-start(bf16[1024,128]{1,0:T(8,128)(2,1)S(1)} %get-tuple-element.14.refs_1_), channel_id=1, source_target_pairs={{0,2},{1,3},{2,4},{3,5},{4,6},{5,7},{6,0},{7,1},{8,10},{9,11},{10,... | collective-permute-start | bytes 786440 | tf_op jit(solution)/shard_map/ppermute | solution.py:257
  83.2 7.6 %collective-permute-start.10 = (bf16[1024,128]{1,0:T(8,128)(2,1)S(1)}, bf16[1024,128]{1,0:T(8,128)(2,1)S(1)}, u32[]{:S(2)}, u32[]{:S(2)}) collective-permute-start(bf16[1024,128]{1,0:T(8,128)(2,1)S(1)} %get-tuple-element.20), channel_id=1, source_target_pairs={{0,6},{1,7},{2,0},{3,1},{4,2},{5,3},{6,4},{7,5},{8,14},{9,15},{10,... | collective-permute-start | bytes 786440 | tf_op jit(solution)/shard_map/ppermute | solution.py:257
  86.2 6.4 %collective-permute-start.8 = (bf16[1024,128]{1,0:T(8,128)(2,1)S(1)}, bf16[1024,128]{1,0:T(8,128)(2,1)S(1)}, u32[]{:S(2)}, u32[]{:S(2)}) collective-permute-start(bf16[1024,128]{1,0:T(8,128)(2,1)S(1)} %get-tuple-element.16), channel_id=1, source_target_pairs={{0,192},{8,200},{16,208},{24,216},{32,224},{40,232},{48,240},{56,2... | collective-permute-start | bytes 786440 | tf_op jit(solution)/shard_map/ppermute | solution.py:260
  87.0 9.1 %collective-permute-start.7 = (bf16[1024,128]{1,0:T(8,128)(2,1)S(1)}, bf16[1024,128]{1,0:T(8,128)(2,1)S(1)}, u32[]{:S(2)}, u32[]{:S(2)}) collective-permute-start(bf16[1024,128]{1,0:T(8,128)(2,1)S(1)} %get-tuple-element.15), channel_id=1, source_target_pairs={{0,64},{8,72},{16,80},{24,88},{32,96},{40,104},{48,112},{56,120},{... | collective-permute-start | bytes 786440 | tf_op jit(solution)/shard_map/ppermute | solution.py:260
  90.8 5.9 %collective-permute-start.11 = (bf16[2048,128]{1,0:T(8,128)(2,1)S(1)}, bf16[2048,128]{1,0:T(8,128)(2,1)S(1)}, u32[]{:S(2)}, u32[]{:S(2)}) collective-permute-start(bf16[2048,128]{1,0:T(8,128)(2,1)S(1)} %join.1.own), channel_id=1, source_target_pairs={{0,1},{1,0},{2,3},{3,2},{4,5},{5,4},{6,7},{7,6},{8,9},{9,8},{10,11... | collective-permute-start | bytes 1572872 | tf_op jit(solution)/shard_map/ppermute | solution.py:263

commit v21 on v18

--- a/solution.py
+++ b/solution.py
@@ -267,8 +267,8 @@
     y_up, y_down = along_y(sketch, 1), along_y(sketch, -1)
     home = swap(sketch)
     x_low, x_high = halves(x_up, x_down)
-    y_low, y_high = halves(y_up, y_down, home, x_low)
-    y_far = jnp.concatenate([along_y(y_low, 1), along_y(y_high, -1)])
+    y_low, y_high = halves(y_down, y_up, home, x_low)
+    y_far = jnp.concatenate([along_y(y_low, -1), along_y(y_high, 1)])
     own, other = (sketch, x_up, x_down), (home, swap(x_up), swap(x_down))
     left, near = gram_near((sketch, y_down, y_up), own, other)
     x_far = join(along_x(x_low, 1), along_x(x_high, -1), left)

time: 129 us -> 129 us (level)
  waiting for transfers between devices: 18.2 us -> 15 us
  blocking collectives: 90.9 us -> 92.8 us
    ppermute x4, waiting for transfers between devices: 9.02 us -> 7.05 us  [along_y(): lax.ppermute(value, 'dp', [(i, (i + NZ * step) % (NY * NZ)) for i in rang...]
    all_to_all x1, blocking collectives: 30.9 us -> 32.8 us  [on_device(): lax.all_to_all(partial, 'dp', split_axis=0, concat_axis=0, axis_index_gro...]
  transfers between devices with their start and end apart: 12 -> 12, of which waited for: 6 -> 4; matrix products, arithmetic and copies ran while one was open for 0% -> 0% of each run, Pallas kernels for 2% -> 2%
where the time goes in v21:
time: 129 us; the launch traced here: 128 us
  blocking collectives  92.8 us (72%)
  waiting for transfers between devices  15 us (12%)
  starting transfers between devices  11.2 us (9%)
  Pallas kernels  7.59 us (6%)
  local copies, waits for them, and re-layouts  1.67 us (1%)
    all_to_all x1, blocking collectives, on_device(): lax.all_to_all(outgoing, 'dp', split_axis=0, concat_axis=0, tiled=True)  60 us
    all_to_all x1, blocking collectives, on_device(): lax.all_to_all(partial, 'dp', split_axis=0, concat_axis=0, axis_index_gro...  32.8 us
    ppermute x4, waiting for transfers between devices, along_x(): lax.ppermute(value, 'col', [(i, (i + NCORE * step) % (NX * NCORE)) for i...  7.93 us
    ppermute x4, waiting for transfers between devices, along_y(): lax.ppermute(value, 'dp', [(i, (i + NZ * step) % (NY * NZ)) for i in rang...  7.05 us
    ppermute x4, starting transfers between devices, along_y(): lax.ppermute(value, 'dp', [(i, (i + NZ * step) % (NY * NZ)) for i in rang...  5.42 us
    ppermute x4, starting transfers between devices, along_x(): lax.ppermute(value, 'col', [(i, (i + NCORE * step) % (NX * NCORE)) for i...  5.14 us
  transfers between devices with their start and end apart: 12, of which 4 were waited for; matrix products, arithmetic and copies ran while one was open for 0% of the time, Pallas kernels for 2%

profile of v21, /device:TPU:64, one launch (start us, length us, event | category | flops | bytes accessed | tf_op | source)
XLA Modules:
  0.0 128.4 jit_solution(2691276612401676468)
XLA Ops:
  0.0 1.7 %fusion = (bf16[512,512]{1,0:T(8,128)(2,1)S(1)}, bf16[512,512]{1,0:T(8,128)(2,1)S(1)}, bf16[512,512]{1,0:T(8,128)(2,1)S(1)}, bf16[512,512]{1,0:T(8,128)(2,1)S(1)}) fusion(bf16[2048,512]{1,0:T(8,128)(2,1)} %param.3), kind=kLoop, calls=%fused_computation.2 | loop fusion | bytes 4194304 | tf_op jit(solution)/shard_map/slice | solution.py:42
  1.7 0.1 pad_add_fusion.at
  1.8 1.0 pack.1
  2.8 60.0 %all_to_all.10 = bf16[32,16,16,128]{3,2,1,0:T(8,128)(2,1)S(1)} all-to-all(bf16[32,16,16,128]{3,2,1,0:T(8,128)(2,1)S(1)} %bitcast.20), channel_id=1, replica_groups=mesh['dp'=32,'col'=8] {'dp'}, dimensions={0} | all-to-all | bytes 4194304 | tf_op jit(solution)/shard_map/all_to_all | solution.py:254
  62.8 2.1 %mix.1 = bf16[128,16,128]{2,1,0:T(8,128)(2,1)S(1)} custom-call(s32[128]{0:T(128)S(1)} %copy-done.1, bf16[512,16,128]{2,1,0:T(8,128)(2,1)S(1)} %bitcast.21), custom_call_target="tpu_custom_call" | custom-call | tf_op jit(solution)/shard_map/mix/pallas_call | solution.py:87
  64.9 1.6 %collective-permute-start.2 = (bf16[2048,128]{1,0:T(8,128)(2,1)S(1)}, bf16[2048,128]{1,0:T(8,128)(2,1)S(1)}, u32[]{:S(2)}, u32[]{:S(2)}) collective-permute-start(bf16[2048,128]{1,0:T(8,128)(2,1)S(1)} %bitcast.12), channel_id=1, source_target_pairs={{0,2},{1,3},{2,4},{3,5},{4,6},{5,7},{6,0},{7,1},{8,10},{9,11},{10,... | collective-permute-start | bytes 1572872 | tf_op jit(solution)/shard_map/ppermute | solution.py:258
  66.5 1.7 %collective-permute-start.3 = (bf16[2048,128]{1,0:T(8,128)(2,1)S(1)}, bf16[2048,128]{1,0:T(8,128)(2,1)S(1)}, u32[]{:S(2)}, u32[]{:S(2)}) collective-permute-start(bf16[2048,128]{1,0:T(8,128)(2,1)S(1)} %bitcast.13), channel_id=1, source_target_pairs={{0,6},{1,7},{2,0},{3,1},{4,2},{5,3},{6,4},{7,5},{8,14},{9,15},{10,... | collective-permute-start | bytes 1572872 | tf_op jit(solution)/shard_map/ppermute | solution.py:258
  68.2 2.1 %collective-permute-start = (bf16[2048,128]{1,0:T(8,128)(2,1)S(1)}, bf16[2048,128]{1,0:T(8,128)(2,1)S(1)}, u32[]{:S(2)}, u32[]{:S(2)}) collective-permute-start(bf16[2048,128]{1,0:T(8,128)(2,1)S(1)} %bitcast.14), channel_id=1, source_target_pairs={{0,192},{8,200},{16,208},{24,216},{32,224},{40,232},{48,240},{56,2... | collective-permute-start | bytes 1572872 | tf_op jit(solution)/shard_map/ppermute | solution.py:261
  70.4 7.9 %collective-permute-done.2.refs_4_.up.refs_2_ = bf16[2048,128]{1,0:T(8,128)(2,1)S(1)} collective-permute-done((bf16[2048,128]{1,0:T(8,128)(2,1)S(1)}, bf16[2048,128]{1,0:T(8,128)(2,1)S(1)}, u32[]{:S(2)}, u32[]{:S(2)}) %collective-permute-start.2) | collective-permute-done | bytes 524320 | tf_op jit(solution)/shard_map/ppermute | solution.py:258
  78.3 0.5 collective-permute-start.6
  78.8 1.2 collective-permute-done.refs_1_.up
  80.0 0.3 collective-permute-start.9
  80.3 3.1 %collective-permute-done.1.refs_2_.down = bf16[2048,128]{1,0:T(8,128)(2,1)S(1)} collective-permute-done((bf16[2048,128]{1,0:T(8,128)(2,1)S(1)}, bf16[2048,128]{1,0:T(8,128)(2,1)S(1)}, u32[]{:S(2)}, u32[]{:S(2)}) %collective-permute-start.1) | collective-permute-done | bytes 524320 | tf_op jit(solution)/shard_map/ppermute | solution.py:261
  83.4 1.5 %collective-permute-start.10 = (bf16[1024,128]{1,0:T(8,128)(2,1)S(1)}, bf16[1024,128]{1,0:T(8,128)(2,1)S(1)}, u32[]{:S(2)}, u32[]{:S(2)}) collective-permute-start(bf16[1024,128]{1,0:T(8,128)(2,1)S(1)} %get-tuple-element.20), channel_id=1, source_target_pairs={{0,6},{1,7},{2,0},{3,1},{4,2},{5,3},{6,4},{7,5},{8,14},{9,15},{10,... | collective-permute-start | bytes 786440 | tf_op jit(solution)/shard_map/ppermute | solution.py:258
  85.0 0.1 collective-permute-start.8
  85.1 3.2 %collective-permute-start.7 = (bf16[1024,128]{1,0:T(8,128)(2,1)S(1)}, bf16[1024,128]{1,0:T(8,128)(2,1)S(1)}, u32[]{:S(2)}, u32[]{:S(2)}) collective-permute-start(bf16[1024,128]{1,0:T(8,128)(2,1)S(1)} %get-tuple-element.15), channel_id=1, source_target_pairs={{0,192},{8,200},{16,208},{24,216},{32,224},{40,232},{48,240},{56,2... | collective-permute-start | bytes 786440 | tf_op jit(solution)/shard_map/ppermute | solution.py:261
  88.3 1.4 %gram_near.1 = (bf16[384,2048]{1,0:T(8,128)(2,1)S(1)}, bf16[3,384,256]{2,1,0:T(8,128)(2,1)S(1)}) custom-call(bf16[2048,128]{1,0:T(8,128)(2,1)S(1)} %bitcast.17, bf16[2048,128]{1,0:T(8,128)(2,1)S(1)} %collective-permute-done.refs_1_.up, bf16[2048,128]{1,0:T(8,128)(2,1)S(1)} %collective-permute-done.1.refs_2_.down, bf16[2048,128]{1,0:T(8,128)(2,1)S(1)} %bitcast.18, ...), custom_call_target="tpu_custom_call" | custom-call | flops 1207959552 | bytes 8388608 | tf_op jit(solution)/shard_map/gram_near/pallas_call | solution.py:159
  89.7 0.0 collective-permute-done.10.second
  89.8 0.1 collective-permute-start.11
  89.9 2.7 %collective-permute-done.8 = bf16[1024,128]{1,0:T(8,128)(2,1)S(1)} collective-permute-done((bf16[1024,128]{1,0:T(8,128)(2,1)S(1)}, bf16[1024,128]{1,0:T(8,128)(2,1)S(1)}, u32[]{:S(2)}, u32[]{:S(2)}) %collective-permute-start.8) | collective-permute-done | bytes 262176 | tf_op jit(solution)/shard_map/ppermute | solution.py:261
  92.7 0.6 gram_side.1
  93.4 1.4 %gram_far.1 = bf16[8,512,128]{2,1,0:T(8,128)(2,1)S(1)} custom-call(s32[4]{0:T(128)S(1)} %pad_add_fusion.at, bf16[3,384,256]{2,1,0:T(8,128)(2,1)S(1)} %get-tuple-element.13.near_ref, bf16[3,128,256]{2,1,0:T(8,128)(2,1)S(1)} %get-tuple-element.17.side_ref, bf16[384,2048]{1,0:T(8,128)(2,1)S(1)} %get-tuple-element.18.refs_0_.left, ...), custom_call_target="tpu_custom_call" | custom-call | flops 536870912 | bytes 8388608 | tf_op jit(solution)/shard_map/gram_far/pallas_call | solution.py:217
  94.7 32.8 %all_to_all.11.parts_ref = bf16[8,512,128]{2,1,0:T(8,128)(2,1)S(1)} all-to-all(bf16[8,512,128]{2,1,0:T(8,128)(2,1)S(1)} %gram_far.1), channel_id=1, replica_groups={{0,32,72,104,144,176,216,248},{8,40,80,112,152,184,224,192},{16,48,88,1..., dimensions={0} | all-to-all | bytes 2097152 | tf_op jit(solution)/shard_map/all_to_all | solution.py:282
  127.5 0.9 finish.1
  (18 shorter events, 0.2 us)
Async XLA Ops:
  0.0 1.8 %copy-start = (s32[2048]{0:T(1024)S(1)}, s32[2048]{0:T(1024)}, u32[]{:S(2)}) copy-start(s32[2048]{0:T(1024)} %param.4) | copy-start | bytes 24580
  2.8 60.0 %copy-start.1 = (s32[128]{0:T(128)S(1)}, s32[128]{0:T(128)}, u32[]{:S(2)}) copy-start(s32[128]{0:T(128)} %picks_ref.1) | copy-start | bytes 1540
  64.9 13.3 %collective-permute-start.2 = (bf16[2048,128]{1,0:T(8,128)(2,1)S(1)}, bf16[2048,128]{1,0:T(8,128)(2,1)S(1)}, u32[]{:S(2)}, u32[]{:S(2)}) collective-permute-start(bf16[2048,128]{1,0:T(8,128)(2,1)S(1)} %bitcast.12), channel_id=1, source_target_pairs={{0,2},{1,3},{2,4},{3,5},{4,6},{5,7},{6,0},{7,1},{8,10},{9,11},{10,... | collective-permute-start | bytes 1572872 | tf_op jit(solution)/shard_map/ppermute | solution.py:258
  66.5 11.8 %collective-permute-start.3 = (bf16[2048,128]{1,0:T(8,128)(2,1)S(1)}, bf16[2048,128]{1,0:T(8,128)(2,1)S(1)}, u32[]{:S(2)}, u32[]{:S(2)}) collective-permute-start(bf16[2048,128]{1,0:T(8,128)(2,1)S(1)} %bitcast.13), channel_id=1, source_target_pairs={{0,6},{1,7},{2,0},{3,1},{4,2},{5,3},{6,4},{7,5},{8,14},{9,15},{10,... | collective-permute-start | bytes 1572872 | tf_op jit(solution)/shard_map/ppermute | solution.py:258
  68.2 11.7 %collective-permute-start = (bf16[2048,128]{1,0:T(8,128)(2,1)S(1)}, bf16[2048,128]{1,0:T(8,128)(2,1)S(1)}, u32[]{:S(2)}, u32[]{:S(2)}) collective-permute-start(bf16[2048,128]{1,0:T(8,128)(2,1)S(1)} %bitcast.14), channel_id=1, source_target_pairs={{0,192},{8,200},{16,208},{24,216},{32,224},{40,232},{48,240},{56,2... | collective-permute-start | bytes 1572872 | tf_op jit(solution)/shard_map/ppermute | solution.py:261
  70.4 13.0 %collective-permute-start.1 = (bf16[2048,128]{1,0:T(8,128)(2,1)S(1)}, bf16[2048,128]{1,0:T(8,128)(2,1)S(1)}, u32[]{:S(2)}, u32[]{:S(2)}) collective-permute-start(bf16[2048,128]{1,0:T(8,128)(2,1)S(1)} %bitcast.15), channel_id=1, source_target_pairs={{0,64},{8,72},{16,80},{24,88},{32,96},{40,104},{48,112},{56,120},{... | collective-permute-start | bytes 1572872 | tf_op jit(solution)/shard_map/ppermute | solution.py:261
  70.4 14.6 %collective-permute-start.4 = (bf16[2048,128]{1,0:T(8,128)(2,1)S(1)}, bf16[2048,128]{1,0:T(8,128)(2,1)S(1)}, u32[]{:S(2)}, u32[]{:S(2)}) collective-permute-start(bf16[2048,128]{1,0:T(8,128)(2,1)S(1)} %bitcast.16), channel_id=1, source_target_pairs={{0,1},{1,0},{2,3},{3,2},{4,5},{5,4},{6,7},{7,6},{8,9},{9,8},{10,11... | collective-permute-start | bytes 1572872 | tf_op jit(solution)/shard_map/ppermute | solution.py:264
  78.3 6.8 %collective-permute-start.5 = (bf16[2048,128]{1,0:T(8,128)(2,1)S(1)}, bf16[2048,128]{1,0:T(8,128)(2,1)S(1)}, u32[]{:S(2)}, u32[]{:S(2)}) collective-permute-start(bf16[2048,128]{1,0:T(8,128)(2,1)S(1)} %collective-permute-done.2.refs_4_.up.refs_2_), channel_id=1, source_target_pairs={{0,1},{1,0},{2,3},{3,2},{4,5},{5,4},{6,7},{7,6},{8,9},{9,8},{10,11... | collective-permute-start | bytes 1572872 | tf_op jit(solution)/shard_map/ppermute | solution.py:264
  78.3 10.0 %collective-permute-start.6 = (bf16[2048,128]{1,0:T(8,128)(2,1)S(1)}, bf16[2048,128]{1,0:T(8,128)(2,1)S(1)}, u32[]{:S(2)}, u32[]{:S(2)}) collective-permute-start(bf16[2048,128]{1,0:T(8,128)(2,1)S(1)} %collective-permute-done.3.refs_5_.down.refs_3_), channel_id=1, source_target_pairs={{0,1},{1,0},{2,3},{3,2},{4,5},{5,4},{6,7},{7,6},{8,9},{9,8},{10,11... | collective-permute-start | bytes 1572872 | tf_op jit(solution)/shard_map/ppermute | solution.py:264
  80.0 9.7 %collective-permute-start.9 = (bf16[1024,128]{1,0:T(8,128)(2,1)S(1)}, bf16[1024,128]{1,0:T(8,128)(2,1)S(1)}, u32[]{:S(2)}, u32[]{:S(2)}) collective-permute-start(bf16[1024,128]{1,0:T(8,128)(2,1)S(1)} %get-tuple-element.14.refs_1_), channel_id=1, source_target_pairs={{0,2},{1,3},{2,4},{3,5},{4,6},{5,7},{6,0},{7,1},{8,10},{9,11},{10,... | collective-permute-start | bytes 786440 | tf_op jit(solution)/shard_map/ppermute | solution.py:258
  83.4 6.4 %collective-permute-start.10 = (bf16[1024,128]{1,0:T(8,128)(2,1)S(1)}, bf16[1024,128]{1,0:T(8,128)(2,1)S(1)}, u32[]{:S(2)}, u32[]{:S(2)}) collective-permute-start(bf16[1024,128]{1,0:T(8,128)(2,1)S(1)} %get-tuple-element.20), channel_id=1, source_target_pairs={{0,6},{1,7},{2,0},{3,1},{4,2},{5,3},{6,4},{7,5},{8,14},{9,15},{10,... | collective-permute-start | bytes 786440 | tf_op jit(solution)/shard_map/ppermute | solution.py:258
  85.0 7.7 %collective-permute-start.8 = (bf16[1024,128]{1,0:T(8,128)(2,1)S(1)}, bf16[1024,128]{1,0:T(8,128)(2,1)S(1)}, u32[]{:S(2)}, u32[]{:S(2)}) collective-permute-start(bf16[1024,128]{1,0:T(8,128)(2,1)S(1)} %get-tuple-element.16), channel_id=1, source_target_pairs={{0,64},{8,72},{16,80},{24,88},{32,96},{40,104},{48,112},{56,120},{... | collective-permute-start | bytes 786440 | tf_op jit(solution)/shard_map/ppermute | solution.py:261
  85.1 7.6 %collective-permute-start.7 = (bf16[1024,128]{1,0:T(8,128)(2,1)S(1)}, bf16[1024,128]{1,0:T(8,128)(2,1)S(1)}, u32[]{:S(2)}, u32[]{:S(2)}) collective-permute-start(bf16[1024,128]{1,0:T(8,128)(2,1)S(1)} %get-tuple-element.15), channel_id=1, source_target_pairs={{0,192},{8,200},{16,208},{24,216},{32,224},{40,232},{48,240},{56,2... | collective-permute-start | bytes 786440 | tf_op jit(solution)/shard_map/ppermute | solution.py:261
  89.8 3.5 %collective-permute-start.11 = (bf16[2048,128]{1,0:T(8,128)(2,1)S(1)}, bf16[2048,128]{1,0:T(8,128)(2,1)S(1)}, u32[]{:S(2)}, u32[]{:S(2)}) collective-permute-start(bf16[2048,128]{1,0:T(8,128)(2,1)S(1)} %join.1.own), channel_id=1, source_target_pairs={{0,1},{1,0},{2,3},{3,2},{4,5},{5,4},{6,7},{7,6},{8,9},{9,8},{10,11... | collective-permute-start | bytes 1572872 | tf_op jit(solution)/shard_map/ppermute | solution.py:264

commit v22 on v18

--- a/solution.py
+++ b/solution.py
@@ -14,7 +14,7 @@
 N_BLOCKS = 512
 CHUNK = BLOCK // NZ
 MIB = 1 << 20
-PIECES = 4
+PIECES = 2
 
 
 SCALARS = pl.BlockSpec(memory_space=pltpu.SMEM)

time: 129 us -> 129 us (level)
  no operation moved by 1% of the time
where the time goes in v22:
time: 129 us
  blocking collectives  90.9 us (70%)
  waiting for transfers between devices  18.2 us (14%)
  starting transfers between devices  9.97 us (8%)
  Pallas kernels  7.58 us (6%)
  local copies, waits for them, and re-layouts  1.7 us (1%)
    all_to_all x1, blocking collectives, on_device(): lax.all_to_all(outgoing, 'dp', split_axis=0, concat_axis=0, tiled=True)  60 us
    all_to_all x1, blocking collectives, on_device(): lax.all_to_all(partial, 'dp', split_axis=0, concat_axis=0, axis_index_gro...  30.9 us
    ppermute x4, waiting for transfers between devices, along_x(): lax.ppermute(value, 'col', [(i, (i + NCORE * step) % (NX * NCORE)) for i...  9.14 us
    ppermute x4, waiting for transfers between devices, along_y(): lax.ppermute(value, 'dp', [(i, (i + NZ * step) % (NY * NZ)) for i in rang...  9.02 us
    ppermute x4, starting transfers between devices, along_x(): lax.ppermute(value, 'col', [(i, (i + NCORE * step) % (NX * NCORE)) for i...  5.14 us
    ppermute x4, starting transfers between devices, along_y(): lax.ppermute(value, 'dp', [(i, (i + NZ * step) % (NY * NZ)) for i in rang...  4.22 us
  transfers between devices with their start and end apart: 12, of which 6 were waited for; matrix products, arithmetic and copies ran while one was open for 0% of the time, Pallas kernels for 2%

profile of v22, /device:TPU:64, one launch (start us, length us, event | category | flops | bytes accessed | tf_op | source)
XLA Modules:
  0.0 128.5 jit_solution(298149098543400226)
XLA Ops:
  0.0 1.7 %fusion = (bf16[1024,512]{1,0:T(8,128)(2,1)S(1)}, bf16[1024,512]{1,0:T(8,128)(2,1)S(1)}) fusion(bf16[2048,512]{1,0:T(8,128)(2,1)} %param.3), kind=kLoop, calls=%fused_computation.2 | loop fusion | bytes 4194304 | tf_op jit(solution)/shard_map/slice | solution.py:42
  1.7 0.1 pad_add_fusion.at
  1.8 1.0 pack.1
  2.8 60.0 %all_to_all.10 = bf16[32,16,16,128]{3,2,1,0:T(8,128)(2,1)S(1)} all-to-all(bf16[32,16,16,128]{3,2,1,0:T(8,128)(2,1)S(1)} %bitcast.18), channel_id=1, replica_groups=mesh['dp'=32,'col'=8] {'dp'}, dimensions={0} | all-to-all | bytes 4194304 | tf_op jit(solution)/shard_map/all_to_all | solution.py:254
  62.8 2.1 %mix.1 = bf16[128,16,128]{2,1,0:T(8,128)(2,1)S(1)} custom-call(s32[128]{0:T(128)S(1)} %copy-done.1, bf16[512,16,128]{2,1,0:T(8,128)(2,1)S(1)} %bitcast.19), custom_call_target="tpu_custom_call" | custom-call | tf_op jit(solution)/shard_map/mix/pallas_call | solution.py:87
  64.9 1.6 %collective-permute-start.2 = (bf16[2048,128]{1,0:T(8,128)(2,1)S(1)}, bf16[2048,128]{1,0:T(8,128)(2,1)S(1)}, u32[]{:S(2)}, u32[]{:S(2)}) collective-permute-start(bf16[2048,128]{1,0:T(8,128)(2,1)S(1)} %bitcast.10), channel_id=1, source_target_pairs={{0,2},{1,3},{2,4},{3,5},{4,6},{5,7},{6,0},{7,1},{8,10},{9,11},{10,... | collective-permute-start | bytes 1572872 | tf_op jit(solution)/shard_map/ppermute | solution.py:258
  66.5 1.7 %collective-permute-start.3 = (bf16[2048,128]{1,0:T(8,128)(2,1)S(1)}, bf16[2048,128]{1,0:T(8,128)(2,1)S(1)}, u32[]{:S(2)}, u32[]{:S(2)}) collective-permute-start(bf16[2048,128]{1,0:T(8,128)(2,1)S(1)} %bitcast.11), channel_id=1, source_target_pairs={{0,6},{1,7},{2,0},{3,1},{4,2},{5,3},{6,4},{7,5},{8,14},{9,15},{10,... | collective-permute-start | bytes 1572872 | tf_op jit(solution)/shard_map/ppermute | solution.py:258
  68.3 2.1 %collective-permute-start = (bf16[2048,128]{1,0:T(8,128)(2,1)S(1)}, bf16[2048,128]{1,0:T(8,128)(2,1)S(1)}, u32[]{:S(2)}, u32[]{:S(2)}) collective-permute-start(bf16[2048,128]{1,0:T(8,128)(2,1)S(1)} %bitcast.12), channel_id=1, source_target_pairs={{0,192},{8,200},{16,208},{24,216},{32,224},{40,232},{48,240},{56,2... | collective-permute-start | bytes 1572872 | tf_op jit(solution)/shard_map/ppermute | solution.py:261
  70.4 7.9 %collective-permute-done.2.refs_4_.up.refs_2_ = bf16[2048,128]{1,0:T(8,128)(2,1)S(1)} collective-permute-done((bf16[2048,128]{1,0:T(8,128)(2,1)S(1)}, bf16[2048,128]{1,0:T(8,128)(2,1)S(1)}, u32[]{:S(2)}, u32[]{:S(2)}) %collective-permute-start.2) | collective-permute-done | bytes 524320 | tf_op jit(solution)/shard_map/ppermute | solution.py:258
  78.3 0.5 collective-permute-start.6
  78.8 1.2 collective-permute-done.refs_1_.down
  80.0 0.3 collective-permute-start.9
  80.3 3.1 %collective-permute-done.1.refs_2_.up = bf16[2048,128]{1,0:T(8,128)(2,1)S(1)} collective-permute-done((bf16[2048,128]{1,0:T(8,128)(2,1)S(1)}, bf16[2048,128]{1,0:T(8,128)(2,1)S(1)}, u32[]{:S(2)}, u32[]{:S(2)}) %collective-permute-start.1) | collective-permute-done | bytes 524320 | tf_op jit(solution)/shard_map/ppermute | solution.py:261
  83.4 1.5 %collective-permute-start.10 = (bf16[1024,128]{1,0:T(8,128)(2,1)S(1)}, bf16[1024,128]{1,0:T(8,128)(2,1)S(1)}, u32[]{:S(2)}, u32[]{:S(2)}) collective-permute-start(bf16[1024,128]{1,0:T(8,128)(2,1)S(1)} %get-tuple-element.20), channel_id=1, source_target_pairs={{0,6},{1,7},{2,0},{3,1},{4,2},{5,3},{6,4},{7,5},{8,14},{9,15},{10,... | collective-permute-start | bytes 786440 | tf_op jit(solution)/shard_map/ppermute | solution.py:258
  85.0 2.0 %collective-permute-start.8 = (bf16[1024,128]{1,0:T(8,128)(2,1)S(1)}, bf16[1024,128]{1,0:T(8,128)(2,1)S(1)}, u32[]{:S(2)}, u32[]{:S(2)}) collective-permute-start(bf16[1024,128]{1,0:T(8,128)(2,1)S(1)} %get-tuple-element.16), channel_id=1, source_target_pairs={{0,192},{8,200},{16,208},{24,216},{32,224},{40,232},{48,240},{56,2... | collective-permute-start | bytes 786440 | tf_op jit(solution)/shard_map/ppermute | solution.py:261
  87.1 1.4 %gram_near.1 = (bf16[384,2048]{1,0:T(8,128)(2,1)S(1)}, bf16[3,384,256]{2,1,0:T(8,128)(2,1)S(1)}) custom-call(bf16[2048,128]{1,0:T(8,128)(2,1)S(1)} %bitcast.15, bf16[2048,128]{1,0:T(8,128)(2,1)S(1)} %collective-permute-done.refs_1_.down, bf16[2048,128]{1,0:T(8,128)(2,1)S(1)} %collective-permute-done.1.refs_2_.up, bf16[2048,128]{1,0:T(8,128)(2,1)S(1)} %bitcast.16, ...), custom_call_target="tpu_custom_call" | custom-call | flops 1207959552 | bytes 8388608 | tf_op jit(solution)/shard_map/gram_near/pallas_call | solution.py:159
  88.6 1.2 collective-permute-done.10.second
  89.8 0.1 collective-permute-start.11
  89.9 1.5 %collective-permute-done.8 = bf16[1024,128]{1,0:T(8,128)(2,1)S(1)} collective-permute-done((bf16[1024,128]{1,0:T(8,128)(2,1)S(1)}, bf16[1024,128]{1,0:T(8,128)(2,1)S(1)}, u32[]{:S(2)}, u32[]{:S(2)}) %collective-permute-start.8) | collective-permute-done | bytes 262176 | tf_op jit(solution)/shard_map/ppermute | solution.py:261
  91.5 3.2 %collective-permute-done.7 = bf16[1024,128]{1,0:T(8,128)(2,1)S(1)} collective-permute-done((bf16[1024,128]{1,0:T(8,128)(2,1)S(1)}, bf16[1024,128]{1,0:T(8,128)(2,1)S(1)}, u32[]{:S(2)}, u32[]{:S(2)}) %collective-permute-start.7) | collective-permute-done | bytes 262176 | tf_op jit(solution)/shard_map/ppermute | solution.py:261
  94.7 0.6 gram_side.1
  95.3 1.4 %gram_far.1 = bf16[8,512,128]{2,1,0:T(8,128)(2,1)S(1)} custom-call(s32[4]{0:T(128)S(1)} %pad_add_fusion.at, bf16[3,384,256]{2,1,0:T(8,128)(2,1)S(1)} %get-tuple-element.13.near_ref, bf16[3,128,256]{2,1,0:T(8,128)(2,1)S(1)} %get-tuple-element.17.side_ref, bf16[384,2048]{1,0:T(8,128)(2,1)S(1)} %get-tuple-element.18.refs_0_.left, ...), custom_call_target="tpu_custom_call" | custom-call | flops 536870912 | bytes 8388608 | tf_op jit(solution)/shard_map/gram_far/pallas_call | solution.py:217
  96.7 30.9 %all_to_all.11.parts_ref = bf16[8,512,128]{2,1,0:T(8,128)(2,1)S(1)} all-to-all(bf16[8,512,128]{2,1,0:T(8,128)(2,1)S(1)} %gram_far.1), channel_id=1, replica_groups={{0,32,72,104,144,176,216,248},{8,40,80,112,152,184,224,192},{16,48,88,1..., dimensions={0} | all-to-all | bytes 2097152 | tf_op jit(solution)/shard_map/all_to_all | solution.py:282
  127.6 0.9 finish.1
  (18 shorter events, 0.2 us)
Async XLA Ops:
  0.0 1.8 %copy-start = (s32[2048]{0:T(1024)S(1)}, s32[2048]{0:T(1024)}, u32[]{:S(2)}) copy-start(s32[2048]{0:T(1024)} %param.4) | copy-start | bytes 24580
  2.8 60.0 %copy-start.1 = (s32[128]{0:T(128)S(1)}, s32[128]{0:T(128)}, u32[]{:S(2)}) copy-start(s32[128]{0:T(128)} %picks_ref.1) | copy-start | bytes 1540
  64.9 13.3 %collective-permute-start.2 = (bf16[2048,128]{1,0:T(8,128)(2,1)S(1)}, bf16[2048,128]{1,0:T(8,128)(2,1)S(1)}, u32[]{:S(2)}, u32[]{:S(2)}) collective-permute-start(bf16[2048,128]{1,0:T(8,128)(2,1)S(1)} %bitcast.10), channel_id=1, source_target_pairs={{0,2},{1,3},{2,4},{3,5},{4,6},{5,7},{6,0},{7,1},{8,10},{9,11},{10,... | collective-permute-start | bytes 1572872 | tf_op jit(solution)/shard_map/ppermute | solution.py:258
  66.5 11.8 %collective-permute-start.3 = (bf16[2048,128]{1,0:T(8,128)(2,1)S(1)}, bf16[2048,128]{1,0:T(8,128)(2,1)S(1)}, u32[]{:S(2)}, u32[]{:S(2)}) collective-permute-start(bf16[2048,128]{1,0:T(8,128)(2,1)S(1)} %bitcast.11), channel_id=1, source_target_pairs={{0,6},{1,7},{2,0},{3,1},{4,2},{5,3},{6,4},{7,5},{8,14},{9,15},{10,... | collective-permute-start | bytes 1572872 | tf_op jit(solution)/shard_map/ppermute | solution.py:258
  68.3 11.7 %collective-permute-start = (bf16[2048,128]{1,0:T(8,128)(2,1)S(1)}, bf16[2048,128]{1,0:T(8,128)(2,1)S(1)}, u32[]{:S(2)}, u32[]{:S(2)}) collective-permute-start(bf16[2048,128]{1,0:T(8,128)(2,1)S(1)} %bitcast.12), channel_id=1, source_target_pairs={{0,192},{8,200},{16,208},{24,216},{32,224},{40,232},{48,240},{56,2... | collective-permute-start | bytes 1572872 | tf_op jit(solution)/shard_map/ppermute | solution.py:261
  70.4 13.0 %collective-permute-start.1 = (bf16[2048,128]{1,0:T(8,128)(2,1)S(1)}, bf16[2048,128]{1,0:T(8,128)(2,1)S(1)}, u32[]{:S(2)}, u32[]{:S(2)}) collective-permute-start(bf16[2048,128]{1,0:T(8,128)(2,1)S(1)} %bitcast.13), channel_id=1, source_target_pairs={{0,64},{8,72},{16,80},{24,88},{32,96},{40,104},{48,112},{56,120},{... | collective-permute-start | bytes 1572872 | tf_op jit(solution)/shard_map/ppermute | solution.py:261
  70.4 14.6 %collective-permute-start.4 = (bf16[2048,128]{1,0:T(8,128)(2,1)S(1)}, bf16[2048,128]{1,0:T(8,128)(2,1)S(1)}, u32[]{:S(2)}, u32[]{:S(2)}) collective-permute-start(bf16[2048,128]{1,0:T(8,128)(2,1)S(1)} %bitcast.14), channel_id=1, source_target_pairs={{0,1},{1,0},{2,3},{3,2},{4,5},{5,4},{6,7},{7,6},{8,9},{9,8},{10,11... | collective-permute-start | bytes 1572872 | tf_op jit(solution)/shard_map/ppermute | solution.py:264
  78.3 8.8 %collective-permute-start.5 = (bf16[2048,128]{1,0:T(8,128)(2,1)S(1)}, bf16[2048,128]{1,0:T(8,128)(2,1)S(1)}, u32[]{:S(2)}, u32[]{:S(2)}) collective-permute-start(bf16[2048,128]{1,0:T(8,128)(2,1)S(1)} %collective-permute-done.2.refs_4_.up.refs_2_), channel_id=1, source_target_pairs={{0,1},{1,0},{2,3},{3,2},{4,5},{5,4},{6,7},{7,6},{8,9},{9,8},{10,11... | collective-permute-start | bytes 1572872 | tf_op jit(solution)/shard_map/ppermute | solution.py:264
  78.3 8.8 %collective-permute-start.6 = (bf16[2048,128]{1,0:T(8,128)(2,1)S(1)}, bf16[2048,128]{1,0:T(8,128)(2,1)S(1)}, u32[]{:S(2)}, u32[]{:S(2)}) collective-permute-start(bf16[2048,128]{1,0:T(8,128)(2,1)S(1)} %collective-permute-done.3.refs_5_.down.refs_3_), channel_id=1, source_target_pairs={{0,1},{1,0},{2,3},{3,2},{4,5},{5,4},{6,7},{7,6},{8,9},{9,8},{10,11... | collective-permute-start | bytes 1572872 | tf_op jit(solution)/shard_map/ppermute | solution.py:264
  80.0 8.5 %collective-permute-start.9 = (bf16[1024,128]{1,0:T(8,128)(2,1)S(1)}, bf16[1024,128]{1,0:T(8,128)(2,1)S(1)}, u32[]{:S(2)}, u32[]{:S(2)}) collective-permute-start(bf16[1024,128]{1,0:T(8,128)(2,1)S(1)} %get-tuple-element.14.refs_1_), channel_id=1, source_target_pairs={{0,2},{1,3},{2,4},{3,5},{4,6},{5,7},{6,0},{7,1},{8,10},{9,11},{10,... | collective-permute-start | bytes 786440 | tf_op jit(solution)/shard_map/ppermute | solution.py:258
  83.4 6.4 %collective-permute-start.10 = (bf16[1024,128]{1,0:T(8,128)(2,1)S(1)}, bf16[1024,128]{1,0:T(8,128)(2,1)S(1)}, u32[]{:S(2)}, u32[]{:S(2)}) collective-permute-start(bf16[1024,128]{1,0:T(8,128)(2,1)S(1)} %get-tuple-element.20), channel_id=1, source_target_pairs={{0,6},{1,7},{2,0},{3,1},{4,2},{5,3},{6,4},{7,5},{8,14},{9,15},{10,... | collective-permute-start | bytes 786440 | tf_op jit(solution)/shard_map/ppermute | solution.py:258
  85.0 6.4 %collective-permute-start.8 = (bf16[1024,128]{1,0:T(8,128)(2,1)S(1)}, bf16[1024,128]{1,0:T(8,128)(2,1)S(1)}, u32[]{:S(2)}, u32[]{:S(2)}) collective-permute-start(bf16[1024,128]{1,0:T(8,128)(2,1)S(1)} %get-tuple-element.16), channel_id=1, source_target_pairs={{0,192},{8,200},{16,208},{24,216},{32,224},{40,232},{48,240},{56,2... | collective-permute-start | bytes 786440 | tf_op jit(solution)/shard_map/ppermute | solution.py:261
  87.1 7.6 %collective-permute-start.7 = (bf16[1024,128]{1,0:T(8,128)(2,1)S(1)}, bf16[1024,128]{1,0:T(8,128)(2,1)S(1)}, u32[]{:S(2)}, u32[]{:S(2)}) collective-permute-start(bf16[1024,128]{1,0:T(8,128)(2,1)S(1)} %get-tuple-element.15), channel_id=1, source_target_pairs={{0,64},{8,72},{16,80},{24,88},{32,96},{40,104},{48,112},{56,120},{... | collective-permute-start | bytes 786440 | tf_op jit(solution)/shard_map/ppermute | solution.py:261
  89.8 5.5 %collective-permute-start.11 = (bf16[2048,128]{1,0:T(8,128)(2,1)S(1)}, bf16[2048,128]{1,0:T(8,128)(2,1)S(1)}, u32[]{:S(2)}, u32[]{:S(2)}) collective-permute-start(bf16[2048,128]{1,0:T(8,128)(2,1)S(1)} %join.1.own), channel_id=1, source_target_pairs={{0,1},{1,0},{2,3},{3,2},{4,5},{5,4},{6,7},{7,6},{8,9},{9,8},{10,11... | collective-permute-start | bytes 1572872 | tf_op jit(solution)/shard_map/ppermute | solution.py:264
